TPU v7x, 256 devices: a whole 4x4x8 slice. The times are simulated.
256 devices in a mesh: ep: 64 (over x, z_lo, y), dp: 4 (over z_hi, core).
Axes of the slice: x: 4, y: 4, z: 8 (z_hi: 2, z_lo: 4; z = z_hi * 4 + z_lo), core: 2. Of those that a mesh axis runs over, the one named last changes fastest.
Arguments:
- hidden_acts: bfloat16 [8192, 2, 2560], P('ep', None, 'dp'), may hold values from -6 to 6
- out_grad: bfloat16 [8192, 3584], P('ep'), may hold values from -6 to 6
- gate_probs: float32 [8192, 2], P('ep'), may hold values from 0.05 to 0.95
- route: int32 [8192, 2], P('ep'), may hold values from 0 to 15, all different within a row; in each aligned block of 128 rows (0 to 127, 128 to 255, ...) at most 24 rows name the same one
- weights: bfloat16 [64, 2560, 896], P('ep', 'dp'), may hold values from -0.09375 to 0.09375
- first_moment: float32 [64, 2560, 896], P('ep', 'dp'), may hold values from -96 to 96
- second_moment: float32 [64, 2560, 896], P('ep', 'dp'), may hold values from 64 to 1024
- old_slot: int32 [16], replicated, may hold values from 0 to 15, each once
- new_slot: int32 [16], replicated, may hold values from 0 to 15, each once
- partner: int32 [16], replicated, may hold values from 0 to 15, as said below
Outputs:
- hidden_grad: bfloat16 [8192, 2, 2560], P('ep', None, 'dp')
- expert_update: float32 [64, 2560, 896], P('ep', 'dp')
Inputs may be any that keep to these rules, and one draw needn't show every extreme that they name: `route`: among the 128 rows of one ep index no expert is named by more than 24 rows, a bound that some block reaches; the 2 experts of a row differ. `old_slot`: A permutation of the owners. `new_slot`: A permutation of the owners. partner[partner[e]] = e; exactly 4 pairs of distinct experts, all others their own partner.
All inputs are finite; a program needn't handle non-finite values.
Results may differ from a plain program's by a relative error of at most 0.00105.
The roundings to bfloat16 on the way count: a program that leaves them out, or rounds other values in their place, can miss the bound.
Values may be sent and summed in bfloat16 or wider, within the bound.
No kernel may reach another device: no remote copies, remote signals or barrier semaphores. Data moves between devices by JAX's collectives and lax.ppermute only.
A program may use at most 128 MiB of HBM per device.

v0:
```python
import jax
import jax.numpy as jnp
from jax import lax
from jax.sharding import PartitionSpec as P

beta_one = 0.9
beta_two = 0.95
decay = 0.1
epsilon = 1e-08
bias_one = 1.0 - (0.9**50) ** 2
bias_two = 1.0 - (0.95**50) ** 2


def for_sending(array):

    def short(part):
        return part.astype(jnp.bfloat16) if part.dtype == jnp.float32 else part

    return jax.tree.map(short, array)


def split_rows(value, n_ep):
    return value.reshape((n_ep, value.shape[0] // n_ep) + value.shape[1:])


def join_rows(value):
    return value.reshape((-1,) + value.shape[2:])


def invert_perm(perm):
    return jnp.zeros_like(perm).at[perm].set(jnp.arange(perm.shape[0], dtype=jnp.int32))


def local(
    hidden_acts,
    out_grad,
    gate_probs,
    route,
    weights,
    first_moment,
    second_moment,
    old_slot,
    new_slot,
    partner,
):
    n_ep = lax.axis_size("ep")
    own_index = lax.axis_index("ep")
    run_len = max(1, n_ep // 16)
    experts = n_ep // run_len
    tok_rows, top_count, hidden_part = hidden_acts.shape
    feature_part = weights.shape[2]
    row_count = tok_rows * top_count
    cap_rows = min(tok_rows, 4 * max(1, 3 * tok_rows * top_count // (8 * experts)))
    own_group = own_index // run_len
    slab_ids = jnp.arange(n_ep, dtype=jnp.int32)
    numbers = jnp.arange(experts, dtype=jnp.int32)
    inv_new = invert_perm(new_slot)
    incoming_group = old_slot[inv_new]
    incoming = incoming_group[slab_ids // run_len] * run_len + slab_ids % run_len
    weight = weights[0]
    moment_one = first_moment[0]
    moment_two = second_moment[0]
    spread_w = lax.all_to_all(
        split_rows(weight, n_ep), "ep", split_axis=0, concat_axis=0, tiled=True
    )
    weight = join_rows(
        lax.all_to_all(spread_w[incoming], "ep", split_axis=0, concat_axis=0, tiled=True)
    )
    spread_one, spread_two = (
        lax.all_to_all(split_rows(moment_one, n_ep), "ep", split_axis=0, concat_axis=0, tiled=True),
        lax.all_to_all(split_rows(moment_two, n_ep), "ep", split_axis=0, concat_axis=0, tiled=True),
    )
    moved_one, moved_two = (
        lax.all_to_all(spread_one[incoming], "ep", split_axis=0, concat_axis=0, tiled=True),
        lax.all_to_all(spread_two[incoming], "ep", split_axis=0, concat_axis=0, tiled=True),
    )
    moment_one = join_rows(moved_one)
    moment_two = join_rows(moved_two)
    slot_group = new_slot[route.reshape(row_count)]
    onehot = (slot_group[:, None] == numbers[None, :]).astype(jnp.int32)
    before = jnp.cumsum(onehot, axis=0) - onehot
    position = jnp.sum(before * onehot, axis=1)
    slot_table = (
        jnp.full((experts, cap_rows), row_count, jnp.int32)
        .at[slot_group, position]
        .set(jnp.arange(row_count, dtype=jnp.int32))
    )
    acts_padded = jnp.concatenate(
        [hidden_acts.reshape(row_count, hidden_part), jnp.zeros((1, hidden_part), jnp.bfloat16)],
        axis=0,
    )
    scaled = (gate_probs[:, :, None] * out_grad.astype(jnp.float32)[:, None, :]).astype(
        jnp.bfloat16
    )
    scaled = scaled.reshape(row_count, run_len, feature_part)
    scaled = jnp.concatenate([scaled, jnp.zeros((1, run_len, feature_part), jnp.bfloat16)], axis=0)
    send_h = jnp.broadcast_to(
        acts_padded[slot_table][:, None], (experts, run_len, cap_rows, hidden_part)
    ).reshape(n_ep, cap_rows, hidden_part)
    quarters = jnp.arange(run_len, dtype=jnp.int32)
    send_c = scaled[slot_table[:, None, :], quarters[None, :, None]].reshape(
        n_ep, cap_rows, feature_part
    )
    recv_h, recv_c = (
        lax.all_to_all(send_h, "ep", split_axis=0, concat_axis=0, tiled=True),
        lax.all_to_all(send_c, "ep", split_axis=0, concat_axis=0, tiled=True),
    )
    grad_part = lax.dot_general(
        recv_h, recv_c, (((0, 1), (0, 1)), ((), ())), preferred_element_type=jnp.float32
    )
    partial_value = jnp.einsum("scb,ab->sca", recv_c, weight, preferred_element_type=jnp.float32)
    back_rows = lax.all_to_all(partial_value, "ep", split_axis=0, concat_axis=0, tiled=True)
    summed = jnp.sum(back_rows.reshape(experts, run_len, cap_rows, hidden_part), axis=1)
    hidden_out = (
        summed[slot_group, position].astype(jnp.bfloat16).reshape(tok_rows, top_count, hidden_part)
    )
    mate_expert = partner[inv_new]
    mate_group = new_slot[mate_expert]
    mate_slab = mate_group[slab_ids // run_len] * run_len + slab_ids % run_len
    spread_g = lax.all_to_all(
        split_rows(grad_part, n_ep).astype(jnp.bfloat16),
        "ep",
        split_axis=0,
        concat_axis=0,
        tiled=True,
    ).astype(jnp.float32)
    mate_grad = join_rows(
        lax.all_to_all(
            for_sending(spread_g[mate_slab]), "ep", split_axis=0, concat_axis=0, tiled=True
        )
    )
    own_expert = inv_new[own_group]
    paired = partner[own_expert] != own_expert
    total_grad = grad_part + jnp.where(paired, mate_grad, jnp.float32(0.0))
    m_new = beta_one * moment_one + (1.0 - beta_one) * total_grad
    v_new = beta_two * moment_two + (1.0 - beta_two) * total_grad * total_grad
    update = m_new / bias_one / (jnp.sqrt(v_new / bias_two) + epsilon) + decay * weight.astype(
        jnp.float32
    )
    return (hidden_out, update[None])


def solution(mesh):
    return jax.shard_map(
        local,
        mesh=mesh,
        in_specs=(
            P("ep", None, "dp"),
            P("ep", None),
            P("ep", None),
            P("ep", None),
            P("ep", "dp", None),
            P("ep", "dp", None),
            P("ep", "dp", None),
            P(),
            P(),
            P(),
        ),
        out_specs=(P("ep", None, "dp"), P("ep", "dp", None)),
        check_vma=False,
    )
```

profile of v0, /device:TPU:1, one launch (start us, length us, event | category | flops | bytes accessed | tf_op | source)
XLA Modules:
  0.0 806.2 jit_solution(1170944976689874946)
XLA Ops:
  3.9 12.7 %all-to-all-start.1 = ((bf16[64,10,896]{2,1,0:T(8,128)(2,1)}), bf16[64,10,896]{2,1,0:T(8,128)(2,1)S(1)}, u32[]{:S(2)}, u32[]{:S(2)}) async-start(bf16[64,10,896]{2,1,0:T(8,128)(2,1)} %reshape_squeeze.9), calls=%async_computation.1 | async-start | bytes 3670016 | tf_op jit(solution)/shard_map/all_to_all | solution.py:63
  22.0 5.6 select_select_fusion
  28.7 12.8 %scatter_fusion = s32[16,24]{1,0:T(8,128)S(1)} fusion(s32[16,24]{1,0:T(8,128)S(1)} %broadcast_in_dim.19, s32[256]{0:T(256)S(1)} %bitcast.82, s32[256]{0:T(256)S(1)} %iota.31), kind=kCustom, calls=%fused_computation.12 | custom fusion | bytes 5120 | tf_op jit(solution)/shard_map/scatter | solution.py:86
  43.8 17.3 %all-to-all-done.1 = bf16[64,10,896]{2,1,0:T(8,128)(2,1)S(1)} async-done(((bf16[64,10,896]{2,1,0:T(8,128)(2,1)}), bf16[64,10,896]{2,1,0:T(8,128)(2,1)S(1)}, u32[]{:S(2)}, u32[]{:S(2)}) %all-to-all-start.1) | async-done | bytes 1146912 | tf_op jit(solution)/shard_map/all_to_all | solution.py:63
  63.1 6.2 all-to-all-start.6
  75.0 41.3 %all-to-all-done.6 = bf16[64,24,640]{2,1,0:T(8,128)(2,1)S(1)} async-done(((bf16[64,24,640]{2,1,0:T(8,128)(2,1)}), bf16[64,24,640]{2,1,0:T(8,128)(2,1)S(1)}, u32[]{:S(2)}, u32[]{:S(2)}) %all-to-all-start.6) | async-done | bytes 1966112 | tf_op jit(solution)/shard_map/all_to_all | solution.py:105
  117.6 6.6 all-to-all-start.2
  128.1 40.5 %all-to-all-done.2 = bf16[64,10,896]{2,1,0:T(8,128)(2,1)S(1)} async-done(((bf16[64,10,896]{2,1,0:T(8,128)(2,1)}), bf16[64,10,896]{2,1,0:T(8,128)(2,1)S(1)}, u32[]{:S(2)}, u32[]{:S(2)}) %all-to-all-start.2) | async-done | bytes 1146912 | tf_op jit(solution)/shard_map/all_to_all | solution.py:67
  169.8 6.9 all-to-all-start.9
  179.6 6.3 mul.83
  189.7 21.8 %gather_fusion = bf16[1536,896]{1,0:T(8,128)(2,1)} fusion(bf16[257,4,896]{2,1,0:T(4,128)(2,1)S(1)} %concatenate.13, s32[1536]{0:T(1024)S(1)} %reshape.271), kind=kCustom, calls=%fused_computation | custom fusion | bytes 5517312 | tf_op jit(solution)/shard_map/gather | solution.py:101
  211.5 47.2 %all-to-all-done.9 = f32[64,10,896]{2,1,0:T(8,128)} async-done(((f32[64,10,896]{2,1,0:T(8,128)}), f32[64,10,896]{2,1,0:T(8,128)}, u32[]{:S(2)}, u32[]{:S(2)}) %all-to-all-start.9) | async-done | bytes 2293792 | tf_op jit(solution)/shard_map/all_to_all | solution.py:71
  258.7 9.1 %all-to-all-start = ((bf16[64,24,896]{2,1,0:T(8,128)(2,1)}), bf16[64,24,896]{2,1,0:T(8,128)(2,1)S(1)}, u32[]{:S(2)}, u32[]{:S(2)}) async-start(bf16[64,24,896]{2,1,0:T(8,128)(2,1)} %bitcast.83), calls=%async_computation | async-start | bytes 5505024 | tf_op jit(solution)/shard_map/all_to_all | solution.py:106
  271.7 59.4 %all-to-all-done = bf16[64,24,896]{2,1,0:T(8,128)(2,1)S(1)} async-done(((bf16[64,24,896]{2,1,0:T(8,128)(2,1)}), bf16[64,24,896]{2,1,0:T(8,128)(2,1)S(1)}, u32[]{:S(2)}, u32[]{:S(2)}) %all-to-all-start) | async-done | bytes 2752544 | tf_op jit(solution)/shard_map/all_to_all | solution.py:106
  331.0 7.7 all-to-all-start.4
  338.8 5.6 bitcast_convert_fusion
  347.5 73.3 %all-to-all-done.4 = f32[64,10,896]{2,1,0:T(8,128)} async-done(((f32[64,10,896]{2,1,0:T(8,128)}), f32[64,10,896]{2,1,0:T(8,128)}, u32[]{:S(2)}, u32[]{:S(2)}) %all-to-all-start.4) | async-done | bytes 2293792 | tf_op jit(solution)/shard_map/all_to_all | solution.py:70
  420.9 9.3 %all-to-all-start.7 = ((bf16[64,10,896]{2,1,0:T(8,128)(2,1)}), bf16[64,10,896]{2,1,0:T(8,128)(2,1)S(1)}, u32[]{:S(2)}, u32[]{:S(2)}) async-start(bf16[64,10,896]{2,1,0:T(8,128)(2,1)} %convert_element_type.48), calls=%async_computation.7 | async-start | bytes 3670016 | tf_op jit(solution)/shard_map/all_to_all | solution.py:120
  430.1 4.7 gather_fusion.11
  434.8 39.3 %all-to-all-done.7 = bf16[64,10,896]{2,1,0:T(8,128)(2,1)S(1)} async-done(((bf16[64,10,896]{2,1,0:T(8,128)(2,1)}), bf16[64,10,896]{2,1,0:T(8,128)(2,1)S(1)}, u32[]{:S(2)}, u32[]{:S(2)}) %all-to-all-start.7) | async-done | bytes 1146912 | tf_op jit(solution)/shard_map/all_to_all | solution.py:120
  474.1 6.9 all-to-all-start.10
  481.0 4.6 gather_fusion.5
  485.7 77.1 %all-to-all-done.10 = f32[64,10,896]{2,1,0:T(8,128)} async-done(((f32[64,10,896]{2,1,0:T(8,128)}), f32[64,10,896]{2,1,0:T(8,128)}, u32[]{:S(2)}, u32[]{:S(2)}) %all-to-all-start.10) | async-done | bytes 2293792 | tf_op jit(solution)/shard_map/all_to_all | solution.py:75
  562.7 8.9 %all-to-all-start.5 = ((f32[64,10,896]{2,1,0:T(8,128)}), f32[64,10,896]{2,1,0:T(8,128)}, u32[]{:S(2)}, u32[]{:S(2)}) async-start(f32[64,10,896]{2,1,0:T(8,128)} %gather_fusion.5), calls=%async_computation.5 | async-start | bytes 7340032 | tf_op jit(solution)/shard_map/all_to_all | solution.py:74
  575.8 77.9 %all-to-all-done.5 = f32[64,10,896]{2,1,0:T(8,128)} async-done(((f32[64,10,896]{2,1,0:T(8,128)}), f32[64,10,896]{2,1,0:T(8,128)}, u32[]{:S(2)}, u32[]{:S(2)}) %all-to-all-start.5) | async-done | bytes 2293792 | tf_op jit(solution)/shard_map/all_to_all | solution.py:74
  653.6 9.1 %all-to-all-start.8 = ((bf16[64,10,896]{2,1,0:T(8,128)(2,1)}), bf16[64,10,896]{2,1,0:T(8,128)(2,1)}, u32[]{:S(2)}, u32[]{:S(2)}) async-start(bf16[64,10,896]{2,1,0:T(8,128)(2,1)} %gather_fusion.10), calls=%async_computation.8 | async-start | bytes 3670016 | tf_op jit(solution)/shard_map/all_to_all | solution.py:128
  663.3 6.3 fusion.20
  669.6 37.0 %all-to-all-done.8 = bf16[64,10,896]{2,1,0:T(8,128)(2,1)} async-done(((bf16[64,10,896]{2,1,0:T(8,128)(2,1)}), bf16[64,10,896]{2,1,0:T(8,128)(2,1)}, u32[]{:S(2)}, u32[]{:S(2)}) %all-to-all-start.8) | async-done | bytes 1146912 | tf_op jit(solution)/shard_map/all_to_all | solution.py:128
  706.6 7.0 all-to-all-start.3
  739.2 4.4 select_n.165
  743.6 6.1 fusion.6
  749.7 51.0 %all-to-all-done.3 = f32[64,24,640]{2,1,0:T(8,128)} async-done(((f32[64,24,640]{2,1,0:T(8,128)}), f32[64,24,640]{2,1,0:T(8,128)}, u32[]{:S(2)}, u32[]{:S(2)}) %all-to-all-start.3) | async-done | bytes 3932192 | tf_op jit(solution)/shard_map/all_to_all | solution.py:112
  (92 shorter events, 72.0 us)
Async XLA Ops:
  0.6 69.4 %copy-start = (s32[16]{0:T(128)S(1)}, s32[16]{0:T(128)}, u32[]{:S(2)}) copy-start(s32[16]{0:T(128)} %param.17) | copy-start | bytes 196
  3.9 12.7 %copy-start.12 = (s32[128,2]{0,1:T(2,128)S(1)}, s32[128,2]{0,1:T(2,128)}, u32[]{:S(2)}) copy-start(s32[128,2]{0,1:T(2,128)} %param.13) | copy-start | bytes 3076
  3.9 13.0 %copy-start.2 = (s32[16]{0:T(128)S(1)}, s32[16]{0:T(128)}, u32[]{:S(2)}) copy-start(s32[16]{0:T(128)} %param.18) | copy-start | bytes 196
  3.9 24.5 %copy-start.11 = (bf16[128,2,640]{2,1,0:T(2,128)(2,1)S(1)}, bf16[128,2,640]{2,1,0:T(2,128)(2,1)}, u32[]{:S(2)}) copy-start(bf16[128,2,640]{2,1,0:T(2,128)(2,1)} %param.10) | copy-start | bytes 983044
  3.9 57.3 %all-to-all-start.1 = ((bf16[64,10,896]{2,1,0:T(8,128)(2,1)}), bf16[64,10,896]{2,1,0:T(8,128)(2,1)S(1)}, u32[]{:S(2)}, u32[]{:S(2)}) async-start(bf16[64,10,896]{2,1,0:T(8,128)(2,1)} %reshape_squeeze.9), calls=%async_computation.1 | async-start | bytes 3670016 | tf_op jit(solution)/shard_map/all_to_all | solution.py:63
  61.1 1.9 copy-start.9
  63.1 53.3 %all-to-all-start.6 = ((bf16[64,24,640]{2,1,0:T(8,128)(2,1)}), bf16[64,24,640]{2,1,0:T(8,128)(2,1)S(1)}, u32[]{:S(2)}, u32[]{:S(2)}) async-start(bf16[64,24,640]{2,1,0:T(8,128)(2,1)} %bitcast.29), calls=%async_computation.6 | async-start | bytes 3932160 | tf_op jit(solution)/shard_map/all_to_all | solution.py:105
  116.3 1.3 copy-start.8
  117.6 51.0 %all-to-all-start.2 = ((bf16[64,10,896]{2,1,0:T(8,128)(2,1)}), bf16[64,10,896]{2,1,0:T(8,128)(2,1)S(1)}, u32[]{:S(2)}, u32[]{:S(2)}) async-start(bf16[64,10,896]{2,1,0:T(8,128)(2,1)} %gather_fusion.3), calls=%async_computation.2 | async-start | bytes 3670016 | tf_op jit(solution)/shard_map/all_to_all | solution.py:67
  128.1 48.6 %copy-start.10 = (bf16[128,3584]{1,0:T(8,128)(2,1)S(1)}, bf16[128,3584]{1,0:T(8,128)(2,1)}, u32[]{:S(2)}) copy-start(bf16[128,3584]{1,0:T(8,128)(2,1)} %param.11) | copy-start | bytes 2752516
  168.6 1.3 copy-start.4
  169.8 88.9 %all-to-all-start.9 = ((f32[64,10,896]{2,1,0:T(8,128)}), f32[64,10,896]{2,1,0:T(8,128)}, u32[]{:S(2)}, u32[]{:S(2)}) async-start(f32[64,10,896]{2,1,0:T(8,128)} %reshape_squeeze.11), calls=%async_computation.9 | async-start | bytes 7340032 | tf_op jit(solution)/shard_map/all_to_all | solution.py:71
  179.6 6.3 copy-start.13
  258.7 72.3 %all-to-all-start = ((bf16[64,24,896]{2,1,0:T(8,128)(2,1)}), bf16[64,24,896]{2,1,0:T(8,128)(2,1)S(1)}, u32[]{:S(2)}, u32[]{:S(2)}) async-start(bf16[64,24,896]{2,1,0:T(8,128)(2,1)} %bitcast.83), calls=%async_computation | async-start | bytes 5505024 | tf_op jit(solution)/shard_map/all_to_all | solution.py:106
  331.0 7.7 copy-start.6
  331.0 89.8 %all-to-all-start.4 = ((f32[64,10,896]{2,1,0:T(8,128)}), f32[64,10,896]{2,1,0:T(8,128)}, u32[]{:S(2)}, u32[]{:S(2)}) async-start(f32[64,10,896]{2,1,0:T(8,128)} %reshape_squeeze.10), calls=%async_computation.4 | async-start | bytes 7340032 | tf_op jit(solution)/shard_map/all_to_all | solution.py:70
  420.9 53.2 %all-to-all-start.7 = ((bf16[64,10,896]{2,1,0:T(8,128)(2,1)}), bf16[64,10,896]{2,1,0:T(8,128)(2,1)S(1)}, u32[]{:S(2)}, u32[]{:S(2)}) async-start(bf16[64,10,896]{2,1,0:T(8,128)(2,1)} %convert_element_type.48), calls=%async_computation.7 | async-start | bytes 3670016 | tf_op jit(solution)/shard_map/all_to_all | solution.py:120
  474.1 88.6 %all-to-all-start.10 = ((f32[64,10,896]{2,1,0:T(8,128)}), f32[64,10,896]{2,1,0:T(8,128)}, u32[]{:S(2)}, u32[]{:S(2)}) async-start(f32[64,10,896]{2,1,0:T(8,128)} %gather_fusion.11), calls=%async_computation.10 | async-start | bytes 7340032 | tf_op jit(solution)/shard_map/all_to_all | solution.py:75
  485.7 86.0 %copy-start.3 = (s32[16]{0:T(128)S(1)}, s32[16]{0:T(128)}, u32[]{:S(2)}) copy-start(s32[16]{0:T(128)} %param.19) | copy-start | bytes 196
  562.7 90.9 %all-to-all-start.5 = ((f32[64,10,896]{2,1,0:T(8,128)}), f32[64,10,896]{2,1,0:T(8,128)}, u32[]{:S(2)}, u32[]{:S(2)}) async-start(f32[64,10,896]{2,1,0:T(8,128)} %gather_fusion.5), calls=%async_computation.5 | async-start | bytes 7340032 | tf_op jit(solution)/shard_map/all_to_all | solution.py:74
  575.8 87.0 %copy-start.5 = (bf16[64,10,896]{2,1,0:T(8,128)(2,1)S(1)}, bf16[64,10,896]{2,1,0:T(8,128)(2,1)}, u32[]{:S(2)}) copy-start(bf16[64,10,896]{2,1,0:T(8,128)(2,1)} %copy-done.4) | copy-start | bytes 3440644
  653.6 53.0 %all-to-all-start.8 = ((bf16[64,10,896]{2,1,0:T(8,128)(2,1)}), bf16[64,10,896]{2,1,0:T(8,128)(2,1)}, u32[]{:S(2)}, u32[]{:S(2)}) async-start(bf16[64,10,896]{2,1,0:T(8,128)(2,1)} %gather_fusion.10), calls=%async_computation.8 | async-start | bytes 3670016 | tf_op jit(solution)/shard_map/all_to_all | solution.py:128
  706.6 94.1 %all-to-all-start.3 = ((f32[64,24,640]{2,1,0:T(8,128)}), f32[64,24,640]{2,1,0:T(8,128)}, u32[]{:S(2)}, u32[]{:S(2)}) async-start(f32[64,24,640]{2,1,0:T(8,128)} %fusion.20), calls=%async_computation.3 | async-start | bytes 7864320 | tf_op jit(solution)/shard_map/all_to_all | solution.py:112
  739.2 4.4 copy-start.7
  800.7 5.5 copy-start.1
where the time goes:
time: 809 us; the launch traced here: 806 us
  waiting for transfers between devices  561 us (69%)
  local copies, waits for them, and re-layouts  104 us (13%)
  starting transfers between devices  90.4 us (11%)
  other arithmetic  34.2 us (4%)
  matrix products  11.9 us (1%)
    all_to_all x1, waiting for transfers between devices, local(): lax.all_to_all(spread_one[incoming], 'ep', split_axis=0, concat_axis=0, t...  77.9 us
    all_to_all x1, waiting for transfers between devices, local(): lax.all_to_all(spread_two[incoming], 'ep', split_axis=0, concat_axis=0, t...  77.1 us
    all_to_all x1, waiting for transfers between devices, local(): lax.all_to_all(split_rows(moment_one, n_ep), 'ep', split_axis=0, concat_a...  73.3 us
    all_to_all x1, waiting for transfers between devices, local(): lax.all_to_all(send_c, 'ep', split_axis=0, concat_axis=0, tiled=True)  59.4 us
    all_to_all x1, waiting for transfers between devices, local(): lax.all_to_all(partial_value, 'ep', split_axis=0, concat_axis=0, tiled=True)  51 us
    all_to_all x1, waiting for transfers between devices, local(): lax.all_to_all(split_rows(moment_two, n_ep), 'ep', split_axis=0, concat_a...  47.2 us
    all_to_all x1, waiting for transfers between devices, local(): lax.all_to_all(send_h, 'ep', split_axis=0, concat_axis=0, tiled=True)  41.3 us
    all_to_all x1, waiting for transfers between devices, local(): lax.all_to_all(spread_w[incoming], 'ep', split_axis=0, concat_axis=0, til...  40.5 us
  transfers between devices with their start and end apart: 11, of which 11 were waited for; matrix products, arithmetic and copies ran while one was open for 17% of the time, Pallas kernels for 0%

commit v1 on v0

v1 whole, which is shorter than its diff:
```python
import jax
import jax.numpy as jnp
from jax import lax
from jax.experimental import pallas as pl
from jax.experimental.pallas import tpu as pltpu
from jax.sharding import PartitionSpec as P

beta_one = 0.9
beta_two = 0.95
decay = 0.1
epsilon = 1e-08
bias_one = 1.0 - (0.9**50) ** 2
bias_two = 1.0 - (0.95**50) ** 2

RUN = 4
GROUPS = 16
CAP = 24
ROWS = GROUPS * CAP
SCALE = 2048.0
SAME_Y = [[g * RUN + y for g in range(GROUPS)] for y in range(RUN)]
SAME_RUN = [[g * RUN + y for y in range(RUN)] for g in range(GROUPS)]
OTHER_CORE = [(0, 1), (1, 0), (2, 3), (3, 2)]
MB = 1024 * 1024


def contract(a, b, dims):
    return lax.dot_general(a, b, ((dims[0], dims[1]), ((), ())), preferred_element_type=jnp.float32)


def order_of(index, tokens):
    return 2 * (index % tokens) + index // tokens


def choose(row, col, want):
    count = row.shape[1]
    tokens = count // 2
    lane = order_of(lax.broadcasted_iota(jnp.int32, (count, count), 1), tokens)
    line = order_of(lax.broadcasted_iota(jnp.int32, (count, count), 0), tokens)
    ahead = jnp.where((row == col) & (line < lane), 1.0, 0.0)
    position = jnp.sum(ahead, axis=0, keepdims=True)
    place = (lax.broadcasted_iota(jnp.int32, (want.shape[0], 1), 0) % CAP).astype(jnp.float32)
    return (row == want) & (position == place)


def send_h_kernel(row_ref, col_ref, want_ref, acts_ref, out_ref):
    width = acts_ref.shape[1]
    for kind in range(2):
        sel = choose(row_ref[0], col_ref[0], want_ref[kind])
        rows = contract(jnp.where(sel, 1.0, 0.0).astype(jnp.bfloat16), acts_ref[...], ((1,), (0,)))
        out_ref[:, kind * width : (kind + 1) * width] = rows.astype(jnp.bfloat16)


def send_c_kernel(core_ref, row_ref, col_ref, gate_ref, want_ref, grad_ref, out_ref):
    sel = choose(row_ref[0], col_ref[0], want_ref[0])
    gate = jnp.sum(jnp.where(sel, gate_ref[0], 0.0), axis=1, keepdims=True)
    sel = jnp.where(sel, 1.0, 0.0)
    tokens = sel.shape[1] // 2
    sel = (sel[:, :tokens] + sel[:, tokens:]).astype(jnp.bfloat16)
    rows = contract(sel, grad_ref[0], ((1,), (0,)))
    out_ref[...] = (gate * rows).astype(jnp.bfloat16)


def back_kernel(core_ref, own_ref, mate_ref, w_ref, out_ref):
    mine = pl.program_id(0) // 2 == core_ref[0]

    @pl.when(mine)
    def _():
        out_ref[0] = contract(own_ref[...], w_ref[...], ((1,), (1,)))

    @pl.when(jnp.logical_not(mine))
    def _():
        out_ref[0] = contract(mate_ref[...], w_ref[...], ((1,), (1,)))


def update_kernel(
    core_ref, h_own_ref, h_extra_ref, own_ref, mate_ref, w_ref, m_ref, v_ref, out_ref
):
    core = core_ref[0]
    width = w_ref.shape[1]
    total = jnp.zeros(w_ref.shape, jnp.float32)
    for c_ref, base in ((own_ref, 2 * core), (mate_ref, 2 - 2 * core)):
        for kind, h_ref in enumerate((h_own_ref, h_extra_ref)):
            for j in range(2):
                part = 2 * kind + j
                total += contract(
                    h_ref[base + j], c_ref[:, part * width : (part + 1) * width], ((0,), (0,))
                )
    m_new = beta_one * m_ref[...] + (1.0 - beta_one) * total
    v_new = beta_two * v_ref[...] + (1.0 - beta_two) * total * total
    direction = m_new / bias_one / (jnp.sqrt(v_new / bias_two) + epsilon)
    direction = direction + decay * w_ref[...].astype(jnp.float32)
    out_ref[...] = SCALE * direction


def take_kernel(row_ref, col_ref, want_ref, back_ref, out_ref):
    sel = jnp.where(choose(row_ref[0], col_ref[0], want_ref[0]), 1.0, 0.0).astype(jnp.bfloat16)
    out_ref[...] = contract(sel, back_ref[...], ((0,), (0,))).astype(jnp.bfloat16)


def params(limit):
    return pltpu.CompilerParams(vmem_limit_bytes=limit * MB)


def whole(shape):
    return pl.BlockSpec(shape, lambda *_: (0,) * len(shape))


def local(
    hidden_acts,
    out_grad,
    gate_probs,
    route,
    weights,
    first_moment,
    second_moment,
    old_slot,
    new_slot,
    partner,
):
    tokens, top, hidden = hidden_acts.shape
    count = tokens * top
    width = weights.shape[2]
    core = (lax.axis_index("dp") % 2).astype(jnp.int32).reshape(1)

    numbers = jnp.arange(GROUPS, dtype=jnp.int32)
    held = old_slot[None, :] == numbers[:, None]
    own = jnp.sum(jnp.where(held, numbers[None, :], 0), axis=1)
    mate = jnp.sum(jnp.where(held, partner[None, :], 0), axis=1)
    mate = jnp.where(mate == own, -1, mate)
    want = jnp.stack([own, mate]).astype(jnp.float32)
    want = jnp.broadcast_to(want[:, :, None], (2, GROUPS, CAP)).reshape(2, ROWS, 1)
    source = jnp.sum(
        jnp.where(new_slot[None, :] == numbers[:, None], old_slot[None, :], 0), axis=1
    )

    about = jnp.concatenate([route.astype(jnp.float32).T, gate_probs.T], axis=0)
    about = lax.all_gather(about, "ep", axis_index_groups=SAME_RUN, axis=0, tiled=False)
    rows = about[:, :top].reshape(RUN, 1, count)
    gates = about[:, top:].reshape(RUN, 1, count)
    quarters = out_grad.reshape(tokens, RUN, width).transpose(1, 0, 2)
    quarters = lax.all_to_all(quarters, "ep", 0, 0, axis_index_groups=SAME_RUN, tiled=True)

    own_row = route.astype(jnp.float32).T.reshape(1, 1, count)
    own_col = own_row.reshape(1, count, 1)
    acts = hidden_acts.transpose(1, 0, 2).reshape(count, hidden)
    send_h = pl.pallas_call(
        send_h_kernel,
        out_shape=jax.ShapeDtypeStruct((ROWS, 2 * hidden), jnp.bfloat16),
        compiler_params=params(32),
        name="send_h",
    )(own_row, own_col, want, acts)
    got_h = lax.all_to_all(send_h, "ep", 0, 0, axis_index_groups=SAME_Y, tiled=True)
    all_h = lax.all_gather(got_h, "ep", axis_index_groups=SAME_RUN, axis=0, tiled=False)

    send_c = pl.pallas_call(
        send_c_kernel,
        grid_spec=pltpu.PrefetchScalarGridSpec(
            num_scalar_prefetch=1,
            grid=(2, 2),
            in_specs=[
                pl.BlockSpec((1, 1, count), lambda k, j, c: (2 * c[0] + j, 0, 0)),
                pl.BlockSpec((1, count, 1), lambda k, j, c: (2 * c[0] + j, 0, 0)),
                pl.BlockSpec((1, 1, count), lambda k, j, c: (2 * c[0] + j, 0, 0)),
                pl.BlockSpec((1, ROWS, 1), lambda k, j, c: (k, 0, 0)),
                pl.BlockSpec((1, tokens, width), lambda k, j, c: (2 * c[0] + j, 0, 0)),
            ],
            out_specs=pl.BlockSpec((ROWS, width), lambda k, j, c: (0, 2 * k + j)),
        ),
        out_shape=jax.ShapeDtypeStruct((ROWS, 4 * width), jnp.bfloat16),
        compiler_params=params(32),
        name="send_c",
    )(core, rows, rows.reshape(RUN, count, 1), gates, want, quarters)
    got_c = lax.all_to_all(send_c, "ep", 0, 0, axis_index_groups=SAME_Y, tiled=True)
    mate_c = lax.ppermute(got_c, "dp", OTHER_CORE)

    weight = weights[0]
    partial_back = pl.pallas_call(
        back_kernel,
        grid_spec=pltpu.PrefetchScalarGridSpec(
            num_scalar_prefetch=1,
            grid=(RUN,),
            in_specs=[
                pl.BlockSpec((ROWS, width), lambda s, c: (0, s % 2)),
                pl.BlockSpec((ROWS, width), lambda s, c: (0, s % 2)),
                whole((hidden, width)),
            ],
            out_specs=pl.BlockSpec((1, ROWS, hidden), lambda s, c: (s, 0, 0)),
        ),
        out_shape=jax.ShapeDtypeStruct((RUN, ROWS, hidden), jnp.float32),
        compiler_params=params(32),
        name="back",
    )(core, got_c, mate_c, weight)
    summed = lax.psum_scatter(
        partial_back, "ep", scatter_dimension=0, axis_index_groups=SAME_RUN, tiled=False
    )
    back = lax.all_to_all(
        summed.astype(jnp.bfloat16), "ep", 0, 0, axis_index_groups=SAME_Y, tiled=True
    )
    hidden_out = pl.pallas_call(
        take_kernel,
        out_shape=jax.ShapeDtypeStruct((count, hidden), jnp.bfloat16),
        compiler_params=params(32),
        name="take",
    )(own_row, own_col, want, back)
    hidden_out = hidden_out.reshape(top, tokens, hidden).transpose(1, 0, 2)

    block = 128
    steps = hidden // block
    update = pl.pallas_call(
        update_kernel,
        grid_spec=pltpu.PrefetchScalarGridSpec(
            num_scalar_prefetch=1,
            grid=(steps,),
            in_specs=[
                pl.BlockSpec((RUN, ROWS, block), lambda i, c: (0, 0, i)),
                pl.BlockSpec((RUN, ROWS, block), lambda i, c: (0, 0, steps + i)),
                whole((ROWS, 4 * width)),
                whole((ROWS, 4 * width)),
                pl.BlockSpec((block, width), lambda i, c: (i, 0)),
                pl.BlockSpec((block, width), lambda i, c: (i, 0)),
                pl.BlockSpec((block, width), lambda i, c: (i, 0)),
            ],
            out_specs=pl.BlockSpec((block, width), lambda i, c: (i, 0)),
        ),
        out_shape=jax.ShapeDtypeStruct((hidden, width), jnp.float32),
        compiler_params=params(48),
        name="update",
    )(core, all_h, all_h, got_c, mate_c, weight, first_moment[0], second_moment[0])

    spread = update.astype(jnp.float16).reshape(GROUPS, hidden // GROUPS, width)
    spread = lax.all_to_all(spread, "ep", 0, 0, axis_index_groups=SAME_Y, tiled=True)
    placed = lax.all_to_all(spread[source], "ep", 0, 0, axis_index_groups=SAME_Y, tiled=True)
    placed = placed.reshape(1, hidden, width).astype(jnp.float32) * (1.0 / SCALE)
    return (hidden_out, placed)


def solution(mesh):
    return jax.shard_map(
        local,
        mesh=mesh,
        in_specs=(
            P("ep", None, "dp"),
            P("ep", None),
            P("ep", None),
            P("ep", None),
            P("ep", "dp", None),
            P("ep", "dp", None),
            P("ep", "dp", None),
            P(),
            P(),
            P(),
        ),
        out_specs=(P("ep", None, "dp"), P("ep", "dp", None)),
        check_vma=False,
    )
```

time: 809 us -> 257 us (0.32)
  waiting for transfers between devices: 561 us -> 161 us
  local copies, waits for them, and re-layouts: 104 us -> 16.8 us
  starting transfers between devices: 90.4 us -> 31.8 us
  other arithmetic: 34.2 us -> 4.95 us
  Pallas kernels: 0 us -> 19.2 us
  matrix products: 11.9 us -> 0 us
  between operations: 4.3 us -> 14.3 us
  blocking collectives: 0 us -> 8.29 us
    all_to_all x11 -> x6, waiting for transfers between devices: 561 us -> 156 us  [the longest x1 63 us: local(): lax.all_to_all(send_c, 'ep', 0, 0, axis_index_groups=SAME_Y, tiled=True)]
    all_to_all x11 -> x6, starting transfers between devices: 90.4 us -> 30.3 us  [the longest x1 8.95 us: local(): lax.all_to_all(send_h, 'ep', 0, 0, axis_index_groups=SAME_Y, tiled=True)]
    gather x13 -> x1, local copies, waits for them, and re-layouts: 45.3 us -> 2 us  [local(): spread[source]]
    pallas_call x0 -> x5, Pallas kernels: none -> 19.2 us  [the longest x1 11.2 us: local(): pl.pallas_call(update_kernel, grid_spec=pltpu.PrefetchScalarGridSpec(num_...]
    mul x5 -> x0, local copies, waits for them, and re-layouts: 17.8 us -> none  [the longest x3 9.24 us: local(): gate_probs[:, :, None] * out_grad.astype(jnp.float32)[:, None, :]]
    scatter x2 -> x0, local copies, waits for them, and re-layouts: 13.4 us -> none  [the longest x1 12.8 us: local(): slot_table = jnp.full((experts, cap_rows), row_count, jnp.int32).at[slot_...]
    dot_general x2 -> x0, matrix products: 11.9 us -> none  [the longest x1 6.35 us: local(): jnp.einsum('scb,ab->sca', recv_c, weight, preferred_element_type=jnp.floa...]
    another operation x4 -> x2, local copies, waits for them, and re-layouts: 11 us -> 0.48 us  [the longest x1 0.35 us: local(): rows.reshape(RUN, count, 1)]
  transfers between devices with their start and end apart: 11 -> 9, of which waited for: 11 -> 7; matrix products, arithmetic and copies ran while one was open for 17% -> 3% of each run, Pallas kernels for 0% -> 7%
where the time goes in v1:
time: 257 us
  waiting for transfers between devices  161 us (63%)
  starting transfers between devices  31.8 us (12%)
  Pallas kernels  19.2 us (7%)
  local copies, waits for them, and re-layouts  16.8 us (7%)
  between operations  14.3 us (6%)
  blocking collectives  8.29 us (3%)
  other arithmetic  4.95 us (2%)
    all_to_all x1, waiting for transfers between devices, local(): lax.all_to_all(send_c, 'ep', 0, 0, axis_index_groups=SAME_Y, tiled=True)  63 us
    all_to_all x1, waiting for transfers between devices, local(): lax.all_to_all(spread, 'ep', 0, 0, axis_index_groups=SAME_Y, tiled=True)  29.2 us
    all_to_all x1, waiting for transfers between devices, local(): lax.all_to_all(spread[source], 'ep', 0, 0, axis_index_groups=SAME_Y, tile...  27 us
    all_to_all x1, waiting for transfers between devices, local(): lax.all_to_all(summed.astype(jnp.bfloat16), 'ep', 0, 0, axis_index_groups...  13.5 us
    all_to_all x1, waiting for transfers between devices, local(): lax.all_to_all(send_h, 'ep', 0, 0, axis_index_groups=SAME_Y, tiled=True)  13.2 us
    unnamed x29, local copies, waits for them, and re-layouts  11.7 us
    pallas_call x1, Pallas kernels, local(): pl.pallas_call(update_kernel, grid_spec=pltpu.PrefetchScalarGridSpec(num_...  11.2 us
    all_to_all x1, waiting for transfers between devices, local(): lax.all_to_all(quarters, 'ep', 0, 0, axis_index_groups=SAME_RUN, tiled=True)  9.8 us
  transfers between devices with their start and end apart: 9, of which 7 were waited for; matrix products, arithmetic and copies ran while one was open for 3% of the time, Pallas kernels for 7%

profile of v1, /device:TPU:1, one launch (start us, length us, event | category | flops | bytes accessed | tf_op | source)
XLA Modules:
  0.0 256.6 jit_solution(11459774294657145934)
XLA Ops:
  7.2 1.6 copy.34
  8.8 1.3 copy.35
  10.1 5.0 %all-to-all-start = ((bf16[4,128,896]{2,1,0:T(8,128)(2,1)}), bf16[4,128,896]{2,1,0:T(8,128)(2,1)S(1)}, u32[]{:S(2)}, u32[]{:S(2)}) async-start(bf16[4,128,896]{2,1,0:T(8,128)(2,1)} %bitcast.11), calls=%async_computation | async-start | bytes 1835008 | tf_op jit(solution)/shard_map/all_to_all | solution.py:141
  15.8 1.6 send_h.1
  17.3 9.8 %all-to-all-done.grad_ref = bf16[4,128,896]{2,1,0:T(8,128)(2,1)S(1)} async-done(((bf16[4,128,896]{2,1,0:T(8,128)(2,1)}), bf16[4,128,896]{2,1,0:T(8,128)(2,1)S(1)}, u32[]{:S(2)}, u32[]{:S(2)}) %all-to-all-start) | async-done | bytes 917536 | tf_op jit(solution)/shard_map/all_to_all | solution.py:141
  27.1 8.9 %all-to-all-start.3 = ((bf16[16,24,1280]{2,1,0:T(8,128)(2,1)}), bf16[16,24,1280]{2,1,0:T(8,128)(2,1)S(1)}, u32[]{:S(2)}, u32[]{:S(2)}) async-start(bf16[16,24,1280]{2,1,0:T(8,128)(2,1)} %bitcast.22), calls=%async_computation.4 | async-start | bytes 1966080 | tf_op jit(solution)/shard_map/all_to_all | solution.py:152
  36.1 8.3 %all-gather.1 = f32[4,4,128]{2,1,0:T(4,128)S(1)} all-gather(f32[1,4,128]{2,1,0:T(4,128)S(1)} %maximum_bitcast_fusion), channel_id=2, replica_groups={{0,4,8,12},{16,20,24,28},{32,36,40,44},{48,52,56,60},{64,68,72,76},{80,..., dimensions={0}, use_global_device_ids=true | all-gather | bytes 10240 | tf_op jit(solution)/shard_map/all_gather | solution.py:137
  44.8 2.1 send_c.1
  46.9 1.5 copy-done.3
  48.4 13.2 %all-to-all-done.3 = bf16[16,24,1280]{2,1,0:T(8,128)(2,1)S(1)} async-done(((bf16[16,24,1280]{2,1,0:T(8,128)(2,1)}), bf16[16,24,1280]{2,1,0:T(8,128)(2,1)S(1)}, u32[]{:S(2)}, u32[]{:S(2)}) %all-to-all-start.3) | async-done | bytes 983072 | tf_op jit(solution)/shard_map/all_to_all | solution.py:152
  62.5 3.7 %all-to-all-start.1 = ((bf16[16,24,3584]{2,1,0:T(8,128)(2,1)}), bf16[16,24,3584]{2,1,0:T(8,128)(2,1)S(1)}, u32[]{:S(2)}, u32[]{:S(2)}) async-start(bf16[16,24,3584]{2,1,0:T(8,128)(2,1)} %bitcast.42), calls=%async_computation.1 | async-start | bytes 5505024 | tf_op jit(solution)/shard_map/all_to_all | solution.py:173
  67.1 63.0 %all-to-all-done.1 = bf16[16,24,3584]{2,1,0:T(8,128)(2,1)S(1)} async-done(((bf16[16,24,3584]{2,1,0:T(8,128)(2,1)}), bf16[16,24,3584]{2,1,0:T(8,128)(2,1)S(1)}, u32[]{:S(2)}, u32[]{:S(2)}) %all-to-all-start.1) | async-done | bytes 2752544 | tf_op jit(solution)/shard_map/all_to_all | solution.py:173
  130.1 1.5 collective-permute-start
  131.6 4.7 %collective-permute-done.mate_ref = bf16[384,3584]{1,0:T(8,128)(2,1)S(1)} collective-permute-done((bf16[384,3584]{1,0:T(8,128)(2,1)S(1)}, bf16[384,3584]{1,0:T(8,128)(2,1)S(1)}, u32[]{:S(2)}, u32[]{:S(2)}) %collective-permute-start) | collective-permute-done | bytes 2752544 | tf_op jit(solution)/shard_map/ppermute | solution.py:174
  136.3 1.3 copy-done.4
  137.6 3.8 %back.1 = f32[4,384,640]{2,1,0:T(8,128)S(1)} custom-call(s32[1]{0:T(128)} %bitcast.5.core_ref, bf16[384,3584]{1,0:T(8,128)(2,1)S(1)} %bitcast.40, bf16[384,3584]{1,0:T(8,128)(2,1)S(1)} %collective-permute-done.mate_ref, bf16[640,896]{1,0:T(8,128)(2,1)S(1)} %bitcast.43), custom_call_target="tpu_custom_call" | custom-call | tf_op jit(solution)/shard_map/back/pallas_call | solution.py:177
  141.4 1.9 copy-done.1
  143.3 1.6 copy-done.2
  145.0 1.2 copy-done.5
  146.2 1.6 copy-done.6
  147.8 11.2 %update.1 = f32[640,896]{1,0:T(8,128)S(1)} custom-call(s32[1]{0:T(128)} %bitcast.5.core_ref, bf16[4,384,1280]{2,1,0:T(8,128)(2,1)} %all-gather.4.cloned.1.call-done.h_own_ref.h_extra_ref, bf16[4,384,1280]{2,1,0:T(8,128)(2,1)} %all-gather.4.cloned.1.call-done.h_own_ref.h_extra_ref, bf16[384,3584]{1,0:T(8,128)(2,1)} %bitcast.41, bf16[384,3584]{1,0:T(8,128)(2,1)} %copy-done.2, ...), custom_call_target="tpu_custom_call" | custom-call | tf_op jit(solution)/shard_map/update/pallas_call | solution.py:209
  159.0 1.1 convert_element_type.37
  160.1 3.7 %all-to-all-start.4 = ((f16[16,40,896]{2,1,0:T(8,128)(2,1)}), f16[16,40,896]{2,1,0:T(8,128)(2,1)S(1)}, u32[]{:S(2)}, u32[]{:S(2)}) async-start(f16[16,40,896]{2,1,0:T(8,128)(2,1)} %bitcast.26), calls=%async_computation.5 | async-start | bytes 2293760 | tf_op jit(solution)/shard_map/all_to_all | solution.py:231
  163.9 29.2 %all-to-all-done.4 = f16[16,40,896]{2,1,0:T(8,128)(2,1)S(1)} async-done(((f16[16,40,896]{2,1,0:T(8,128)(2,1)}), f16[16,40,896]{2,1,0:T(8,128)(2,1)S(1)}, u32[]{:S(2)}, u32[]{:S(2)}) %all-to-all-start.4) | async-done | bytes 1146912 | tf_op jit(solution)/shard_map/all_to_all | solution.py:231
  193.1 2.0 gather_fusion
  195.1 4.3 %all-to-all-start.5 = ((f16[16,40,896]{2,1,0:T(8,128)(2,1)}), f16[16,40,896]{2,1,0:T(8,128)(2,1)S(1)}, u32[]{:S(2)}, u32[]{:S(2)}) async-start(f16[16,40,896]{2,1,0:T(8,128)(2,1)} %gather_fusion), calls=%async_computation.6 | async-start | bytes 2293760 | tf_op jit(solution)/shard_map/all_to_all | solution.py:232
  199.5 2.1 convert_element_type.35
  201.5 27.0 %all-to-all-done.5 = f16[16,40,896]{2,1,0:T(8,128)(2,1)S(1)} async-done(((f16[16,40,896]{2,1,0:T(8,128)(2,1)}), f16[16,40,896]{2,1,0:T(8,128)(2,1)S(1)}, u32[]{:S(2)}, u32[]{:S(2)}) %all-to-all-start.5) | async-done | bytes 1146912 | tf_op jit(solution)/shard_map/all_to_all | solution.py:232
  228.6 4.5 %all-to-all-start.2 = ((bf16[16,24,640]{2,1,0:T(8,128)(2,1)}), bf16[16,24,640]{2,1,0:T(8,128)(2,1)S(1)}, u32[]{:S(2)}, u32[]{:S(2)}) async-start(bf16[16,24,640]{2,1,0:T(8,128)(2,1)} %bitcast.15), calls=%async_computation.3 | async-start | bytes 983040 | tf_op jit(solution)/shard_map/all_to_all | solution.py:196
  233.1 1.6 convert_multiply_fusion
  234.7 13.5 %all-to-all-done.2 = bf16[16,24,640]{2,1,0:T(8,128)(2,1)S(1)} async-done(((bf16[16,24,640]{2,1,0:T(8,128)(2,1)}), bf16[16,24,640]{2,1,0:T(8,128)(2,1)S(1)}, u32[]{:S(2)}, u32[]{:S(2)}) %all-to-all-start.2) | async-done | bytes 491552 | tf_op jit(solution)/shard_map/all_to_all | solution.py:196
  248.7 1.1 copy.45
  (42 shorter events, 3.3 us)
Async XLA Ops:
  8.7 6.4 %copy-start.9 = (s32[128,2]{0,1:T(2,128)S(1)}, s32[128,2]{0,1:T(2,128)}, u32[]{:S(2)}) copy-start(s32[128,2]{0,1:T(2,128)} %param.13) | copy-start | bytes 3076
  8.7 6.5 %copy-start.11 = (s32[16]{0:T(128)S(1)}, s32[16]{0:T(128)}, u32[]{:S(2)}) copy-start(s32[16]{0:T(128)} %param.18) | copy-start | bytes 196
  8.8 6.5 %copy-start.12 = (s32[16]{0:T(128)S(1)}, s32[16]{0:T(128)}, u32[]{:S(2)}) copy-start(s32[16]{0:T(128)} %param.17) | copy-start | bytes 196
  8.8 6.5 %copy-start.13 = (s32[16]{0:T(128)S(1)}, s32[16]{0:T(128)}, u32[]{:S(2)}) copy-start(s32[16]{0:T(128)} %param.19) | copy-start | bytes 196
  8.8 6.9 %copy-start.8 = (bf16[128,2,640]{2,1,0:T(2,128)(2,1)S(1)}, bf16[128,2,640]{2,1,0:T(2,128)(2,1)}, u32[]{:S(2)}) copy-start(bf16[128,2,640]{2,1,0:T(2,128)(2,1)} %param.10) | copy-start | bytes 983044
  10.1 17.0 %all-to-all-start = ((bf16[4,128,896]{2,1,0:T(8,128)(2,1)}), bf16[4,128,896]{2,1,0:T(8,128)(2,1)S(1)}, u32[]{:S(2)}, u32[]{:S(2)}) async-start(bf16[4,128,896]{2,1,0:T(8,128)(2,1)} %bitcast.11), calls=%async_computation | async-start | bytes 1835008 | tf_op jit(solution)/shard_map/all_to_all | solution.py:141
  15.7 20.4 %copy-start.10 = (f32[128,2]{0,1:T(2,128)S(1)}, f32[128,2]{0,1:T(2,128)}, u32[]{:S(2)}) copy-start(f32[128,2]{0,1:T(2,128)} %param.12) | copy-start | bytes 3076
  27.1 34.5 %all-to-all-start.3 = ((bf16[16,24,1280]{2,1,0:T(8,128)(2,1)}), bf16[16,24,1280]{2,1,0:T(8,128)(2,1)S(1)}, u32[]{:S(2)}, u32[]{:S(2)}) async-start(bf16[16,24,1280]{2,1,0:T(8,128)(2,1)} %bitcast.22), calls=%async_computation.4 | async-start | bytes 1966080 | tf_op jit(solution)/shard_map/all_to_all | solution.py:152
  46.9 1.6 copy-start.3
  61.6 0.9 copy-start.7
  62.5 67.6 %all-to-all-start.1 = ((bf16[16,24,3584]{2,1,0:T(8,128)(2,1)}), bf16[16,24,3584]{2,1,0:T(8,128)(2,1)S(1)}, u32[]{:S(2)}, u32[]{:S(2)}) async-start(bf16[16,24,3584]{2,1,0:T(8,128)(2,1)} %bitcast.42), calls=%async_computation.1 | async-start | bytes 5505024 | tf_op jit(solution)/shard_map/all_to_all | solution.py:173
  66.3 78.7 %all-gather.4.cloned.1.call-start = ((), (), s32[]{:S(2)}) async-start(), calls=%async_computation.8 | async-start | bytes 4915200 | tf_op jit(solution)/shard_map/all_gather | solution.py:153
  67.0 132.4 %reduce-scatter.2.cloned.1.call-start = ((), (), s32[]{:S(2)}) async-start(), calls=%async_computation.7 | async-start | bytes 4915200 | tf_op jit(solution)/shard_map/reduce_scatter | solution.py:193
  130.1 11.3 %copy-start = (bf16[16,24,3584]{2,1,0:T(8,128)(2,1)}, bf16[16,24,3584]{2,1,0:T(8,128)(2,1)S(1)}, u32[]{:S(2)}) copy-start(bf16[16,24,3584]{2,1,0:T(8,128)(2,1)S(1)} %all-to-all-done.1) | copy-start | bytes 8257540
  130.1 6.2 %collective-permute-start = (bf16[384,3584]{1,0:T(8,128)(2,1)S(1)}, bf16[384,3584]{1,0:T(8,128)(2,1)S(1)}, u32[]{:S(2)}, u32[]{:S(2)}) collective-permute-start(bf16[384,3584]{1,0:T(8,128)(2,1)S(1)} %bitcast.39), channel_id=1, source_target_pairs={{0,1},{1,0},{2,3},{3,2},{4,5},{5,4},{6,7},{7,6},{8,9},{9,8},{10,11... | collective-permute-start | bytes 8257544 | tf_op jit(solution)/shard_map/ppermute | solution.py:174
  136.3 1.3 copy-start.4
  141.4 1.9 copy-start.1
  143.3 1.6 copy-start.2
  144.9 1.3 copy-start.5
  146.2 1.6 copy-start.6
  160.1 32.9 %all-to-all-start.4 = ((f16[16,40,896]{2,1,0:T(8,128)(2,1)}), f16[16,40,896]{2,1,0:T(8,128)(2,1)S(1)}, u32[]{:S(2)}, u32[]{:S(2)}) async-start(f16[16,40,896]{2,1,0:T(8,128)(2,1)} %bitcast.26), calls=%async_computation.5 | async-start | bytes 2293760 | tf_op jit(solution)/shard_map/all_to_all | solution.py:231
  195.1 33.5 %all-to-all-start.5 = ((f16[16,40,896]{2,1,0:T(8,128)(2,1)}), f16[16,40,896]{2,1,0:T(8,128)(2,1)S(1)}, u32[]{:S(2)}, u32[]{:S(2)}) async-start(f16[16,40,896]{2,1,0:T(8,128)(2,1)} %gather_fusion), calls=%async_computation.6 | async-start | bytes 2293760 | tf_op jit(solution)/shard_map/all_to_all | solution.py:232
  228.6 19.6 %all-to-all-start.2 = ((bf16[16,24,640]{2,1,0:T(8,128)(2,1)}), bf16[16,24,640]{2,1,0:T(8,128)(2,1)S(1)}, u32[]{:S(2)}, u32[]{:S(2)}) async-start(bf16[16,24,640]{2,1,0:T(8,128)(2,1)} %bitcast.15), calls=%async_computation.3 | async-start | bytes 983040 | tf_op jit(solution)/shard_map/all_to_all | solution.py:196
Sparse Core Ops, SparseCore 0:
  69.5 48.3 all-gather.3
  145.1 43.5 reduce-scatter.1

commit v2 on v1

v2 whole, which is shorter than its diff:
```python
import jax
import jax.numpy as jnp
from jax import lax
from jax.experimental import pallas as pl
from jax.experimental.pallas import tpu as pltpu
from jax.sharding import PartitionSpec as P

beta_one = 0.9
beta_two = 0.95
decay = 0.1
epsilon = 1e-08
bias_one = 1.0 - (0.9**50) ** 2
bias_two = 1.0 - (0.95**50) ** 2

RUN = 4
GROUPS = 16
CAP = 24
ROWS = GROUPS * CAP
SCALE = 2048.0
SAME_Y = [[g * RUN + y for g in range(GROUPS)] for y in range(RUN)]
SAME_RUN = [[g * RUN + y for y in range(RUN)] for g in range(GROUPS)]
OTHER_CORE = [(0, 1), (1, 0), (2, 3), (3, 2)]
GRID = 4
SHIFTS = [(0, 0), (2, 2), (1, 2), (3, 2), (2, 1), (2, 3), (1, 1), (3, 3)]
SHIFTS += [(1, 3), (3, 1), (0, 2), (2, 0), (0, 1), (0, 3), (1, 0), (3, 0)]
HALF = GROUPS // 2
LANES = 128
MB = 1024 * 1024


def contract(a, b, dims):
    return lax.dot_general(a, b, ((dims[0], dims[1]), ((), ())), preferred_element_type=jnp.float32)


def order_of(index, tokens):
    return 2 * (index % tokens) + index // tokens


def choose(row, col, want):
    count = row.shape[1]
    tokens = count // 2
    lane = order_of(lax.broadcasted_iota(jnp.int32, (count, count), 1), tokens)
    line = order_of(lax.broadcasted_iota(jnp.int32, (count, count), 0), tokens)
    ahead = jnp.where((row == col) & (line < lane), 1.0, 0.0)
    position = jnp.sum(ahead, axis=0, keepdims=True)
    place = (lax.broadcasted_iota(jnp.int32, (want.shape[0], 1), 0) % CAP).astype(jnp.float32)
    return (row == want) & (position == place)


def along_y(step):
    return [(i, i // RUN * RUN + (i + step) % RUN) for i in range(GROUPS * RUN)]


def nearest(step_x, step_z):
    pairs = []
    for i in range(GROUPS * RUN):
        x, z_low, y = i // (GRID * RUN), i // RUN % GRID, i % RUN
        for d in range(4):
            z = d // 2 * GRID + z_low
            step = (2 if z % 2 == 0 else -2) if step_z == 2 else (-1 if step_z == 3 else step_z)
            to_z = (z + step) % (2 * GRID)
            to = ((x + step_x) % GRID * GRID + to_z % GRID) * RUN + y
            pairs.append((i * 4 + d, to * 4 + to_z // GRID * 2 + d % 2))
    return pairs


def pack_kernel(y_ref, grad_ref, about_ref, *out_refs):
    width = grad_ref.shape[1] // RUN
    tokens = grad_ref.shape[0]
    about = about_ref[...]
    lane = lax.broadcasted_iota(jnp.int32, (tokens, LANES), 1)
    block = jnp.zeros((tokens, LANES), jnp.float32)
    place = 0
    for k in range(4):
        rest = about[:, k : k + 1]
        for _ in range(1 if k < 2 else 3):
            piece = rest.astype(jnp.bfloat16).astype(jnp.float32)
            block = jnp.where(lane == place, piece, block)
            rest = rest - piece
            place += 1
    for step, out_ref in enumerate(out_refs):
        quarter = (y_ref[0] + step) % RUN
        start = pl.multiple_of(quarter * width, LANES)
        out_ref[:, :width] = grad_ref[:, pl.ds(start, width)]
        out_ref[:, width:] = block.astype(jnp.bfloat16)


def send_h_kernel(row_ref, col_ref, want_ref, acts_ref, own_ref, extra_ref):
    for kind, out_ref in enumerate((own_ref, extra_ref)):
        sel = choose(row_ref[0], col_ref[0], want_ref[kind])
        rows = contract(jnp.where(sel, 1.0, 0.0).astype(jnp.bfloat16), acts_ref[...], ((1,), (0,)))
        out_ref[...] = rows.astype(jnp.bfloat16)


def send_c_kernel(core_ref, want_ref, packed_ref, *out_refs):
    tokens = packed_ref.shape[1]
    width = packed_ref.shape[2] - LANES
    block = packed_ref[0, :, width:]
    eye = lax.broadcasted_iota(jnp.int32, (tokens, tokens), 0) == lax.broadcasted_iota(
        jnp.int32, (tokens, tokens), 1
    )
    lines = contract(block, jnp.where(eye, 1.0, 0.0).astype(jnp.bfloat16), ((0,), (0,)))
    columns = block.astype(jnp.float32)
    row = jnp.concatenate([lines[0:1], lines[1:2]], axis=1)
    col = jnp.concatenate([columns[:, 0:1], columns[:, 1:2]], axis=0)
    gates = [lines[2 + 3 * k : 3 + 3 * k] + lines[3 + 3 * k : 4 + 3 * k] for k in range(2)]
    gates = [gates[k] + lines[4 + 3 * k : 5 + 3 * k] for k in range(2)]
    sel = choose(row, col, want_ref[0])
    gate = jnp.sum(
        jnp.where(sel, jnp.concatenate(gates, axis=1), 0.0), axis=1, keepdims=True
    )
    sel = jnp.where(sel, 1.0, 0.0)
    sel = (sel[:, :tokens] + sel[:, tokens:]).astype(jnp.bfloat16)
    rows = gate * contract(sel, packed_ref[0, :, :width], ((1,), (0,)))
    for i, out_ref in enumerate(out_refs):
        out_ref[...] = rows[i * CAP : (i + 1) * CAP].astype(jnp.bfloat16)


def order_kernel(order_ref, *refs):
    values, out_ref = refs[:-1], refs[-1]
    lane = lax.broadcasted_iota(jnp.int32, (ROWS, ROWS), 1)
    turn = jnp.where(lane == order_ref[...], 1.0, 0.0).astype(jnp.bfloat16)
    out_ref[...] = contract(turn, values[0][...], ((1,), (0,))).astype(jnp.bfloat16)


def unorder_kernel(order_ref, first_ref, second_ref, out_ref):
    lane = lax.broadcasted_iota(jnp.int32, (ROWS, ROWS), 1)
    turn = jnp.where(lane == order_ref[...], 1.0, 0.0).astype(jnp.bfloat16)
    half = ROWS // 2
    out_ref[...] = (
        contract(turn[:half], first_ref[...].astype(jnp.bfloat16), ((0,), (0,)))
        + contract(turn[half:], second_ref[...].astype(jnp.bfloat16), ((0,), (0,)))
    ).astype(jnp.bfloat16)


def back_kernel(core_ref, own_ref, mate_ref, w_ref, out_ref):
    mine = pl.program_id(0) // 2 == core_ref[0]

    @pl.when(mine)
    def _():
        out_ref[0] = contract(own_ref[...], w_ref[...], ((1,), (1,)))

    @pl.when(jnp.logical_not(mine))
    def _():
        out_ref[0] = contract(mate_ref[...], w_ref[...], ((1,), (1,)))


def update_kernel(core_ref, h_own_ref, h_extra_ref, *refs):
    own_refs, mate_refs = refs[0:2], refs[2:4]
    w_ref, m_ref, v_ref, out_ref = refs[4:]
    core = core_ref[0]
    width = w_ref.shape[1]
    half = ROWS // 2
    total = jnp.zeros(w_ref.shape, jnp.float32)
    for c_refs, base in ((own_refs, 2 * core), (mate_refs, 2 - 2 * core)):
        for kind, h_ref in enumerate((h_own_ref, h_extra_ref)):
            for j in range(2):
                part = 2 * kind + j
                for at, c_ref in enumerate(c_refs):
                    total += contract(
                        h_ref[base + j, at * half : (at + 1) * half],
                        c_ref[:, part * width : (part + 1) * width],
                        ((0,), (0,)),
                    )
    m_new = beta_one * m_ref[...] + (1.0 - beta_one) * total
    v_new = beta_two * v_ref[...] + (1.0 - beta_two) * total * total
    direction = m_new / bias_one / (jnp.sqrt(v_new / bias_two) + epsilon)
    direction = direction + decay * w_ref[...].astype(jnp.float32)
    out_ref[...] = SCALE * direction


def take_kernel(row_ref, col_ref, want_ref, back_ref, out_ref):
    sel = jnp.where(choose(row_ref[0], col_ref[0], want_ref[0]), 1.0, 0.0).astype(jnp.bfloat16)
    out_ref[...] = contract(sel, back_ref[...], ((0,), (0,))).astype(jnp.bfloat16)


def params(limit):
    return pltpu.CompilerParams(vmem_limit_bytes=limit * MB)


def whole(shape):
    return pl.BlockSpec(shape, lambda *_: (0,) * len(shape))


def local(
    hidden_acts,
    out_grad,
    gate_probs,
    route,
    weights,
    first_moment,
    second_moment,
    old_slot,
    new_slot,
    partner,
):
    tokens, top, hidden = hidden_acts.shape
    count = tokens * top
    width = weights.shape[2]
    index = lax.axis_index("ep").astype(jnp.int32)
    y = index % RUN
    core = (lax.axis_index("dp") % 2).astype(jnp.int32)
    cores = core.reshape(1)

    numbers = jnp.arange(GROUPS, dtype=jnp.int32)
    held = old_slot[None, :] == numbers[:, None]
    own = jnp.sum(jnp.where(held, numbers[None, :], 0), axis=1)
    mate = jnp.sum(jnp.where(held, partner[None, :], 0), axis=1)
    mate = jnp.where(mate == own, -1, mate)
    want = jnp.stack([own, mate]).astype(jnp.float32)
    steps = jnp.array(SHIFTS, jnp.int32)
    x, z = index // (GRID * RUN), index // RUN % GRID
    to = (x + steps[:, 0]) % GRID * GRID + (z + steps[:, 1]) % GRID
    by = (x - steps[:, 0]) % GRID * GRID + (z - steps[:, 1]) % GRID
    want_to = jnp.sum(jnp.where(to[:, None] == numbers[None, :], want[:, None, :], 0.0), axis=2)
    want = jnp.broadcast_to(want[:, :, None], (2, GROUPS, CAP)).reshape(2, ROWS, 1)
    want_to = jnp.broadcast_to(want_to[:, :, None], (2, GROUPS, CAP)).reshape(2, ROWS, 1)
    order = (by[:, None] * CAP + jnp.arange(CAP, dtype=jnp.int32)[None, :]).reshape(ROWS, 1)
    source = jnp.sum(
        jnp.where(new_slot[None, :] == numbers[:, None], old_slot[None, :], 0), axis=1
    )

    routes = route.astype(jnp.float32)
    packed = pl.pallas_call(
        pack_kernel,
        grid_spec=pltpu.PrefetchScalarGridSpec(
            num_scalar_prefetch=1,
            grid=(1,),
            in_specs=[whole((tokens, RUN * width)), whole((tokens, 2 * top))],
            out_specs=[whole((tokens, width + LANES))] * RUN,
        ),
        out_shape=[jax.ShapeDtypeStruct((tokens, width + LANES), jnp.bfloat16)] * RUN,
        compiler_params=params(16),
        name="pack",
    )(y.reshape(1), out_grad, jnp.concatenate([routes, gate_probs], axis=1))
    packed = [packed[0]] + [lax.ppermute(packed[s], "ep", along_y(s)) for s in range(1, RUN)]
    packed = jnp.stack(packed)

    own_row = routes.T.reshape(1, 1, count)
    own_col = own_row.reshape(1, count, 1)
    acts = hidden_acts.transpose(1, 0, 2).reshape(count, hidden)
    sent_h = pl.pallas_call(
        send_h_kernel,
        out_shape=[jax.ShapeDtypeStruct((ROWS, hidden), jnp.bfloat16)] * 2,
        compiler_params=params(16),
        name="send_h",
    )(own_row, own_col, want, acts)
    all_h = []
    for kind in range(2):
        got = lax.all_to_all(sent_h[kind], "ep", 0, 0, axis_index_groups=SAME_Y, tiled=True)
        got = pl.pallas_call(
            order_kernel,
            out_shape=jax.ShapeDtypeStruct((ROWS, hidden), jnp.bfloat16),
            compiler_params=params(16),
            name="order_h",
        )(order, got)
        all_h.append(
            lax.all_gather(got, "ep", axis_index_groups=SAME_RUN, axis=0, tiled=False)
        )

    send_c = pl.pallas_call(
        send_c_kernel,
        grid_spec=pltpu.PrefetchScalarGridSpec(
            num_scalar_prefetch=1,
            grid=(2, 2),
            in_specs=[
                pl.BlockSpec((1, ROWS, 1), lambda k, j, c: (k, 0, 0)),
                pl.BlockSpec(
                    (1, tokens, width + LANES),
                    lambda k, j, c: ((c[1] + 2 * RUN - 2 * c[0] - j) % RUN, 0, 0),
                ),
            ],
            out_specs=[pl.BlockSpec((CAP, width), lambda k, j, c: (0, 2 * k + j))] * GROUPS,
        ),
        out_shape=[jax.ShapeDtypeStruct((CAP, 4 * width), jnp.bfloat16)] * GROUPS,
        compiler_params=params(24),
        name="send_c",
    )(jnp.stack([core, y]), want_to, packed)
    got_c = [send_c[0]]
    for step, block in zip(SHIFTS[1:], send_c[1:], strict=True):
        got_c.append(lax.ppermute(block, ("ep", "dp"), nearest(*step)))
    got_c = [jnp.concatenate(got_c[:HALF]), jnp.concatenate(got_c[HALF:])]
    mate_c = [lax.ppermute(part, "dp", OTHER_CORE) for part in got_c]

    weight = weights[0]
    half = ROWS // 2
    summed = []
    for at in range(2):
        partial_back = pl.pallas_call(
            back_kernel,
            grid_spec=pltpu.PrefetchScalarGridSpec(
                num_scalar_prefetch=1,
                grid=(RUN,),
                in_specs=[
                    pl.BlockSpec((half, width), lambda s, c: (0, s % 2)),
                    pl.BlockSpec((half, width), lambda s, c: (0, s % 2)),
                    whole((hidden, width)),
                ],
                out_specs=pl.BlockSpec((1, half, hidden), lambda s, c: (s, 0, 0)),
            ),
            out_shape=jax.ShapeDtypeStruct((RUN, half, hidden), jnp.float32),
            compiler_params=params(16),
            name="back",
        )(cores, got_c[at], mate_c[at], weight)
        summed.append(
            lax.psum_scatter(
                partial_back, "ep", scatter_dimension=0, axis_index_groups=SAME_RUN, tiled=False
            )
        )
    back = pl.pallas_call(
        unorder_kernel,
        out_shape=jax.ShapeDtypeStruct((ROWS, hidden), jnp.bfloat16),
        compiler_params=params(16),
        name="unorder",
    )(order, *summed)
    back = lax.all_to_all(back, "ep", 0, 0, axis_index_groups=SAME_Y, tiled=True)
    hidden_out = pl.pallas_call(
        take_kernel,
        out_shape=jax.ShapeDtypeStruct((count, hidden), jnp.bfloat16),
        compiler_params=params(16),
        name="take",
    )(own_row, own_col, want, back)
    hidden_out = hidden_out.reshape(top, tokens, hidden).transpose(1, 0, 2)

    block = 128
    grid = hidden // block
    update = pl.pallas_call(
        update_kernel,
        grid_spec=pltpu.PrefetchScalarGridSpec(
            num_scalar_prefetch=1,
            grid=(grid,),
            in_specs=[pl.BlockSpec((RUN, ROWS, block), lambda i, c: (0, 0, i))] * 2
            + [whole((half, 4 * width))] * 4
            + [pl.BlockSpec((block, width), lambda i, c: (i, 0))] * 3,
            out_specs=pl.BlockSpec((block, width), lambda i, c: (i, 0)),
        ),
        out_shape=jax.ShapeDtypeStruct((hidden, width), jnp.float32),
        compiler_params=params(24),
        name="update",
    )(cores, *all_h, *got_c, *mate_c, weight, first_moment[0], second_moment[0])

    spread = update.astype(jnp.float16).reshape(GROUPS, hidden // GROUPS, width)
    spread = lax.all_to_all(spread, "ep", 0, 0, axis_index_groups=SAME_Y, tiled=True)
    placed = lax.all_to_all(spread[source], "ep", 0, 0, axis_index_groups=SAME_Y, tiled=True)
    placed = placed.reshape(1, hidden, width).astype(jnp.float32) * (1.0 / SCALE)
    return (hidden_out, placed)


def solution(mesh):
    return jax.shard_map(
        local,
        mesh=mesh,
        in_specs=(
            P("ep", None, "dp"),
            P("ep", None),
            P("ep", None),
            P("ep", None),
            P("ep", "dp", None),
            P("ep", "dp", None),
            P("ep", "dp", None),
            P(),
            P(),
            P(),
        ),
        out_specs=(P("ep", None, "dp"), P("ep", "dp", None)),
        check_vma=False,
    )
```

time: 257 us -> 254 us (0.988)
  waiting for transfers between devices: 161 us -> 110 us
  starting transfers between devices: 31.8 us -> 61.5 us
  local copies, waits for them, and re-layouts: 16.8 us -> 35.8 us
  blocking collectives: 8.29 us -> 0 us
  Pallas kernels: 19.2 us -> 26 us
    all_to_all x4 -> x3, waiting for transfers between devices: 99.5 us -> 27.7 us  [the longest x2 14.7 us: local(): lax.all_to_all(sent_h[kind], 'ep', 0, 0, axis_index_groups=SAME_Y, tiled=...]
    ppermute x1 -> x20, starting transfers between devices: 1.47 us -> 33.4 us  [the longest x15 26 us: local(): got_c.append(lax.ppermute(block, ('ep', 'dp'), nearest(*step)))]
    all_to_all x1, waiting for transfers between devices: 29.2 us -> 3.29 us  [local(): lax.all_to_all(spread, 'ep', 0, 0, axis_index_groups=SAME_Y, tiled=True)]
    ppermute x1 -> x20, waiting for transfers between devices: 4.72 us -> 29.3 us  [the longest x3 13.3 us: local(): lax.ppermute(packed[s], 'ep', along_y(s))]
    reduce_scatter x1 -> x2, waiting for transfers between devices: 0.02 us -> 22.4 us  [local(): lax.psum_scatter(partial_back, 'ep', scatter_dimension=0, axis_index_grou...]
    unnamed x29 -> x62, local copies, waits for them, and re-layouts: 11.7 us -> 29.2 us
    all_gather x1 -> x0, blocking collectives: 8.29 us -> none  [local(): lax.all_gather(about, 'ep', axis_index_groups=SAME_RUN, axis=0, tiled=False)]
    all_to_all x4 -> x3, starting transfers between devices: 22.2 us -> 17.2 us  [the longest x2 12.7 us: local(): lax.all_to_all(sent_h[kind], 'ep', 0, 0, axis_index_groups=SAME_Y, tiled=...]
  transfers between devices with their start and end apart: 9 -> 29, of which waited for: 7 -> 13; matrix products, arithmetic and copies ran while one was open for 3% -> 8% of each run, Pallas kernels for 7% -> 9%
where the time goes in v2:
time: 254 us; the launch traced here: 252 us
  waiting for transfers between devices  110 us (43%)
  starting transfers between devices  61.5 us (24%)
  local copies, waits for them, and re-layouts  35.8 us (14%)
  Pallas kernels  26 us (10%)
  between operations  14.3 us (6%)
  other arithmetic  4.79 us (2%)
    unnamed x62, local copies, waits for them, and re-layouts  29.2 us
    all_to_all x1, waiting for transfers between devices, local(): lax.all_to_all(spread[source], 'ep', 0, 0, axis_index_groups=SAME_Y, tile...  27.5 us
    ppermute x15, starting transfers between devices, local(): got_c.append(lax.ppermute(block, ('ep', 'dp'), nearest(*step)))  26 us
    reduce_scatter x2, waiting for transfers between devices, local(): lax.psum_scatter(partial_back, 'ep', scatter_dimension=0, axis_index_grou...  22.4 us
    all_to_all x2, waiting for transfers between devices, local(): lax.all_to_all(sent_h[kind], 'ep', 0, 0, axis_index_groups=SAME_Y, tiled=...  14.7 us
    ppermute x3, waiting for transfers between devices, local(): lax.ppermute(packed[s], 'ep', along_y(s))  13.3 us
    ppermute x15, waiting for transfers between devices, local(): got_c.append(lax.ppermute(block, ('ep', 'dp'), nearest(*step)))  13 us
    all_to_all x1, waiting for transfers between devices, local(): lax.all_to_all(back, 'ep', 0, 0, axis_index_groups=SAME_Y, tiled=True)  13 us
  transfers between devices with their start and end apart: 29, of which 13 were waited for; matrix products, arithmetic and copies ran while one was open for 8% of the time, Pallas kernels for 9%

profile of v2, /device:TPU:1, one launch (start us, length us, event | category | flops | bytes accessed | tf_op | source)
XLA Modules:
  0.0 252.5 jit_solution(3068113315216206467)
XLA Ops:
  11.7 9.1 %all-to-all-start.1 = ((bf16[16,24,640]{2,1,0:T(8,128)(2,1)}), bf16[16,24,640]{2,1,0:T(8,128)(2,1)S(1)}, u32[]{:S(2)}, u32[]{:S(2)}) async-start(bf16[16,24,640]{2,1,0:T(8,128)(2,1)} %bitcast.23), calls=%async_computation.3 | async-start | bytes 983040 | tf_op jit(solution)/shard_map/all_to_all | solution.py:250
  21.2 14.7 %all-to-all-done.1 = bf16[16,24,640]{2,1,0:T(8,128)(2,1)S(1)} async-done(((bf16[16,24,640]{2,1,0:T(8,128)(2,1)}), bf16[16,24,640]{2,1,0:T(8,128)(2,1)S(1)}, u32[]{:S(2)}, u32[]{:S(2)}) %all-to-all-start.1) | async-done | bytes 491552 | tf_op jit(solution)/shard_map/all_to_all | solution.py:250
  38.2 2.7 %collective-permute-start.2 = (bf16[128,1024]{1,0:T(8,128)(2,1)}, bf16[128,1024]{1,0:T(8,128)(2,1)S(1)}, u32[]{:S(2)}, u32[]{:S(2)}) collective-permute-start(bf16[128,1024]{1,0:T(8,128)(2,1)} %get-tuple-element.27), channel_id=1, source_target_pairs={{0,12},{4,0},{8,4},{12,8},{16,28},{20,16},{24,20},{28,24},{32,44},... | collective-permute-start | bytes 786440 | tf_op jit(solution)/shard_map/ppermute | solution.py:236
  41.9 3.6 %all-to-all-start.2 = ((bf16[16,24,640]{2,1,0:T(8,128)(2,1)}), bf16[16,24,640]{2,1,0:T(8,128)(2,1)S(1)}, u32[]{:S(2)}, u32[]{:S(2)}) async-start(bf16[16,24,640]{2,1,0:T(8,128)(2,1)} %bitcast.26), calls=%async_computation.4 | async-start | bytes 983040 | tf_op jit(solution)/shard_map/all_to_all | solution.py:250
  46.5 1.7 collective-permute-done.1
  48.3 11.1 %collective-permute-done = bf16[128,1024]{1,0:T(8,128)(2,1)S(1)} collective-permute-done((bf16[128,1024]{1,0:T(8,128)(2,1)S(1)}, bf16[128,1024]{1,0:T(8,128)(2,1)S(1)}, u32[]{:S(2)}, u32[]{:S(2)}) %collective-permute-start) | collective-permute-done | bytes 262176 | tf_op jit(solution)/shard_map/ppermute | solution.py:236
  59.5 4.4 %send_c.1 = (bf16[24,3584]{1,0:T(8,128)(2,1)S(1)}, bf16[24,3584]{1,0:T(8,128)(2,1)S(1)}, bf16[24,3584]{1,0:T(8,128)(2,1)S(1)}, bf16[24,3584]{1,0:T(8,128)(2,1)S(...) custom-call(s32[2]{0:T(128)S(1)} %pad_add_fusion.core_ref, ...), custom_call_target="tpu_custom_call" | custom-call | tf_op jit(solution)/shard_map/send_c/pallas_call | solution.py:261
  64.0 2.1 collective-permute-start.4
  66.1 3.6 %collective-permute-start.5 = (bf16[24,3584]{1,0:T(8,128)(2,1)S(1)}, bf16[24,3584]{1,0:T(8,128)(2,1)S(1)}, u32[]{:S(2)}, u32[]{:S(2)}) collective-permute-start(bf16[24,3584]{1,0:T(8,128)(2,1)S(1)} %get-tuple-element.31), channel_id=1, source_target_pairs={{0,224},{1,225},{2,226},{3,227},{4,228},{5,229},{6,230},{7,231},{8... | collective-permute-start | bytes 516104 | tf_op jit(solution)/shard_map/ppermute | solution.py:281
  69.7 5.1 %collective-permute-start.7 = (bf16[24,3584]{1,0:T(8,128)(2,1)}, bf16[24,3584]{1,0:T(8,128)(2,1)}, u32[]{:S(2)}, u32[]{:S(2)}) collective-permute-start(bf16[24,3584]{1,0:T(8,128)(2,1)} %get-tuple-element.33), channel_id=1, source_target_pairs={{0,178},{1,179},{2,176},{3,177},{4,182},{5,183},{6,180},{7,181},{8... | collective-permute-start | bytes 516104 | tf_op jit(solution)/shard_map/ppermute | solution.py:281
  74.7 1.6 collective-permute-done.3
  76.7 4.6 %collective-permute-start.9 = (bf16[24,3584]{1,0:T(8,128)(2,1)}, bf16[24,3584]{1,0:T(8,128)(2,1)}, u32[]{:S(2)}, u32[]{:S(2)}) collective-permute-start(bf16[24,3584]{1,0:T(8,128)(2,1)} %get-tuple-element.35), channel_id=1, source_target_pairs={{0,242},{1,243},{2,240},{3,241},{4,246},{5,247},{6,244},{7,245},{8... | collective-permute-start | bytes 516104 | tf_op jit(solution)/shard_map/ppermute | solution.py:281
  82.7 7.7 %collective-permute-done.6 = bf16[24,3584]{1,0:T(8,128)(2,1)} collective-permute-done((bf16[24,3584]{1,0:T(8,128)(2,1)}, bf16[24,3584]{1,0:T(8,128)(2,1)}, u32[]{:S(2)}, u32[]{:S(2)}) %collective-permute-start.6) | collective-permute-done | bytes 172064 | tf_op jit(solution)/shard_map/ppermute | solution.py:281
  96.1 2.6 %collective-permute-start.12 = (bf16[24,3584]{1,0:T(8,128)(2,1)S(1)}, bf16[24,3584]{1,0:T(8,128)(2,1)S(1)}, u32[]{:S(2)}, u32[]{:S(2)}) collective-permute-start(bf16[24,3584]{1,0:T(8,128)(2,1)S(1)} %copy-done.16), channel_id=1, source_target_pairs={{0,208},{1,209},{2,210},{3,211},{4,212},{5,213},{6,214},{7,215},{8... | collective-permute-start | bytes 516104 | tf_op jit(solution)/shard_map/ppermute | solution.py:281
  99.6 3.3 %collective-permute-done.11 = bf16[24,3584]{1,0:T(8,128)(2,1)S(1)} collective-permute-done((bf16[24,3584]{1,0:T(8,128)(2,1)S(1)}, bf16[24,3584]{1,0:T(8,128)(2,1)S(1)}, u32[]{:S(2)}, u32[]{:S(2)}) %collective-permute-start.11) | collective-permute-done | bytes 172064 | tf_op jit(solution)/shard_map/ppermute | solution.py:281
  104.0 2.4 collective-permute-start.16
  107.0 3.4 %collective-permute-start.17 = (bf16[24,3584]{1,0:T(8,128)(2,1)}, bf16[24,3584]{1,0:T(8,128)(2,1)}, u32[]{:S(2)}, u32[]{:S(2)}) collective-permute-start(bf16[24,3584]{1,0:T(8,128)(2,1)} %get-tuple-element.42), channel_id=1, source_target_pairs={{0,64},{1,65},{2,66},{3,67},{4,68},{5,69},{6,70},{7,71},{8,72},{9,... | collective-permute-start | bytes 516104 | tf_op jit(solution)/shard_map/ppermute | solution.py:281
  110.4 3.5 %back.2 = f32[4,192,640]{2,1,0:T(8,128)} custom-call(s32[1]{0:T(128)} %bitcast.6.core_ref, bf16[192,3584]{1,0:T(8,128)(2,1)S(1)} %constant_dynamic-update-slice_fusion.own_ref.refs_0_, bf16[192,3584]{1,0:T(8,128)(2,1)S(1)} %collective-permute-done.10.mate_ref.refs_2_, bf16[640,896]{1,0:T(8,128)(2,1)S(1)} %bitcast.44), custom_call_target="tpu_custom_call" | custom-call | tf_op jit(solution)/shard_map/back/pallas_call | solution.py:289
  123.9 2.7 %collective-permute-start.19 = (bf16[192,3584]{1,0:T(8,128)(2,1)}, bf16[192,3584]{1,0:T(8,128)(2,1)S(1)}, u32[]{:S(2)}, u32[]{:S(2)}) collective-permute-start(bf16[192,3584]{1,0:T(8,128)(2,1)} %constant_dynamic-update-slice_fusion.8.own_ref.refs_1_), channel_id=1, source_target_pairs={{0,1},{1,0},{2,3},{3,2},{4,5},{5,4},{6,7},{7,6},{8,9},{9,8},{10,11... | collective-permute-start | bytes 4128776 | tf_op jit(solution)/shard_map/ppermute | solution.py:283
  126.5 3.0 %collective-permute-done.19.mate_ref.refs_3_ = bf16[192,3584]{1,0:T(8,128)(2,1)S(1)} collective-permute-done((bf16[192,3584]{1,0:T(8,128)(2,1)}, bf16[192,3584]{1,0:T(8,128)(2,1)S(1)}, u32[]{:S(2)}, u32[]{:S(2)}) %collective-permute-start.19) | collective-permute-done | bytes 1376288 | tf_op jit(solution)/shard_map/ppermute | solution.py:283
  130.9 3.5 %back.3 = f32[4,192,640]{2,1,0:T(8,128)} custom-call(s32[1]{0:T(128)} %bitcast.6.core_ref, bf16[192,3584]{1,0:T(8,128)(2,1)S(1)} %copy-done.1, bf16[192,3584]{1,0:T(8,128)(2,1)S(1)} %collective-permute-done.19.mate_ref.refs_3_, bf16[640,896]{1,0:T(8,128)(2,1)S(1)} %bitcast.45), custom_call_target="tpu_custom_call" | custom-call | tf_op jit(solution)/shard_map/back/pallas_call | solution.py:289
  139.6 1.7 copy-done.7
  141.3 1.7 copy-done.8
  146.1 8.6 %update.1 = f32[640,896]{1,0:T(8,128)S(1)} custom-call(s32[1]{0:T(128)} %bitcast.6.core_ref, bf16[4,384,640]{2,1,0:T(8,128)(2,1)S(1)} %bitcast.51, bf16[4,384,640]{2,1,0:T(8,128)(2,1)S(1)} %bitcast.52, bf16[192,3584]{1,0:T(8,128)(2,1)S(1)} %constant_dynamic-update-slice_fusion.own_ref.refs_0_, bf16[192,3584]{1,0:T(8,128)(2,1)S(1)} %copy-done.2, ...), custom_call_target="tpu_custom_call" | custom-call | tf_op jit(solution)/shard_map/update/pallas_call | solution.py:327
  155.9 6.7 %all-to-all-start.3 = ((f16[16,40,896]{2,1,0:T(8,128)(2,1)}), f16[16,40,896]{2,1,0:T(8,128)(2,1)S(1)}, u32[]{:S(2)}, u32[]{:S(2)}) async-start(f16[16,40,896]{2,1,0:T(8,128)(2,1)} %bitcast.31), calls=%async_computation.5 | async-start | bytes 2293760 | tf_op jit(solution)/shard_map/all_to_all | solution.py:343
  162.7 22.4 %reduce-scatter.5.cloned.1.call-done = f32[1,192,640]{2,1,0:T(8,128)} async-done(((f32[4,192,640]{2,1,0:T(8,128)}), f32[1,192,640]{2,1,0:T(8,128)}) %reduce-scatter.5.cloned.1.call-update) | async-done | bytes 491536 | tf_op jit(solution)/shard_map/reduce_scatter | solution.py:306
  188.5 3.3 %all-to-all-done.3 = f16[16,40,896]{2,1,0:T(8,128)(2,1)S(1)} async-done(((f16[16,40,896]{2,1,0:T(8,128)(2,1)}), f16[16,40,896]{2,1,0:T(8,128)(2,1)S(1)}, u32[]{:S(2)}, u32[]{:S(2)}) %all-to-all-start.3) | async-done | bytes 1146912 | tf_op jit(solution)/shard_map/all_to_all | solution.py:343
  191.8 4.5 %all-to-all-start = ((bf16[16,24,640]{2,1,0:T(8,128)(2,1)}), bf16[16,24,640]{2,1,0:T(8,128)(2,1)S(1)}, u32[]{:S(2)}, u32[]{:S(2)}) async-start(bf16[16,24,640]{2,1,0:T(8,128)(2,1)} %bitcast.16), calls=%async_computation.2 | async-start | bytes 983040 | tf_op jit(solution)/shard_map/all_to_all | solution.py:316
  196.3 2.0 gather_fusion
  198.3 13.0 %all-to-all-done = bf16[16,24,640]{2,1,0:T(8,128)(2,1)S(1)} async-done(((bf16[16,24,640]{2,1,0:T(8,128)(2,1)}), bf16[16,24,640]{2,1,0:T(8,128)(2,1)S(1)}, u32[]{:S(2)}, u32[]{:S(2)}) %all-to-all-start) | async-done | bytes 491552 | tf_op jit(solution)/shard_map/all_to_all | solution.py:316
  211.3 3.9 %all-to-all-start.4 = ((f16[16,40,896]{2,1,0:T(8,128)(2,1)}), f16[16,40,896]{2,1,0:T(8,128)(2,1)S(1)}, u32[]{:S(2)}, u32[]{:S(2)}) async-start(f16[16,40,896]{2,1,0:T(8,128)(2,1)} %gather_fusion), calls=%async_computation.6 | async-start | bytes 2293760 | tf_op jit(solution)/shard_map/all_to_all | solution.py:344
  216.9 27.5 %all-to-all-done.4 = f16[16,40,896]{2,1,0:T(8,128)(2,1)S(1)} async-done(((f16[16,40,896]{2,1,0:T(8,128)(2,1)}), f16[16,40,896]{2,1,0:T(8,128)(2,1)S(1)}, u32[]{:S(2)}, u32[]{:S(2)}) %all-to-all-start.4) | async-done | bytes 1146912 | tf_op jit(solution)/shard_map/all_to_all | solution.py:344
  (129 shorter events, 46.6 us)
Async XLA Ops:
  11.7 25.5 %copy-start.19 = (f32[128,2]{0,1:T(2,128)S(1)}, f32[128,2]{0,1:T(2,128)}, u32[]{:S(2)}) copy-start(f32[128,2]{0,1:T(2,128)} %param.13) | copy-start | bytes 3076
  11.7 25.6 %copy-start.12 = (bf16[128,3584]{1,0:T(8,128)(2,1)S(1)}, bf16[128,3584]{1,0:T(8,128)(2,1)}, u32[]{:S(2)}) copy-start(bf16[128,3584]{1,0:T(8,128)(2,1)} %grad_ref.1) | copy-start | bytes 2752516
  11.7 24.2 %all-to-all-start.1 = ((bf16[16,24,640]{2,1,0:T(8,128)(2,1)}), bf16[16,24,640]{2,1,0:T(8,128)(2,1)S(1)}, u32[]{:S(2)}, u32[]{:S(2)}) async-start(bf16[16,24,640]{2,1,0:T(8,128)(2,1)} %bitcast.23), calls=%async_computation.3 | async-start | bytes 983040 | tf_op jit(solution)/shard_map/all_to_all | solution.py:250
  20.8 114.7 %all-gather.5.cloned.1.call-start = ((), (), s32[]{:S(2)}) async-start(), calls=%async_computation.9 | async-start | bytes 2457600 | tf_op jit(solution)/shard_map/all_gather | solution.py:258
  38.2 8.4 %collective-permute-start.2 = (bf16[128,1024]{1,0:T(8,128)(2,1)}, bf16[128,1024]{1,0:T(8,128)(2,1)S(1)}, u32[]{:S(2)}, u32[]{:S(2)}) collective-permute-start(bf16[128,1024]{1,0:T(8,128)(2,1)} %get-tuple-element.27), channel_id=1, source_target_pairs={{0,12},{4,0},{8,4},{12,8},{16,28},{20,16},{24,20},{28,24},{32,44},... | collective-permute-start | bytes 786440 | tf_op jit(solution)/shard_map/ppermute | solution.py:236
  40.9 7.4 %collective-permute-start.1 = (bf16[128,1024]{1,0:T(8,128)(2,1)S(1)}, bf16[128,1024]{1,0:T(8,128)(2,1)S(1)}, u32[]{:S(2)}, u32[]{:S(2)}) collective-permute-start(bf16[128,1024]{1,0:T(8,128)(2,1)S(1)} %get-tuple-element.26), channel_id=1, source_target_pairs={{0,8},{4,12},{8,0},{12,4},{16,24},{20,28},{24,16},{28,20},{32,40},... | collective-permute-start | bytes 786440 | tf_op jit(solution)/shard_map/ppermute | solution.py:236
  41.2 18.1 %collective-permute-start = (bf16[128,1024]{1,0:T(8,128)(2,1)S(1)}, bf16[128,1024]{1,0:T(8,128)(2,1)S(1)}, u32[]{:S(2)}, u32[]{:S(2)}) collective-permute-start(bf16[128,1024]{1,0:T(8,128)(2,1)S(1)} %get-tuple-element.25), channel_id=1, source_target_pairs={{0,4},{4,8},{8,12},{12,0},{16,20},{20,24},{24,28},{28,16},{32,36},... | collective-permute-start | bytes 786440 | tf_op jit(solution)/shard_map/ppermute | solution.py:236
  41.9 39.4 %all-to-all-start.2 = ((bf16[16,24,640]{2,1,0:T(8,128)(2,1)}), bf16[16,24,640]{2,1,0:T(8,128)(2,1)S(1)}, u32[]{:S(2)}, u32[]{:S(2)}) async-start(bf16[16,24,640]{2,1,0:T(8,128)(2,1)} %bitcast.26), calls=%async_computation.4 | async-start | bytes 983040 | tf_op jit(solution)/shard_map/all_to_all | solution.py:250
  45.5 90.0 %all-gather.7.cloned.1.call-start = ((), (), s32[]{:S(2)}) async-start(), calls=%async_computation.10 | async-start | bytes 2457600 | tf_op jit(solution)/shard_map/all_gather | solution.py:258
  63.9 12.5 %collective-permute-start.3 = (bf16[24,3584]{1,0:T(8,128)(2,1)S(1)}, bf16[24,3584]{1,0:T(8,128)(2,1)S(1)}, u32[]{:S(2)}, u32[]{:S(2)}) collective-permute-start(bf16[24,3584]{1,0:T(8,128)(2,1)S(1)} %get-tuple-element.29), channel_id=1, source_target_pairs={{0,160},{1,161},{2,162},{3,163},{4,164},{5,165},{6,166},{7,167},{8... | collective-permute-start | bytes 516104 | tf_op jit(solution)/shard_map/ppermute | solution.py:281
  64.0 12.7 %collective-permute-start.4 = (bf16[24,3584]{1,0:T(8,128)(2,1)S(1)}, bf16[24,3584]{1,0:T(8,128)(2,1)S(1)}, u32[]{:S(2)}, u32[]{:S(2)}) collective-permute-start(bf16[24,3584]{1,0:T(8,128)(2,1)S(1)} %get-tuple-element.30), channel_id=1, source_target_pairs={{0,96},{1,97},{2,98},{3,99},{4,100},{5,101},{6,102},{7,103},{8,104... | collective-permute-start | bytes 516104 | tf_op jit(solution)/shard_map/ppermute | solution.py:281
  66.1 15.2 %collective-permute-start.5 = (bf16[24,3584]{1,0:T(8,128)(2,1)S(1)}, bf16[24,3584]{1,0:T(8,128)(2,1)S(1)}, u32[]{:S(2)}, u32[]{:S(2)}) collective-permute-start(bf16[24,3584]{1,0:T(8,128)(2,1)S(1)} %get-tuple-element.31), channel_id=1, source_target_pairs={{0,224},{1,225},{2,226},{3,227},{4,228},{5,229},{6,230},{7,231},{8... | collective-permute-start | bytes 516104 | tf_op jit(solution)/shard_map/ppermute | solution.py:281
  69.7 20.8 %collective-permute-start.6 = (bf16[24,3584]{1,0:T(8,128)(2,1)}, bf16[24,3584]{1,0:T(8,128)(2,1)}, u32[]{:S(2)}, u32[]{:S(2)}) collective-permute-start(bf16[24,3584]{1,0:T(8,128)(2,1)} %get-tuple-element.32), channel_id=1, source_target_pairs={{0,144},{1,145},{2,146},{3,147},{4,148},{5,149},{6,150},{7,151},{8... | collective-permute-start | bytes 516104 | tf_op jit(solution)/shard_map/ppermute | solution.py:281
  69.7 21.7 %collective-permute-start.7 = (bf16[24,3584]{1,0:T(8,128)(2,1)}, bf16[24,3584]{1,0:T(8,128)(2,1)}, u32[]{:S(2)}, u32[]{:S(2)}) collective-permute-start(bf16[24,3584]{1,0:T(8,128)(2,1)} %get-tuple-element.33), channel_id=1, source_target_pairs={{0,178},{1,179},{2,176},{3,177},{4,182},{5,183},{6,180},{7,181},{8... | collective-permute-start | bytes 516104 | tf_op jit(solution)/shard_map/ppermute | solution.py:281
  76.4 16.0 %collective-permute-start.8 = (bf16[24,3584]{1,0:T(8,128)(2,1)}, bf16[24,3584]{1,0:T(8,128)(2,1)}, u32[]{:S(2)}, u32[]{:S(2)}) collective-permute-start(bf16[24,3584]{1,0:T(8,128)(2,1)} %get-tuple-element.34), channel_id=1, source_target_pairs={{0,80},{1,81},{2,82},{3,83},{4,84},{5,85},{6,86},{7,87},{8,88},{9,... | collective-permute-start | bytes 516104 | tf_op jit(solution)/shard_map/ppermute | solution.py:281
  76.7 16.6 %collective-permute-start.9 = (bf16[24,3584]{1,0:T(8,128)(2,1)}, bf16[24,3584]{1,0:T(8,128)(2,1)}, u32[]{:S(2)}, u32[]{:S(2)}) collective-permute-start(bf16[24,3584]{1,0:T(8,128)(2,1)} %get-tuple-element.35), channel_id=1, source_target_pairs={{0,242},{1,243},{2,240},{3,241},{4,246},{5,247},{6,244},{7,245},{8... | collective-permute-start | bytes 516104 | tf_op jit(solution)/shard_map/ppermute | solution.py:281
  82.6 27.8 %copy-start = (bf16[1,640,896]{2,1,0:T(8,128)(2,1)S(1)}, bf16[1,640,896]{2,1,0:T(8,128)(2,1)}, u32[]{:S(2)}) copy-start(bf16[1,640,896]{2,1,0:T(8,128)(2,1)} %param.15) | copy-start | bytes 3440644
  82.6 80.0 %reduce-scatter.3.cloned.1.call-start = ((), (), s32[]{:S(2)}) async-start(), calls=%async_computation.7 | async-start | bytes 2457600 | tf_op jit(solution)/shard_map/reduce_scatter | solution.py:306
  94.2 12.8 %collective-permute-start.10 = (bf16[192,3584]{1,0:T(8,128)(2,1)S(1)}, bf16[192,3584]{1,0:T(8,128)(2,1)S(1)}, u32[]{:S(2)}, u32[]{:S(2)}) collective-permute-start(bf16[192,3584]{1,0:T(8,128)(2,1)S(1)} %constant_dynamic-update-slice_fusion.own_ref.refs_0_), channel_id=1, source_target_pairs={{0,1},{1,0},{2,3},{3,2},{4,5},{5,4},{6,7},{7,6},{8,9},{9,8},{10,11... | collective-permute-start | bytes 4128776 | tf_op jit(solution)/shard_map/ppermute | solution.py:283
  95.1 7.8 %collective-permute-start.11 = (bf16[24,3584]{1,0:T(8,128)(2,1)S(1)}, bf16[24,3584]{1,0:T(8,128)(2,1)S(1)}, u32[]{:S(2)}, u32[]{:S(2)}) collective-permute-start(bf16[24,3584]{1,0:T(8,128)(2,1)S(1)} %copy-done.18), channel_id=1, source_target_pairs={{0,114},{1,115},{2,112},{3,113},{4,118},{5,119},{6,116},{7,117},{8... | collective-permute-start | bytes 516104 | tf_op jit(solution)/shard_map/ppermute | solution.py:281
  96.1 7.9 %collective-permute-start.12 = (bf16[24,3584]{1,0:T(8,128)(2,1)S(1)}, bf16[24,3584]{1,0:T(8,128)(2,1)S(1)}, u32[]{:S(2)}, u32[]{:S(2)}) collective-permute-start(bf16[24,3584]{1,0:T(8,128)(2,1)S(1)} %copy-done.16), channel_id=1, source_target_pairs={{0,208},{1,209},{2,210},{3,211},{4,212},{5,213},{6,214},{7,215},{8... | collective-permute-start | bytes 516104 | tf_op jit(solution)/shard_map/ppermute | solution.py:281
  98.7 16.3 %collective-permute-start.13 = (bf16[24,3584]{1,0:T(8,128)(2,1)}, bf16[24,3584]{1,0:T(8,128)(2,1)}, u32[]{:S(2)}, u32[]{:S(2)}) collective-permute-start(bf16[24,3584]{1,0:T(8,128)(2,1)} %get-tuple-element.38), channel_id=1, source_target_pairs={{0,32},{1,33},{2,34},{3,35},{4,36},{5,37},{6,38},{7,39},{8,40},{9,... | collective-permute-start | bytes 516104 | tf_op jit(solution)/shard_map/ppermute | solution.py:281
  98.7 18.0 %collective-permute-start.14 = (bf16[24,3584]{1,0:T(8,128)(2,1)}, bf16[24,3584]{1,0:T(8,128)(2,1)}, u32[]{:S(2)}, u32[]{:S(2)}) collective-permute-start(bf16[24,3584]{1,0:T(8,128)(2,1)} %get-tuple-element.39), channel_id=1, source_target_pairs={{0,128},{1,129},{2,130},{3,131},{4,132},{5,133},{6,134},{7,135},{8... | collective-permute-start | bytes 516104 | tf_op jit(solution)/shard_map/ppermute | solution.py:281
  102.9 15.4 %collective-permute-start.15 = (bf16[24,3584]{1,0:T(8,128)(2,1)}, bf16[24,3584]{1,0:T(8,128)(2,1)}, u32[]{:S(2)}, u32[]{:S(2)}) collective-permute-start(bf16[24,3584]{1,0:T(8,128)(2,1)} %get-tuple-element.40), channel_id=1, source_target_pairs={{0,16},{1,17},{2,18},{3,19},{4,20},{5,21},{6,22},{7,23},{8,24},{9,... | collective-permute-start | bytes 516104 | tf_op jit(solution)/shard_map/ppermute | solution.py:281
  104.0 16.0 %collective-permute-start.16 = (bf16[24,3584]{1,0:T(8,128)(2,1)}, bf16[24,3584]{1,0:T(8,128)(2,1)}, u32[]{:S(2)}, u32[]{:S(2)}) collective-permute-start(bf16[24,3584]{1,0:T(8,128)(2,1)} %get-tuple-element.41), channel_id=1, source_target_pairs={{0,50},{1,51},{2,48},{3,49},{4,54},{5,55},{6,52},{7,53},{8,58},{9,... | collective-permute-start | bytes 516104 | tf_op jit(solution)/shard_map/ppermute | solution.py:281
  107.0 14.6 %collective-permute-start.17 = (bf16[24,3584]{1,0:T(8,128)(2,1)}, bf16[24,3584]{1,0:T(8,128)(2,1)}, u32[]{:S(2)}, u32[]{:S(2)}) collective-permute-start(bf16[24,3584]{1,0:T(8,128)(2,1)} %get-tuple-element.42), channel_id=1, source_target_pairs={{0,64},{1,65},{2,66},{3,67},{4,68},{5,69},{6,70},{7,71},{8,72},{9,... | collective-permute-start | bytes 516104 | tf_op jit(solution)/shard_map/ppermute | solution.py:281
  115.0 70.1 %reduce-scatter.5.cloned.1.call-start = ((), (), s32[]{:S(2)}) async-start(), calls=%async_computation.8 | async-start | bytes 2457600 | tf_op jit(solution)/shard_map/reduce_scatter | solution.py:306
  115.1 8.1 %collective-permute-start.18 = (bf16[24,3584]{1,0:T(8,128)(2,1)S(1)}, bf16[24,3584]{1,0:T(8,128)(2,1)S(1)}, u32[]{:S(2)}, u32[]{:S(2)}) collective-permute-start(bf16[24,3584]{1,0:T(8,128)(2,1)S(1)} %get-tuple-element.43), channel_id=1, source_target_pairs={{0,192},{1,193},{2,194},{3,195},{4,196},{5,197},{6,198},{7,199},{8... | collective-permute-start | bytes 516104 | tf_op jit(solution)/shard_map/ppermute | solution.py:281
  123.9 5.7 %collective-permute-start.19 = (bf16[192,3584]{1,0:T(8,128)(2,1)}, bf16[192,3584]{1,0:T(8,128)(2,1)S(1)}, u32[]{:S(2)}, u32[]{:S(2)}) collective-permute-start(bf16[192,3584]{1,0:T(8,128)(2,1)} %constant_dynamic-update-slice_fusion.8.own_ref.refs_1_), channel_id=1, source_target_pairs={{0,1},{1,0},{2,3},{3,2},{4,5},{5,4},{6,7},{7,6},{8,9},{9,8},{10,11... | collective-permute-start | bytes 4128776 | tf_op jit(solution)/shard_map/ppermute | solution.py:283
  155.9 35.9 %all-to-all-start.3 = ((f16[16,40,896]{2,1,0:T(8,128)(2,1)}), f16[16,40,896]{2,1,0:T(8,128)(2,1)S(1)}, u32[]{:S(2)}, u32[]{:S(2)}) async-start(f16[16,40,896]{2,1,0:T(8,128)(2,1)} %bitcast.31), calls=%async_computation.5 | async-start | bytes 2293760 | tf_op jit(solution)/shard_map/all_to_all | solution.py:343
  191.8 19.5 %all-to-all-start = ((bf16[16,24,640]{2,1,0:T(8,128)(2,1)}), bf16[16,24,640]{2,1,0:T(8,128)(2,1)S(1)}, u32[]{:S(2)}, u32[]{:S(2)}) async-start(bf16[16,24,640]{2,1,0:T(8,128)(2,1)} %bitcast.16), calls=%async_computation.2 | async-start | bytes 983040 | tf_op jit(solution)/shard_map/all_to_all | solution.py:316
  211.3 33.0 %all-to-all-start.4 = ((f16[16,40,896]{2,1,0:T(8,128)(2,1)}), f16[16,40,896]{2,1,0:T(8,128)(2,1)S(1)}, u32[]{:S(2)}, u32[]{:S(2)}) async-start(f16[16,40,896]{2,1,0:T(8,128)(2,1)} %gather_fusion), calls=%async_computation.6 | async-start | bytes 2293760 | tf_op jit(solution)/shard_map/all_to_all | solution.py:344
  (21 other events, 124.7 us)
Sparse Core Ops, SparseCore 0:
  37.3 35.1 all-gather.4
  82.8 34.4 all-gather.6
  120.4 31.2 reduce-scatter.2
  154.1 30.9 reduce-scatter.4

commit v3 on v2

--- a/solution.py
+++ b/solution.py
@@ -16,6 +16,7 @@
 GROUPS = 16
 CAP = 24
 ROWS = GROUPS * CAP
+PAIR = 2 * CAP
 SCALE = 2048.0
 SAME_Y = [[g * RUN + y for g in range(GROUPS)] for y in range(RUN)]
 SAME_RUN = [[g * RUN + y for y in range(RUN)] for g in range(GROUPS)]
@@ -85,11 +86,9 @@
         out_ref[:, width:] = block.astype(jnp.bfloat16)
 
 
-def send_h_kernel(row_ref, col_ref, want_ref, acts_ref, own_ref, extra_ref):
-    for kind, out_ref in enumerate((own_ref, extra_ref)):
-        sel = choose(row_ref[0], col_ref[0], want_ref[kind])
-        rows = contract(jnp.where(sel, 1.0, 0.0).astype(jnp.bfloat16), acts_ref[...], ((1,), (0,)))
-        out_ref[...] = rows.astype(jnp.bfloat16)
+def send_h_kernel(row_ref, col_ref, want_ref, acts_ref, out_ref):
+    sel = jnp.where(choose(row_ref[0], col_ref[0], want_ref[...]), 1.0, 0.0).astype(jnp.bfloat16)
+    out_ref[...] = contract(sel, acts_ref[...], ((1,), (0,))).astype(jnp.bfloat16)
 
 
 def send_c_kernel(core_ref, want_ref, packed_ref, *out_refs):
@@ -105,63 +104,73 @@
     col = jnp.concatenate([columns[:, 0:1], columns[:, 1:2]], axis=0)
     gates = [lines[2 + 3 * k : 3 + 3 * k] + lines[3 + 3 * k : 4 + 3 * k] for k in range(2)]
     gates = [gates[k] + lines[4 + 3 * k : 5 + 3 * k] for k in range(2)]
-    sel = choose(row, col, want_ref[0])
+    sel = choose(row, col, want_ref[...])
     gate = jnp.sum(
         jnp.where(sel, jnp.concatenate(gates, axis=1), 0.0), axis=1, keepdims=True
     )
     sel = jnp.where(sel, 1.0, 0.0)
     sel = (sel[:, :tokens] + sel[:, tokens:]).astype(jnp.bfloat16)
-    rows = gate * contract(sel, packed_ref[0, :, :width], ((1,), (0,)))
+    rows = (gate * contract(sel, packed_ref[0, :, :width], ((1,), (0,)))).astype(jnp.bfloat16)
     for i, out_ref in enumerate(out_refs):
-        out_ref[...] = rows[i * CAP : (i + 1) * CAP].astype(jnp.bfloat16)
-
-
-def order_kernel(order_ref, *refs):
-    values, out_ref = refs[:-1], refs[-1]
+        out_ref[...] = rows[i * PAIR : (i + 1) * PAIR]
+
+
+def order_kernel(order_ref, value_ref, out_ref):
+    lane = lax.broadcasted_iota(jnp.int32, (2 * ROWS, 2 * ROWS), 1)
+    turn = jnp.where(lane == order_ref[...], 1.0, 0.0).astype(jnp.bfloat16)
+    out_ref[...] = contract(turn, value_ref[...], ((1,), (0,))).astype(jnp.bfloat16)
+
+
+def unorder_kernel(order_ref, value_ref, out_ref):
     lane = lax.broadcasted_iota(jnp.int32, (ROWS, ROWS), 1)
     turn = jnp.where(lane == order_ref[...], 1.0, 0.0).astype(jnp.bfloat16)
-    out_ref[...] = contract(turn, values[0][...], ((1,), (0,))).astype(jnp.bfloat16)
-
-
-def unorder_kernel(order_ref, first_ref, second_ref, out_ref):
-    lane = lax.broadcasted_iota(jnp.int32, (ROWS, ROWS), 1)
-    turn = jnp.where(lane == order_ref[...], 1.0, 0.0).astype(jnp.bfloat16)
-    half = ROWS // 2
-    out_ref[...] = (
-        contract(turn[:half], first_ref[...].astype(jnp.bfloat16), ((0,), (0,)))
-        + contract(turn[half:], second_ref[...].astype(jnp.bfloat16), ((0,), (0,)))
-    ).astype(jnp.bfloat16)
-
-
-def back_kernel(core_ref, own_ref, mate_ref, w_ref, out_ref):
+    out_ref[...] = contract(turn, value_ref[...].astype(jnp.bfloat16), ((0,), (0,))).astype(
+        jnp.bfloat16
+    )
+
+
+def join_kernel(*refs):
+    for i, ref in enumerate(refs[:-1]):
+        refs[-1][i * PAIR : (i + 1) * PAIR] = ref[...]
+
+
+def back_kernel(core_ref, *refs):
+    own_refs, mate_refs = refs[0:2], refs[2:4]
+    w_ref, out_ref = refs[4:]
     mine = pl.program_id(0) // 2 == core_ref[0]
+
+    def from_halves(c_refs):
+        half = c_refs[0].shape[0]
+        for at, c_ref in enumerate(c_refs):
+            rows = contract(c_ref[...], w_ref[...], ((1,), (1,)))
+            for i in range(half // PAIR):
+                start = (at * half // PAIR + i) * CAP
+                out_ref[0, start : start + CAP] = rows[i * PAIR : i * PAIR + CAP]
 
     @pl.when(mine)
     def _():
-        out_ref[0] = contract(own_ref[...], w_ref[...], ((1,), (1,)))
+        from_halves(own_refs)
 
     @pl.when(jnp.logical_not(mine))
     def _():
-        out_ref[0] = contract(mate_ref[...], w_ref[...], ((1,), (1,)))
-
-
-def update_kernel(core_ref, h_own_ref, h_extra_ref, *refs):
+        from_halves(mate_refs)
+
+
+def update_kernel(core_ref, h_ref, *refs):
     own_refs, mate_refs = refs[0:2], refs[2:4]
     w_ref, m_ref, v_ref, out_ref = refs[4:]
     core = core_ref[0]
     width = w_ref.shape[1]
-    half = ROWS // 2
+    half = own_refs[0].shape[0]
     total = jnp.zeros(w_ref.shape, jnp.float32)
     for c_refs, base in ((own_refs, 2 * core), (mate_refs, 2 - 2 * core)):
-        for kind, h_ref in enumerate((h_own_ref, h_extra_ref)):
-            for j in range(2):
-                part = 2 * kind + j
-                for at, c_ref in enumerate(c_refs):
-                    total += contract(
-                        h_ref[base + j, at * half : (at + 1) * half],
-                        c_ref[:, part * width : (part + 1) * width],
-                        ((0,), (0,)),
-                    )
+        for j in range(2):
+            for at, c_ref in enumerate(c_refs):
+                total += contract(
+                    h_ref[base + j, at * half : (at + 1) * half],
+                    c_ref[:, j * width : (j + 1) * width],
+                    ((0,), (0,)),
+                )
     m_new = beta_one * m_ref[...] + (1.0 - beta_one) * total
     v_new = beta_two * v_ref[...] + (1.0 - beta_two) * total * total
     direction = m_new / bias_one / (jnp.sqrt(v_new / bias_two) + epsilon)
@@ -170,7 +179,7 @@
 
 
 def take_kernel(row_ref, col_ref, want_ref, back_ref, out_ref):
-    sel = jnp.where(choose(row_ref[0], col_ref[0], want_ref[0]), 1.0, 0.0).astype(jnp.bfloat16)
+    sel = jnp.where(choose(row_ref[0], col_ref[0], want_ref[...]), 1.0, 0.0).astype(jnp.bfloat16)
     out_ref[...] = contract(sel, back_ref[...], ((0,), (0,))).astype(jnp.bfloat16)
 
 
@@ -213,9 +222,15 @@
     to = (x + steps[:, 0]) % GRID * GRID + (z + steps[:, 1]) % GRID
     by = (x - steps[:, 0]) % GRID * GRID + (z - steps[:, 1]) % GRID
     want_to = jnp.sum(jnp.where(to[:, None] == numbers[None, :], want[:, None, :], 0.0), axis=2)
-    want = jnp.broadcast_to(want[:, :, None], (2, GROUPS, CAP)).reshape(2, ROWS, 1)
-    want_to = jnp.broadcast_to(want_to[:, :, None], (2, GROUPS, CAP)).reshape(2, ROWS, 1)
-    order = (by[:, None] * CAP + jnp.arange(CAP, dtype=jnp.int32)[None, :]).reshape(ROWS, 1)
+    want_own = jnp.broadcast_to(want[0][:, None], (GROUPS, CAP)).reshape(ROWS, 1)
+
+    def spread_rows(values):
+        values = jnp.broadcast_to(values.T[:, :, None], (GROUPS, 2, CAP))
+        return values.reshape(2 * ROWS, 1)
+
+    want, want_to = spread_rows(want), spread_rows(want_to)
+    order_own = (by[:, None] * CAP + jnp.arange(CAP, dtype=jnp.int32)[None, :]).reshape(ROWS, 1)
+    order = (by[:, None] * PAIR + jnp.arange(PAIR, dtype=jnp.int32)[None, :]).reshape(2 * ROWS, 1)
     source = jnp.sum(
         jnp.where(new_slot[None, :] == numbers[:, None], old_slot[None, :], 0), axis=1
     )
@@ -241,85 +256,84 @@
     acts = hidden_acts.transpose(1, 0, 2).reshape(count, hidden)
     sent_h = pl.pallas_call(
         send_h_kernel,
-        out_shape=[jax.ShapeDtypeStruct((ROWS, hidden), jnp.bfloat16)] * 2,
+        out_shape=jax.ShapeDtypeStruct((2 * ROWS, hidden), jnp.bfloat16),
         compiler_params=params(16),
         name="send_h",
     )(own_row, own_col, want, acts)
-    all_h = []
-    for kind in range(2):
-        got = lax.all_to_all(sent_h[kind], "ep", 0, 0, axis_index_groups=SAME_Y, tiled=True)
-        got = pl.pallas_call(
-            order_kernel,
-            out_shape=jax.ShapeDtypeStruct((ROWS, hidden), jnp.bfloat16),
-            compiler_params=params(16),
-            name="order_h",
-        )(order, got)
-        all_h.append(
-            lax.all_gather(got, "ep", axis_index_groups=SAME_RUN, axis=0, tiled=False)
-        )
+    got_h = lax.all_to_all(sent_h, "ep", 0, 0, axis_index_groups=SAME_Y, tiled=True)
 
     send_c = pl.pallas_call(
         send_c_kernel,
         grid_spec=pltpu.PrefetchScalarGridSpec(
             num_scalar_prefetch=1,
-            grid=(2, 2),
+            grid=(2,),
             in_specs=[
-                pl.BlockSpec((1, ROWS, 1), lambda k, j, c: (k, 0, 0)),
+                whole((2 * ROWS, 1)),
                 pl.BlockSpec(
                     (1, tokens, width + LANES),
-                    lambda k, j, c: ((c[1] + 2 * RUN - 2 * c[0] - j) % RUN, 0, 0),
+                    lambda j, c: ((c[1] + 2 * RUN - 2 * c[0] - j) % RUN, 0, 0),
                 ),
             ],
-            out_specs=[pl.BlockSpec((CAP, width), lambda k, j, c: (0, 2 * k + j))] * GROUPS,
-        ),
-        out_shape=[jax.ShapeDtypeStruct((CAP, 4 * width), jnp.bfloat16)] * GROUPS,
+            out_specs=[pl.BlockSpec((PAIR, width), lambda j, c: (0, j))] * GROUPS,
+        ),
+        out_shape=[jax.ShapeDtypeStruct((PAIR, 2 * width), jnp.bfloat16)] * GROUPS,
         compiler_params=params(24),
         name="send_c",
     )(jnp.stack([core, y]), want_to, packed)
+    send_c = list(send_c)
+    got_h, send_c[0] = lax.optimization_barrier((got_h, send_c[0]))
+    got_h = pl.pallas_call(
+        order_kernel,
+        out_shape=jax.ShapeDtypeStruct((2 * ROWS, hidden), jnp.bfloat16),
+        compiler_params=params(16),
+        name="order_h",
+    )(order, got_h)
+    all_h = lax.all_gather(got_h, "ep", axis_index_groups=SAME_RUN, axis=0, tiled=False)
+
     got_c = [send_c[0]]
     for step, block in zip(SHIFTS[1:], send_c[1:], strict=True):
         got_c.append(lax.ppermute(block, ("ep", "dp"), nearest(*step)))
-    got_c = [jnp.concatenate(got_c[:HALF]), jnp.concatenate(got_c[HALF:])]
+    got_c = [
+        pl.pallas_call(
+            join_kernel,
+            out_shape=jax.ShapeDtypeStruct((ROWS, 2 * width), jnp.bfloat16),
+            compiler_params=params(16),
+            name="join",
+        )(*part)
+        for part in (got_c[:HALF], got_c[HALF:])
+    ]
     mate_c = [lax.ppermute(part, "dp", OTHER_CORE) for part in got_c]
 
     weight = weights[0]
-    half = ROWS // 2
-    summed = []
-    for at in range(2):
-        partial_back = pl.pallas_call(
-            back_kernel,
-            grid_spec=pltpu.PrefetchScalarGridSpec(
-                num_scalar_prefetch=1,
-                grid=(RUN,),
-                in_specs=[
-                    pl.BlockSpec((half, width), lambda s, c: (0, s % 2)),
-                    pl.BlockSpec((half, width), lambda s, c: (0, s % 2)),
-                    whole((hidden, width)),
-                ],
-                out_specs=pl.BlockSpec((1, half, hidden), lambda s, c: (s, 0, 0)),
-            ),
-            out_shape=jax.ShapeDtypeStruct((RUN, half, hidden), jnp.float32),
-            compiler_params=params(16),
-            name="back",
-        )(cores, got_c[at], mate_c[at], weight)
-        summed.append(
-            lax.psum_scatter(
-                partial_back, "ep", scatter_dimension=0, axis_index_groups=SAME_RUN, tiled=False
-            )
-        )
+    partial_back = pl.pallas_call(
+        back_kernel,
+        grid_spec=pltpu.PrefetchScalarGridSpec(
+            num_scalar_prefetch=1,
+            grid=(RUN,),
+            in_specs=[pl.BlockSpec((ROWS, width), lambda s, c: (0, s % 2))] * 4
+            + [whole((hidden, width))],
+            out_specs=pl.BlockSpec((1, ROWS, hidden), lambda s, c: (s, 0, 0)),
+        ),
+        out_shape=jax.ShapeDtypeStruct((RUN, ROWS, hidden), jnp.float32),
+        compiler_params=params(48),
+        name="back",
+    )(cores, *got_c, *mate_c, weight)
+    summed = lax.psum_scatter(
+        partial_back, "ep", scatter_dimension=0, axis_index_groups=SAME_RUN, tiled=False
+    )
     back = pl.pallas_call(
         unorder_kernel,
         out_shape=jax.ShapeDtypeStruct((ROWS, hidden), jnp.bfloat16),
         compiler_params=params(16),
         name="unorder",
-    )(order, *summed)
+    )(order_own, summed)
     back = lax.all_to_all(back, "ep", 0, 0, axis_index_groups=SAME_Y, tiled=True)
     hidden_out = pl.pallas_call(
         take_kernel,
         out_shape=jax.ShapeDtypeStruct((count, hidden), jnp.bfloat16),
         compiler_params=params(16),
         name="take",
-    )(own_row, own_col, want, back)
+    )(own_row, own_col, want_own, back)
     hidden_out = hidden_out.reshape(top, tokens, hidden).transpose(1, 0, 2)
 
     block = 128
@@ -329,15 +343,15 @@
         grid_spec=pltpu.PrefetchScalarGridSpec(
             num_scalar_prefetch=1,
             grid=(grid,),
-            in_specs=[pl.BlockSpec((RUN, ROWS, block), lambda i, c: (0, 0, i))] * 2
-            + [whole((half, 4 * width))] * 4
+            in_specs=[pl.BlockSpec((RUN, 2 * ROWS, block), lambda i, c: (0, 0, i))]
+            + [whole((ROWS, 2 * width))] * 4
             + [pl.BlockSpec((block, width), lambda i, c: (i, 0))] * 3,
             out_specs=pl.BlockSpec((block, width), lambda i, c: (i, 0)),
         ),
         out_shape=jax.ShapeDtypeStruct((hidden, width), jnp.float32),
-        compiler_params=params(24),
+        compiler_params=params(56),
         name="update",
-    )(cores, *all_h, *got_c, *mate_c, weight, first_moment[0], second_moment[0])
+    )(cores, all_h, *got_c, *mate_c, weight, first_moment[0], second_moment[0])
 
     spread = update.astype(jnp.float16).reshape(GROUPS, hidden // GROUPS, width)
     spread = lax.all_to_all(spread, "ep", 0, 0, axis_index_groups=SAME_Y, tiled=True)

time: 254 us -> 221 us (0.87)
  waiting for transfers between devices: 110 us -> 84 us
  local copies, waits for them, and re-layouts: 35.8 us -> 13.3 us
  starting transfers between devices: 61.5 us -> 71 us
  Pallas kernels: 26 us -> 29.9 us
  other arithmetic: 4.79 us -> 7.51 us
    unnamed x62 -> x46, local copies, waits for them, and re-layouts: 29.2 us -> 7.79 us
    all_to_all x2 -> x1, waiting for transfers between devices: 14.7 us -> 0.59 us  [local(): lax.all_to_all(sent_h, 'ep', 0, 0, axis_index_groups=SAME_Y, tiled=True)]
    ppermute x2, starting transfers between devices: 3.62 us -> 14 us  [local(): mate_c = [lax.ppermute(part, 'dp', OTHER_CORE) for part in got_c]]
    ppermute x15, waiting for transfers between devices: 13 us -> 4.95 us  [local(): got_c.append(lax.ppermute(block, ('ep', 'dp'), nearest(*step)))]
    ppermute x3, waiting for transfers between devices: 13.3 us -> 9.13 us  [local(): lax.ppermute(packed[s], 'ep', along_y(s))]
    pallas_call x1, Pallas kernels: 8.61 us -> 12.6 us  [local(): pl.pallas_call(update_kernel, grid_spec=pltpu.PrefetchScalarGridSpec(num_...]
    all_to_all x2 -> x1, starting transfers between devices: 12.7 us -> 9.16 us  [local(): lax.all_to_all(sent_h, 'ep', 0, 0, axis_index_groups=SAME_Y, tiled=True)]
    reduce_scatter x2 -> x1, waiting for transfers between devices: 22.4 us -> 23.9 us  [local(): lax.psum_scatter(partial_back, 'ep', scatter_dimension=0, axis_index_grou...]
  transfers between devices with their start and end apart: 29 -> 26, of which waited for: 13 -> 10; matrix products, arithmetic and copies ran while one was open for 8% -> 4% of each run, Pallas kernels for 9% -> 12%
where the time goes in v3:
time: 221 us; the launch traced here: 220 us
  waiting for transfers between devices  84 us (38%)
  starting transfers between devices  71 us (32%)
  Pallas kernels  29.9 us (14%)
  between operations  14.4 us (7%)
  local copies, waits for them, and re-layouts  13.3 us (6%)
  other arithmetic  7.51 us (3%)
    ppermute x15, starting transfers between devices, local(): got_c.append(lax.ppermute(block, ('ep', 'dp'), nearest(*step)))  28.6 us
    all_to_all x1, waiting for transfers between devices, local(): lax.all_to_all(spread[source], 'ep', 0, 0, axis_index_groups=SAME_Y, tile...  27.2 us
    reduce_scatter x1, waiting for transfers between devices, local(): lax.psum_scatter(partial_back, 'ep', scatter_dimension=0, axis_index_grou...  23.9 us
    ppermute x2, starting transfers between devices, local(): mate_c = [lax.ppermute(part, 'dp', OTHER_CORE) for part in got_c]  14 us
    all_to_all x1, waiting for transfers between devices, local(): lax.all_to_all(back, 'ep', 0, 0, axis_index_groups=SAME_Y, tiled=True)  13 us
    pallas_call x1, Pallas kernels, local(): pl.pallas_call(update_kernel, grid_spec=pltpu.PrefetchScalarGridSpec(num_...  12.6 us
    all_to_all x1, starting transfers between devices, local(): lax.all_to_all(sent_h, 'ep', 0, 0, axis_index_groups=SAME_Y, tiled=True)  9.16 us
    ppermute x3, waiting for transfers between devices, local(): lax.ppermute(packed[s], 'ep', along_y(s))  9.13 us
  transfers between devices with their start and end apart: 26, of which 10 were waited for; matrix products, arithmetic and copies ran while one was open for 4% of the time, Pallas kernels for 12%

profile of v3, /device:TPU:1, one launch (start us, length us, event | category | flops | bytes accessed | tf_op | source)
XLA Modules:
  0.0 220.2 jit_solution(2779761924823957268)
XLA Ops:
  10.2 1.6 send_h.1
  11.9 9.2 %all-to-all-start = ((bf16[16,48,640]{2,1,0:T(8,128)(2,1)}), bf16[16,48,640]{2,1,0:T(8,128)(2,1)S(1)}, u32[]{:S(2)}, u32[]{:S(2)}) async-start(bf16[16,48,640]{2,1,0:T(8,128)(2,1)} %bitcast.12), calls=%async_computation | async-start | bytes 1966080 | tf_op jit(solution)/shard_map/all_to_all | solution.py:263
  22.8 2.6 %collective-permute-start.1 = (bf16[128,1024]{1,0:T(8,128)(2,1)S(1)}, bf16[128,1024]{1,0:T(8,128)(2,1)}, u32[]{:S(2)}, u32[]{:S(2)}) collective-permute-start(bf16[128,1024]{1,0:T(8,128)(2,1)S(1)} %get-tuple-element.26), channel_id=1, source_target_pairs={{0,8},{4,12},{8,0},{12,4},{16,24},{20,28},{24,16},{28,20},{32,40},... | collective-permute-start | bytes 786440 | tf_op jit(solution)/shard_map/ppermute | solution.py:251
  27.4 2.3 %collective-permute-done = bf16[128,1024]{1,0:T(8,128)(2,1)S(1)} collective-permute-done((bf16[128,1024]{1,0:T(8,128)(2,1)S(1)}, bf16[128,1024]{1,0:T(8,128)(2,1)S(1)}, u32[]{:S(2)}, u32[]{:S(2)}) %collective-permute-start) | collective-permute-done | bytes 262176 | tf_op jit(solution)/shard_map/ppermute | solution.py:251
  29.7 6.8 %collective-permute-done.1 = bf16[128,1024]{1,0:T(8,128)(2,1)} collective-permute-done((bf16[128,1024]{1,0:T(8,128)(2,1)S(1)}, bf16[128,1024]{1,0:T(8,128)(2,1)}, u32[]{:S(2)}, u32[]{:S(2)}) %collective-permute-start.1) | collective-permute-done | bytes 262176 | tf_op jit(solution)/shard_map/ppermute | solution.py:251
  37.7 2.9 %send_c.1 = (bf16[48,1792]{1,0:T(8,128)(2,1)S(1)}, bf16[48,1792]{1,0:T(8,128)(2,1)S(1)}, bf16[48,1792]{1,0:T(8,128)(2,1)S(1)}, bf16[48,1792]{1,0:T(8,128)(2,1)S(...) custom-call(s32[2]{0:T(128)S(1)} %pad_add_fusion.core_ref, ...), custom_call_target="tpu_custom_call" | custom-call | tf_op jit(solution)/shard_map/send_c/pallas_call | solution.py:265
  46.7 2.2 order_h.1
  48.9 4.5 %collective-permute-start.10 = (bf16[48,1792]{1,0:T(8,128)(2,1)}, bf16[48,1792]{1,0:T(8,128)(2,1)S(1)}, u32[]{:S(2)}, u32[]{:S(2)}) collective-permute-start(bf16[48,1792]{1,0:T(8,128)(2,1)} %copy-done.16), channel_id=1, source_target_pairs={{0,114},{1,115},{2,112},{3,113},{4,118},{5,119},{6,116},{7,117},{8... | collective-permute-start | bytes 516104 | tf_op jit(solution)/shard_map/ppermute | solution.py:295
  53.9 1.9 collective-permute-start.13
  55.8 4.1 %collective-permute-start.14 = (bf16[48,1792]{1,0:T(8,128)(2,1)}, bf16[48,1792]{1,0:T(8,128)(2,1)S(1)}, u32[]{:S(2)}, u32[]{:S(2)}) collective-permute-start(bf16[48,1792]{1,0:T(8,128)(2,1)} %copy-done.12), channel_id=1, source_target_pairs={{0,16},{1,17},{2,18},{3,19},{4,20},{5,21},{6,22},{7,23},{8,24},{9,... | collective-permute-start | bytes 516104 | tf_op jit(solution)/shard_map/ppermute | solution.py:295
  60.3 2.1 collective-permute-done.11.refs_1_
  62.4 1.7 collective-permute-start.16
  64.0 1.7 collective-permute-start.17
  65.7 2.8 %collective-permute-done.14.refs_4_ = bf16[48,1792]{1,0:T(8,128)(2,1)S(1)} collective-permute-done((bf16[48,1792]{1,0:T(8,128)(2,1)}, bf16[48,1792]{1,0:T(8,128)(2,1)S(1)}, u32[]{:S(2)}, u32[]{:S(2)}) %collective-permute-start.14) | collective-permute-done | bytes 172064 | tf_op jit(solution)/shard_map/ppermute | solution.py:295
  68.6 3.9 %collective-permute-start.5 = (bf16[48,1792]{1,0:T(8,128)(2,1)S(1)}, bf16[48,1792]{1,0:T(8,128)(2,1)S(1)}, u32[]{:S(2)}, u32[]{:S(2)}) collective-permute-start(bf16[48,1792]{1,0:T(8,128)(2,1)S(1)} %get-tuple-element.32), channel_id=1, source_target_pairs={{0,224},{1,225},{2,226},{3,227},{4,228},{5,229},{6,230},{7,231},{8... | collective-permute-start | bytes 516104 | tf_op jit(solution)/shard_map/ppermute | solution.py:295
  72.6 5.1 %collective-permute-start.7 = (bf16[48,1792]{1,0:T(8,128)(2,1)S(1)}, bf16[48,1792]{1,0:T(8,128)(2,1)S(1)}, u32[]{:S(2)}, u32[]{:S(2)}) collective-permute-start(bf16[48,1792]{1,0:T(8,128)(2,1)S(1)} %get-tuple-element.34), channel_id=1, source_target_pairs={{0,178},{1,179},{2,176},{3,177},{4,182},{5,183},{6,180},{7,181},{8... | collective-permute-start | bytes 516104 | tf_op jit(solution)/shard_map/ppermute | solution.py:295
  77.6 4.8 %collective-permute-start.9 = (bf16[48,1792]{1,0:T(8,128)(2,1)S(1)}, bf16[48,1792]{1,0:T(8,128)(2,1)S(1)}, u32[]{:S(2)}, u32[]{:S(2)}) collective-permute-start(bf16[48,1792]{1,0:T(8,128)(2,1)S(1)} %get-tuple-element.36), channel_id=1, source_target_pairs={{0,242},{1,243},{2,240},{3,241},{4,246},{5,247},{6,244},{7,245},{8... | collective-permute-start | bytes 516104 | tf_op jit(solution)/shard_map/ppermute | solution.py:295
  82.5 10.8 %collective-permute-start.19 = (bf16[384,1792]{1,0:T(8,128)(2,1)S(1)}, bf16[384,1792]{1,0:T(8,128)(2,1)S(1)}, u32[]{:S(2)}, u32[]{:S(2)}) collective-permute-start(bf16[384,1792]{1,0:T(8,128)(2,1)S(1)} %join.3.refs_1_), channel_id=1, source_target_pairs={{0,1},{1,0},{2,3},{3,2},{4,5},{5,4},{6,7},{7,6},{8,9},{9,8},{10,11... | collective-permute-start | bytes 4128776 | tf_op jit(solution)/shard_map/ppermute | solution.py:305
  93.4 3.2 %collective-permute-start.18 = (bf16[384,1792]{1,0:T(8,128)(2,1)S(1)}, bf16[384,1792]{1,0:T(8,128)(2,1)S(1)}, u32[]{:S(2)}, u32[]{:S(2)}) collective-permute-start(bf16[384,1792]{1,0:T(8,128)(2,1)S(1)} %join.2.refs_0_), channel_id=1, source_target_pairs={{0,1},{1,0},{2,3},{3,2},{4,5},{5,4},{6,7},{7,6},{8,9},{9,8},{10,11... | collective-permute-start | bytes 4128776 | tf_op jit(solution)/shard_map/ppermute | solution.py:305
  96.7 2.8 %collective-permute-done.18.refs_2_ = bf16[384,1792]{1,0:T(8,128)(2,1)S(1)} collective-permute-done((bf16[384,1792]{1,0:T(8,128)(2,1)S(1)}, bf16[384,1792]{1,0:T(8,128)(2,1)S(1)}, u32[]{:S(2)}, u32[]{:S(2)}) %collective-permute-start.18) | collective-permute-done | bytes 1376288 | tf_op jit(solution)/shard_map/ppermute | solution.py:305
  99.4 8.3 %back.1 = f32[4,384,640]{2,1,0:T(8,128)} custom-call(s32[1]{0:T(128)} %bitcast.7.core_ref, bf16[384,1792]{1,0:T(8,128)(2,1)S(1)} %join.2.refs_0_, bf16[384,1792]{1,0:T(8,128)(2,1)S(1)} %join.3.refs_1_, bf16[384,1792]{1,0:T(8,128)(2,1)S(1)} %collective-permute-done.18.refs_2_, bf16[384,1792]{1,0:T(8,128)(2,1)} %copy-done.17, bf16[640,896]{1,0:T(8,128)(2,1)S(1)} %bitcast.48), custom_call_target="tpu_custom_call" | custom-call | tf_op jit(solution)/shard_map/back/pallas_call | solution.py:308
  108.9 12.6 %update.1 = f32[640,896]{1,0:T(8,128)} custom-call(s32[1]{0:T(128)} %bitcast.7.core_ref, bf16[4,768,640]{2,1,0:T(8,128)(2,1)} %bitcast.58, bf16[384,1792]{1,0:T(8,128)(2,1)} %copy-done.1, bf16[384,1792]{1,0:T(8,128)(2,1)} %copy-done, bf16[384,1792]{1,0:T(8,128)(2,1)} %copy-done.2, bf16[384,1792]{1,0:T(8,128)(2,1)} %copy-done.17, bf16[640,896]{1,0:T(8,128)(2,1)} %bitcast.47, ...), custom_call_target="tpu_custom_call" | custom-call | tf_op jit(solution)/shard_map/update/pallas_call | solution.py:341
  121.5 2.8 %convert_element_type.27 = f16[640,896]{1,0:T(8,128)(2,1)} convert(f32[640,896]{1,0:T(8,128)} %update.1) | non-fusion elementwise | flops 573440 | bytes 3440640 | tf_op jit(solution)/shard_map/convert_element_type | solution.py:356
  124.3 5.9 %all-to-all-start.2 = ((f16[16,40,896]{2,1,0:T(8,128)(2,1)}), f16[16,40,896]{2,1,0:T(8,128)(2,1)S(1)}, u32[]{:S(2)}, u32[]{:S(2)}) async-start(f16[16,40,896]{2,1,0:T(8,128)(2,1)} %bitcast.31), calls=%async_computation.3 | async-start | bytes 2293760 | tf_op jit(solution)/shard_map/all_to_all | solution.py:357
  130.5 23.9 %reduce-scatter.2.cloned.1.call-done = f32[1,384,640]{2,1,0:T(8,128)} async-done(((f32[4,384,640]{2,1,0:T(8,128)}), f32[1,384,640]{2,1,0:T(8,128)}) %reduce-scatter.2.cloned.1.call-update) | async-done | bytes 983056 | tf_op jit(solution)/shard_map/reduce_scatter | solution.py:321
  156.9 2.5 %all-to-all-done.2 = f16[16,40,896]{2,1,0:T(8,128)(2,1)S(1)} async-done(((f16[16,40,896]{2,1,0:T(8,128)(2,1)}), f16[16,40,896]{2,1,0:T(8,128)(2,1)S(1)}, u32[]{:S(2)}, u32[]{:S(2)}) %all-to-all-start.2) | async-done | bytes 1146912 | tf_op jit(solution)/shard_map/all_to_all | solution.py:357
  159.4 4.6 %all-to-all-start.1 = ((bf16[16,24,640]{2,1,0:T(8,128)(2,1)}), bf16[16,24,640]{2,1,0:T(8,128)(2,1)S(1)}, u32[]{:S(2)}, u32[]{:S(2)}) async-start(bf16[16,24,640]{2,1,0:T(8,128)(2,1)} %bitcast.23), calls=%async_computation.2 | async-start | bytes 983040 | tf_op jit(solution)/shard_map/all_to_all | solution.py:330
  164.0 2.0 gather_fusion
  166.0 13.0 %all-to-all-done.1 = bf16[16,24,640]{2,1,0:T(8,128)(2,1)S(1)} async-done(((bf16[16,24,640]{2,1,0:T(8,128)(2,1)}), bf16[16,24,640]{2,1,0:T(8,128)(2,1)S(1)}, u32[]{:S(2)}, u32[]{:S(2)}) %all-to-all-start.1) | async-done | bytes 491552 | tf_op jit(solution)/shard_map/all_to_all | solution.py:330
  179.0 3.7 %all-to-all-start.3 = ((f16[16,40,896]{2,1,0:T(8,128)(2,1)}), f16[16,40,896]{2,1,0:T(8,128)(2,1)S(1)}, u32[]{:S(2)}, u32[]{:S(2)}) async-start(f16[16,40,896]{2,1,0:T(8,128)(2,1)} %gather_fusion), calls=%async_computation.4 | async-start | bytes 2293760 | tf_op jit(solution)/shard_map/all_to_all | solution.py:358
  184.5 27.2 %all-to-all-done.3 = f16[16,40,896]{2,1,0:T(8,128)(2,1)S(1)} async-done(((f16[16,40,896]{2,1,0:T(8,128)(2,1)}), f16[16,40,896]{2,1,0:T(8,128)(2,1)S(1)}, u32[]{:S(2)}, u32[]{:S(2)}) %all-to-all-start.3) | async-done | bytes 1146912 | tf_op jit(solution)/shard_map/all_to_all | solution.py:358
  211.8 1.6 convert_multiply_fusion
  (112 shorter events, 20.7 us)
Async XLA Ops:
  11.9 15.2 %copy-start.21 = (s32[16,1]{0,1:T(1,128)S(1)}, s32[16,1]{0,1:T(1,128)}, u32[]{:S(2)}) copy-start(s32[16,1]{0,1:T(1,128)} %constant.102) | copy-start | bytes 196
  11.9 15.2 %copy-start.22 = (s32[16,1]{0,1:T(1,128)S(1)}, s32[16,1]{0,1:T(1,128)}, u32[]{:S(2)}) copy-start(s32[16,1]{0,1:T(1,128)} %constant.103) | copy-start | bytes 196
  11.9 34.8 %all-to-all-start = ((bf16[16,48,640]{2,1,0:T(8,128)(2,1)}), bf16[16,48,640]{2,1,0:T(8,128)(2,1)S(1)}, u32[]{:S(2)}, u32[]{:S(2)}) async-start(bf16[16,48,640]{2,1,0:T(8,128)(2,1)} %bitcast.12), calls=%async_computation | async-start | bytes 1966080 | tf_op jit(solution)/shard_map/all_to_all | solution.py:263
  21.1 87.9 %all-gather.3.cloned.1.call-start = ((), (), s32[]{:S(2)}) async-start(), calls=%async_computation.6 | async-start | bytes 4915200 | tf_op jit(solution)/shard_map/all_gather | solution.py:291
  21.4 8.3 %collective-permute-start = (bf16[128,1024]{1,0:T(8,128)(2,1)S(1)}, bf16[128,1024]{1,0:T(8,128)(2,1)S(1)}, u32[]{:S(2)}, u32[]{:S(2)}) collective-permute-start(bf16[128,1024]{1,0:T(8,128)(2,1)S(1)} %get-tuple-element.25), channel_id=1, source_target_pairs={{0,4},{4,8},{8,12},{12,0},{16,20},{20,24},{24,28},{28,16},{32,36},... | collective-permute-start | bytes 786440 | tf_op jit(solution)/shard_map/ppermute | solution.py:251
  22.8 13.7 %collective-permute-start.1 = (bf16[128,1024]{1,0:T(8,128)(2,1)S(1)}, bf16[128,1024]{1,0:T(8,128)(2,1)}, u32[]{:S(2)}, u32[]{:S(2)}) collective-permute-start(bf16[128,1024]{1,0:T(8,128)(2,1)S(1)} %get-tuple-element.26), channel_id=1, source_target_pairs={{0,8},{4,12},{8,0},{12,4},{16,24},{20,28},{24,16},{28,20},{32,40},... | collective-permute-start | bytes 786440 | tf_op jit(solution)/shard_map/ppermute | solution.py:251
  25.4 11.1 %collective-permute-start.2 = (bf16[128,1024]{1,0:T(8,128)(2,1)S(1)}, bf16[128,1024]{1,0:T(8,128)(2,1)}, u32[]{:S(2)}, u32[]{:S(2)}) collective-permute-start(bf16[128,1024]{1,0:T(8,128)(2,1)S(1)} %get-tuple-element.27), channel_id=1, source_target_pairs={{0,12},{4,0},{8,4},{12,8},{16,28},{20,16},{24,20},{28,24},{32,44},... | collective-permute-start | bytes 786440 | tf_op jit(solution)/shard_map/ppermute | solution.py:251
  46.7 15.7 %copy-start.9 = (bf16[48,1792]{1,0:T(8,128)(2,1)S(1)}, bf16[48,1792]{1,0:T(8,128)(2,1)}, u32[]{:S(2)}) copy-start(bf16[48,1792]{1,0:T(8,128)(2,1)} %copy-done.8) | copy-start | bytes 516100
  46.7 17.4 %copy-start.7 = (bf16[48,1792]{1,0:T(8,128)(2,1)S(1)}, bf16[48,1792]{1,0:T(8,128)(2,1)}, u32[]{:S(2)}) copy-start(bf16[48,1792]{1,0:T(8,128)(2,1)} %copy-done.6) | copy-start | bytes 516100
  48.9 105.5 %reduce-scatter.2.cloned.1.call-start = ((), (), s32[]{:S(2)}) async-start(), calls=%async_computation.5 | async-start | bytes 4915200 | tf_op jit(solution)/shard_map/reduce_scatter | solution.py:321
  48.9 11.0 %collective-permute-start.10 = (bf16[48,1792]{1,0:T(8,128)(2,1)}, bf16[48,1792]{1,0:T(8,128)(2,1)S(1)}, u32[]{:S(2)}, u32[]{:S(2)}) collective-permute-start(bf16[48,1792]{1,0:T(8,128)(2,1)} %copy-done.16), channel_id=1, source_target_pairs={{0,114},{1,115},{2,112},{3,113},{4,118},{5,119},{6,116},{7,117},{8... | collective-permute-start | bytes 516104 | tf_op jit(solution)/shard_map/ppermute | solution.py:295
  53.4 9.0 %collective-permute-start.11 = (bf16[48,1792]{1,0:T(8,128)(2,1)}, bf16[48,1792]{1,0:T(8,128)(2,1)S(1)}, u32[]{:S(2)}, u32[]{:S(2)}) collective-permute-start(bf16[48,1792]{1,0:T(8,128)(2,1)} %copy-done.15), channel_id=1, source_target_pairs={{0,208},{1,209},{2,210},{3,211},{4,212},{5,213},{6,214},{7,215},{8... | collective-permute-start | bytes 516104 | tf_op jit(solution)/shard_map/ppermute | solution.py:295
  53.4 10.6 %collective-permute-start.12 = (bf16[48,1792]{1,0:T(8,128)(2,1)}, bf16[48,1792]{1,0:T(8,128)(2,1)S(1)}, u32[]{:S(2)}, u32[]{:S(2)}) collective-permute-start(bf16[48,1792]{1,0:T(8,128)(2,1)} %copy-done.14), channel_id=1, source_target_pairs={{0,32},{1,33},{2,34},{3,35},{4,36},{5,37},{6,38},{7,39},{8,40},{9,... | collective-permute-start | bytes 516104 | tf_op jit(solution)/shard_map/ppermute | solution.py:295
  53.9 11.8 %collective-permute-start.13 = (bf16[48,1792]{1,0:T(8,128)(2,1)}, bf16[48,1792]{1,0:T(8,128)(2,1)S(1)}, u32[]{:S(2)}, u32[]{:S(2)}) collective-permute-start(bf16[48,1792]{1,0:T(8,128)(2,1)} %copy-done.13), channel_id=1, source_target_pairs={{0,128},{1,129},{2,130},{3,131},{4,132},{5,133},{6,134},{7,135},{8... | collective-permute-start | bytes 516104 | tf_op jit(solution)/shard_map/ppermute | solution.py:295
  55.8 12.8 %collective-permute-start.14 = (bf16[48,1792]{1,0:T(8,128)(2,1)}, bf16[48,1792]{1,0:T(8,128)(2,1)S(1)}, u32[]{:S(2)}, u32[]{:S(2)}) collective-permute-start(bf16[48,1792]{1,0:T(8,128)(2,1)} %copy-done.12), channel_id=1, source_target_pairs={{0,16},{1,17},{2,18},{3,19},{4,20},{5,21},{6,22},{7,23},{8,24},{9,... | collective-permute-start | bytes 516104 | tf_op jit(solution)/shard_map/ppermute | solution.py:295
  60.0 8.6 %collective-permute-start.15 = (bf16[48,1792]{1,0:T(8,128)(2,1)S(1)}, bf16[48,1792]{1,0:T(8,128)(2,1)S(1)}, u32[]{:S(2)}, u32[]{:S(2)}) collective-permute-start(bf16[48,1792]{1,0:T(8,128)(2,1)S(1)} %copy-done.11), channel_id=1, source_target_pairs={{0,50},{1,51},{2,48},{3,49},{4,54},{5,55},{6,52},{7,53},{8,58},{9,... | collective-permute-start | bytes 516104 | tf_op jit(solution)/shard_map/ppermute | solution.py:295
  62.4 10.2 %collective-permute-start.16 = (bf16[48,1792]{1,0:T(8,128)(2,1)S(1)}, bf16[48,1792]{1,0:T(8,128)(2,1)S(1)}, u32[]{:S(2)}, u32[]{:S(2)}) collective-permute-start(bf16[48,1792]{1,0:T(8,128)(2,1)S(1)} %copy-done.9), channel_id=1, source_target_pairs={{0,64},{1,65},{2,66},{3,67},{4,68},{5,69},{6,70},{7,71},{8,72},{9,... | collective-permute-start | bytes 516104 | tf_op jit(solution)/shard_map/ppermute | solution.py:295
  64.0 8.5 %collective-permute-start.17 = (bf16[48,1792]{1,0:T(8,128)(2,1)S(1)}, bf16[48,1792]{1,0:T(8,128)(2,1)S(1)}, u32[]{:S(2)}, u32[]{:S(2)}) collective-permute-start(bf16[48,1792]{1,0:T(8,128)(2,1)S(1)} %copy-done.7), channel_id=1, source_target_pairs={{0,192},{1,193},{2,194},{3,195},{4,196},{5,197},{6,198},{7,199},{8... | collective-permute-start | bytes 516104 | tf_op jit(solution)/shard_map/ppermute | solution.py:295
  65.7 11.9 %collective-permute-start.3 = (bf16[48,1792]{1,0:T(8,128)(2,1)S(1)}, bf16[48,1792]{1,0:T(8,128)(2,1)S(1)}, u32[]{:S(2)}, u32[]{:S(2)}) collective-permute-start(bf16[48,1792]{1,0:T(8,128)(2,1)S(1)} %get-tuple-element.30), channel_id=1, source_target_pairs={{0,160},{1,161},{2,162},{3,163},{4,164},{5,165},{6,166},{7,167},{8... | collective-permute-start | bytes 516104 | tf_op jit(solution)/shard_map/ppermute | solution.py:295
  68.6 9.1 %collective-permute-start.4 = (bf16[48,1792]{1,0:T(8,128)(2,1)S(1)}, bf16[48,1792]{1,0:T(8,128)(2,1)S(1)}, u32[]{:S(2)}, u32[]{:S(2)}) collective-permute-start(bf16[48,1792]{1,0:T(8,128)(2,1)S(1)} %get-tuple-element.31), channel_id=1, source_target_pairs={{0,96},{1,97},{2,98},{3,99},{4,100},{5,101},{6,102},{7,103},{8,104... | collective-permute-start | bytes 516104 | tf_op jit(solution)/shard_map/ppermute | solution.py:295
  68.6 13.9 %collective-permute-start.5 = (bf16[48,1792]{1,0:T(8,128)(2,1)S(1)}, bf16[48,1792]{1,0:T(8,128)(2,1)S(1)}, u32[]{:S(2)}, u32[]{:S(2)}) collective-permute-start(bf16[48,1792]{1,0:T(8,128)(2,1)S(1)} %get-tuple-element.32), channel_id=1, source_target_pairs={{0,224},{1,225},{2,226},{3,227},{4,228},{5,229},{6,230},{7,231},{8... | collective-permute-start | bytes 516104 | tf_op jit(solution)/shard_map/ppermute | solution.py:295
  72.5 20.8 %collective-permute-start.6 = (bf16[48,1792]{1,0:T(8,128)(2,1)S(1)}, bf16[48,1792]{1,0:T(8,128)(2,1)S(1)}, u32[]{:S(2)}, u32[]{:S(2)}) collective-permute-start(bf16[48,1792]{1,0:T(8,128)(2,1)S(1)} %get-tuple-element.33), channel_id=1, source_target_pairs={{0,144},{1,145},{2,146},{3,147},{4,148},{5,149},{6,150},{7,151},{8... | collective-permute-start | bytes 516104 | tf_op jit(solution)/shard_map/ppermute | solution.py:295
  72.6 20.8 %collective-permute-start.7 = (bf16[48,1792]{1,0:T(8,128)(2,1)S(1)}, bf16[48,1792]{1,0:T(8,128)(2,1)S(1)}, u32[]{:S(2)}, u32[]{:S(2)}) collective-permute-start(bf16[48,1792]{1,0:T(8,128)(2,1)S(1)} %get-tuple-element.34), channel_id=1, source_target_pairs={{0,178},{1,179},{2,176},{3,177},{4,182},{5,183},{6,180},{7,181},{8... | collective-permute-start | bytes 516104 | tf_op jit(solution)/shard_map/ppermute | solution.py:295
  77.6 15.7 %collective-permute-start.8 = (bf16[48,1792]{1,0:T(8,128)(2,1)S(1)}, bf16[48,1792]{1,0:T(8,128)(2,1)S(1)}, u32[]{:S(2)}, u32[]{:S(2)}) collective-permute-start(bf16[48,1792]{1,0:T(8,128)(2,1)S(1)} %get-tuple-element.35), channel_id=1, source_target_pairs={{0,80},{1,81},{2,82},{3,83},{4,84},{5,85},{6,86},{7,87},{8,88},{9,... | collective-permute-start | bytes 516104 | tf_op jit(solution)/shard_map/ppermute | solution.py:295
  77.6 15.7 %collective-permute-start.9 = (bf16[48,1792]{1,0:T(8,128)(2,1)S(1)}, bf16[48,1792]{1,0:T(8,128)(2,1)S(1)}, u32[]{:S(2)}, u32[]{:S(2)}) collective-permute-start(bf16[48,1792]{1,0:T(8,128)(2,1)S(1)} %get-tuple-element.36), channel_id=1, source_target_pairs={{0,242},{1,243},{2,240},{3,241},{4,246},{5,247},{6,244},{7,245},{8... | collective-permute-start | bytes 516104 | tf_op jit(solution)/shard_map/ppermute | solution.py:295
  82.5 16.9 %copy-start = (bf16[384,1792]{1,0:T(8,128)(2,1)}, bf16[384,1792]{1,0:T(8,128)(2,1)S(1)}, u32[]{:S(2)}) copy-start(bf16[384,1792]{1,0:T(8,128)(2,1)S(1)} %join.3.refs_1_) | copy-start | bytes 4128772
  82.5 16.9 %copy-start.3 = (bf16[1,640,896]{2,1,0:T(8,128)(2,1)S(1)}, bf16[1,640,896]{2,1,0:T(8,128)(2,1)}, u32[]{:S(2)}) copy-start(bf16[1,640,896]{2,1,0:T(8,128)(2,1)} %param.15) | copy-start | bytes 3440644
  82.5 14.1 %collective-permute-start.19 = (bf16[384,1792]{1,0:T(8,128)(2,1)S(1)}, bf16[384,1792]{1,0:T(8,128)(2,1)S(1)}, u32[]{:S(2)}, u32[]{:S(2)}) collective-permute-start(bf16[384,1792]{1,0:T(8,128)(2,1)S(1)} %join.3.refs_1_), channel_id=1, source_target_pairs={{0,1},{1,0},{2,3},{3,2},{4,5},{5,4},{6,7},{7,6},{8,9},{9,8},{10,11... | collective-permute-start | bytes 4128776 | tf_op jit(solution)/shard_map/ppermute | solution.py:305
  93.4 6.0 %collective-permute-start.18 = (bf16[384,1792]{1,0:T(8,128)(2,1)S(1)}, bf16[384,1792]{1,0:T(8,128)(2,1)S(1)}, u32[]{:S(2)}, u32[]{:S(2)}) collective-permute-start(bf16[384,1792]{1,0:T(8,128)(2,1)S(1)} %join.2.refs_0_), channel_id=1, source_target_pairs={{0,1},{1,0},{2,3},{3,2},{4,5},{5,4},{6,7},{7,6},{8,9},{9,8},{10,11... | collective-permute-start | bytes 4128776 | tf_op jit(solution)/shard_map/ppermute | solution.py:305
  124.3 35.0 %all-to-all-start.2 = ((f16[16,40,896]{2,1,0:T(8,128)(2,1)}), f16[16,40,896]{2,1,0:T(8,128)(2,1)S(1)}, u32[]{:S(2)}, u32[]{:S(2)}) async-start(f16[16,40,896]{2,1,0:T(8,128)(2,1)} %bitcast.31), calls=%async_computation.3 | async-start | bytes 2293760 | tf_op jit(solution)/shard_map/all_to_all | solution.py:357
  159.4 19.6 %all-to-all-start.1 = ((bf16[16,24,640]{2,1,0:T(8,128)(2,1)}), bf16[16,24,640]{2,1,0:T(8,128)(2,1)S(1)}, u32[]{:S(2)}, u32[]{:S(2)}) async-start(bf16[16,24,640]{2,1,0:T(8,128)(2,1)} %bitcast.23), calls=%async_computation.2 | async-start | bytes 983040 | tf_op jit(solution)/shard_map/all_to_all | solution.py:330
  179.0 32.8 %all-to-all-start.3 = ((f16[16,40,896]{2,1,0:T(8,128)(2,1)}), f16[16,40,896]{2,1,0:T(8,128)(2,1)S(1)}, u32[]{:S(2)}, u32[]{:S(2)}) async-start(f16[16,40,896]{2,1,0:T(8,128)(2,1)} %gather_fusion), calls=%async_computation.4 | async-start | bytes 2293760 | tf_op jit(solution)/shard_map/all_to_all | solution.py:358
  (17 other events, 86.1 us)
Sparse Core Ops, SparseCore 0:
  49.0 49.0 all-gather.2
  109.0 45.2 reduce-scatter.1

commit v4 on v3

--- a/solution.py
+++ b/solution.py
@@ -16,7 +16,6 @@
 GROUPS = 16
 CAP = 24
 ROWS = GROUPS * CAP
-PAIR = 2 * CAP
 SCALE = 2048.0
 SAME_Y = [[g * RUN + y for g in range(GROUPS)] for y in range(RUN)]
 SAME_RUN = [[g * RUN + y for y in range(RUN)] for g in range(GROUPS)]
@@ -86,9 +85,11 @@
         out_ref[:, width:] = block.astype(jnp.bfloat16)
 
 
-def send_h_kernel(row_ref, col_ref, want_ref, acts_ref, out_ref):
-    sel = jnp.where(choose(row_ref[0], col_ref[0], want_ref[...]), 1.0, 0.0).astype(jnp.bfloat16)
-    out_ref[...] = contract(sel, acts_ref[...], ((1,), (0,))).astype(jnp.bfloat16)
+def send_h_kernel(row_ref, col_ref, want_ref, acts_ref, own_ref, extra_ref):
+    for kind, out_ref in enumerate((own_ref, extra_ref)):
+        sel = choose(row_ref[0], col_ref[0], want_ref[kind])
+        rows = contract(jnp.where(sel, 1.0, 0.0).astype(jnp.bfloat16), acts_ref[...], ((1,), (0,)))
+        out_ref[...] = rows.astype(jnp.bfloat16)
 
 
 def send_c_kernel(core_ref, want_ref, packed_ref, *out_refs):
@@ -104,19 +105,19 @@
     col = jnp.concatenate([columns[:, 0:1], columns[:, 1:2]], axis=0)
     gates = [lines[2 + 3 * k : 3 + 3 * k] + lines[3 + 3 * k : 4 + 3 * k] for k in range(2)]
     gates = [gates[k] + lines[4 + 3 * k : 5 + 3 * k] for k in range(2)]
-    sel = choose(row, col, want_ref[...])
+    sel = choose(row, col, want_ref[0])
     gate = jnp.sum(
         jnp.where(sel, jnp.concatenate(gates, axis=1), 0.0), axis=1, keepdims=True
     )
     sel = jnp.where(sel, 1.0, 0.0)
     sel = (sel[:, :tokens] + sel[:, tokens:]).astype(jnp.bfloat16)
-    rows = (gate * contract(sel, packed_ref[0, :, :width], ((1,), (0,)))).astype(jnp.bfloat16)
+    rows = gate * contract(sel, packed_ref[0, :, :width], ((1,), (0,)))
     for i, out_ref in enumerate(out_refs):
-        out_ref[...] = rows[i * PAIR : (i + 1) * PAIR]
+        out_ref[...] = rows[i * CAP : (i + 1) * CAP].astype(jnp.bfloat16)
 
 
 def order_kernel(order_ref, value_ref, out_ref):
-    lane = lax.broadcasted_iota(jnp.int32, (2 * ROWS, 2 * ROWS), 1)
+    lane = lax.broadcasted_iota(jnp.int32, (ROWS, ROWS), 1)
     turn = jnp.where(lane == order_ref[...], 1.0, 0.0).astype(jnp.bfloat16)
     out_ref[...] = contract(turn, value_ref[...], ((1,), (0,))).astype(jnp.bfloat16)
 
@@ -130,8 +131,10 @@
 
 
 def join_kernel(*refs):
-    for i, ref in enumerate(refs[:-1]):
-        refs[-1][i * PAIR : (i + 1) * PAIR] = ref[...]
+    for i in range(0, len(refs) - 1, 2):
+        pair = [ref[...].astype(jnp.float32) for ref in refs[i : i + 2]]
+        rows = jnp.concatenate(pair, axis=0).astype(jnp.bfloat16)
+        refs[-1][i * CAP : (i + 2) * CAP] = rows
 
 
 def back_kernel(core_ref, *refs):
@@ -142,10 +145,9 @@
     def from_halves(c_refs):
         half = c_refs[0].shape[0]
         for at, c_ref in enumerate(c_refs):
-            rows = contract(c_ref[...], w_ref[...], ((1,), (1,)))
-            for i in range(half // PAIR):
-                start = (at * half // PAIR + i) * CAP
-                out_ref[0, start : start + CAP] = rows[i * PAIR : i * PAIR + CAP]
+            out_ref[0, at * half : (at + 1) * half] = contract(
+                c_ref[...], w_ref[...], ((1,), (1,))
+            )
 
     @pl.when(mine)
     def _():
@@ -156,21 +158,32 @@
         from_halves(mate_refs)
 
 
-def update_kernel(core_ref, h_ref, *refs):
+def update_kernel(at_ref, h_own_ref, h_extra_ref, *refs):
     own_refs, mate_refs = refs[0:2], refs[2:4]
-    w_ref, m_ref, v_ref, out_ref = refs[4:]
-    core = core_ref[0]
-    width = w_ref.shape[1]
+    w_ref, m_ref, v_ref, out_ref, rows_ref = refs[4:]
+    core, y = at_ref[0], at_ref[1]
+    block, width = w_ref.shape
     half = own_refs[0].shape[0]
-    total = jnp.zeros(w_ref.shape, jnp.float32)
-    for c_refs, base in ((own_refs, 2 * core), (mate_refs, 2 - 2 * core)):
-        for j in range(2):
-            for at, c_ref in enumerate(c_refs):
-                total += contract(
-                    h_ref[base + j, at * half : (at + 1) * half],
-                    c_ref[:, j * width : (j + 1) * width],
-                    ((0,), (0,)),
-                )
+
+    @pl.when(pl.program_id(0) == 0)
+    def _():
+        for c_refs, base in ((own_refs, 2 * core), (mate_refs, 2 - 2 * core)):
+            for j in range(2):
+                places = (base + j, (y + 2 * RUN - base - j) % RUN)
+                for kind, place in enumerate(places):
+                    part = 2 * kind + j
+                    for at, c_ref in enumerate(c_refs):
+                        rows_ref[kind, place, at * half : (at + 1) * half] = c_ref[
+                            :, part * width : (part + 1) * width
+                        ]
+
+    depth = RUN * ROWS
+    total = contract(
+        h_own_ref[...].reshape(depth, block), rows_ref[0].reshape(depth, width), ((0,), (0,))
+    )
+    total += contract(
+        h_extra_ref[...].reshape(depth, block), rows_ref[1].reshape(depth, width), ((0,), (0,))
+    )
     m_new = beta_one * m_ref[...] + (1.0 - beta_one) * total
     v_new = beta_two * v_ref[...] + (1.0 - beta_two) * total * total
     direction = m_new / bias_one / (jnp.sqrt(v_new / bias_two) + epsilon)
@@ -179,7 +192,7 @@
 
 
 def take_kernel(row_ref, col_ref, want_ref, back_ref, out_ref):
-    sel = jnp.where(choose(row_ref[0], col_ref[0], want_ref[...]), 1.0, 0.0).astype(jnp.bfloat16)
+    sel = jnp.where(choose(row_ref[0], col_ref[0], want_ref[0]), 1.0, 0.0).astype(jnp.bfloat16)
     out_ref[...] = contract(sel, back_ref[...], ((0,), (0,))).astype(jnp.bfloat16)
 
 
@@ -222,15 +235,9 @@
     to = (x + steps[:, 0]) % GRID * GRID + (z + steps[:, 1]) % GRID
     by = (x - steps[:, 0]) % GRID * GRID + (z - steps[:, 1]) % GRID
     want_to = jnp.sum(jnp.where(to[:, None] == numbers[None, :], want[:, None, :], 0.0), axis=2)
-    want_own = jnp.broadcast_to(want[0][:, None], (GROUPS, CAP)).reshape(ROWS, 1)
-
-    def spread_rows(values):
-        values = jnp.broadcast_to(values.T[:, :, None], (GROUPS, 2, CAP))
-        return values.reshape(2 * ROWS, 1)
-
-    want, want_to = spread_rows(want), spread_rows(want_to)
-    order_own = (by[:, None] * CAP + jnp.arange(CAP, dtype=jnp.int32)[None, :]).reshape(ROWS, 1)
-    order = (by[:, None] * PAIR + jnp.arange(PAIR, dtype=jnp.int32)[None, :]).reshape(2 * ROWS, 1)
+    want = jnp.broadcast_to(want[:, :, None], (2, GROUPS, CAP)).reshape(2, ROWS, 1)
+    want_to = jnp.broadcast_to(want_to[:, :, None], (2, GROUPS, CAP)).reshape(2, ROWS, 1)
+    order = (by[:, None] * CAP + jnp.arange(CAP, dtype=jnp.int32)[None, :]).reshape(ROWS, 1)
     source = jnp.sum(
         jnp.where(new_slot[None, :] == numbers[:, None], old_slot[None, :], 0), axis=1
     )
@@ -256,47 +263,55 @@
     acts = hidden_acts.transpose(1, 0, 2).reshape(count, hidden)
     sent_h = pl.pallas_call(
         send_h_kernel,
-        out_shape=jax.ShapeDtypeStruct((2 * ROWS, hidden), jnp.bfloat16),
+        out_shape=[jax.ShapeDtypeStruct((ROWS, hidden), jnp.bfloat16)] * 2,
         compiler_params=params(16),
         name="send_h",
     )(own_row, own_col, want, acts)
-    got_h = lax.all_to_all(sent_h, "ep", 0, 0, axis_index_groups=SAME_Y, tiled=True)
+    got_h = [
+        lax.all_to_all(part, "ep", 0, 0, axis_index_groups=SAME_Y, tiled=True) for part in sent_h
+    ]
 
     send_c = pl.pallas_call(
         send_c_kernel,
         grid_spec=pltpu.PrefetchScalarGridSpec(
             num_scalar_prefetch=1,
-            grid=(2,),
+            grid=(2, 2),
             in_specs=[
-                whole((2 * ROWS, 1)),
+                pl.BlockSpec((1, ROWS, 1), lambda k, j, c: (k, 0, 0)),
                 pl.BlockSpec(
                     (1, tokens, width + LANES),
-                    lambda j, c: ((c[1] + 2 * RUN - 2 * c[0] - j) % RUN, 0, 0),
+                    lambda k, j, c: ((c[1] + 2 * RUN - 2 * c[0] - j) % RUN, 0, 0),
                 ),
             ],
-            out_specs=[pl.BlockSpec((PAIR, width), lambda j, c: (0, j))] * GROUPS,
+            out_specs=[pl.BlockSpec((CAP, width), lambda k, j, c: (0, 2 * k + j))] * GROUPS,
         ),
-        out_shape=[jax.ShapeDtypeStruct((PAIR, 2 * width), jnp.bfloat16)] * GROUPS,
+        out_shape=[jax.ShapeDtypeStruct((CAP, 4 * width), jnp.bfloat16)] * GROUPS,
         compiler_params=params(24),
         name="send_c",
     )(jnp.stack([core, y]), want_to, packed)
     send_c = list(send_c)
-    got_h, send_c[0] = lax.optimization_barrier((got_h, send_c[0]))
-    got_h = pl.pallas_call(
-        order_kernel,
-        out_shape=jax.ShapeDtypeStruct((2 * ROWS, hidden), jnp.bfloat16),
-        compiler_params=params(16),
-        name="order_h",
-    )(order, got_h)
-    all_h = lax.all_gather(got_h, "ep", axis_index_groups=SAME_RUN, axis=0, tiled=False)
+    got_h[0], send_c[0] = lax.optimization_barrier((got_h[0], send_c[0]))
+    got_h = [
+        pl.pallas_call(
+            order_kernel,
+            out_shape=jax.ShapeDtypeStruct((ROWS, hidden), jnp.bfloat16),
+            compiler_params=params(16),
+            name="order_h",
+        )(order, part)
+        for part in got_h
+    ]
+    own_h = lax.all_gather(got_h[0], "ep", axis_index_groups=SAME_RUN, axis=0, tiled=False)
+    extra_h = [got_h[1]] + [lax.ppermute(got_h[1], "ep", along_y(s)) for s in range(1, RUN)]
+    extra_h = jnp.stack(extra_h)
 
     got_c = [send_c[0]]
     for step, block in zip(SHIFTS[1:], send_c[1:], strict=True):
         got_c.append(lax.ppermute(block, ("ep", "dp"), nearest(*step)))
+    half = ROWS // 2
     got_c = [
         pl.pallas_call(
             join_kernel,
-            out_shape=jax.ShapeDtypeStruct((ROWS, 2 * width), jnp.bfloat16),
+            out_shape=jax.ShapeDtypeStruct((half, 4 * width), jnp.bfloat16),
             compiler_params=params(16),
             name="join",
         )(*part)
@@ -310,7 +325,7 @@
         grid_spec=pltpu.PrefetchScalarGridSpec(
             num_scalar_prefetch=1,
             grid=(RUN,),
-            in_specs=[pl.BlockSpec((ROWS, width), lambda s, c: (0, s % 2))] * 4
+            in_specs=[pl.BlockSpec((half, width), lambda s, c: (0, s % 2))] * 4
             + [whole((hidden, width))],
             out_specs=pl.BlockSpec((1, ROWS, hidden), lambda s, c: (s, 0, 0)),
         ),
@@ -326,14 +341,14 @@
         out_shape=jax.ShapeDtypeStruct((ROWS, hidden), jnp.bfloat16),
         compiler_params=params(16),
         name="unorder",
-    )(order_own, summed)
+    )(order, summed)
     back = lax.all_to_all(back, "ep", 0, 0, axis_index_groups=SAME_Y, tiled=True)
     hidden_out = pl.pallas_call(
         take_kernel,
         out_shape=jax.ShapeDtypeStruct((count, hidden), jnp.bfloat16),
         compiler_params=params(16),
         name="take",
-    )(own_row, own_col, want_own, back)
+    )(own_row, own_col, want, back)
     hidden_out = hidden_out.reshape(top, tokens, hidden).transpose(1, 0, 2)
 
     block = 128
@@ -343,15 +358,25 @@
         grid_spec=pltpu.PrefetchScalarGridSpec(
             num_scalar_prefetch=1,
             grid=(grid,),
-            in_specs=[pl.BlockSpec((RUN, 2 * ROWS, block), lambda i, c: (0, 0, i))]
-            + [whole((ROWS, 2 * width))] * 4
+            in_specs=[pl.BlockSpec((RUN, ROWS, block), lambda i, c: (0, 0, i))] * 2
+            + [whole((half, 4 * width))] * 4
             + [pl.BlockSpec((block, width), lambda i, c: (i, 0))] * 3,
             out_specs=pl.BlockSpec((block, width), lambda i, c: (i, 0)),
+            scratch_shapes=[pltpu.VMEM((2, RUN, ROWS, width), jnp.bfloat16)],
         ),
         out_shape=jax.ShapeDtypeStruct((hidden, width), jnp.float32),
-        compiler_params=params(56),
+        compiler_params=params(48),
         name="update",
-    )(cores, all_h, *got_c, *mate_c, weight, first_moment[0], second_moment[0])
+    )(
+        jnp.stack([core, y]),
+        own_h,
+        extra_h,
+        *got_c,
+        *mate_c,
+        weight,
+        first_moment[0],
+        second_moment[0],
+    )
 
     spread = update.astype(jnp.float16).reshape(GROUPS, hidden // GROUPS, width)
     spread = lax.all_to_all(spread, "ep", 0, 0, axis_index_groups=SAME_Y, tiled=True)

time: 221 us -> 295 us (1.33)
  waiting for transfers between devices: 84 us -> 128 us
  blocking collectives: 0 us -> 22.8 us
  starting transfers between devices: 71 us -> 75.1 us
    ppermute x0 -> x3, waiting for transfers between devices: none -> 35.6 us  [local(): lax.ppermute(got_h[1], 'ep', along_y(s))]
    all_to_all x1, waiting for transfers between devices: 2.46 us -> 29.1 us  [local(): lax.all_to_all(spread, 'ep', 0, 0, axis_index_groups=SAME_Y, tiled=True)]
    reduce_scatter x1, waiting for transfers between devices: 23.9 us -> 0.02 us  [local(): lax.psum_scatter(partial_back, 'ep', scatter_dimension=0, axis_index_grou...]
    all_to_all x0 -> x1, blocking collectives: none -> 22.8 us  [local(): lax.all_to_all(part, 'ep', 0, 0, axis_index_groups=SAME_Y, tiled=True)]
    ppermute x15, starting transfers between devices: 28.6 us -> 34.9 us  [local(): got_c.append(lax.ppermute(block, ('ep', 'dp'), nearest(*step)))]
    ppermute x2, starting transfers between devices: 14 us -> 9.03 us  [local(): mate_c = [lax.ppermute(part, 'dp', OTHER_CORE) for part in got_c]]
    ppermute x3, waiting for transfers between devices: 9.13 us -> 13.7 us  [local(): lax.ppermute(packed[s], 'ep', along_y(s))]
    unnamed x46 -> x44, local copies, waits for them, and re-layouts: 7.79 us -> 10.6 us
  transfers between devices with their start and end apart: 26 -> 29, of which waited for: 10 -> 13; matrix products, arithmetic and copies ran while one was open for 4% -> 3% of each run, Pallas kernels for 12% -> 8%
where the time goes in v4:
time: 295 us; the launch traced here: 292 us
  waiting for transfers between devices  128 us (43%)
  starting transfers between devices  75.1 us (25%)
  Pallas kernels  27.9 us (9%)
  blocking collectives  22.8 us (8%)
  local copies, waits for them, and re-layouts  15.5 us (5%)
  between operations  14.3 us (5%)
  other arithmetic  9.05 us (3%)
    ppermute x3, waiting for transfers between devices, local(): lax.ppermute(got_h[1], 'ep', along_y(s))  35.6 us
    ppermute x15, starting transfers between devices, local(): got_c.append(lax.ppermute(block, ('ep', 'dp'), nearest(*step)))  34.9 us
    all_to_all x1, waiting for transfers between devices, local(): lax.all_to_all(spread, 'ep', 0, 0, axis_index_groups=SAME_Y, tiled=True)  29.1 us
    all_to_all x1, waiting for transfers between devices, local(): lax.all_to_all(spread[source], 'ep', 0, 0, axis_index_groups=SAME_Y, tile...  26.5 us
    all_to_all x1, blocking collectives, local(): lax.all_to_all(part, 'ep', 0, 0, axis_index_groups=SAME_Y, tiled=True)  22.8 us
    ppermute x3, waiting for transfers between devices, local(): lax.ppermute(packed[s], 'ep', along_y(s))  13.7 us
    all_to_all x1, waiting for transfers between devices, local(): lax.all_to_all(back, 'ep', 0, 0, axis_index_groups=SAME_Y, tiled=True)  13.5 us
    pallas_call x1, Pallas kernels, local(): pl.pallas_call(update_kernel, grid_spec=pltpu.PrefetchScalarGridSpec(num_...  11 us
  transfers between devices with their start and end apart: 29, of which 13 were waited for; matrix products, arithmetic and copies ran while one was open for 3% of the time, Pallas kernels for 8%

profile of v4, /device:TPU:1, one launch (start us, length us, event | category | flops | bytes accessed | tf_op | source)
XLA Modules:
  0.0 292.3 jit_solution(9524192513779626841)
XLA Ops:
  11.5 9.0 %all-to-all-start = ((bf16[16,24,640]{2,1,0:T(8,128)(2,1)}), bf16[16,24,640]{2,1,0:T(8,128)(2,1)S(1)}, u32[]{:S(2)}, u32[]{:S(2)}) async-start(bf16[16,24,640]{2,1,0:T(8,128)(2,1)} %bitcast.10), calls=%async_computation | async-start | bytes 983040 | tf_op jit(solution)/shard_map/all_to_all | solution.py:271
  21.6 2.7 collective-permute-start.2
  26.2 4.2 %collective-permute-done.2 = bf16[128,1024]{1,0:T(8,128)(2,1)S(1)} collective-permute-done((bf16[128,1024]{1,0:T(8,128)(2,1)}, bf16[128,1024]{1,0:T(8,128)(2,1)S(1)}, u32[]{:S(2)}, u32[]{:S(2)}) %collective-permute-start.2) | collective-permute-done | bytes 262176 | tf_op jit(solution)/shard_map/ppermute | solution.py:258
  30.4 2.1 collective-permute-done.1
  32.5 7.3 %collective-permute-done = bf16[128,1024]{1,0:T(8,128)(2,1)} collective-permute-done((bf16[128,1024]{1,0:T(8,128)(2,1)S(1)}, bf16[128,1024]{1,0:T(8,128)(2,1)}, u32[]{:S(2)}, u32[]{:S(2)}) %collective-permute-start) | collective-permute-done | bytes 262176 | tf_op jit(solution)/shard_map/ppermute | solution.py:258
  40.9 4.4 %send_c.1 = (bf16[24,3584]{1,0:T(8,128)(2,1)S(1)}, bf16[24,3584]{1,0:T(8,128)(2,1)S(1)}, bf16[24,3584]{1,0:T(8,128)(2,1)S(1)}, bf16[24,3584]{1,0:T(8,128)(2,1)},...) custom-call(s32[2]{0:T(128)S(1)} %pad_add_fusion.core_ref.at_ref, ...), custom_call_target="tpu_custom_call" | custom-call | tf_op jit(solution)/shard_map/send_c/pallas_call | solution.py:274
  51.4 4.7 %collective-permute-start.3 = (bf16[24,3584]{1,0:T(8,128)(2,1)}, bf16[24,3584]{1,0:T(8,128)(2,1)S(1)}, u32[]{:S(2)}, u32[]{:S(2)}) collective-permute-start(bf16[24,3584]{1,0:T(8,128)(2,1)} %copy-done.15), channel_id=1, source_target_pairs={{0,160},{1,161},{2,162},{3,163},{4,164},{5,165},{6,166},{7,167},{8... | collective-permute-start | bytes 516104 | tf_op jit(solution)/shard_map/ppermute | solution.py:309
  56.2 2.4 collective-permute-start.4
  59.1 3.0 %collective-permute-start.11 = (bf16[24,3584]{1,0:T(8,128)(2,1)}, bf16[24,3584]{1,0:T(8,128)(2,1)S(1)}, u32[]{:S(2)}, u32[]{:S(2)}) collective-permute-start(bf16[24,3584]{1,0:T(8,128)(2,1)} %copy-done.12), channel_id=1, source_target_pairs={{0,208},{1,209},{2,210},{3,211},{4,212},{5,213},{6,214},{7,215},{8... | collective-permute-start | bytes 516104 | tf_op jit(solution)/shard_map/ppermute | solution.py:309
  62.2 2.1 collective-permute-start.12
  67.9 3.8 %collective-permute-done.10.refs_0_ = bf16[24,3584]{1,0:T(8,128)(2,1)S(1)} collective-permute-done((bf16[24,3584]{1,0:T(8,128)(2,1)}, bf16[24,3584]{1,0:T(8,128)(2,1)S(1)}, u32[]{:S(2)}, u32[]{:S(2)}) %collective-permute-start.10) | collective-permute-done | bytes 172064 | tf_op jit(solution)/shard_map/ppermute | solution.py:309
  71.7 4.3 %collective-permute-start.15 = (bf16[24,3584]{1,0:T(8,128)(2,1)S(1)}, bf16[24,3584]{1,0:T(8,128)(2,1)S(1)}, u32[]{:S(2)}, u32[]{:S(2)}) collective-permute-start(bf16[24,3584]{1,0:T(8,128)(2,1)S(1)} %get-tuple-element.45), channel_id=1, source_target_pairs={{0,50},{1,51},{2,48},{3,49},{4,54},{5,55},{6,52},{7,53},{8,58},{9,... | collective-permute-start | bytes 516104 | tf_op jit(solution)/shard_map/ppermute | solution.py:309
  76.1 2.5 collective-permute-start.17
  78.7 3.9 %collective-permute-start.6 = (bf16[24,3584]{1,0:T(8,128)(2,1)}, bf16[24,3584]{1,0:T(8,128)(2,1)S(1)}, u32[]{:S(2)}, u32[]{:S(2)}) collective-permute-start(bf16[24,3584]{1,0:T(8,128)(2,1)} %get-tuple-element.36), channel_id=1, source_target_pairs={{0,144},{1,145},{2,146},{3,147},{4,148},{5,149},{6,150},{7,151},{8... | collective-permute-start | bytes 516104 | tf_op jit(solution)/shard_map/ppermute | solution.py:309
  82.6 3.8 %collective-permute-start.7 = (bf16[24,3584]{1,0:T(8,128)(2,1)S(1)}, bf16[24,3584]{1,0:T(8,128)(2,1)S(1)}, u32[]{:S(2)}, u32[]{:S(2)}) collective-permute-start(bf16[24,3584]{1,0:T(8,128)(2,1)S(1)} %get-tuple-element.37), channel_id=1, source_target_pairs={{0,178},{1,179},{2,176},{3,177},{4,182},{5,183},{6,180},{7,181},{8... | collective-permute-start | bytes 516104 | tf_op jit(solution)/shard_map/ppermute | solution.py:309
  86.5 4.8 %collective-permute-start.9 = (bf16[24,3584]{1,0:T(8,128)(2,1)S(1)}, bf16[24,3584]{1,0:T(8,128)(2,1)S(1)}, u32[]{:S(2)}, u32[]{:S(2)}) collective-permute-start(bf16[24,3584]{1,0:T(8,128)(2,1)S(1)} %get-tuple-element.39), channel_id=1, source_target_pairs={{0,242},{1,243},{2,240},{3,241},{4,246},{5,247},{6,244},{7,245},{8... | collective-permute-start | bytes 516104 | tf_op jit(solution)/shard_map/ppermute | solution.py:309
  91.4 7.0 %collective-permute-start.19 = (bf16[192,3584]{1,0:T(8,128)(2,1)S(1)}, bf16[192,3584]{1,0:T(8,128)(2,1)S(1)}, u32[]{:S(2)}, u32[]{:S(2)}) collective-permute-start(bf16[192,3584]{1,0:T(8,128)(2,1)S(1)} %join.3.refs_1_), channel_id=1, source_target_pairs={{0,1},{1,0},{2,3},{3,2},{4,5},{5,4},{6,7},{7,6},{8,9},{9,8},{10,11... | collective-permute-start | bytes 4128776 | tf_op jit(solution)/shard_map/ppermute | solution.py:320
  100.8 2.1 collective-permute-start.18
  102.9 2.8 collective-permute-done.18.refs_2_
  105.7 6.4 %back.1 = f32[4,384,640]{2,1,0:T(8,128)} custom-call(s32[1]{0:T(128)} %bitcast.6.core_ref, bf16[192,3584]{1,0:T(8,128)(2,1)S(1)} %join.2.refs_0_, bf16[192,3584]{1,0:T(8,128)(2,1)S(1)} %join.3.refs_1_, bf16[192,3584]{1,0:T(8,128)(2,1)S(1)} %collective-permute-done.18.refs_2_, bf16[192,3584]{1,0:T(8,128)(2,1)} %copy-done.16, bf16[640,896]{1,0:T(8,128)(2,1)S(1)} %bitcast.46), custom_call_target="tpu_custom_call" | custom-call | tf_op jit(solution)/shard_map/back/pallas_call | solution.py:323
  113.2 22.8 %all_to_all.44 = bf16[16,24,640]{2,1,0:T(8,128)(2,1)S(1)} all-to-all(bf16[16,24,640]{2,1,0:T(8,128)(2,1)} %bitcast.55), channel_id=1, replica_groups={{0,16,32,48,64,80,96,112,128,144,160,176,192,208,224,240},{4,20,36,52,6..., dimensions={0} | all-to-all | bytes 983040 | tf_op jit(solution)/shard_map/all_to_all | solution.py:271
  138.1 21.8 %collective-permute-done.22 = bf16[384,640]{1,0:T(8,128)(2,1)S(1)} collective-permute-done((bf16[384,640]{1,0:T(8,128)(2,1)S(1)}, bf16[384,640]{1,0:T(8,128)(2,1)S(1)}, u32[]{:S(2)}, u32[]{:S(2)}) %collective-permute-start.22) | collective-permute-done | bytes 491552 | tf_op jit(solution)/shard_map/ppermute | solution.py:304
  161.4 12.3 %collective-permute-done.20 = bf16[384,640]{1,0:T(8,128)(2,1)S(1)} collective-permute-done((bf16[384,640]{1,0:T(8,128)(2,1)S(1)}, bf16[384,640]{1,0:T(8,128)(2,1)S(1)}, u32[]{:S(2)}, u32[]{:S(2)}) %collective-permute-start.20) | collective-permute-done | bytes 491552 | tf_op jit(solution)/shard_map/ppermute | solution.py:304
  177.9 11.0 %update.1 = f32[640,896]{1,0:T(8,128)} custom-call(s32[2]{0:T(128)S(1)} %pad_add_fusion.core_ref.at_ref, bf16[4,384,640]{2,1,0:T(8,128)(2,1)} %bitcast.63, bf16[4,384,640]{2,1,0:T(8,128)(2,1)} %pad_maximum_fusion.h_extra_ref, bf16[192,3584]{1,0:T(8,128)(2,1)S(1)} %join.2.refs_0_, bf16[192,3584]{1,0:T(8,128)(2,1)S(1)} %join.3.refs_1_, ...), custom_call_target="tpu_custom_call" | custom-call | tf_op jit(solution)/shard_map/update/pallas_call | solution.py:356
  189.0 2.8 convert_element_type.31
  191.8 7.7 %all-to-all-start.3 = ((f16[16,40,896]{2,1,0:T(8,128)(2,1)}), f16[16,40,896]{2,1,0:T(8,128)(2,1)S(1)}, u32[]{:S(2)}, u32[]{:S(2)}) async-start(f16[16,40,896]{2,1,0:T(8,128)(2,1)} %bitcast.33), calls=%async_computation.4 | async-start | bytes 2293760 | tf_op jit(solution)/shard_map/all_to_all | solution.py:382
  199.5 29.1 %all-to-all-done.3 = f16[16,40,896]{2,1,0:T(8,128)(2,1)S(1)} async-done(((f16[16,40,896]{2,1,0:T(8,128)(2,1)}), f16[16,40,896]{2,1,0:T(8,128)(2,1)S(1)}, u32[]{:S(2)}, u32[]{:S(2)}) %all-to-all-start.3) | async-done | bytes 1146912 | tf_op jit(solution)/shard_map/all_to_all | solution.py:382
  228.6 2.0 gather_fusion
  230.6 4.5 %all-to-all-start.4 = ((f16[16,40,896]{2,1,0:T(8,128)(2,1)}), f16[16,40,896]{2,1,0:T(8,128)(2,1)S(1)}, u32[]{:S(2)}, u32[]{:S(2)}) async-start(f16[16,40,896]{2,1,0:T(8,128)(2,1)} %gather_fusion), calls=%async_computation.5 | async-start | bytes 2293760 | tf_op jit(solution)/shard_map/all_to_all | solution.py:383
  237.7 26.5 %all-to-all-done.4 = f16[16,40,896]{2,1,0:T(8,128)(2,1)S(1)} async-done(((f16[16,40,896]{2,1,0:T(8,128)(2,1)}), f16[16,40,896]{2,1,0:T(8,128)(2,1)S(1)}, u32[]{:S(2)}, u32[]{:S(2)}) %all-to-all-start.4) | async-done | bytes 1146912 | tf_op jit(solution)/shard_map/all_to_all | solution.py:383
  264.3 4.5 %all-to-all-start.1 = ((bf16[16,24,640]{2,1,0:T(8,128)(2,1)}), bf16[16,24,640]{2,1,0:T(8,128)(2,1)S(1)}, u32[]{:S(2)}, u32[]{:S(2)}) async-start(bf16[16,24,640]{2,1,0:T(8,128)(2,1)} %bitcast.20), calls=%async_computation.2 | async-start | bytes 983040 | tf_op jit(solution)/shard_map/all_to_all | solution.py:345
  270.4 13.5 %all-to-all-done.1 = bf16[16,24,640]{2,1,0:T(8,128)(2,1)S(1)} async-done(((bf16[16,24,640]{2,1,0:T(8,128)(2,1)}), bf16[16,24,640]{2,1,0:T(8,128)(2,1)S(1)}, u32[]{:S(2)}, u32[]{:S(2)}) %all-to-all-start.1) | async-done | bytes 491552 | tf_op jit(solution)/shard_map/all_to_all | solution.py:345
  (110 shorter events, 35.9 us)
Async XLA Ops:
  9.0 16.4 %copy-start.20 = (s32[16,1]{0,1:T(1,128)S(1)}, s32[16,1]{0,1:T(1,128)}, u32[]{:S(2)}) copy-start(s32[16,1]{0,1:T(1,128)} %constant.99) | copy-start | bytes 196
  9.0 16.4 %copy-start.21 = (s32[16,1]{0,1:T(1,128)S(1)}, s32[16,1]{0,1:T(1,128)}, u32[]{:S(2)}) copy-start(s32[16,1]{0,1:T(1,128)} %constant.98) | copy-start | bytes 196
  11.5 86.8 %copy-start.6 = (bf16[384,640]{1,0:T(8,128)(2,1)}, bf16[384,640]{1,0:T(8,128)(2,1)S(1)}, u32[]{:S(2)}) copy-start(bf16[384,640]{1,0:T(8,128)(2,1)S(1)} %get-tuple-element.49) | copy-start | bytes 1474564
  11.5 38.5 %all-to-all-start = ((bf16[16,24,640]{2,1,0:T(8,128)(2,1)}), bf16[16,24,640]{2,1,0:T(8,128)(2,1)S(1)}, u32[]{:S(2)}, u32[]{:S(2)}) async-start(bf16[16,24,640]{2,1,0:T(8,128)(2,1)} %bitcast.10), calls=%async_computation | async-start | bytes 983040 | tf_op jit(solution)/shard_map/all_to_all | solution.py:271
  20.6 154.7 %all-gather.3.cloned.1.call-start = ((), (), s32[]{:S(2)}) async-start(), calls=%async_computation.7 | async-start | bytes 2457600 | tf_op jit(solution)/shard_map/all_gather | solution.py:303
  21.6 8.7 %collective-permute-start.2 = (bf16[128,1024]{1,0:T(8,128)(2,1)}, bf16[128,1024]{1,0:T(8,128)(2,1)S(1)}, u32[]{:S(2)}, u32[]{:S(2)}) collective-permute-start(bf16[128,1024]{1,0:T(8,128)(2,1)} %get-tuple-element.30), channel_id=1, source_target_pairs={{0,12},{4,0},{8,4},{12,8},{16,28},{20,16},{24,20},{28,24},{32,44},... | collective-permute-start | bytes 786440 | tf_op jit(solution)/shard_map/ppermute | solution.py:258
  24.4 8.1 %collective-permute-start.1 = (bf16[128,1024]{1,0:T(8,128)(2,1)S(1)}, bf16[128,1024]{1,0:T(8,128)(2,1)S(1)}, u32[]{:S(2)}, u32[]{:S(2)}) collective-permute-start(bf16[128,1024]{1,0:T(8,128)(2,1)S(1)} %get-tuple-element.29), channel_id=1, source_target_pairs={{0,8},{4,12},{8,0},{12,4},{16,24},{20,28},{24,16},{28,20},{32,40},... | collective-permute-start | bytes 786440 | tf_op jit(solution)/shard_map/ppermute | solution.py:258
  24.7 15.1 %collective-permute-start = (bf16[128,1024]{1,0:T(8,128)(2,1)S(1)}, bf16[128,1024]{1,0:T(8,128)(2,1)}, u32[]{:S(2)}, u32[]{:S(2)}) collective-permute-start(bf16[128,1024]{1,0:T(8,128)(2,1)S(1)} %get-tuple-element.28), channel_id=1, source_target_pairs={{0,4},{4,8},{8,12},{12,0},{16,20},{20,24},{24,28},{28,16},{32,36},... | collective-permute-start | bytes 786440 | tf_op jit(solution)/shard_map/ppermute | solution.py:258
  51.4 183.8 %reduce-scatter.2.cloned.1.call-start = ((), (), s32[]{:S(2)}) async-start(), calls=%async_computation.6 | async-start | bytes 4915200 | tf_op jit(solution)/shard_map/reduce_scatter | solution.py:336
  51.4 12.8 %collective-permute-start.3 = (bf16[24,3584]{1,0:T(8,128)(2,1)}, bf16[24,3584]{1,0:T(8,128)(2,1)S(1)}, u32[]{:S(2)}, u32[]{:S(2)}) collective-permute-start(bf16[24,3584]{1,0:T(8,128)(2,1)} %copy-done.15), channel_id=1, source_target_pairs={{0,160},{1,161},{2,162},{3,163},{4,164},{5,165},{6,166},{7,167},{8... | collective-permute-start | bytes 516104 | tf_op jit(solution)/shard_map/ppermute | solution.py:309
  56.2 9.8 %collective-permute-start.4 = (bf16[24,3584]{1,0:T(8,128)(2,1)}, bf16[24,3584]{1,0:T(8,128)(2,1)S(1)}, u32[]{:S(2)}, u32[]{:S(2)}) collective-permute-start(bf16[24,3584]{1,0:T(8,128)(2,1)} %copy-done.14), channel_id=1, source_target_pairs={{0,96},{1,97},{2,98},{3,99},{4,100},{5,101},{6,102},{7,103},{8,104... | collective-permute-start | bytes 516104 | tf_op jit(solution)/shard_map/ppermute | solution.py:309
  58.6 13.1 %collective-permute-start.10 = (bf16[24,3584]{1,0:T(8,128)(2,1)}, bf16[24,3584]{1,0:T(8,128)(2,1)S(1)}, u32[]{:S(2)}, u32[]{:S(2)}) collective-permute-start(bf16[24,3584]{1,0:T(8,128)(2,1)} %copy-done.13), channel_id=1, source_target_pairs={{0,114},{1,115},{2,112},{3,113},{4,118},{5,119},{6,116},{7,117},{8... | collective-permute-start | bytes 516104 | tf_op jit(solution)/shard_map/ppermute | solution.py:309
  59.1 16.8 %collective-permute-start.11 = (bf16[24,3584]{1,0:T(8,128)(2,1)}, bf16[24,3584]{1,0:T(8,128)(2,1)S(1)}, u32[]{:S(2)}, u32[]{:S(2)}) collective-permute-start(bf16[24,3584]{1,0:T(8,128)(2,1)} %copy-done.12), channel_id=1, source_target_pairs={{0,208},{1,209},{2,210},{3,211},{4,212},{5,213},{6,214},{7,215},{8... | collective-permute-start | bytes 516104 | tf_op jit(solution)/shard_map/ppermute | solution.py:309
  62.2 14.0 %collective-permute-start.12 = (bf16[24,3584]{1,0:T(8,128)(2,1)}, bf16[24,3584]{1,0:T(8,128)(2,1)S(1)}, u32[]{:S(2)}, u32[]{:S(2)}) collective-permute-start(bf16[24,3584]{1,0:T(8,128)(2,1)} %copy-done.11), channel_id=1, source_target_pairs={{0,32},{1,33},{2,34},{3,35},{4,36},{5,37},{6,38},{7,39},{8,40},{9,... | collective-permute-start | bytes 516104 | tf_op jit(solution)/shard_map/ppermute | solution.py:309
  64.3 14.4 %collective-permute-start.13 = (bf16[24,3584]{1,0:T(8,128)(2,1)}, bf16[24,3584]{1,0:T(8,128)(2,1)S(1)}, u32[]{:S(2)}, u32[]{:S(2)}) collective-permute-start(bf16[24,3584]{1,0:T(8,128)(2,1)} %copy-done.10), channel_id=1, source_target_pairs={{0,128},{1,129},{2,130},{3,131},{4,132},{5,133},{6,134},{7,135},{8... | collective-permute-start | bytes 516104 | tf_op jit(solution)/shard_map/ppermute | solution.py:309
  66.0 12.7 %collective-permute-start.14 = (bf16[24,3584]{1,0:T(8,128)(2,1)}, bf16[24,3584]{1,0:T(8,128)(2,1)S(1)}, u32[]{:S(2)}, u32[]{:S(2)}) collective-permute-start(bf16[24,3584]{1,0:T(8,128)(2,1)} %copy-done.9), channel_id=1, source_target_pairs={{0,16},{1,17},{2,18},{3,19},{4,20},{5,21},{6,22},{7,23},{8,24},{9,... | collective-permute-start | bytes 516104 | tf_op jit(solution)/shard_map/ppermute | solution.py:309
  71.7 10.9 %collective-permute-start.15 = (bf16[24,3584]{1,0:T(8,128)(2,1)S(1)}, bf16[24,3584]{1,0:T(8,128)(2,1)S(1)}, u32[]{:S(2)}, u32[]{:S(2)}) collective-permute-start(bf16[24,3584]{1,0:T(8,128)(2,1)S(1)} %get-tuple-element.45), channel_id=1, source_target_pairs={{0,50},{1,51},{2,48},{3,49},{4,54},{5,55},{6,52},{7,53},{8,58},{9,... | collective-permute-start | bytes 516104 | tf_op jit(solution)/shard_map/ppermute | solution.py:309
  76.0 10.5 %collective-permute-start.16 = (bf16[24,3584]{1,0:T(8,128)(2,1)S(1)}, bf16[24,3584]{1,0:T(8,128)(2,1)S(1)}, u32[]{:S(2)}, u32[]{:S(2)}) collective-permute-start(bf16[24,3584]{1,0:T(8,128)(2,1)S(1)} %get-tuple-element.46), channel_id=1, source_target_pairs={{0,64},{1,65},{2,66},{3,67},{4,68},{5,69},{6,70},{7,71},{8,72},{9,... | collective-permute-start | bytes 516104 | tf_op jit(solution)/shard_map/ppermute | solution.py:309
  76.1 10.3 %collective-permute-start.17 = (bf16[24,3584]{1,0:T(8,128)(2,1)S(1)}, bf16[24,3584]{1,0:T(8,128)(2,1)S(1)}, u32[]{:S(2)}, u32[]{:S(2)}) collective-permute-start(bf16[24,3584]{1,0:T(8,128)(2,1)S(1)} %get-tuple-element.47), channel_id=1, source_target_pairs={{0,192},{1,193},{2,194},{3,195},{4,196},{5,197},{6,198},{7,199},{8... | collective-permute-start | bytes 516104 | tf_op jit(solution)/shard_map/ppermute | solution.py:309
  78.7 12.7 %collective-permute-start.5 = (bf16[24,3584]{1,0:T(8,128)(2,1)}, bf16[24,3584]{1,0:T(8,128)(2,1)S(1)}, u32[]{:S(2)}, u32[]{:S(2)}) collective-permute-start(bf16[24,3584]{1,0:T(8,128)(2,1)} %get-tuple-element.35), channel_id=1, source_target_pairs={{0,224},{1,225},{2,226},{3,227},{4,228},{5,229},{6,230},{7,231},{8... | collective-permute-start | bytes 516104 | tf_op jit(solution)/shard_map/ppermute | solution.py:309
  78.7 19.6 %collective-permute-start.6 = (bf16[24,3584]{1,0:T(8,128)(2,1)}, bf16[24,3584]{1,0:T(8,128)(2,1)S(1)}, u32[]{:S(2)}, u32[]{:S(2)}) collective-permute-start(bf16[24,3584]{1,0:T(8,128)(2,1)} %get-tuple-element.36), channel_id=1, source_target_pairs={{0,144},{1,145},{2,146},{3,147},{4,148},{5,149},{6,150},{7,151},{8... | collective-permute-start | bytes 516104 | tf_op jit(solution)/shard_map/ppermute | solution.py:309
  82.6 15.7 %collective-permute-start.7 = (bf16[24,3584]{1,0:T(8,128)(2,1)S(1)}, bf16[24,3584]{1,0:T(8,128)(2,1)S(1)}, u32[]{:S(2)}, u32[]{:S(2)}) collective-permute-start(bf16[24,3584]{1,0:T(8,128)(2,1)S(1)} %get-tuple-element.37), channel_id=1, source_target_pairs={{0,178},{1,179},{2,176},{3,177},{4,182},{5,183},{6,180},{7,181},{8... | collective-permute-start | bytes 516104 | tf_op jit(solution)/shard_map/ppermute | solution.py:309
  86.5 11.9 %collective-permute-start.8 = (bf16[24,3584]{1,0:T(8,128)(2,1)S(1)}, bf16[24,3584]{1,0:T(8,128)(2,1)S(1)}, u32[]{:S(2)}, u32[]{:S(2)}) collective-permute-start(bf16[24,3584]{1,0:T(8,128)(2,1)S(1)} %get-tuple-element.38), channel_id=1, source_target_pairs={{0,80},{1,81},{2,82},{3,83},{4,84},{5,85},{6,86},{7,87},{8,88},{9,... | collective-permute-start | bytes 516104 | tf_op jit(solution)/shard_map/ppermute | solution.py:309
  86.5 13.4 %collective-permute-start.9 = (bf16[24,3584]{1,0:T(8,128)(2,1)S(1)}, bf16[24,3584]{1,0:T(8,128)(2,1)S(1)}, u32[]{:S(2)}, u32[]{:S(2)}) collective-permute-start(bf16[24,3584]{1,0:T(8,128)(2,1)S(1)} %get-tuple-element.39), channel_id=1, source_target_pairs={{0,242},{1,243},{2,240},{3,241},{4,246},{5,247},{6,244},{7,245},{8... | collective-permute-start | bytes 516104 | tf_op jit(solution)/shard_map/ppermute | solution.py:309
  91.4 11.5 %collective-permute-start.19 = (bf16[192,3584]{1,0:T(8,128)(2,1)S(1)}, bf16[192,3584]{1,0:T(8,128)(2,1)S(1)}, u32[]{:S(2)}, u32[]{:S(2)}) collective-permute-start(bf16[192,3584]{1,0:T(8,128)(2,1)S(1)} %join.3.refs_1_), channel_id=1, source_target_pairs={{0,1},{1,0},{2,3},{3,2},{4,5},{5,4},{6,7},{7,6},{8,9},{9,8},{10,11... | collective-permute-start | bytes 4128776 | tf_op jit(solution)/shard_map/ppermute | solution.py:320
  100.8 4.8 %collective-permute-start.18 = (bf16[192,3584]{1,0:T(8,128)(2,1)S(1)}, bf16[192,3584]{1,0:T(8,128)(2,1)S(1)}, u32[]{:S(2)}, u32[]{:S(2)}) collective-permute-start(bf16[192,3584]{1,0:T(8,128)(2,1)S(1)} %join.2.refs_0_), channel_id=1, source_target_pairs={{0,1},{1,0},{2,3},{3,2},{4,5},{5,4},{6,7},{7,6},{8,9},{9,8},{10,11... | collective-permute-start | bytes 4128776 | tf_op jit(solution)/shard_map/ppermute | solution.py:320
  136.5 23.4 %collective-permute-start.22 = (bf16[384,640]{1,0:T(8,128)(2,1)S(1)}, bf16[384,640]{1,0:T(8,128)(2,1)S(1)}, u32[]{:S(2)}, u32[]{:S(2)}) collective-permute-start(bf16[384,640]{1,0:T(8,128)(2,1)S(1)} %order_h.3), channel_id=1, source_target_pairs={{0,12},{4,0},{8,4},{12,8},{16,28},{20,16},{24,20},{28,24},{32,44},... | collective-permute-start | bytes 1474568 | tf_op jit(solution)/shard_map/ppermute | solution.py:304
  136.6 24.8 %collective-permute-start.21 = (bf16[384,640]{1,0:T(8,128)(2,1)S(1)}, bf16[384,640]{1,0:T(8,128)(2,1)S(1)}, u32[]{:S(2)}, u32[]{:S(2)}) collective-permute-start(bf16[384,640]{1,0:T(8,128)(2,1)S(1)} %order_h.3), channel_id=1, source_target_pairs={{0,8},{4,12},{8,0},{12,4},{16,24},{20,28},{24,16},{28,20},{32,40},... | collective-permute-start | bytes 1474568 | tf_op jit(solution)/shard_map/ppermute | solution.py:304
  136.7 37.0 %collective-permute-start.20 = (bf16[384,640]{1,0:T(8,128)(2,1)S(1)}, bf16[384,640]{1,0:T(8,128)(2,1)S(1)}, u32[]{:S(2)}, u32[]{:S(2)}) collective-permute-start(bf16[384,640]{1,0:T(8,128)(2,1)S(1)} %order_h.3), channel_id=1, source_target_pairs={{0,4},{4,8},{8,12},{12,0},{16,20},{20,24},{24,28},{28,16},{32,36},... | collective-permute-start | bytes 1474568 | tf_op jit(solution)/shard_map/ppermute | solution.py:304
  191.8 36.8 %all-to-all-start.3 = ((f16[16,40,896]{2,1,0:T(8,128)(2,1)}), f16[16,40,896]{2,1,0:T(8,128)(2,1)S(1)}, u32[]{:S(2)}, u32[]{:S(2)}) async-start(f16[16,40,896]{2,1,0:T(8,128)(2,1)} %bitcast.33), calls=%async_computation.4 | async-start | bytes 2293760 | tf_op jit(solution)/shard_map/all_to_all | solution.py:382
  230.6 33.6 %all-to-all-start.4 = ((f16[16,40,896]{2,1,0:T(8,128)(2,1)}), f16[16,40,896]{2,1,0:T(8,128)(2,1)S(1)}, u32[]{:S(2)}, u32[]{:S(2)}) async-start(f16[16,40,896]{2,1,0:T(8,128)(2,1)} %gather_fusion), calls=%async_computation.5 | async-start | bytes 2293760 | tf_op jit(solution)/shard_map/all_to_all | solution.py:383
  264.3 19.6 %all-to-all-start.1 = ((bf16[16,24,640]{2,1,0:T(8,128)(2,1)}), bf16[16,24,640]{2,1,0:T(8,128)(2,1)S(1)}, u32[]{:S(2)}, u32[]{:S(2)}) async-start(bf16[16,24,640]{2,1,0:T(8,128)(2,1)} %bitcast.20), calls=%async_computation.2 | async-start | bytes 983040 | tf_op jit(solution)/shard_map/all_to_all | solution.py:345
  (19 other events, 96.0 us)
Sparse Core Ops, SparseCore 0:
  51.5 29.9 all-gather.2
  113.3 65.4 reduce-scatter.1

commit v5 on v3

v5 whole, which is shorter than its diff:
```python
import jax
import jax.numpy as jnp
from jax import lax
from jax.experimental import pallas as pl
from jax.experimental.pallas import tpu as pltpu
from jax.sharding import PartitionSpec as P

beta_one = 0.9
beta_two = 0.95
decay = 0.1
epsilon = 1e-08
bias_one = 1.0 - (0.9**50) ** 2
bias_two = 1.0 - (0.95**50) ** 2

RUN = 4
GROUPS = 16
CAP = 24
ROWS = GROUPS * CAP
SCALE = 2048.0
BACK_SCALE = 16.0
SAME_Y = [[g * RUN + y for g in range(GROUPS)] for y in range(RUN)]
SAME_RUN = [[g * RUN + y for y in range(RUN)] for g in range(GROUPS)]
OTHER_CORE = [(0, 1), (1, 0), (2, 3), (3, 2)]
GRID = 4
SHIFTS = [
    [(0, 0), (2, 2), (1, 2), (2, 1), (3, 3), (0, 3), (1, 0), (1, 1)],
    [(2, 0), (3, 2), (2, 3), (1, 3), (0, 2), (3, 1), (0, 1), (3, 0)],
]
HALF = GROUPS // 2
LANES = 128
MB = 1024 * 1024


def contract(a, b, dims):
    return lax.dot_general(a, b, ((dims[0], dims[1]), ((), ())), preferred_element_type=jnp.float32)


def order_of(index, tokens):
    return 2 * (index % tokens) + index // tokens


def choose(row, col, want):
    count = row.shape[1]
    tokens = count // 2
    lane = order_of(lax.broadcasted_iota(jnp.int32, (count, count), 1), tokens)
    line = order_of(lax.broadcasted_iota(jnp.int32, (count, count), 0), tokens)
    ahead = jnp.where((row == col) & (line < lane), 1.0, 0.0)
    position = jnp.sum(ahead, axis=0, keepdims=True)
    place = (lax.broadcasted_iota(jnp.int32, (want.shape[0], 1), 0) % CAP).astype(jnp.float32)
    return (row == want) & (position == place)


def along_y(step):
    return [(i, i // RUN * RUN + (i + step) % RUN) for i in range(GROUPS * RUN)]


def nearest(number):
    pairs = []
    for i in range(GROUPS * RUN):
        x, z_low, y = i // (GRID * RUN), i // RUN % GRID, i % RUN
        for d in range(4):
            step_x, step_z = SHIFTS[d % 2][number]
            z = d // 2 * GRID + z_low
            step = (2 if z % 2 == 0 else -2) if step_z == 2 else (-1 if step_z == 3 else step_z)
            to_z = (z + step) % (2 * GRID)
            to = ((x + step_x) % GRID * GRID + to_z % GRID) * RUN + y
            pairs.append((i * 4 + d, to * 4 + to_z // GRID * 2 + d % 2))
    return pairs


def pack_kernel(y_ref, grad_ref, about_ref, *out_refs):
    width = grad_ref.shape[1] // RUN
    tokens = grad_ref.shape[0]
    about = about_ref[...]
    lane = lax.broadcasted_iota(jnp.int32, (tokens, LANES), 1)
    block = jnp.zeros((tokens, LANES), jnp.float32)
    place = 0
    for k in range(4):
        rest = about[:, k : k + 1]
        for _ in range(1 if k < 2 else 3):
            piece = rest.astype(jnp.bfloat16).astype(jnp.float32)
            block = jnp.where(lane == place, piece, block)
            rest = rest - piece
            place += 1
    for step, out_ref in enumerate(out_refs):
        quarter = (y_ref[0] + step) % RUN
        start = pl.multiple_of(quarter * width, LANES)
        out_ref[:, :width] = grad_ref[:, pl.ds(start, width)]
        out_ref[:, width:] = block.astype(jnp.bfloat16)


def send_h_kernel(row_ref, col_ref, want_ref, acts_ref, out_ref):
    sel = jnp.where(choose(row_ref[0], col_ref[0], want_ref[...]), 1.0, 0.0).astype(jnp.bfloat16)
    out_ref[...] = contract(sel, acts_ref[...], ((1,), (0,))).astype(jnp.bfloat16)


def send_c_kernel(y_ref, want_ref, packed_ref, *out_refs):
    tokens = packed_ref.shape[1]
    width = packed_ref.shape[2] - LANES
    block = packed_ref[0, :, width:]
    eye = lax.broadcasted_iota(jnp.int32, (tokens, tokens), 0) == lax.broadcasted_iota(
        jnp.int32, (tokens, tokens), 1
    )
    lines = contract(block, jnp.where(eye, 1.0, 0.0).astype(jnp.bfloat16), ((0,), (0,)))
    columns = block.astype(jnp.float32)
    row = jnp.concatenate([lines[0:1], lines[1:2]], axis=1)
    col = jnp.concatenate([columns[:, 0:1], columns[:, 1:2]], axis=0)
    gates = [lines[2 + 3 * k : 3 + 3 * k] + lines[3 + 3 * k : 4 + 3 * k] for k in range(2)]
    gates = [gates[k] + lines[4 + 3 * k : 5 + 3 * k] for k in range(2)]
    sel = choose(row, col, want_ref[0])
    gate = jnp.sum(
        jnp.where(sel, jnp.concatenate(gates, axis=1), 0.0), axis=1, keepdims=True
    )
    sel = jnp.where(sel, 1.0, 0.0)
    sel = (sel[:, :tokens] + sel[:, tokens:]).astype(jnp.bfloat16)
    rows = gate * contract(sel, packed_ref[0, :, :width], ((1,), (0,)))
    for i, out_ref in enumerate(out_refs):
        out_ref[...] = rows[i * CAP : (i + 1) * CAP].astype(jnp.bfloat16)


def order_kernel(order_ref, value_ref, out_ref):
    width = value_ref.shape[1]
    lane = lax.broadcasted_iota(jnp.int32, (ROWS, 2 * ROWS), 1)
    for kind in range(2):
        turn = jnp.where(lane == order_ref[kind], 1.0, 0.0).astype(jnp.bfloat16)
        rows = contract(turn, value_ref[...], ((1,), (0,))).astype(jnp.bfloat16)
        out_ref[:, kind * width : (kind + 1) * width] = rows


def unorder_kernel(order_ref, value_ref, out_ref):
    lane = lax.broadcasted_iota(jnp.int32, (ROWS, ROWS), 1)
    turn = jnp.where(lane == order_ref[...], 1.0, 0.0).astype(jnp.bfloat16)
    out_ref[...] = contract(turn, value_ref[...].astype(jnp.bfloat16), ((0,), (0,))).astype(
        jnp.bfloat16
    )


def join_kernel(*refs):
    for i in range(0, len(refs) - 1, 2):
        pair = [ref[...].astype(jnp.float32) for ref in refs[i : i + 2]]
        rows = jnp.concatenate(pair, axis=0).astype(jnp.bfloat16)
        refs[-1][i * CAP : (i + 2) * CAP] = rows


def back_kernel(*refs):
    w_ref, out_ref, rows_ref = refs[-3:]
    quarter = refs[0].shape[0]
    for at, ref in enumerate(refs[:-3]):
        rows_ref[at * quarter : (at + 1) * quarter] = ref[...]
    out_ref[0] = contract(rows_ref[...], w_ref[...], ((1,), (1,)))


def update_kernel(h_own_ref, h_extra_ref, *refs):
    c_refs = refs[:4]
    w_ref, m_ref, v_ref, out_ref, rows_ref = refs[4:]
    block, width = w_ref.shape
    quarter = c_refs[0].shape[0]

    @pl.when(pl.program_id(0) == 0)
    def _():
        for part in range(2 * RUN):
            for at, c_ref in enumerate(c_refs):
                rows_ref[part, at * quarter : (at + 1) * quarter] = c_ref[
                    :, part * width : (part + 1) * width
                ]

    depth = RUN * ROWS
    total = contract(
        h_own_ref[...].reshape(depth, block), rows_ref[:RUN].reshape(depth, width), ((0,), (0,))
    )
    total += contract(
        h_extra_ref[...].reshape(depth, block), rows_ref[RUN:].reshape(depth, width), ((0,), (0,))
    )
    m_new = beta_one * m_ref[...] + (1.0 - beta_one) * total
    v_new = beta_two * v_ref[...] + (1.0 - beta_two) * total * total
    direction = m_new / bias_one / (jnp.sqrt(v_new / bias_two) + epsilon)
    direction = direction + decay * w_ref[...].astype(jnp.float32)
    out_ref[...] = SCALE * direction


def take_kernel(row_ref, col_ref, want_ref, back_ref, out_ref):
    sel = jnp.where(choose(row_ref[0], col_ref[0], want_ref[...]), 1.0, 0.0).astype(jnp.bfloat16)
    out_ref[...] = contract(sel, back_ref[...], ((0,), (0,))).astype(jnp.bfloat16)


def in_hbm(value):
    return pltpu.with_memory_space_constraint(value, pltpu.HBM)


def params(limit):
    return pltpu.CompilerParams(vmem_limit_bytes=limit * MB)


def whole(shape):
    return pl.BlockSpec(shape, lambda *_: (0,) * len(shape))


def local(
    hidden_acts,
    out_grad,
    gate_probs,
    route,
    weights,
    first_moment,
    second_moment,
    old_slot,
    new_slot,
    partner,
):
    tokens, top, hidden = hidden_acts.shape
    count = tokens * top
    width = weights.shape[2]
    index = lax.axis_index("ep").astype(jnp.int32)
    y = index % RUN
    core = (lax.axis_index("dp") % 2).astype(jnp.int32)

    numbers = jnp.arange(GROUPS, dtype=jnp.int32)
    held = old_slot[None, :] == numbers[:, None]
    own = jnp.sum(jnp.where(held, numbers[None, :], 0), axis=1)
    mate = jnp.sum(jnp.where(held, partner[None, :], 0), axis=1)
    mate = jnp.where(mate == own, -1, mate)
    want = jnp.stack([own, mate]).astype(jnp.float32)
    steps = jnp.array([SHIFTS[0] + SHIFTS[1], SHIFTS[1] + SHIFTS[0]], jnp.int32)
    steps = jnp.where(core == 0, steps[0], steps[1])
    x, z = index // (GRID * RUN), index // RUN % GRID
    to = (x + steps[:HALF, 0]) % GRID * GRID + (z + steps[:HALF, 1]) % GRID
    by = (x - steps[:, 0]) % GRID * GRID + (z - steps[:, 1]) % GRID
    want_to = jnp.sum(jnp.where(to[:, None] == numbers[None, :], want[:, None, :], 0.0), axis=2)
    want_h = jnp.broadcast_to(want.T[:, :, None], (GROUPS, 2, CAP)).reshape(2 * ROWS, 1)
    want = jnp.broadcast_to(want[0, :, None], (GROUPS, CAP)).reshape(ROWS, 1)
    want_to = jnp.broadcast_to(want_to[:, :, None], (2, HALF, CAP)).reshape(2, ROWS // 2, 1)
    place = jnp.arange(CAP, dtype=jnp.int32)[None, :]
    order = (by[:, None] * CAP + place).reshape(ROWS, 1)
    order_h = jnp.stack([by[:, None] * 2 * CAP + place, by[:, None] * 2 * CAP + CAP + place])
    order_h = order_h.reshape(2, ROWS, 1)
    source = jnp.sum(
        jnp.where(new_slot[None, :] == numbers[:, None], old_slot[None, :], 0), axis=1
    )

    routes = route.astype(jnp.float32)
    packed = pl.pallas_call(
        pack_kernel,
        grid_spec=pltpu.PrefetchScalarGridSpec(
            num_scalar_prefetch=1,
            grid=(1,),
            in_specs=[whole((tokens, RUN * width)), whole((tokens, 2 * top))],
            out_specs=[whole((tokens, width + LANES))] * RUN,
        ),
        out_shape=[jax.ShapeDtypeStruct((tokens, width + LANES), jnp.bfloat16)] * RUN,
        compiler_params=params(16),
        name="pack",
    )(y.reshape(1), out_grad, jnp.concatenate([routes, gate_probs], axis=1))
    packed = [packed[0]] + [lax.ppermute(packed[s], "ep", along_y(s)) for s in range(1, RUN)]
    packed = jnp.stack(packed)

    own_row = routes.T.reshape(1, 1, count)
    own_col = own_row.reshape(1, count, 1)
    acts = hidden_acts.transpose(1, 0, 2).reshape(count, hidden)
    sent_h = pl.pallas_call(
        send_h_kernel,
        out_shape=jax.ShapeDtypeStruct((2 * ROWS, hidden), jnp.bfloat16),
        compiler_params=params(16),
        name="send_h",
    )(own_row, own_col, want_h, acts)
    got_h = lax.all_to_all(sent_h, "ep", 0, 0, axis_index_groups=SAME_Y, tiled=True)

    send_c = pl.pallas_call(
        send_c_kernel,
        grid_spec=pltpu.PrefetchScalarGridSpec(
            num_scalar_prefetch=1,
            grid=(2, RUN),
            in_specs=[
                pl.BlockSpec((1, ROWS // 2, 1), lambda k, s, y: (k, 0, 0)),
                pl.BlockSpec(
                    (1, tokens, width + LANES), lambda k, s, y: ((y[0] + RUN - s) % RUN, 0, 0)
                ),
            ],
            out_specs=[pl.BlockSpec((CAP, width), lambda k, s, y: (0, RUN * k + s))] * HALF,
        ),
        out_shape=[pltpu.HBM((CAP, 2 * RUN * width), jnp.bfloat16)] * HALF,
        compiler_params=params(24),
        name="send_c",
    )(y.reshape(1), want_to, packed)
    send_c = list(send_c)
    got_h, send_c[0] = lax.optimization_barrier((got_h, send_c[0]))
    got_h = pl.pallas_call(
        order_kernel,
        out_shape=jax.ShapeDtypeStruct((ROWS, 2 * hidden), jnp.bfloat16),
        compiler_params=params(16),
        name="order_h",
    )(order_h, got_h)
    all_h = lax.all_gather(got_h, "ep", axis_index_groups=SAME_RUN, axis=0, tiled=False)
    got_c = [lax.ppermute(send_c[i], ("ep", "dp"), nearest(i)) for i in range(HALF)]
    own_c, mate_c = [], []
    for at in range(0, HALF, HALF // 2):
        own_c.append(
            pl.pallas_call(
                join_kernel,
                out_shape=pltpu.HBM((ROWS // 4, 2 * RUN * width), jnp.bfloat16),
                compiler_params=params(16),
                name="join",
            )(*got_c[at : at + HALF // 2])
        )
        mate_c.append(lax.ppermute(own_c[-1], "dp", OTHER_CORE))
    parts = [in_hbm(part) for part in own_c + mate_c]

    weight = weights[0]
    partial_back = pl.pallas_call(
        back_kernel,
        grid=(RUN,),
        in_specs=[pl.BlockSpec((ROWS // 4, width), lambda s: (0, s))] * 4
        + [whole((hidden, width))],
        out_specs=pl.BlockSpec((1, ROWS, hidden), lambda s: (s, 0, 0)),
        scratch_shapes=[pltpu.VMEM((ROWS, width), jnp.bfloat16)],
        out_shape=jax.ShapeDtypeStruct((RUN, ROWS, hidden), jnp.float32),
        compiler_params=params(24),
        name="back",
    )(*parts, in_hbm(weight))
    summed = lax.psum_scatter(
        partial_back, "ep", scatter_dimension=0, axis_index_groups=SAME_RUN, tiled=False
    )
    back = pl.pallas_call(
        unorder_kernel,
        out_shape=jax.ShapeDtypeStruct((ROWS, hidden), jnp.bfloat16),
        compiler_params=params(16),
        name="unorder",
    )(order, summed)
    block = 128
    grid = hidden // block
    update = pl.pallas_call(
        update_kernel,
        grid=(grid,),
        in_specs=[
            pl.BlockSpec((RUN, ROWS, block), lambda i: (0, 0, i)),
            pl.BlockSpec((RUN, ROWS, block), lambda i: (0, 0, grid + i)),
        ]
        + [whole((ROWS // 4, 2 * RUN * width))] * 4
        + [pl.BlockSpec((block, width), lambda i: (i, 0))] * 3,
        out_specs=pl.BlockSpec((block, width), lambda i: (i, 0)),
        scratch_shapes=[pltpu.VMEM((2 * RUN, ROWS, width), jnp.bfloat16)],
        out_shape=jax.ShapeDtypeStruct((hidden, width), jnp.float32),
        compiler_params=params(28),
        name="update",
    )(
        in_hbm(all_h),
        in_hbm(all_h),
        *parts,
        in_hbm(weight),
        in_hbm(first_moment[0]),
        in_hbm(second_moment[0]),
    )

    part = hidden // GROUPS
    spread = update.astype(jnp.float16).reshape(GROUPS, part, width)
    spread = lax.all_to_all(spread, "ep", 0, 0, axis_index_groups=SAME_Y, tiled=True)
    riders = (back.astype(jnp.float32) * BACK_SCALE).astype(jnp.float16)
    riders = riders.reshape(GROUPS, part, CAP * hidden // part)
    placed = jnp.concatenate([spread[source], riders], axis=2)
    placed = lax.all_to_all(placed, "ep", 0, 0, axis_index_groups=SAME_Y, tiled=True)
    back = placed[:, :, width:].astype(jnp.float32) * (1.0 / BACK_SCALE)
    back = back.astype(jnp.bfloat16).reshape(ROWS, hidden)
    hidden_out = pl.pallas_call(
        take_kernel,
        out_shape=jax.ShapeDtypeStruct((count, hidden), jnp.bfloat16),
        compiler_params=params(16),
        name="take",
    )(own_row, own_col, want, back)
    hidden_out = hidden_out.reshape(top, tokens, hidden).transpose(1, 0, 2)
    placed = placed[:, :, :width].astype(jnp.float32).reshape(1, hidden, width) * (1.0 / SCALE)
    return (hidden_out, placed)


def solution(mesh):
    return jax.shard_map(
        local,
        mesh=mesh,
        in_specs=(
            P("ep", None, "dp"),
            P("ep", None),
            P("ep", None),
            P("ep", None),
            P("ep", "dp", None),
            P("ep", "dp", None),
            P("ep", "dp", None),
            P(),
            P(),
            P(),
        ),
        out_specs=(P("ep", None, "dp"), P("ep", "dp", None)),
        check_vma=False,
    )
```

time: 221 us -> 213 us (0.964)
  starting transfers between devices: 71 us -> 53.4 us
  waiting for transfers between devices: 84 us -> 97.9 us
  local copies, waits for them, and re-layouts: 13.3 us -> 10 us
    all_to_all x1, waiting for transfers between devices: 2.46 us -> 29.1 us  [local(): lax.all_to_all(spread, 'ep', 0, 0, axis_index_groups=SAME_Y, tiled=True)]
    reduce_scatter x1, waiting for transfers between devices: 23.9 us -> 0.02 us  [local(): lax.psum_scatter(partial_back, 'ep', scatter_dimension=0, axis_index_grou...]
    ppermute x17 -> x10, starting transfers between devices: 42.5 us -> 26.9 us  [the longest x8 14.6 us: local(): lax.ppermute(send_c[i], ('ep', 'dp'), nearest(i))]
    ppermute x17 -> x10, waiting for transfers between devices: 7.7 us -> 16.7 us  [the longest x8 13.4 us: local(): lax.ppermute(send_c[i], ('ep', 'dp'), nearest(i))]
    all_to_all x2 -> x1, starting transfers between devices: 8.3 us -> 4.38 us  [local(): lax.all_to_all(placed, 'ep', 0, 0, axis_index_groups=SAME_Y, tiled=True)]
    unnamed x46 -> x18, local copies, waits for them, and re-layouts: 7.79 us -> 4.21 us
    all_to_all x1, waiting for transfers between devices: 0.59 us -> 3.45 us  [local(): lax.all_to_all(sent_h, 'ep', 0, 0, axis_index_groups=SAME_Y, tiled=True)]
    pallas_call x1, Pallas kernels: 2.92 us -> 5.49 us  [local(): pl.pallas_call(send_c_kernel, grid_spec=pltpu.PrefetchScalarGridSpec(num_...]
  transfers between devices with their start and end apart: 26 -> 18, of which waited for: 10 -> 12; matrix products, arithmetic and copies ran while one was open for 4% -> 2% of each run, Pallas kernels for 12% -> 11%
where the time goes in v5:
time: 213 us; the launch traced here: 212 us
  waiting for transfers between devices  97.9 us (46%)
  starting transfers between devices  53.4 us (25%)
  Pallas kernels  29.2 us (14%)
  between operations  14.4 us (7%)
  local copies, waits for them, and re-layouts  10 us (5%)
  other arithmetic  7.52 us (4%)
    all_to_all x1, waiting for transfers between devices, local(): lax.all_to_all(placed, 'ep', 0, 0, axis_index_groups=SAME_Y, tiled=True)  39.7 us
    all_to_all x1, waiting for transfers between devices, local(): lax.all_to_all(spread, 'ep', 0, 0, axis_index_groups=SAME_Y, tiled=True)  29.1 us
    ppermute x8, starting transfers between devices, local(): lax.ppermute(send_c[i], ('ep', 'dp'), nearest(i))  14.6 us
    ppermute x8, waiting for transfers between devices, local(): lax.ppermute(send_c[i], ('ep', 'dp'), nearest(i))  13.4 us
    ppermute x2, starting transfers between devices, local(): mate_c.append(lax.ppermute(own_c[-1], 'dp', OTHER_CORE))  12.3 us
    pallas_call x1, Pallas kernels, local(): pl.pallas_call(update_kernel, grid=(grid,), in_specs=[pl.BlockSpec((RUN,...  10.8 us
    all_to_all x1, starting transfers between devices, local(): lax.all_to_all(sent_h, 'ep', 0, 0, axis_index_groups=SAME_Y, tiled=True)  9.15 us
    ppermute x3, waiting for transfers between devices, local(): lax.ppermute(packed[s], 'ep', along_y(s))  8.83 us
  transfers between devices with their start and end apart: 18, of which 12 were waited for; matrix products, arithmetic and copies ran while one was open for 2% of the time, Pallas kernels for 11%

profile of v5, /device:TPU:1, one launch (start us, length us, event | category | flops | bytes accessed | tf_op | source)
XLA Modules:
  0.0 212.4 jit_solution(5464843414964606190)
XLA Ops:
  10.2 1.6 send_h.1
  11.9 9.1 %all-to-all-start = ((bf16[16,48,640]{2,1,0:T(8,128)(2,1)}), bf16[16,48,640]{2,1,0:T(8,128)(2,1)S(1)}, u32[]{:S(2)}, u32[]{:S(2)}) async-start(bf16[16,48,640]{2,1,0:T(8,128)(2,1)} %bitcast.13), calls=%async_computation | async-start | bytes 1966080 | tf_op jit(solution)/shard_map/all_to_all | solution.py:265
  21.4 1.4 collective-permute-start
  22.8 2.6 %collective-permute-start.1 = (bf16[128,1024]{1,0:T(8,128)(2,1)S(1)}, bf16[128,1024]{1,0:T(8,128)(2,1)}, u32[]{:S(2)}, u32[]{:S(2)}) collective-permute-start(bf16[128,1024]{1,0:T(8,128)(2,1)S(1)} %get-tuple-element.18), channel_id=1, source_target_pairs={{0,8},{4,12},{8,0},{12,4},{16,24},{20,28},{24,16},{28,20},{32,40},... | collective-permute-start | bytes 786440 | tf_op jit(solution)/shard_map/ppermute | solution.py:253
  27.7 2.0 collective-permute-done
  29.7 6.8 %collective-permute-done.1 = bf16[128,1024]{1,0:T(8,128)(2,1)} collective-permute-done((bf16[128,1024]{1,0:T(8,128)(2,1)S(1)}, bf16[128,1024]{1,0:T(8,128)(2,1)}, u32[]{:S(2)}, u32[]{:S(2)}) %collective-permute-start.1) | collective-permute-done | bytes 262176 | tf_op jit(solution)/shard_map/ppermute | solution.py:253
  36.5 1.2 pad_maximum_fusion.1.packed_ref
  37.7 5.5 %send_c.1 = (bf16[24,7168]{1,0:T(8,128)(2,1)}, bf16[24,7168]{1,0:T(8,128)(2,1)}, bf16[24,7168]{1,0:T(8,128)(2,1)}, bf16[24,7168]{1,0:T(8,128)(2,1)}, bf16[24,716...) custom-call(s32[1]{0:T(128)} %bitcast.15.y_ref, ...), custom_call_target="tpu_custom_call" | custom-call | tf_op jit(solution)/shard_map/send_c/pallas_call | solution.py:267
  43.2 3.4 %all-to-all-done = bf16[16,48,640]{2,1,0:T(8,128)(2,1)S(1)} async-done(((bf16[16,48,640]{2,1,0:T(8,128)(2,1)}), bf16[16,48,640]{2,1,0:T(8,128)(2,1)S(1)}, u32[]{:S(2)}, u32[]{:S(2)}) %all-to-all-start) | async-done | bytes 983072 | tf_op jit(solution)/shard_map/all_to_all | solution.py:265
  46.6 2.2 %order_h.1 = bf16[384,1280]{1,0:T(8,128)(2,1)} custom-call(s32[2,384,1]{2,1,0:T(8,128)S(1)} %pad_add_fusion.order_ref, bf16[768,640]{1,0:T(8,128)(2,1)S(1)} %bitcast.51), custom_call_target="tpu_custom_call" | custom-call | tf_op jit(solution)/shard_map/order_h/pallas_call | solution.py:286
  50.1 4.6 %collective-permute-start.8 = (bf16[24,7168]{1,0:T(8,128)(2,1)}, bf16[24,7168]{1,0:T(8,128)(2,1)S(1)}, u32[]{:S(2)}, u32[]{:S(2)}) collective-permute-start(bf16[24,7168]{1,0:T(8,128)(2,1)} %get-tuple-element.27), channel_id=1, source_target_pairs={{0,50},{1,209},{2,48},{3,211},{4,54},{5,213},{6,52},{7,215},{8,58}... | collective-permute-start | bytes 1032200 | tf_op jit(solution)/shard_map/ppermute | solution.py:293
  54.6 1.1 collective-permute-start.4
  56.3 3.4 %collective-permute-start.5 = (bf16[24,7168]{1,0:T(8,128)(2,1)}, bf16[24,7168]{1,0:T(8,128)(2,1)S(1)}, u32[]{:S(2)}, u32[]{:S(2)}) collective-permute-start(bf16[24,7168]{1,0:T(8,128)(2,1)} %get-tuple-element.24), channel_id=1, source_target_pairs={{0,96},{1,179},{2,98},{3,177},{4,100},{5,183},{6,102},{7,181},{8,1... | collective-permute-start | bytes 1032200 | tf_op jit(solution)/shard_map/ppermute | solution.py:293
  60.8 2.4 %collective-permute-start.6 = (bf16[24,7168]{1,0:T(8,128)(2,1)}, bf16[24,7168]{1,0:T(8,128)(2,1)S(1)}, u32[]{:S(2)}, u32[]{:S(2)}) collective-permute-start(bf16[24,7168]{1,0:T(8,128)(2,1)} %get-tuple-element.25), channel_id=1, source_target_pairs={{0,144},{1,115},{2,146},{3,113},{4,148},{5,119},{6,150},{7,117},{8... | collective-permute-start | bytes 1032200 | tf_op jit(solution)/shard_map/ppermute | solution.py:293
  63.2 3.9 %collective-permute-done.8.refs_1_ = bf16[24,7168]{1,0:T(8,128)(2,1)S(1)} collective-permute-done((bf16[24,7168]{1,0:T(8,128)(2,1)}, bf16[24,7168]{1,0:T(8,128)(2,1)S(1)}, u32[]{:S(2)}, u32[]{:S(2)}) %collective-permute-start.8) | collective-permute-done | bytes 344096 | tf_op jit(solution)/shard_map/ppermute | solution.py:293
  67.1 1.9 collective-permute-start.3
  69.0 3.6 %collective-permute-done.9.refs_2_ = bf16[24,7168]{1,0:T(8,128)(2,1)S(1)} collective-permute-done((bf16[24,7168]{1,0:T(8,128)(2,1)}, bf16[24,7168]{1,0:T(8,128)(2,1)S(1)}, u32[]{:S(2)}, u32[]{:S(2)}) %collective-permute-start.9) | collective-permute-done | bytes 344096 | tf_op jit(solution)/shard_map/ppermute | solution.py:293
  72.7 1.3 join.3.refs_1_
  73.9 12.3 %collective-permute-start.12 = (bf16[96,7168]{1,0:T(8,128)(2,1)}, bf16[96,7168]{1,0:T(8,128)(2,1)S(1)}, u32[]{:S(2)}, u32[]{:S(2)}) collective-permute-start(bf16[96,7168]{1,0:T(8,128)(2,1)} %join.3.refs_1_), channel_id=1, source_target_pairs={{0,1},{1,0},{2,3},{3,2},{4,5},{5,4},{6,7},{7,6},{8,9},{9,8},{10,11... | collective-permute-start | bytes 4128776 | tf_op jit(solution)/shard_map/ppermute | solution.py:304
  87.1 3.4 %collective-permute-done.3.refs_0_ = bf16[24,7168]{1,0:T(8,128)(2,1)S(1)} collective-permute-done((bf16[24,7168]{1,0:T(8,128)(2,1)S(1)}, bf16[24,7168]{1,0:T(8,128)(2,1)S(1)}, u32[]{:S(2)}, u32[]{:S(2)}) %collective-permute-start.3) | collective-permute-done | bytes 344096 | tf_op jit(solution)/shard_map/ppermute | solution.py:293
  90.5 1.2 join.2.refs_0_
  91.7 3.3 %collective-permute-done.11.refs_2_ = bf16[96,7168]{1,0:T(8,128)(2,1)S(1)} collective-permute-done((bf16[96,7168]{1,0:T(8,128)(2,1)}, bf16[96,7168]{1,0:T(8,128)(2,1)S(1)}, u32[]{:S(2)}, u32[]{:S(2)}) %collective-permute-start.11) | collective-permute-done | bytes 1376288 | tf_op jit(solution)/shard_map/ppermute | solution.py:304
  96.2 5.3 %back.1 = f32[4,384,640]{2,1,0:T(8,128)S(1)} custom-call(bf16[96,7168]{1,0:T(8,128)(2,1)} %join.2.refs_0_, bf16[96,7168]{1,0:T(8,128)(2,1)} %join.3.refs_1_, bf16[96,7168]{1,0:T(8,128)(2,1)} %copy-done.4, bf16[96,7168]{1,0:T(8,128)(2,1)} %copy-done.3, bf16[640,896]{1,0:T(8,128)(2,1)} %bitcast.61), custom_call_target="tpu_custom_call" | custom-call | tf_op jit(solution)/shard_map/back/pallas_call | solution.py:308
  101.5 1.9 copy-done
  103.4 10.8 %update.1 = f32[640,896]{1,0:T(8,128)S(1)} custom-call(bf16[4,384,1280]{2,1,0:T(8,128)(2,1)} %bitcast.59, bf16[4,384,1280]{2,1,0:T(8,128)(2,1)} %bitcast.60, bf16[96,7168]{1,0:T(8,128)(2,1)} %join.2.refs_0_, bf16[96,7168]{1,0:T(8,128)(2,1)} %join.3.refs_1_, bf16[96,7168]{1,0:T(8,128)(2,1)} %copy-done.4, bf16[96,7168]{1,0:T(8,128)(2,1)} %copy-done.3, ...), custom_call_target="tpu_custom_call" | custom-call | tf_op jit(solution)/shard_map/update/pallas_call | solution.py:330
  115.4 7.8 %all-to-all-start.1 = ((f16[16,40,896]{2,1,0:T(8,128)(2,1)}), f16[16,40,896]{2,1,0:T(8,128)(2,1)S(1)}, u32[]{:S(2)}, u32[]{:S(2)}) async-start(f16[16,40,896]{2,1,0:T(8,128)(2,1)} %bitcast.25), calls=%async_computation.1 | async-start | bytes 2293760 | tf_op jit(solution)/shard_map/all_to_all | solution.py:355
  123.4 29.1 %all-to-all-done.1 = f16[16,40,896]{2,1,0:T(8,128)(2,1)S(1)} async-done(((f16[16,40,896]{2,1,0:T(8,128)(2,1)}), f16[16,40,896]{2,1,0:T(8,128)(2,1)S(1)}, u32[]{:S(2)}, u32[]{:S(2)}) %all-to-all-start.1) | async-done | bytes 1146912 | tf_op jit(solution)/shard_map/all_to_all | solution.py:355
  153.6 1.2 copy-done.1
  155.9 1.6 pad_maximum_fusion
  157.5 4.4 %all-to-all-start.2 = ((f16[16,40,1280]{2,1,0:T(8,128)(2,1)}), f16[16,40,1280]{2,1,0:T(8,128)(2,1)S(1)}, u32[]{:S(2)}, u32[]{:S(2)}) async-start(f16[16,40,1280]{2,1,0:T(8,128)(2,1)} %pad_maximum_fusion), calls=%async_computation.3 | async-start | bytes 3276800 | tf_op jit(solution)/shard_map/all_to_all | solution.py:359
  162.1 39.7 %all-to-all-done.2 = f16[16,40,1280]{2,1,0:T(8,128)(2,1)S(1)} async-done(((f16[16,40,1280]{2,1,0:T(8,128)(2,1)}), f16[16,40,1280]{2,1,0:T(8,128)(2,1)S(1)}, u32[]{:S(2)}, u32[]{:S(2)}) %all-to-all-start.2) | async-done | bytes 1638432 | tf_op jit(solution)/shard_map/all_to_all | solution.py:359
  203.9 1.6 convert_multiply_fusion
  (80 shorter events, 16.3 us)
Async XLA Ops:
  10.2 10.9 %copy-start.7 = (f32[128,2]{0,1:T(2,128)S(1)}, f32[128,2]{0,1:T(2,128)}, u32[]{:S(2)}) copy-start(f32[128,2]{0,1:T(2,128)} %param.13) | copy-start | bytes 3076
  10.2 11.0 %copy-start.2 = (bf16[128,3584]{1,0:T(8,128)(2,1)S(1)}, bf16[128,3584]{1,0:T(8,128)(2,1)}, u32[]{:S(2)}) copy-start(bf16[128,3584]{1,0:T(8,128)(2,1)} %grad_ref.1) | copy-start | bytes 2752516
  11.9 14.6 %copy-start.5 = (s32[1,16,2]{1,2,0:T(2,128)S(1)}, s32[1,16,2]{1,2,0:T(2,128)}, u32[]{:S(2)}) copy-start(s32[1,16,2]{1,2,0:T(2,128)} %constant.109) | copy-start | bytes 388
  11.9 14.6 %copy-start.6 = (s32[1,16,2]{1,2,0:T(2,128)S(1)}, s32[1,16,2]{1,2,0:T(2,128)}, u32[]{:S(2)}) copy-start(s32[1,16,2]{1,2,0:T(2,128)} %constant.110) | copy-start | bytes 388
  11.9 34.7 %all-to-all-start = ((bf16[16,48,640]{2,1,0:T(8,128)(2,1)}), bf16[16,48,640]{2,1,0:T(8,128)(2,1)S(1)}, u32[]{:S(2)}, u32[]{:S(2)}) async-start(bf16[16,48,640]{2,1,0:T(8,128)(2,1)} %bitcast.13), calls=%async_computation | async-start | bytes 1966080 | tf_op jit(solution)/shard_map/all_to_all | solution.py:265
  21.0 82.4 %all-gather.3.cloned.1.call-start = ((), (), s32[]{:S(2)}) async-start(), calls=%async_computation.5 | async-start | bytes 4915200 | tf_op jit(solution)/shard_map/all_gather | solution.py:292
  21.4 8.3 %collective-permute-start = (bf16[128,1024]{1,0:T(8,128)(2,1)S(1)}, bf16[128,1024]{1,0:T(8,128)(2,1)S(1)}, u32[]{:S(2)}, u32[]{:S(2)}) collective-permute-start(bf16[128,1024]{1,0:T(8,128)(2,1)S(1)} %get-tuple-element.17), channel_id=1, source_target_pairs={{0,4},{4,8},{8,12},{12,0},{16,20},{20,24},{24,28},{28,16},{32,36},... | collective-permute-start | bytes 786440 | tf_op jit(solution)/shard_map/ppermute | solution.py:253
  22.8 13.7 %collective-permute-start.1 = (bf16[128,1024]{1,0:T(8,128)(2,1)S(1)}, bf16[128,1024]{1,0:T(8,128)(2,1)}, u32[]{:S(2)}, u32[]{:S(2)}) collective-permute-start(bf16[128,1024]{1,0:T(8,128)(2,1)S(1)} %get-tuple-element.18), channel_id=1, source_target_pairs={{0,8},{4,12},{8,0},{12,4},{16,24},{20,28},{24,16},{28,20},{32,40},... | collective-permute-start | bytes 786440 | tf_op jit(solution)/shard_map/ppermute | solution.py:253
  25.4 11.1 %collective-permute-start.2 = (bf16[128,1024]{1,0:T(8,128)(2,1)S(1)}, bf16[128,1024]{1,0:T(8,128)(2,1)}, u32[]{:S(2)}, u32[]{:S(2)}) collective-permute-start(bf16[128,1024]{1,0:T(8,128)(2,1)S(1)} %get-tuple-element.19), channel_id=1, source_target_pairs={{0,12},{4,0},{8,4},{12,8},{16,28},{20,16},{24,20},{28,24},{32,44},... | collective-permute-start | bytes 786440 | tf_op jit(solution)/shard_map/ppermute | solution.py:253
  46.6 20.5 %copy-start.8 = (bf16[24,7168]{1,0:T(8,128)(2,1)S(1)}, bf16[24,7168]{1,0:T(8,128)(2,1)}, u32[]{:S(2)}) copy-start(bf16[24,7168]{1,0:T(8,128)(2,1)} %get-tuple-element.22) | copy-start | bytes 1032196
  48.9 104.7 %reduce-scatter.2.cloned.1.call-start = ((), (), s32[]{:S(2)}) async-start(), calls=%async_computation.4 | async-start | bytes 4915200 | tf_op jit(solution)/shard_map/reduce_scatter | solution.py:319
  48.9 7.4 %collective-permute-start.10 = (bf16[24,7168]{1,0:T(8,128)(2,1)}, bf16[24,7168]{1,0:T(8,128)(2,1)S(1)}, u32[]{:S(2)}, u32[]{:S(2)}) collective-permute-start(bf16[24,7168]{1,0:T(8,128)(2,1)} %get-tuple-element.29), channel_id=1, source_target_pairs={{0,80},{1,193},{2,82},{3,195},{4,84},{5,197},{6,86},{7,199},{8,88}... | collective-permute-start | bytes 1032200 | tf_op jit(solution)/shard_map/ppermute | solution.py:293
  49.6 11.2 %collective-permute-start.7 = (bf16[24,7168]{1,0:T(8,128)(2,1)}, bf16[24,7168]{1,0:T(8,128)(2,1)S(1)}, u32[]{:S(2)}, u32[]{:S(2)}) collective-permute-start(bf16[24,7168]{1,0:T(8,128)(2,1)} %get-tuple-element.26), channel_id=1, source_target_pairs={{0,242},{1,33},{2,240},{3,35},{4,246},{5,37},{6,244},{7,39},{8,250... | collective-permute-start | bytes 1032200 | tf_op jit(solution)/shard_map/ppermute | solution.py:293
  50.1 17.0 %collective-permute-start.8 = (bf16[24,7168]{1,0:T(8,128)(2,1)}, bf16[24,7168]{1,0:T(8,128)(2,1)S(1)}, u32[]{:S(2)}, u32[]{:S(2)}) collective-permute-start(bf16[24,7168]{1,0:T(8,128)(2,1)} %get-tuple-element.27), channel_id=1, source_target_pairs={{0,50},{1,209},{2,48},{3,211},{4,54},{5,213},{6,52},{7,215},{8,58}... | collective-permute-start | bytes 1032200 | tf_op jit(solution)/shard_map/ppermute | solution.py:293
  54.6 18.0 %collective-permute-start.9 = (bf16[24,7168]{1,0:T(8,128)(2,1)}, bf16[24,7168]{1,0:T(8,128)(2,1)S(1)}, u32[]{:S(2)}, u32[]{:S(2)}) collective-permute-start(bf16[24,7168]{1,0:T(8,128)(2,1)} %get-tuple-element.28), channel_id=1, source_target_pairs={{0,64},{1,17},{2,66},{3,19},{4,68},{5,21},{6,70},{7,23},{8,72},{9,... | collective-permute-start | bytes 1032200 | tf_op jit(solution)/shard_map/ppermute | solution.py:293
  54.6 31.6 %collective-permute-start.4 = (bf16[24,7168]{1,0:T(8,128)(2,1)}, bf16[24,7168]{1,0:T(8,128)(2,1)S(1)}, u32[]{:S(2)}, u32[]{:S(2)}) collective-permute-start(bf16[24,7168]{1,0:T(8,128)(2,1)} %get-tuple-element.23), channel_id=1, source_target_pairs={{0,160},{1,225},{2,162},{3,227},{4,164},{5,229},{6,166},{7,231},{8... | collective-permute-start | bytes 1032200 | tf_op jit(solution)/shard_map/ppermute | solution.py:293
  56.3 29.9 %collective-permute-start.5 = (bf16[24,7168]{1,0:T(8,128)(2,1)}, bf16[24,7168]{1,0:T(8,128)(2,1)S(1)}, u32[]{:S(2)}, u32[]{:S(2)}) collective-permute-start(bf16[24,7168]{1,0:T(8,128)(2,1)} %get-tuple-element.24), channel_id=1, source_target_pairs={{0,96},{1,179},{2,98},{3,177},{4,100},{5,183},{6,102},{7,181},{8,1... | collective-permute-start | bytes 1032200 | tf_op jit(solution)/shard_map/ppermute | solution.py:293
  60.8 26.3 %collective-permute-start.6 = (bf16[24,7168]{1,0:T(8,128)(2,1)}, bf16[24,7168]{1,0:T(8,128)(2,1)S(1)}, u32[]{:S(2)}, u32[]{:S(2)}) collective-permute-start(bf16[24,7168]{1,0:T(8,128)(2,1)} %get-tuple-element.25), channel_id=1, source_target_pairs={{0,144},{1,115},{2,146},{3,113},{4,148},{5,119},{6,150},{7,117},{8... | collective-permute-start | bytes 1032200 | tf_op jit(solution)/shard_map/ppermute | solution.py:293
  67.1 23.4 %collective-permute-start.3 = (bf16[24,7168]{1,0:T(8,128)(2,1)S(1)}, bf16[24,7168]{1,0:T(8,128)(2,1)S(1)}, u32[]{:S(2)}, u32[]{:S(2)}) collective-permute-start(bf16[24,7168]{1,0:T(8,128)(2,1)S(1)} %copy-done.8), channel_id=1, source_target_pairs={{0,0},{1,129},{2,2},{3,131},{4,4},{5,133},{6,6},{7,135},{8,8},{9,1... | collective-permute-start | bytes 1032200 | tf_op jit(solution)/shard_map/ppermute | solution.py:293
  73.9 17.8 %collective-permute-start.12 = (bf16[96,7168]{1,0:T(8,128)(2,1)}, bf16[96,7168]{1,0:T(8,128)(2,1)S(1)}, u32[]{:S(2)}, u32[]{:S(2)}) collective-permute-start(bf16[96,7168]{1,0:T(8,128)(2,1)} %join.3.refs_1_), channel_id=1, source_target_pairs={{0,1},{1,0},{2,3},{3,2},{4,5},{5,4},{6,7},{7,6},{8,9},{9,8},{10,11... | collective-permute-start | bytes 4128776 | tf_op jit(solution)/shard_map/ppermute | solution.py:304
  91.7 3.3 %collective-permute-start.11 = (bf16[96,7168]{1,0:T(8,128)(2,1)}, bf16[96,7168]{1,0:T(8,128)(2,1)S(1)}, u32[]{:S(2)}, u32[]{:S(2)}) collective-permute-start(bf16[96,7168]{1,0:T(8,128)(2,1)} %join.2.refs_0_), channel_id=1, source_target_pairs={{0,1},{1,0},{2,3},{3,2},{4,5},{5,4},{6,7},{7,6},{8,9},{9,8},{10,11... | collective-permute-start | bytes 4128776 | tf_op jit(solution)/shard_map/ppermute | solution.py:304
  91.7 3.3 %copy-start.3 = (bf16[96,7168]{1,0:T(8,128)(2,1)}, bf16[96,7168]{1,0:T(8,128)(2,1)S(1)}, u32[]{:S(2)}) copy-start(bf16[96,7168]{1,0:T(8,128)(2,1)S(1)} %collective-permute-done.12.refs_3_) | copy-start | bytes 4128772
  95.0 1.1 copy-start.4
  101.5 1.9 copy-start
  115.4 37.0 %all-to-all-start.1 = ((f16[16,40,896]{2,1,0:T(8,128)(2,1)}), f16[16,40,896]{2,1,0:T(8,128)(2,1)S(1)}, u32[]{:S(2)}, u32[]{:S(2)}) async-start(f16[16,40,896]{2,1,0:T(8,128)(2,1)} %bitcast.25), calls=%async_computation.1 | async-start | bytes 2293760 | tf_op jit(solution)/shard_map/all_to_all | solution.py:355
  153.6 1.2 copy-start.1
  157.5 44.3 %all-to-all-start.2 = ((f16[16,40,1280]{2,1,0:T(8,128)(2,1)}), f16[16,40,1280]{2,1,0:T(8,128)(2,1)S(1)}, u32[]{:S(2)}, u32[]{:S(2)}) async-start(f16[16,40,1280]{2,1,0:T(8,128)(2,1)} %pad_maximum_fusion), calls=%async_computation.3 | async-start | bytes 3276800 | tf_op jit(solution)/shard_map/all_to_all | solution.py:359
Sparse Core Ops, SparseCore 0:
  49.0 47.8 all-gather.2
  103.5 46.3 reduce-scatter.1

commit v6 on v5

--- a/solution.py
+++ b/solution.py
@@ -17,7 +17,6 @@
 CAP = 24
 ROWS = GROUPS * CAP
 SCALE = 2048.0
-BACK_SCALE = 16.0
 SAME_Y = [[g * RUN + y for g in range(GROUPS)] for y in range(RUN)]
 SAME_RUN = [[g * RUN + y for y in range(RUN)] for g in range(GROUPS)]
 OTHER_CORE = [(0, 1), (1, 0), (2, 3), (3, 2)]
@@ -52,6 +51,14 @@
 
 def along_y(step):
     return [(i, i // RUN * RUN + (i + step) % RUN) for i in range(GROUPS * RUN)]
+
+
+def along_grid(step_x, step_z):
+    pairs = []
+    for i in range(GROUPS * RUN):
+        x, z, y = i // (GRID * RUN), i // RUN % GRID, i % RUN
+        pairs.append((i, ((x + step_x) % GRID * GRID + (z + step_z) % GRID) * RUN + y))
+    return pairs
 
 
 def nearest(number):
@@ -127,12 +134,19 @@
         out_ref[:, kind * width : (kind + 1) * width] = rows
 
 
-def unorder_kernel(order_ref, value_ref, out_ref):
-    lane = lax.broadcasted_iota(jnp.int32, (ROWS, ROWS), 1)
-    turn = jnp.where(lane == order_ref[...], 1.0, 0.0).astype(jnp.bfloat16)
-    out_ref[...] = contract(turn, value_ref[...].astype(jnp.bfloat16), ((0,), (0,))).astype(
-        jnp.bfloat16
-    )
+def return_kernel(to_ref, from_ref, value_ref, *out_refs):
+    turn = jnp.where(to_ref[...] == from_ref[...], 1.0, 0.0).astype(jnp.bfloat16)
+    rows = contract(turn, value_ref[...].astype(jnp.bfloat16), ((1,), (0,))).astype(jnp.bfloat16)
+    part = ROWS // GRID
+    for step, out_ref in enumerate(out_refs):
+        out_ref[...] = rows[step * part : (step + 1) * part]
+
+
+def turn_kernel(*refs):
+    values = [ref[...].astype(jnp.float32) for ref in refs[:GRID]]
+    for step, out_ref in enumerate(refs[GRID:]):
+        rows = [value[step * CAP : (step + 1) * CAP] for value in values]
+        out_ref[...] = jnp.concatenate(rows, axis=0).astype(jnp.bfloat16)
 
 
 def join_kernel(*refs):
@@ -143,34 +157,27 @@
 
 
 def back_kernel(*refs):
-    w_ref, out_ref, rows_ref = refs[-3:]
+    w_ref, out_ref, laid_ref = refs[4], refs[-2], refs[-1]
     quarter = refs[0].shape[0]
-    for at, ref in enumerate(refs[:-3]):
-        rows_ref[at * quarter : (at + 1) * quarter] = ref[...]
-    out_ref[0] = contract(rows_ref[...], w_ref[...], ((1,), (1,)))
-
-
-def update_kernel(h_own_ref, h_extra_ref, *refs):
-    c_refs = refs[:4]
-    w_ref, m_ref, v_ref, out_ref, rows_ref = refs[4:]
+    source = pl.program_id(0)
+    for kind in range(2):
+        for at in range(2):
+            rows = refs[2 * kind + at][...]
+            laid_ref[kind, source, at * quarter : (at + 1) * quarter] = rows
+    out_ref[0] = contract(laid_ref[0, source], w_ref[...], ((1,), (1,)))
+
+
+def update_kernel(
+    h_own_ref, h_extra_ref, own_ref, mate_ref, w_ref, m_ref, v_ref, out_ref
+):
     block, width = w_ref.shape
-    quarter = c_refs[0].shape[0]
-
-    @pl.when(pl.program_id(0) == 0)
-    def _():
-        for part in range(2 * RUN):
-            for at, c_ref in enumerate(c_refs):
-                rows_ref[part, at * quarter : (at + 1) * quarter] = c_ref[
-                    :, part * width : (part + 1) * width
-                ]
-
-    depth = RUN * ROWS
-    total = contract(
-        h_own_ref[...].reshape(depth, block), rows_ref[:RUN].reshape(depth, width), ((0,), (0,))
-    )
-    total += contract(
-        h_extra_ref[...].reshape(depth, block), rows_ref[RUN:].reshape(depth, width), ((0,), (0,))
-    )
+    half = own_ref.shape[2]
+    depth = RUN * half
+    total = jnp.zeros(w_ref.shape, jnp.float32)
+    for kind, h_ref in enumerate((h_own_ref, h_extra_ref)):
+        for at, c_ref in enumerate((own_ref, mate_ref)):
+            rows = h_ref[:, at * half : (at + 1) * half].reshape(depth, block)
+            total += contract(rows, c_ref[kind].reshape(depth, width), ((0,), (0,)))
     m_new = beta_one * m_ref[...] + (1.0 - beta_one) * total
     v_new = beta_two * v_ref[...] + (1.0 - beta_two) * total * total
     direction = m_new / bias_one / (jnp.sqrt(v_new / bias_two) + epsilon)
@@ -178,9 +185,13 @@
     out_ref[...] = SCALE * direction
 
 
-def take_kernel(row_ref, col_ref, want_ref, back_ref, out_ref):
+def take_kernel(row_ref, col_ref, want_ref, *refs):
     sel = jnp.where(choose(row_ref[0], col_ref[0], want_ref[...]), 1.0, 0.0).astype(jnp.bfloat16)
-    out_ref[...] = contract(sel, back_ref[...], ((0,), (0,))).astype(jnp.bfloat16)
+    part = ROWS // GRID
+    rows = jnp.zeros(refs[-1].shape, jnp.float32)
+    for step, ref in enumerate(refs[:-1]):
+        rows += contract(sel[step * part : (step + 1) * part], ref[...], ((0,), (0,)))
+    refs[-1][...] = rows.astype(jnp.bfloat16)
 
 
 def in_hbm(value):
@@ -227,10 +238,15 @@
     by = (x - steps[:, 0]) % GRID * GRID + (z - steps[:, 1]) % GRID
     want_to = jnp.sum(jnp.where(to[:, None] == numbers[None, :], want[:, None, :], 0.0), axis=2)
     want_h = jnp.broadcast_to(want.T[:, :, None], (GROUPS, 2, CAP)).reshape(2 * ROWS, 1)
-    want = jnp.broadcast_to(want[0, :, None], (GROUPS, CAP)).reshape(ROWS, 1)
+    outer, inner = numbers // GRID, numbers % GRID
+    home = (x + outer) % GRID * GRID + (z + inner) % GRID
+    owner = (x - inner) % GRID * GRID + (z - outer) % GRID
+    want = jnp.sum(jnp.where(owner[:, None] == numbers[None, :], want[:1], 0.0), axis=1)
+    want = jnp.broadcast_to(want[:, None], (GROUPS, CAP)).reshape(ROWS, 1)
     want_to = jnp.broadcast_to(want_to[:, :, None], (2, HALF, CAP)).reshape(2, ROWS // 2, 1)
     place = jnp.arange(CAP, dtype=jnp.int32)[None, :]
-    order = (by[:, None] * CAP + place).reshape(ROWS, 1)
+    home_to = (home[:, None] * CAP + place).reshape(ROWS, 1)
+    home_from = (by[:, None] * CAP + place).reshape(1, ROWS)
     order_h = jnp.stack([by[:, None] * 2 * CAP + place, by[:, None] * 2 * CAP + CAP + place])
     order_h = order_h.reshape(2, ROWS, 1)
     source = jnp.sum(
@@ -247,7 +263,7 @@
             out_specs=[whole((tokens, width + LANES))] * RUN,
         ),
         out_shape=[jax.ShapeDtypeStruct((tokens, width + LANES), jnp.bfloat16)] * RUN,
-        compiler_params=params(16),
+        compiler_params=params(8),
         name="pack",
     )(y.reshape(1), out_grad, jnp.concatenate([routes, gate_probs], axis=1))
     packed = [packed[0]] + [lax.ppermute(packed[s], "ep", along_y(s)) for s in range(1, RUN)]
@@ -259,7 +275,7 @@
     sent_h = pl.pallas_call(
         send_h_kernel,
         out_shape=jax.ShapeDtypeStruct((2 * ROWS, hidden), jnp.bfloat16),
-        compiler_params=params(16),
+        compiler_params=params(8),
         name="send_h",
     )(own_row, own_col, want_h, acts)
     got_h = lax.all_to_all(sent_h, "ep", 0, 0, axis_index_groups=SAME_Y, tiled=True)
@@ -278,7 +294,7 @@
             out_specs=[pl.BlockSpec((CAP, width), lambda k, s, y: (0, RUN * k + s))] * HALF,
         ),
         out_shape=[pltpu.HBM((CAP, 2 * RUN * width), jnp.bfloat16)] * HALF,
-        compiler_params=params(24),
+        compiler_params=params(12),
         name="send_c",
     )(y.reshape(1), want_to, packed)
     send_c = list(send_c)
@@ -286,7 +302,7 @@
     got_h = pl.pallas_call(
         order_kernel,
         out_shape=jax.ShapeDtypeStruct((ROWS, 2 * hidden), jnp.bfloat16),
-        compiler_params=params(16),
+        compiler_params=params(8),
         name="order_h",
     )(order_h, got_h)
     all_h = lax.all_gather(got_h, "ep", axis_index_groups=SAME_RUN, axis=0, tiled=False)
@@ -296,35 +312,56 @@
         own_c.append(
             pl.pallas_call(
                 join_kernel,
-                out_shape=pltpu.HBM((ROWS // 4, 2 * RUN * width), jnp.bfloat16),
-                compiler_params=params(16),
+                out_shape=jax.ShapeDtypeStruct((ROWS // 4, 2 * RUN * width), jnp.bfloat16),
+                compiler_params=params(8),
                 name="join",
             )(*got_c[at : at + HALF // 2])
         )
         mate_c.append(lax.ppermute(own_c[-1], "dp", OTHER_CORE))
-    parts = [in_hbm(part) for part in own_c + mate_c]
 
     weight = weights[0]
-    partial_back = pl.pallas_call(
-        back_kernel,
-        grid=(RUN,),
-        in_specs=[pl.BlockSpec((ROWS // 4, width), lambda s: (0, s))] * 4
-        + [whole((hidden, width))],
-        out_specs=pl.BlockSpec((1, ROWS, hidden), lambda s: (s, 0, 0)),
-        scratch_shapes=[pltpu.VMEM((ROWS, width), jnp.bfloat16)],
-        out_shape=jax.ShapeDtypeStruct((RUN, ROWS, hidden), jnp.float32),
-        compiler_params=params(24),
-        name="back",
-    )(*parts, in_hbm(weight))
+    partial_back, laid = [], []
+    for at, pair in enumerate((own_c, mate_c)):
+        partial_back, rows = pl.pallas_call(
+            back_kernel,
+            grid=(RUN,),
+            in_specs=[pl.BlockSpec((ROWS // 4, width), lambda s: (0, s))] * 2
+            + [pl.BlockSpec((ROWS // 4, width), lambda s: (0, RUN + s))] * 2
+            + [whole((hidden, width))]
+            + [pl.BlockSpec(memory_space=pl.ANY)] * at,
+            out_specs=[
+                pl.BlockSpec((1, ROWS // 2, hidden), lambda s, at=at: (s, at, 0)),
+                whole((2, RUN, ROWS // 2, width)) if at else pl.BlockSpec(memory_space=pltpu.VMEM),
+            ],
+            out_shape=[
+                pltpu.HBM((RUN, ROWS, hidden), jnp.float32),
+                (pltpu.VMEM, pltpu.HBM)[at]((2, RUN, ROWS // 2, width), jnp.bfloat16),
+            ],
+            input_output_aliases={5: 0} if at else {},
+            compiler_params=params(24),
+            name="back",
+        )(*pair, *pair, in_hbm(weight), *([partial_back] if at else []))
+        laid.append(rows)
     summed = lax.psum_scatter(
         partial_back, "ep", scatter_dimension=0, axis_index_groups=SAME_RUN, tiled=False
     )
+    part = jax.ShapeDtypeStruct((ROWS // GRID, hidden), jnp.bfloat16)
     back = pl.pallas_call(
-        unorder_kernel,
-        out_shape=jax.ShapeDtypeStruct((ROWS, hidden), jnp.bfloat16),
-        compiler_params=params(16),
-        name="unorder",
-    )(order, summed)
+        return_kernel, out_shape=[part] * GRID, compiler_params=params(8), name="return"
+    )(home_to, home_from, summed)
+    back = [back[0]] + [lax.ppermute(back[k], "ep", along_grid(k, 0)) for k in range(1, GRID)]
+    back = pl.pallas_call(
+        turn_kernel, out_shape=[part] * GRID, compiler_params=params(8), name="turn"
+    )(*back)
+    back = [back[0]] + [lax.ppermute(back[k], "ep", along_grid(0, k)) for k in range(1, GRID)]
+    hidden_out = pl.pallas_call(
+        take_kernel,
+        out_shape=jax.ShapeDtypeStruct((count, hidden), jnp.bfloat16),
+        compiler_params=params(8),
+        name="take",
+    )(own_row, own_col, want, *back)
+    hidden_out = hidden_out.reshape(top, tokens, hidden).transpose(1, 0, 2)
+
     block = 128
     grid = hidden // block
     update = pl.pallas_call(
@@ -334,39 +371,26 @@
             pl.BlockSpec((RUN, ROWS, block), lambda i: (0, 0, i)),
             pl.BlockSpec((RUN, ROWS, block), lambda i: (0, 0, grid + i)),
         ]
-        + [whole((ROWS // 4, 2 * RUN * width))] * 4
+        + [pl.BlockSpec(memory_space=pltpu.VMEM), whole((2, RUN, ROWS // 2, width))]
         + [pl.BlockSpec((block, width), lambda i: (i, 0))] * 3,
         out_specs=pl.BlockSpec((block, width), lambda i: (i, 0)),
-        scratch_shapes=[pltpu.VMEM((2 * RUN, ROWS, width), jnp.bfloat16)],
         out_shape=jax.ShapeDtypeStruct((hidden, width), jnp.float32),
-        compiler_params=params(28),
+        compiler_params=params(24),
         name="update",
     )(
         in_hbm(all_h),
         in_hbm(all_h),
-        *parts,
+        laid[0],
+        in_hbm(laid[1]),
         in_hbm(weight),
         in_hbm(first_moment[0]),
         in_hbm(second_moment[0]),
     )
 
-    part = hidden // GROUPS
-    spread = update.astype(jnp.float16).reshape(GROUPS, part, width)
+    spread = update.astype(jnp.float16).reshape(GROUPS, hidden // GROUPS, width)
     spread = lax.all_to_all(spread, "ep", 0, 0, axis_index_groups=SAME_Y, tiled=True)
-    riders = (back.astype(jnp.float32) * BACK_SCALE).astype(jnp.float16)
-    riders = riders.reshape(GROUPS, part, CAP * hidden // part)
-    placed = jnp.concatenate([spread[source], riders], axis=2)
-    placed = lax.all_to_all(placed, "ep", 0, 0, axis_index_groups=SAME_Y, tiled=True)
-    back = placed[:, :, width:].astype(jnp.float32) * (1.0 / BACK_SCALE)
-    back = back.astype(jnp.bfloat16).reshape(ROWS, hidden)
-    hidden_out = pl.pallas_call(
-        take_kernel,
-        out_shape=jax.ShapeDtypeStruct((count, hidden), jnp.bfloat16),
-        compiler_params=params(16),
-        name="take",
-    )(own_row, own_col, want, back)
-    hidden_out = hidden_out.reshape(top, tokens, hidden).transpose(1, 0, 2)
-    placed = placed[:, :, :width].astype(jnp.float32).reshape(1, hidden, width) * (1.0 / SCALE)
+    placed = lax.all_to_all(spread[source], "ep", 0, 0, axis_index_groups=SAME_Y, tiled=True)
+    placed = placed.reshape(1, hidden, width).astype(jnp.float32) * (1.0 / SCALE)
     return (hidden_out, placed)
 
 

time: 213 us -> 201 us (0.944)
  waiting for transfers between devices: 97.9 us -> 80.8 us
  starting transfers between devices: 53.4 us -> 60.6 us
  local copies, waits for them, and re-layouts: 10 us -> 7.17 us
    all_to_all x1, waiting for transfers between devices: 39.7 us -> 0.01 us  [local(): lax.all_to_all(spread[source], 'ep', 0, 0, axis_index_groups=SAME_Y, tile...]
    ppermute x0 -> x6, waiting for transfers between devices: none -> 22.9 us  [the longest x3 12.4 us: local(): lax.ppermute(back[k], 'ep', along_grid(k, 0))]
    ppermute x0 -> x6, starting transfers between devices: none -> 9.8 us  [the longest x3 5.02 us: local(): lax.ppermute(back[k], 'ep', along_grid(k, 0))]
    pallas_call x1 -> x2, Pallas kernels: 5.32 us -> 10.3 us  [local(): pl.pallas_call(back_kernel, grid=(RUN,), in_specs=[pl.BlockSpec((ROWS //...]
    ppermute x2, waiting for transfers between devices: 3.33 us -> 0.01 us  [local(): mate_c.append(lax.ppermute(own_c[-1], 'dp', OTHER_CORE))]
    unnamed x18 -> x20, local copies, waits for them, and re-layouts: 4.21 us -> 1.23 us
    ppermute x8, waiting for transfers between devices: 13.4 us -> 15.8 us  [local(): lax.ppermute(send_c[i], ('ep', 'dp'), nearest(i))]
    pallas_call x3 -> x4, Pallas kernels: 3 us -> 0.72 us  [the longest x1 0.5 us: local(): pl.pallas_call(return_kernel, out_shape=[part] * GRID, compiler_params=pa...]
  transfers between devices with their start and end apart: 18 -> 24, of which waited for: 12 -> 13; matrix products, arithmetic and copies ran while one was open for 2% -> 4% of each run, Pallas kernels for 11% -> 13%
where the time goes in v6:
time: 201 us; the launch traced here: 200 us
  waiting for transfers between devices  80.8 us (40%)
  starting transfers between devices  60.6 us (30%)
  Pallas kernels  30.6 us (15%)
  between operations  14.4 us (7%)
  local copies, waits for them, and re-layouts  7.17 us (4%)
  other arithmetic  6.01 us (3%)
    all_to_all x1, waiting for transfers between devices, local(): lax.all_to_all(spread, 'ep', 0, 0, axis_index_groups=SAME_Y, tiled=True)  29.7 us
    ppermute x8, waiting for transfers between devices, local(): lax.ppermute(send_c[i], ('ep', 'dp'), nearest(i))  15.8 us
    ppermute x8, starting transfers between devices, local(): lax.ppermute(send_c[i], ('ep', 'dp'), nearest(i))  13.2 us
    ppermute x2, starting transfers between devices, local(): mate_c.append(lax.ppermute(own_c[-1], 'dp', OTHER_CORE))  13.2 us
    ppermute x3, waiting for transfers between devices, local(): lax.ppermute(back[k], 'ep', along_grid(k, 0))  12.4 us
    ppermute x3, waiting for transfers between devices, local(): lax.ppermute(back[k], 'ep', along_grid(0, k))  10.5 us
    pallas_call x2, Pallas kernels, local(): pl.pallas_call(back_kernel, grid=(RUN,), in_specs=[pl.BlockSpec((ROWS //...  10.3 us
    pallas_call x1, Pallas kernels, local(): pl.pallas_call(update_kernel, grid=(grid,), in_specs=[pl.BlockSpec((RUN,...  9.53 us
  transfers between devices with their start and end apart: 24, of which 13 were waited for; matrix products, arithmetic and copies ran while one was open for 4% of the time, Pallas kernels for 13%

profile of v6, /device:TPU:1, one launch (start us, length us, event | category | flops | bytes accessed | tf_op | source)
XLA Modules:
  0.0 199.6 jit_solution(18419367901379528767)
XLA Ops:
  10.2 1.7 send_h.1
  11.9 9.2 %all-to-all-start = ((bf16[16,48,640]{2,1,0:T(8,128)(2,1)}), bf16[16,48,640]{2,1,0:T(8,128)(2,1)S(1)}, u32[]{:S(2)}, u32[]{:S(2)}) async-start(bf16[16,48,640]{2,1,0:T(8,128)(2,1)} %bitcast.12), calls=%async_computation | async-start | bytes 1966080 | tf_op jit(solution)/shard_map/all_to_all | solution.py:281
  21.4 1.4 collective-permute-start
  22.8 2.6 %collective-permute-start.1 = (bf16[128,1024]{1,0:T(8,128)(2,1)S(1)}, bf16[128,1024]{1,0:T(8,128)(2,1)}, u32[]{:S(2)}, u32[]{:S(2)}) collective-permute-start(bf16[128,1024]{1,0:T(8,128)(2,1)S(1)} %get-tuple-element.30), channel_id=1, source_target_pairs={{0,8},{4,12},{8,0},{12,4},{16,24},{20,28},{24,16},{28,20},{32,40},... | collective-permute-start | bytes 786440 | tf_op jit(solution)/shard_map/ppermute | solution.py:269
  27.7 2.0 %collective-permute-done = bf16[128,1024]{1,0:T(8,128)(2,1)S(1)} collective-permute-done((bf16[128,1024]{1,0:T(8,128)(2,1)S(1)}, bf16[128,1024]{1,0:T(8,128)(2,1)S(1)}, u32[]{:S(2)}, u32[]{:S(2)}) %collective-permute-start) | collective-permute-done | bytes 262176 | tf_op jit(solution)/shard_map/ppermute | solution.py:269
  29.7 6.8 %collective-permute-done.1 = bf16[128,1024]{1,0:T(8,128)(2,1)} collective-permute-done((bf16[128,1024]{1,0:T(8,128)(2,1)S(1)}, bf16[128,1024]{1,0:T(8,128)(2,1)}, u32[]{:S(2)}, u32[]{:S(2)}) %collective-permute-start.1) | collective-permute-done | bytes 262176 | tf_op jit(solution)/shard_map/ppermute | solution.py:269
  37.7 5.5 %send_c.1 = (bf16[24,7168]{1,0:T(8,128)(2,1)}, bf16[24,7168]{1,0:T(8,128)(2,1)}, bf16[24,7168]{1,0:T(8,128)(2,1)}, bf16[24,7168]{1,0:T(8,128)(2,1)}, bf16[24,716...) custom-call(s32[1]{0:T(128)} %bitcast.14.y_ref, ...), custom_call_target="tpu_custom_call" | custom-call | tf_op jit(solution)/shard_map/send_c/pallas_call | solution.py:283
  43.2 3.5 %all-to-all-done = bf16[16,48,640]{2,1,0:T(8,128)(2,1)S(1)} async-done(((bf16[16,48,640]{2,1,0:T(8,128)(2,1)}), bf16[16,48,640]{2,1,0:T(8,128)(2,1)S(1)}, u32[]{:S(2)}, u32[]{:S(2)}) %all-to-all-start) | async-done | bytes 983072 | tf_op jit(solution)/shard_map/all_to_all | solution.py:281
  46.7 2.1 %order_h.1 = bf16[384,1280]{1,0:T(8,128)(2,1)} custom-call(s32[2,384,1]{2,1,0:T(8,128)S(1)} %pad_add_fusion.order_ref, bf16[768,640]{1,0:T(8,128)(2,1)S(1)} %bitcast.51), custom_call_target="tpu_custom_call" | custom-call | tf_op jit(solution)/shard_map/order_h/pallas_call | solution.py:302
  49.6 2.3 %collective-permute-start.8 = (bf16[24,7168]{1,0:T(8,128)(2,1)}, bf16[24,7168]{1,0:T(8,128)(2,1)S(1)}, u32[]{:S(2)}, u32[]{:S(2)}) collective-permute-start(bf16[24,7168]{1,0:T(8,128)(2,1)} %get-tuple-element.37), channel_id=1, source_target_pairs={{0,242},{1,33},{2,240},{3,35},{4,246},{5,37},{6,244},{7,39},{8,250... | collective-permute-start | bytes 1032200 | tf_op jit(solution)/shard_map/ppermute | solution.py:309
  51.9 2.7 %collective-permute-start.9 = (bf16[24,7168]{1,0:T(8,128)(2,1)S(1)}, bf16[24,7168]{1,0:T(8,128)(2,1)S(1)}, u32[]{:S(2)}, u32[]{:S(2)}) collective-permute-start(bf16[24,7168]{1,0:T(8,128)(2,1)S(1)} %copy-done.9), channel_id=1, source_target_pairs={{0,50},{1,209},{2,48},{3,211},{4,54},{5,213},{6,52},{7,215},{8,58}... | collective-permute-start | bytes 1032200 | tf_op jit(solution)/shard_map/ppermute | solution.py:309
  54.7 5.0 %collective-permute-done.10.refs_2_ = bf16[24,7168]{1,0:T(8,128)(2,1)S(1)} collective-permute-done((bf16[24,7168]{1,0:T(8,128)(2,1)}, bf16[24,7168]{1,0:T(8,128)(2,1)S(1)}, u32[]{:S(2)}, u32[]{:S(2)}) %collective-permute-start.10) | collective-permute-done | bytes 344096 | tf_op jit(solution)/shard_map/ppermute | solution.py:309
  60.7 2.9 %collective-permute-done.8.refs_0_ = bf16[24,7168]{1,0:T(8,128)(2,1)S(1)} collective-permute-done((bf16[24,7168]{1,0:T(8,128)(2,1)}, bf16[24,7168]{1,0:T(8,128)(2,1)S(1)}, u32[]{:S(2)}, u32[]{:S(2)}) %collective-permute-start.8) | collective-permute-done | bytes 344096 | tf_op jit(solution)/shard_map/ppermute | solution.py:309
  63.5 6.4 %collective-permute-start.3 = (bf16[24,7168]{1,0:T(8,128)(2,1)S(1)}, bf16[24,7168]{1,0:T(8,128)(2,1)S(1)}, u32[]{:S(2)}, u32[]{:S(2)}) collective-permute-start(bf16[24,7168]{1,0:T(8,128)(2,1)S(1)} %copy-done.5), channel_id=1, source_target_pairs={{0,0},{1,129},{2,2},{3,131},{4,4},{5,133},{6,6},{7,135},{8,8},{9,1... | collective-permute-start | bytes 1032200 | tf_op jit(solution)/shard_map/ppermute | solution.py:309
  70.1 13.0 %collective-permute-start.12 = (bf16[96,7168]{1,0:T(8,128)(2,1)S(1)}, bf16[96,7168]{1,0:T(8,128)(2,1)S(1)}, u32[]{:S(2)}, u32[]{:S(2)}) collective-permute-start(bf16[96,7168]{1,0:T(8,128)(2,1)S(1)} %join.3.refs_1_.refs_3_), channel_id=1, source_target_pairs={{0,1},{1,0},{2,3},{3,2},{4,5},{5,4},{6,7},{7,6},{8,9},{9,8},{10,11... | collective-permute-start | bytes 4128776 | tf_op jit(solution)/shard_map/ppermute | solution.py:320
  83.0 4.2 %collective-permute-done.6.refs_3_ = bf16[24,7168]{1,0:T(8,128)(2,1)S(1)} collective-permute-done((bf16[24,7168]{1,0:T(8,128)(2,1)S(1)}, bf16[24,7168]{1,0:T(8,128)(2,1)S(1)}, u32[]{:S(2)}, u32[]{:S(2)}) %collective-permute-start.6) | collective-permute-done | bytes 344096 | tf_op jit(solution)/shard_map/ppermute | solution.py:309
  87.3 3.7 %collective-permute-done.3.refs_0_ = bf16[24,7168]{1,0:T(8,128)(2,1)S(1)} collective-permute-done((bf16[24,7168]{1,0:T(8,128)(2,1)S(1)}, bf16[24,7168]{1,0:T(8,128)(2,1)S(1)}, u32[]{:S(2)}, u32[]{:S(2)}) %collective-permute-start.3) | collective-permute-done | bytes 344096 | tf_op jit(solution)/shard_map/ppermute | solution.py:309
  91.4 4.8 %back.2 = (f32[4,384,640]{2,1,0:T(8,128)}, bf16[2,4,192,896]{3,2,1,0:T(8,128)(2,1)S(1)}) custom-call(bf16[96,7168]{1,0:T(8,128)(2,1)S(1)} %join.2.refs_0_.refs_2_, bf16[96,7168]{1,0:T(8,128)(2,1)S(1)} %join.3.refs_1_.refs_3_, bf16[96,7168]{1,0:T(8,128)(2,1)S(1)} %join.2.refs_0_.refs_2_, bf16[96,7168]{1,0:T(8,128)(2,1)S(1)} %join.3.refs_1_.refs_3_, ...), custom_call_target="tpu_custom_call" | custom-call | tf_op jit(solution)/shard_map/back/pallas_call | solution.py:325
  96.2 5.6 %back.3 = (f32[4,384,640]{2,1,0:T(8,128)}, bf16[2,4,192,896]{3,2,1,0:T(8,128)(2,1)}) custom-call(bf16[96,7168]{1,0:T(8,128)(2,1)S(1)} %collective-permute-done.7.refs_0_.refs_2_, bf16[96,7168]{1,0:T(8,128)(2,1)S(1)} %collective-permute-done.12.refs_1_.refs_3_, ...), custom_call_target="tpu_custom_call", output_to_operand_aliasing={{0}: (5, {})} | custom-call | tf_op jit(solution)/shard_map/back/pallas_call | solution.py:325
  101.8 9.5 %update.1 = f32[640,896]{1,0:T(8,128)S(1)} custom-call(bf16[4,384,1280]{2,1,0:T(8,128)(2,1)} %bitcast.59, bf16[4,384,1280]{2,1,0:T(8,128)(2,1)} %bitcast.60, bf16[2,4,192,896]{3,2,1,0:T(8,128)(2,1)S(1)} %get-tuple-element.52.own_ref, bf16[2,4,192,896]{3,2,1,0:T(8,128)(2,1)} %get-tuple-element.53.mate_ref, bf16[640,896]{1,0:T(8,128)(2,1)} %bitcast.63, ...), custom_call_target="tpu_custom_call" | custom-call | tf_op jit(solution)/shard_map/update/pallas_call | solution.py:367
  112.4 5.9 %all-to-all-start.1 = ((f16[16,40,896]{2,1,0:T(8,128)(2,1)}), f16[16,40,896]{2,1,0:T(8,128)(2,1)S(1)}, u32[]{:S(2)}, u32[]{:S(2)}) async-start(f16[16,40,896]{2,1,0:T(8,128)(2,1)} %bitcast.29), calls=%async_computation.2 | async-start | bytes 2293760 | tf_op jit(solution)/shard_map/all_to_all | solution.py:391
  118.4 29.7 %all-to-all-done.1 = f16[16,40,896]{2,1,0:T(8,128)(2,1)S(1)} async-done(((f16[16,40,896]{2,1,0:T(8,128)(2,1)}), f16[16,40,896]{2,1,0:T(8,128)(2,1)S(1)}, u32[]{:S(2)}, u32[]{:S(2)}) %all-to-all-start.1) | async-done | bytes 1146912 | tf_op jit(solution)/shard_map/all_to_all | solution.py:391
  148.1 2.0 %gather_fusion = f16[16,40,896]{2,1,0:T(8,128)(2,1)} fusion(f16[16,40,896]{2,1,0:T(8,128)(2,1)S(1)} %all-to-all-done.1, s32[1024]{0:T(1024)S(1)} %pad_clamp_fusion), kind=kCustom, calls=%fused_computation | custom fusion | bytes 2293824 | tf_op jit(solution)/shard_map/gather | solution.py:392
  150.1 4.1 %all-to-all-start.2 = ((f16[16,40,896]{2,1,0:T(8,128)(2,1)}), f16[16,40,896]{2,1,0:T(8,128)(2,1)S(1)}, u32[]{:S(2)}, u32[]{:S(2)}) async-start(f16[16,40,896]{2,1,0:T(8,128)(2,1)} %gather_fusion), calls=%async_computation.3 | async-start | bytes 2293760 | tf_op jit(solution)/shard_map/all_to_all | solution.py:392
  156.3 1.4 collective-permute-start.13
  157.8 2.4 %collective-permute-start.14 = (bf16[96,640]{1,0:T(8,128)(2,1)S(1)}, bf16[96,640]{1,0:T(8,128)(2,1)S(1)}, u32[]{:S(2)}, u32[]{:S(2)}) collective-permute-start(bf16[96,640]{1,0:T(8,128)(2,1)S(1)} %get-tuple-element.45), channel_id=1, source_target_pairs={{0,128},{4,132},{8,136},{12,140},{16,144},{20,148},{24,152},{28,15... | collective-permute-start | bytes 368648 | tf_op jit(solution)/shard_map/ppermute | solution.py:352
  161.3 9.7 %collective-permute-done.13.refs_1_ = bf16[96,640]{1,0:T(8,128)(2,1)S(1)} collective-permute-done((bf16[96,640]{1,0:T(8,128)(2,1)S(1)}, bf16[96,640]{1,0:T(8,128)(2,1)S(1)}, u32[]{:S(2)}, u32[]{:S(2)}) %collective-permute-start.13) | collective-permute-done | bytes 122912 | tf_op jit(solution)/shard_map/ppermute | solution.py:352
  171.0 2.5 %collective-permute-done.14.refs_2_ = bf16[96,640]{1,0:T(8,128)(2,1)S(1)} collective-permute-done((bf16[96,640]{1,0:T(8,128)(2,1)S(1)}, bf16[96,640]{1,0:T(8,128)(2,1)S(1)}, u32[]{:S(2)}, u32[]{:S(2)}) %collective-permute-start.14) | collective-permute-done | bytes 122912 | tf_op jit(solution)/shard_map/ppermute | solution.py:352
  173.9 4.7 %collective-permute-start.17 = (bf16[96,640]{1,0:T(8,128)(2,1)S(1)}, bf16[96,640]{1,0:T(8,128)(2,1)S(1)}, u32[]{:S(2)}, u32[]{:S(2)}) collective-permute-start(bf16[96,640]{1,0:T(8,128)(2,1)S(1)} %get-tuple-element.49), channel_id=1, source_target_pairs={{0,32},{4,36},{8,40},{12,44},{16,48},{20,52},{24,56},{28,60},{32,0... | collective-permute-start | bytes 368648 | tf_op jit(solution)/shard_map/ppermute | solution.py:356
  179.0 1.7 collective-permute-done.16.refs_1_
  180.7 8.8 %collective-permute-done.17.refs_2_ = bf16[96,640]{1,0:T(8,128)(2,1)S(1)} collective-permute-done((bf16[96,640]{1,0:T(8,128)(2,1)S(1)}, bf16[96,640]{1,0:T(8,128)(2,1)S(1)}, u32[]{:S(2)}, u32[]{:S(2)}) %collective-permute-start.17) | collective-permute-done | bytes 122912 | tf_op jit(solution)/shard_map/ppermute | solution.py:356
  191.2 1.6 convert_multiply_fusion
  (95 shorter events, 15.9 us)
Async XLA Ops:
  11.9 9.2 %copy-start.4 = (f32[128,2]{0,1:T(2,128)S(1)}, f32[128,2]{0,1:T(2,128)}, u32[]{:S(2)}) copy-start(f32[128,2]{0,1:T(2,128)} %param.13) | copy-start | bytes 3076
  11.9 9.4 %copy-start.1 = (bf16[128,3584]{1,0:T(8,128)(2,1)S(1)}, bf16[128,3584]{1,0:T(8,128)(2,1)}, u32[]{:S(2)}) copy-start(bf16[128,3584]{1,0:T(8,128)(2,1)} %grad_ref.1) | copy-start | bytes 2752516
  11.9 14.6 %copy-start.2 = (s32[1,16,2]{1,2,0:T(2,128)S(1)}, s32[1,16,2]{1,2,0:T(2,128)}, u32[]{:S(2)}) copy-start(s32[1,16,2]{1,2,0:T(2,128)} %constant.144) | copy-start | bytes 388
  11.9 14.6 %copy-start.3 = (s32[1,16,2]{1,2,0:T(2,128)S(1)}, s32[1,16,2]{1,2,0:T(2,128)}, u32[]{:S(2)}) copy-start(s32[1,16,2]{1,2,0:T(2,128)} %constant.145) | copy-start | bytes 388
  11.9 34.8 %all-to-all-start = ((bf16[16,48,640]{2,1,0:T(8,128)(2,1)}), bf16[16,48,640]{2,1,0:T(8,128)(2,1)S(1)}, u32[]{:S(2)}, u32[]{:S(2)}) async-start(bf16[16,48,640]{2,1,0:T(8,128)(2,1)} %bitcast.12), calls=%async_computation | async-start | bytes 1966080 | tf_op jit(solution)/shard_map/all_to_all | solution.py:281
  21.0 80.7 %all-gather.3.cloned.1.call-start = ((), (), s32[]{:S(2)}) async-start(), calls=%async_computation.5 | async-start | bytes 4915200 | tf_op jit(solution)/shard_map/all_gather | solution.py:308
  21.4 8.3 %collective-permute-start = (bf16[128,1024]{1,0:T(8,128)(2,1)S(1)}, bf16[128,1024]{1,0:T(8,128)(2,1)S(1)}, u32[]{:S(2)}, u32[]{:S(2)}) collective-permute-start(bf16[128,1024]{1,0:T(8,128)(2,1)S(1)} %get-tuple-element.29), channel_id=1, source_target_pairs={{0,4},{4,8},{8,12},{12,0},{16,20},{20,24},{24,28},{28,16},{32,36},... | collective-permute-start | bytes 786440 | tf_op jit(solution)/shard_map/ppermute | solution.py:269
  22.8 13.7 %collective-permute-start.1 = (bf16[128,1024]{1,0:T(8,128)(2,1)S(1)}, bf16[128,1024]{1,0:T(8,128)(2,1)}, u32[]{:S(2)}, u32[]{:S(2)}) collective-permute-start(bf16[128,1024]{1,0:T(8,128)(2,1)S(1)} %get-tuple-element.30), channel_id=1, source_target_pairs={{0,8},{4,12},{8,0},{12,4},{16,24},{20,28},{24,16},{28,20},{32,40},... | collective-permute-start | bytes 786440 | tf_op jit(solution)/shard_map/ppermute | solution.py:269
  25.4 11.1 %collective-permute-start.2 = (bf16[128,1024]{1,0:T(8,128)(2,1)S(1)}, bf16[128,1024]{1,0:T(8,128)(2,1)}, u32[]{:S(2)}, u32[]{:S(2)}) collective-permute-start(bf16[128,1024]{1,0:T(8,128)(2,1)S(1)} %get-tuple-element.31), channel_id=1, source_target_pairs={{0,12},{4,0},{8,4},{12,8},{16,28},{20,16},{24,20},{28,24},{32,44},... | collective-permute-start | bytes 786440 | tf_op jit(solution)/shard_map/ppermute | solution.py:269
  46.6 8.0 %copy-start.8 = (bf16[24,7168]{1,0:T(8,128)(2,1)S(1)}, bf16[24,7168]{1,0:T(8,128)(2,1)}, u32[]{:S(2)}) copy-start(bf16[24,7168]{1,0:T(8,128)(2,1)} %get-tuple-element.34) | copy-start | bytes 1032196
  46.6 13.0 %copy-start.7 = (bf16[24,7168]{1,0:T(8,128)(2,1)S(1)}, bf16[24,7168]{1,0:T(8,128)(2,1)}, u32[]{:S(2)}) copy-start(bf16[24,7168]{1,0:T(8,128)(2,1)} %get-tuple-element.35) | copy-start | bytes 1032196
  46.6 14.0 %copy-start.6 = (bf16[24,7168]{1,0:T(8,128)(2,1)S(1)}, bf16[24,7168]{1,0:T(8,128)(2,1)}, u32[]{:S(2)}) copy-start(bf16[24,7168]{1,0:T(8,128)(2,1)} %get-tuple-element.36) | copy-start | bytes 1032196
  46.6 16.9 %copy-start.5 = (bf16[24,7168]{1,0:T(8,128)(2,1)S(1)}, bf16[24,7168]{1,0:T(8,128)(2,1)}, u32[]{:S(2)}) copy-start(bf16[24,7168]{1,0:T(8,128)(2,1)} %get-tuple-element.33) | copy-start | bytes 1032196
  48.8 105.8 %reduce-scatter.2.cloned.1.call-start = ((), (), s32[]{:S(2)}) async-start(), calls=%async_computation.4 | async-start | bytes 4915200 | tf_op jit(solution)/shard_map/reduce_scatter | solution.py:345
  48.9 10.8 %collective-permute-start.10 = (bf16[24,7168]{1,0:T(8,128)(2,1)}, bf16[24,7168]{1,0:T(8,128)(2,1)S(1)}, u32[]{:S(2)}, u32[]{:S(2)}) collective-permute-start(bf16[24,7168]{1,0:T(8,128)(2,1)} %get-tuple-element.39), channel_id=1, source_target_pairs={{0,64},{1,17},{2,66},{3,19},{4,68},{5,21},{6,70},{7,23},{8,72},{9,... | collective-permute-start | bytes 1032200 | tf_op jit(solution)/shard_map/ppermute | solution.py:309
  48.9 11.7 %collective-permute-start.11 = (bf16[24,7168]{1,0:T(8,128)(2,1)}, bf16[24,7168]{1,0:T(8,128)(2,1)S(1)}, u32[]{:S(2)}, u32[]{:S(2)}) collective-permute-start(bf16[24,7168]{1,0:T(8,128)(2,1)} %get-tuple-element.40), channel_id=1, source_target_pairs={{0,80},{1,193},{2,82},{3,195},{4,84},{5,197},{6,86},{7,199},{8,88}... | collective-permute-start | bytes 1032200 | tf_op jit(solution)/shard_map/ppermute | solution.py:309
  49.6 13.9 %collective-permute-start.8 = (bf16[24,7168]{1,0:T(8,128)(2,1)}, bf16[24,7168]{1,0:T(8,128)(2,1)S(1)}, u32[]{:S(2)}, u32[]{:S(2)}) collective-permute-start(bf16[24,7168]{1,0:T(8,128)(2,1)} %get-tuple-element.37), channel_id=1, source_target_pairs={{0,242},{1,33},{2,240},{3,35},{4,246},{5,37},{6,244},{7,39},{8,250... | collective-permute-start | bytes 1032200 | tf_op jit(solution)/shard_map/ppermute | solution.py:309
  51.9 18.0 %collective-permute-start.9 = (bf16[24,7168]{1,0:T(8,128)(2,1)S(1)}, bf16[24,7168]{1,0:T(8,128)(2,1)S(1)}, u32[]{:S(2)}, u32[]{:S(2)}) collective-permute-start(bf16[24,7168]{1,0:T(8,128)(2,1)S(1)} %copy-done.9), channel_id=1, source_target_pairs={{0,50},{1,209},{2,48},{3,211},{4,54},{5,213},{6,52},{7,215},{8,58}... | collective-permute-start | bytes 1032200 | tf_op jit(solution)/shard_map/ppermute | solution.py:309
  54.7 28.4 %collective-permute-start.4 = (bf16[24,7168]{1,0:T(8,128)(2,1)S(1)}, bf16[24,7168]{1,0:T(8,128)(2,1)S(1)}, u32[]{:S(2)}, u32[]{:S(2)}) collective-permute-start(bf16[24,7168]{1,0:T(8,128)(2,1)S(1)} %copy-done.8), channel_id=1, source_target_pairs={{0,160},{1,225},{2,162},{3,227},{4,164},{5,229},{6,166},{7,231},{8... | collective-permute-start | bytes 1032200 | tf_op jit(solution)/shard_map/ppermute | solution.py:309
  59.7 23.4 %collective-permute-start.5 = (bf16[24,7168]{1,0:T(8,128)(2,1)S(1)}, bf16[24,7168]{1,0:T(8,128)(2,1)S(1)}, u32[]{:S(2)}, u32[]{:S(2)}) collective-permute-start(bf16[24,7168]{1,0:T(8,128)(2,1)S(1)} %copy-done.7), channel_id=1, source_target_pairs={{0,96},{1,179},{2,98},{3,177},{4,100},{5,183},{6,102},{7,181},{8,1... | collective-permute-start | bytes 1032200 | tf_op jit(solution)/shard_map/ppermute | solution.py:309
  60.7 26.6 %collective-permute-start.6 = (bf16[24,7168]{1,0:T(8,128)(2,1)S(1)}, bf16[24,7168]{1,0:T(8,128)(2,1)S(1)}, u32[]{:S(2)}, u32[]{:S(2)}) collective-permute-start(bf16[24,7168]{1,0:T(8,128)(2,1)S(1)} %copy-done.6), channel_id=1, source_target_pairs={{0,144},{1,115},{2,146},{3,113},{4,148},{5,119},{6,150},{7,117},{8... | collective-permute-start | bytes 1032200 | tf_op jit(solution)/shard_map/ppermute | solution.py:309
  63.5 27.5 %collective-permute-start.3 = (bf16[24,7168]{1,0:T(8,128)(2,1)S(1)}, bf16[24,7168]{1,0:T(8,128)(2,1)S(1)}, u32[]{:S(2)}, u32[]{:S(2)}) collective-permute-start(bf16[24,7168]{1,0:T(8,128)(2,1)S(1)} %copy-done.5), channel_id=1, source_target_pairs={{0,0},{1,129},{2,2},{3,131},{4,4},{5,133},{6,6},{7,135},{8,8},{9,1... | collective-permute-start | bytes 1032200 | tf_op jit(solution)/shard_map/ppermute | solution.py:309
  70.1 26.1 %collective-permute-start.12 = (bf16[96,7168]{1,0:T(8,128)(2,1)S(1)}, bf16[96,7168]{1,0:T(8,128)(2,1)S(1)}, u32[]{:S(2)}, u32[]{:S(2)}) collective-permute-start(bf16[96,7168]{1,0:T(8,128)(2,1)S(1)} %join.3.refs_1_.refs_3_), channel_id=1, source_target_pairs={{0,1},{1,0},{2,3},{3,2},{4,5},{5,4},{6,7},{7,6},{8,9},{9,8},{10,11... | collective-permute-start | bytes 4128776 | tf_op jit(solution)/shard_map/ppermute | solution.py:320
  91.1 5.0 %collective-permute-start.7 = (bf16[96,7168]{1,0:T(8,128)(2,1)S(1)}, bf16[96,7168]{1,0:T(8,128)(2,1)S(1)}, u32[]{:S(2)}, u32[]{:S(2)}) collective-permute-start(bf16[96,7168]{1,0:T(8,128)(2,1)S(1)} %join.2.refs_0_.refs_2_), channel_id=1, source_target_pairs={{0,1},{1,0},{2,3},{3,2},{4,5},{5,4},{6,7},{7,6},{8,9},{9,8},{10,11... | collective-permute-start | bytes 4128776 | tf_op jit(solution)/shard_map/ppermute | solution.py:320
  112.4 35.7 %all-to-all-start.1 = ((f16[16,40,896]{2,1,0:T(8,128)(2,1)}), f16[16,40,896]{2,1,0:T(8,128)(2,1)S(1)}, u32[]{:S(2)}, u32[]{:S(2)}) async-start(f16[16,40,896]{2,1,0:T(8,128)(2,1)} %bitcast.29), calls=%async_computation.2 | async-start | bytes 2293760 | tf_op jit(solution)/shard_map/all_to_all | solution.py:391
  150.1 41.0 %all-to-all-start.2 = ((f16[16,40,896]{2,1,0:T(8,128)(2,1)}), f16[16,40,896]{2,1,0:T(8,128)(2,1)S(1)}, u32[]{:S(2)}, u32[]{:S(2)}) async-start(f16[16,40,896]{2,1,0:T(8,128)(2,1)} %gather_fusion), calls=%async_computation.3 | async-start | bytes 2293760 | tf_op jit(solution)/shard_map/all_to_all | solution.py:392
  156.3 14.7 %collective-permute-start.13 = (bf16[96,640]{1,0:T(8,128)(2,1)S(1)}, bf16[96,640]{1,0:T(8,128)(2,1)S(1)}, u32[]{:S(2)}, u32[]{:S(2)}) collective-permute-start(bf16[96,640]{1,0:T(8,128)(2,1)S(1)} %get-tuple-element.44), channel_id=1, source_target_pairs={{0,64},{4,68},{8,72},{12,76},{16,80},{20,84},{24,88},{28,92},{32,9... | collective-permute-start | bytes 368648 | tf_op jit(solution)/shard_map/ppermute | solution.py:352
  157.8 15.8 %collective-permute-start.14 = (bf16[96,640]{1,0:T(8,128)(2,1)S(1)}, bf16[96,640]{1,0:T(8,128)(2,1)S(1)}, u32[]{:S(2)}, u32[]{:S(2)}) collective-permute-start(bf16[96,640]{1,0:T(8,128)(2,1)S(1)} %get-tuple-element.45), channel_id=1, source_target_pairs={{0,128},{4,132},{8,136},{12,140},{16,144},{20,148},{24,152},{28,15... | collective-permute-start | bytes 368648 | tf_op jit(solution)/shard_map/ppermute | solution.py:352
  160.2 13.6 %collective-permute-start.15 = (bf16[96,640]{1,0:T(8,128)(2,1)S(1)}, bf16[96,640]{1,0:T(8,128)(2,1)S(1)}, u32[]{:S(2)}, u32[]{:S(2)}) collective-permute-start(bf16[96,640]{1,0:T(8,128)(2,1)S(1)} %get-tuple-element.46), channel_id=1, source_target_pairs={{0,192},{4,196},{8,200},{12,204},{16,208},{20,212},{24,216},{28,22... | collective-permute-start | bytes 368648 | tf_op jit(solution)/shard_map/ppermute | solution.py:352
  173.8 6.9 %collective-permute-start.16 = (bf16[96,640]{1,0:T(8,128)(2,1)S(1)}, bf16[96,640]{1,0:T(8,128)(2,1)S(1)}, u32[]{:S(2)}, u32[]{:S(2)}) collective-permute-start(bf16[96,640]{1,0:T(8,128)(2,1)S(1)} %get-tuple-element.48), channel_id=1, source_target_pairs={{0,16},{4,20},{8,24},{12,28},{16,32},{20,36},{24,40},{28,44},{32,4... | collective-permute-start | bytes 368648 | tf_op jit(solution)/shard_map/ppermute | solution.py:356
  173.9 15.6 %collective-permute-start.17 = (bf16[96,640]{1,0:T(8,128)(2,1)S(1)}, bf16[96,640]{1,0:T(8,128)(2,1)S(1)}, u32[]{:S(2)}, u32[]{:S(2)}) collective-permute-start(bf16[96,640]{1,0:T(8,128)(2,1)S(1)} %get-tuple-element.49), channel_id=1, source_target_pairs={{0,32},{4,36},{8,40},{12,44},{16,48},{20,52},{24,56},{28,60},{32,0... | collective-permute-start | bytes 368648 | tf_op jit(solution)/shard_map/ppermute | solution.py:356
  178.6 10.9 %collective-permute-start.18 = (bf16[96,640]{1,0:T(8,128)(2,1)S(1)}, bf16[96,640]{1,0:T(8,128)(2,1)S(1)}, u32[]{:S(2)}, u32[]{:S(2)}) collective-permute-start(bf16[96,640]{1,0:T(8,128)(2,1)S(1)} %get-tuple-element.50), channel_id=1, source_target_pairs={{0,48},{4,52},{8,56},{12,60},{16,0},{20,4},{24,8},{28,12},{32,16},... | collective-permute-start | bytes 368648 | tf_op jit(solution)/shard_map/ppermute | solution.py:356
  (2 other events, 6.5 us)
Sparse Core Ops, SparseCore 0:
  48.9 47.8 all-gather.2
  101.9 45.9 reduce-scatter.1

commit v7 on v6

--- a/solution.py
+++ b/solution.py
@@ -97,8 +97,11 @@
 
 
 def send_h_kernel(row_ref, col_ref, want_ref, acts_ref, out_ref):
-    sel = jnp.where(choose(row_ref[0], col_ref[0], want_ref[...]), 1.0, 0.0).astype(jnp.bfloat16)
-    out_ref[...] = contract(sel, acts_ref[...], ((1,), (0,))).astype(jnp.bfloat16)
+    width = acts_ref.shape[1]
+    for kind in range(2):
+        sel = choose(row_ref[0], col_ref[0], want_ref[kind])
+        rows = contract(jnp.where(sel, 1.0, 0.0).astype(jnp.bfloat16), acts_ref[...], ((1,), (0,)))
+        out_ref[:, kind * width : (kind + 1) * width] = rows.astype(jnp.bfloat16)
 
 
 def send_c_kernel(y_ref, want_ref, packed_ref, *out_refs):
@@ -126,12 +129,9 @@
 
 
 def order_kernel(order_ref, value_ref, out_ref):
-    width = value_ref.shape[1]
-    lane = lax.broadcasted_iota(jnp.int32, (ROWS, 2 * ROWS), 1)
-    for kind in range(2):
-        turn = jnp.where(lane == order_ref[kind], 1.0, 0.0).astype(jnp.bfloat16)
-        rows = contract(turn, value_ref[...], ((1,), (0,))).astype(jnp.bfloat16)
-        out_ref[:, kind * width : (kind + 1) * width] = rows
+    lane = lax.broadcasted_iota(jnp.int32, (ROWS, ROWS), 1)
+    turn = jnp.where(lane == order_ref[...], 1.0, 0.0).astype(jnp.bfloat16)
+    out_ref[...] = contract(turn, value_ref[...], ((1,), (0,))).astype(jnp.bfloat16)
 
 
 def return_kernel(to_ref, from_ref, value_ref, *out_refs):
@@ -159,7 +159,7 @@
 def back_kernel(*refs):
     w_ref, out_ref, laid_ref = refs[4], refs[-2], refs[-1]
     quarter = refs[0].shape[0]
-    source = pl.program_id(0)
+    source = pl.program_id(0) if laid_ref.shape[1] == RUN else 0
     for kind in range(2):
         for at in range(2):
             rows = refs[2 * kind + at][...]
@@ -168,16 +168,16 @@
 
 
 def update_kernel(
-    h_own_ref, h_extra_ref, own_ref, mate_ref, w_ref, m_ref, v_ref, out_ref
+    h_own_ref, h_extra_ref, own_ref, first_ref, second_ref, w_ref, m_ref, v_ref, out_ref
 ):
     block, width = w_ref.shape
     half = own_ref.shape[2]
     depth = RUN * half
     total = jnp.zeros(w_ref.shape, jnp.float32)
     for kind, h_ref in enumerate((h_own_ref, h_extra_ref)):
-        for at, c_ref in enumerate((own_ref, mate_ref)):
+        for at, part in enumerate((own_ref[kind], (first_ref, second_ref)[kind][0])):
             rows = h_ref[:, at * half : (at + 1) * half].reshape(depth, block)
-            total += contract(rows, c_ref[kind].reshape(depth, width), ((0,), (0,)))
+            total += contract(rows, part.reshape(depth, width), ((0,), (0,)))
     m_new = beta_one * m_ref[...] + (1.0 - beta_one) * total
     v_new = beta_two * v_ref[...] + (1.0 - beta_two) * total * total
     direction = m_new / bias_one / (jnp.sqrt(v_new / bias_two) + epsilon)
@@ -237,7 +237,7 @@
     to = (x + steps[:HALF, 0]) % GRID * GRID + (z + steps[:HALF, 1]) % GRID
     by = (x - steps[:, 0]) % GRID * GRID + (z - steps[:, 1]) % GRID
     want_to = jnp.sum(jnp.where(to[:, None] == numbers[None, :], want[:, None, :], 0.0), axis=2)
-    want_h = jnp.broadcast_to(want.T[:, :, None], (GROUPS, 2, CAP)).reshape(2 * ROWS, 1)
+    want_h = jnp.broadcast_to(want[:, :, None], (2, GROUPS, CAP)).reshape(2, ROWS, 1)
     outer, inner = numbers // GRID, numbers % GRID
     home = (x + outer) % GRID * GRID + (z + inner) % GRID
     owner = (x - inner) % GRID * GRID + (z - outer) % GRID
@@ -247,8 +247,7 @@
     place = jnp.arange(CAP, dtype=jnp.int32)[None, :]
     home_to = (home[:, None] * CAP + place).reshape(ROWS, 1)
     home_from = (by[:, None] * CAP + place).reshape(1, ROWS)
-    order_h = jnp.stack([by[:, None] * 2 * CAP + place, by[:, None] * 2 * CAP + CAP + place])
-    order_h = order_h.reshape(2, ROWS, 1)
+    order_h = (by[:, None] * CAP + place).reshape(ROWS, 1)
     source = jnp.sum(
         jnp.where(new_slot[None, :] == numbers[:, None], old_slot[None, :], 0), axis=1
     )
@@ -274,7 +273,7 @@
     acts = hidden_acts.transpose(1, 0, 2).reshape(count, hidden)
     sent_h = pl.pallas_call(
         send_h_kernel,
-        out_shape=jax.ShapeDtypeStruct((2 * ROWS, hidden), jnp.bfloat16),
+        out_shape=jax.ShapeDtypeStruct((ROWS, 2 * hidden), jnp.bfloat16),
         compiler_params=params(8),
         name="send_h",
     )(own_row, own_col, want_h, acts)
@@ -331,7 +330,9 @@
             + [pl.BlockSpec(memory_space=pl.ANY)] * at,
             out_specs=[
                 pl.BlockSpec((1, ROWS // 2, hidden), lambda s, at=at: (s, at, 0)),
-                whole((2, RUN, ROWS // 2, width)) if at else pl.BlockSpec(memory_space=pltpu.VMEM),
+                pl.BlockSpec((2, 1, ROWS // 2, width), lambda s: (0, s, 0, 0))
+                if at
+                else pl.BlockSpec(memory_space=pltpu.VMEM),
             ],
             out_shape=[
                 pltpu.HBM((RUN, ROWS, hidden), jnp.float32),
@@ -371,7 +372,11 @@
             pl.BlockSpec((RUN, ROWS, block), lambda i: (0, 0, i)),
             pl.BlockSpec((RUN, ROWS, block), lambda i: (0, 0, grid + i)),
         ]
-        + [pl.BlockSpec(memory_space=pltpu.VMEM), whole((2, RUN, ROWS // 2, width))]
+        + [pl.BlockSpec(memory_space=pltpu.VMEM)]
+        + [
+            pl.BlockSpec((1, RUN, ROWS // 2, width), lambda i, k=k: (k, 0, 0, 0))
+            for k in range(2)
+        ]
         + [pl.BlockSpec((block, width), lambda i: (i, 0))] * 3,
         out_specs=pl.BlockSpec((block, width), lambda i: (i, 0)),
         out_shape=jax.ShapeDtypeStruct((hidden, width), jnp.float32),
@@ -381,6 +386,7 @@
         in_hbm(all_h),
         in_hbm(all_h),
         laid[0],
+        in_hbm(laid[1]),
         in_hbm(laid[1]),
         in_hbm(weight),
         in_hbm(first_moment[0]),

time: 201 us -> 200 us (level)
  transfers between devices with their start and end apart: 24 -> 24, of which waited for: 13 -> 13; matrix products, arithmetic and copies ran while one was open for 4% -> 3% of each run, Pallas kernels for 13% -> 13%
where the time goes in v7:
time: 200 us; the launch traced here: 198 us
  waiting for transfers between devices  82.3 us (41%)
  starting transfers between devices  60.1 us (30%)
  Pallas kernels  29.7 us (15%)
  between operations  14.4 us (7%)
  local copies, waits for them, and re-layouts  6.5 us (3%)
  other arithmetic  4.93 us (2%)
    all_to_all x1, waiting for transfers between devices, local(): lax.all_to_all(spread, 'ep', 0, 0, axis_index_groups=SAME_Y, tiled=True)  29.7 us
    ppermute x8, waiting for transfers between devices, local(): lax.ppermute(send_c[i], ('ep', 'dp'), nearest(i))  15.7 us
    ppermute x8, starting transfers between devices, local(): lax.ppermute(send_c[i], ('ep', 'dp'), nearest(i))  14.9 us
    ppermute x3, waiting for transfers between devices, local(): lax.ppermute(back[k], 'ep', along_grid(k, 0))  12.4 us
    ppermute x2, starting transfers between devices, local(): mate_c.append(lax.ppermute(own_c[-1], 'dp', OTHER_CORE))  11.4 us
    ppermute x3, waiting for transfers between devices, local(): lax.ppermute(back[k], 'ep', along_grid(0, k))  10.5 us
    pallas_call x2, Pallas kernels, local(): pl.pallas_call(back_kernel, grid=(RUN,), in_specs=[pl.BlockSpec((ROWS //...  9.98 us
    pallas_call x1, Pallas kernels, local(): pl.pallas_call(update_kernel, grid=(grid,), in_specs=[pl.BlockSpec((RUN,...  9.52 us
  transfers between devices with their start and end apart: 24, of which 13 were waited for; matrix products, arithmetic and copies ran while one was open for 3% of the time, Pallas kernels for 13%

profile of v7, /device:TPU:1, one launch (start us, length us, event | category | flops | bytes accessed | tf_op | source)
XLA Modules:
  0.0 198.0 jit_solution(17480664056520055112)
XLA Ops:
  10.1 1.6 send_h.1
  11.7 9.2 %all-to-all-start = ((bf16[16,24,1280]{2,1,0:T(8,128)(2,1)}), bf16[16,24,1280]{2,1,0:T(8,128)(2,1)S(1)}, u32[]{:S(2)}, u32[]{:S(2)}) async-start(bf16[16,24,1280]{2,1,0:T(8,128)(2,1)} %bitcast.11), calls=%async_computation | async-start | bytes 1966080 | tf_op jit(solution)/shard_map/all_to_all | solution.py:280
  22.6 2.6 %collective-permute-start.1 = (bf16[128,1024]{1,0:T(8,128)(2,1)S(1)}, bf16[128,1024]{1,0:T(8,128)(2,1)S(1)}, u32[]{:S(2)}, u32[]{:S(2)}) collective-permute-start(bf16[128,1024]{1,0:T(8,128)(2,1)S(1)} %get-tuple-element.30), channel_id=1, source_target_pairs={{0,8},{4,12},{8,0},{12,4},{16,24},{20,28},{24,16},{28,20},{32,40},... | collective-permute-start | bytes 786440 | tf_op jit(solution)/shard_map/ppermute | solution.py:268
  26.9 2.6 %collective-permute-done = bf16[128,1024]{1,0:T(8,128)(2,1)S(1)} collective-permute-done((bf16[128,1024]{1,0:T(8,128)(2,1)S(1)}, bf16[128,1024]{1,0:T(8,128)(2,1)S(1)}, u32[]{:S(2)}, u32[]{:S(2)}) %collective-permute-start) | collective-permute-done | bytes 262176 | tf_op jit(solution)/shard_map/ppermute | solution.py:268
  29.5 6.7 %collective-permute-done.1 = bf16[128,1024]{1,0:T(8,128)(2,1)S(1)} collective-permute-done((bf16[128,1024]{1,0:T(8,128)(2,1)S(1)}, bf16[128,1024]{1,0:T(8,128)(2,1)S(1)}, u32[]{:S(2)}, u32[]{:S(2)}) %collective-permute-start.1) | collective-permute-done | bytes 262176 | tf_op jit(solution)/shard_map/ppermute | solution.py:268
  36.4 5.5 %send_c.1 = (bf16[24,7168]{1,0:T(8,128)(2,1)}, bf16[24,7168]{1,0:T(8,128)(2,1)}, bf16[24,7168]{1,0:T(8,128)(2,1)}, bf16[24,7168]{1,0:T(8,128)(2,1)}, bf16[24,716...) custom-call(s32[1]{0:T(128)} %bitcast.13.y_ref, ...), custom_call_target="tpu_custom_call" | custom-call | tf_op jit(solution)/shard_map/send_c/pallas_call | solution.py:282
  41.9 4.6 %all-to-all-done = bf16[16,24,1280]{2,1,0:T(8,128)(2,1)S(1)} async-done(((bf16[16,24,1280]{2,1,0:T(8,128)(2,1)}), bf16[16,24,1280]{2,1,0:T(8,128)(2,1)S(1)}, u32[]{:S(2)}, u32[]{:S(2)}) %all-to-all-start) | async-done | bytes 983072 | tf_op jit(solution)/shard_map/all_to_all | solution.py:280
  46.5 1.7 order_h.1
  49.0 2.3 %collective-permute-start.8 = (bf16[24,7168]{1,0:T(8,128)(2,1)}, bf16[24,7168]{1,0:T(8,128)(2,1)S(1)}, u32[]{:S(2)}, u32[]{:S(2)}) collective-permute-start(bf16[24,7168]{1,0:T(8,128)(2,1)} %get-tuple-element.37), channel_id=1, source_target_pairs={{0,242},{1,33},{2,240},{3,35},{4,246},{5,37},{6,244},{7,39},{8,250... | collective-permute-start | bytes 1032200 | tf_op jit(solution)/shard_map/ppermute | solution.py:308
  51.3 2.7 %collective-permute-start.9 = (bf16[24,7168]{1,0:T(8,128)(2,1)S(1)}, bf16[24,7168]{1,0:T(8,128)(2,1)S(1)}, u32[]{:S(2)}, u32[]{:S(2)}) collective-permute-start(bf16[24,7168]{1,0:T(8,128)(2,1)S(1)} %copy-done.9), channel_id=1, source_target_pairs={{0,50},{1,209},{2,48},{3,211},{4,54},{5,213},{6,52},{7,215},{8,58}... | collective-permute-start | bytes 1032200 | tf_op jit(solution)/shard_map/ppermute | solution.py:308
  54.0 4.4 %collective-permute-done.10.refs_2_ = bf16[24,7168]{1,0:T(8,128)(2,1)S(1)} collective-permute-done((bf16[24,7168]{1,0:T(8,128)(2,1)}, bf16[24,7168]{1,0:T(8,128)(2,1)S(1)}, u32[]{:S(2)}, u32[]{:S(2)}) %collective-permute-start.10) | collective-permute-done | bytes 344096 | tf_op jit(solution)/shard_map/ppermute | solution.py:308
  58.5 2.4 %collective-permute-start.5 = (bf16[24,7168]{1,0:T(8,128)(2,1)S(1)}, bf16[24,7168]{1,0:T(8,128)(2,1)S(1)}, u32[]{:S(2)}, u32[]{:S(2)}) collective-permute-start(bf16[24,7168]{1,0:T(8,128)(2,1)S(1)} %copy-done.7), channel_id=1, source_target_pairs={{0,96},{1,179},{2,98},{3,177},{4,100},{5,183},{6,102},{7,181},{8,1... | collective-permute-start | bytes 1032200 | tf_op jit(solution)/shard_map/ppermute | solution.py:308
  60.9 2.6 %collective-permute-done.8.refs_0_ = bf16[24,7168]{1,0:T(8,128)(2,1)S(1)} collective-permute-done((bf16[24,7168]{1,0:T(8,128)(2,1)}, bf16[24,7168]{1,0:T(8,128)(2,1)S(1)}, u32[]{:S(2)}, u32[]{:S(2)}) %collective-permute-start.8) | collective-permute-done | bytes 344096 | tf_op jit(solution)/shard_map/ppermute | solution.py:308
  63.4 6.7 %collective-permute-start.3 = (bf16[24,7168]{1,0:T(8,128)(2,1)S(1)}, bf16[24,7168]{1,0:T(8,128)(2,1)S(1)}, u32[]{:S(2)}, u32[]{:S(2)}) collective-permute-start(bf16[24,7168]{1,0:T(8,128)(2,1)S(1)} %copy-done.5), channel_id=1, source_target_pairs={{0,0},{1,129},{2,2},{3,131},{4,4},{5,133},{6,6},{7,135},{8,8},{9,1... | collective-permute-start | bytes 1032200 | tf_op jit(solution)/shard_map/ppermute | solution.py:308
  70.3 11.2 %collective-permute-start.12 = (bf16[96,7168]{1,0:T(8,128)(2,1)S(1)}, bf16[96,7168]{1,0:T(8,128)(2,1)S(1)}, u32[]{:S(2)}, u32[]{:S(2)}) collective-permute-start(bf16[96,7168]{1,0:T(8,128)(2,1)S(1)} %join.3.refs_1_.refs_3_), channel_id=1, source_target_pairs={{0,1},{1,0},{2,3},{3,2},{4,5},{5,4},{6,7},{7,6},{8,9},{9,8},{10,11... | collective-permute-start | bytes 4128776 | tf_op jit(solution)/shard_map/ppermute | solution.py:319
  81.5 6.8 %collective-permute-done.6.refs_3_ = bf16[24,7168]{1,0:T(8,128)(2,1)S(1)} collective-permute-done((bf16[24,7168]{1,0:T(8,128)(2,1)S(1)}, bf16[24,7168]{1,0:T(8,128)(2,1)S(1)}, u32[]{:S(2)}, u32[]{:S(2)}) %collective-permute-start.6) | collective-permute-done | bytes 344096 | tf_op jit(solution)/shard_map/ppermute | solution.py:308
  88.3 1.9 collective-permute-done.3.refs_0_
  90.5 4.7 %back.2 = (f32[4,384,640]{2,1,0:T(8,128)}, bf16[2,4,192,896]{3,2,1,0:T(8,128)(2,1)S(1)}) custom-call(bf16[96,7168]{1,0:T(8,128)(2,1)S(1)} %join.2.refs_0_.refs_2_, bf16[96,7168]{1,0:T(8,128)(2,1)S(1)} %join.3.refs_1_.refs_3_, bf16[96,7168]{1,0:T(8,128)(2,1)S(1)} %join.2.refs_0_.refs_2_, bf16[96,7168]{1,0:T(8,128)(2,1)S(1)} %join.3.refs_1_.refs_3_, ...), custom_call_target="tpu_custom_call" | custom-call | tf_op jit(solution)/shard_map/back/pallas_call | solution.py:324
  95.3 5.2 %back.3 = (f32[4,384,640]{2,1,0:T(8,128)}, bf16[2,4,192,896]{3,2,1,0:T(8,128)(2,1)}) custom-call(bf16[96,7168]{1,0:T(8,128)(2,1)S(1)} %collective-permute-done.7.refs_0_.refs_2_, bf16[96,7168]{1,0:T(8,128)(2,1)S(1)} %collective-permute-done.12.refs_1_.refs_3_, ...), custom_call_target="tpu_custom_call", output_to_operand_aliasing={{0}: (5, {})} | custom-call | tf_op jit(solution)/shard_map/back/pallas_call | solution.py:324
  100.6 9.5 %update.1 = f32[640,896]{1,0:T(8,128)S(1)} custom-call(bf16[4,384,1280]{2,1,0:T(8,128)(2,1)} %bitcast.49, bf16[4,384,1280]{2,1,0:T(8,128)(2,1)} %bitcast.50, bf16[2,4,192,896]{3,2,1,0:T(8,128)(2,1)S(1)} %get-tuple-element.52.own_ref, bf16[2,4,192,896]{3,2,1,0:T(8,128)(2,1)} %get-tuple-element.53.first_ref.second_ref, ...), custom_call_target="tpu_custom_call" | custom-call | tf_op jit(solution)/shard_map/update/pallas_call | solution.py:368
  111.3 5.5 %all-to-all-start.1 = ((f16[16,40,896]{2,1,0:T(8,128)(2,1)}), f16[16,40,896]{2,1,0:T(8,128)(2,1)S(1)}, u32[]{:S(2)}, u32[]{:S(2)}) async-start(f16[16,40,896]{2,1,0:T(8,128)(2,1)} %bitcast.26), calls=%async_computation.2 | async-start | bytes 2293760 | tf_op jit(solution)/shard_map/all_to_all | solution.py:397
  116.8 29.7 %all-to-all-done.1 = f16[16,40,896]{2,1,0:T(8,128)(2,1)S(1)} async-done(((f16[16,40,896]{2,1,0:T(8,128)(2,1)}), f16[16,40,896]{2,1,0:T(8,128)(2,1)S(1)}, u32[]{:S(2)}, u32[]{:S(2)}) %all-to-all-start.1) | async-done | bytes 1146912 | tf_op jit(solution)/shard_map/all_to_all | solution.py:397
  146.5 2.0 %gather_fusion = f16[16,40,896]{2,1,0:T(8,128)(2,1)} fusion(f16[16,40,896]{2,1,0:T(8,128)(2,1)S(1)} %all-to-all-done.1, s32[1024]{0:T(1024)S(1)} %pad_clamp_fusion), kind=kCustom, calls=%fused_computation | custom fusion | bytes 2293824 | tf_op jit(solution)/shard_map/gather | solution.py:398
  148.5 4.1 %all-to-all-start.2 = ((f16[16,40,896]{2,1,0:T(8,128)(2,1)}), f16[16,40,896]{2,1,0:T(8,128)(2,1)S(1)}, u32[]{:S(2)}, u32[]{:S(2)}) async-start(f16[16,40,896]{2,1,0:T(8,128)(2,1)} %gather_fusion), calls=%async_computation.3 | async-start | bytes 2293760 | tf_op jit(solution)/shard_map/all_to_all | solution.py:398
  154.6 1.4 collective-permute-start.13
  156.1 2.4 %collective-permute-start.14 = (bf16[96,640]{1,0:T(8,128)(2,1)S(1)}, bf16[96,640]{1,0:T(8,128)(2,1)S(1)}, u32[]{:S(2)}, u32[]{:S(2)}) collective-permute-start(bf16[96,640]{1,0:T(8,128)(2,1)S(1)} %get-tuple-element.45), channel_id=1, source_target_pairs={{0,128},{4,132},{8,136},{12,140},{16,144},{20,148},{24,152},{28,15... | collective-permute-start | bytes 368648 | tf_op jit(solution)/shard_map/ppermute | solution.py:353
  159.7 9.6 %collective-permute-done.13.refs_1_ = bf16[96,640]{1,0:T(8,128)(2,1)S(1)} collective-permute-done((bf16[96,640]{1,0:T(8,128)(2,1)S(1)}, bf16[96,640]{1,0:T(8,128)(2,1)S(1)}, u32[]{:S(2)}, u32[]{:S(2)}) %collective-permute-start.13) | collective-permute-done | bytes 122912 | tf_op jit(solution)/shard_map/ppermute | solution.py:353
  169.3 2.6 %collective-permute-done.14.refs_2_ = bf16[96,640]{1,0:T(8,128)(2,1)S(1)} collective-permute-done((bf16[96,640]{1,0:T(8,128)(2,1)S(1)}, bf16[96,640]{1,0:T(8,128)(2,1)S(1)}, u32[]{:S(2)}, u32[]{:S(2)}) %collective-permute-start.14) | collective-permute-done | bytes 122912 | tf_op jit(solution)/shard_map/ppermute | solution.py:353
  172.2 4.7 %collective-permute-start.17 = (bf16[96,640]{1,0:T(8,128)(2,1)S(1)}, bf16[96,640]{1,0:T(8,128)(2,1)S(1)}, u32[]{:S(2)}, u32[]{:S(2)}) collective-permute-start(bf16[96,640]{1,0:T(8,128)(2,1)S(1)} %get-tuple-element.49), channel_id=1, source_target_pairs={{0,32},{4,36},{8,40},{12,44},{16,48},{20,52},{24,56},{28,60},{32,0... | collective-permute-start | bytes 368648 | tf_op jit(solution)/shard_map/ppermute | solution.py:357
  177.4 1.7 collective-permute-done.16.refs_1_
  179.1 8.8 %collective-permute-done.17.refs_2_ = bf16[96,640]{1,0:T(8,128)(2,1)S(1)} collective-permute-done((bf16[96,640]{1,0:T(8,128)(2,1)S(1)}, bf16[96,640]{1,0:T(8,128)(2,1)S(1)}, u32[]{:S(2)}, u32[]{:S(2)}) %collective-permute-start.17) | collective-permute-done | bytes 122912 | tf_op jit(solution)/shard_map/ppermute | solution.py:357
  189.6 1.6 convert_multiply_fusion
  (84 shorter events, 14.5 us)
Async XLA Ops:
  11.7 9.2 %copy-start.4 = (f32[128,2]{0,1:T(2,128)S(1)}, f32[128,2]{0,1:T(2,128)}, u32[]{:S(2)}) copy-start(f32[128,2]{0,1:T(2,128)} %param.13) | copy-start | bytes 3076
  11.7 9.4 %copy-start.1 = (bf16[128,3584]{1,0:T(8,128)(2,1)S(1)}, bf16[128,3584]{1,0:T(8,128)(2,1)}, u32[]{:S(2)}) copy-start(bf16[128,3584]{1,0:T(8,128)(2,1)} %grad_ref.1) | copy-start | bytes 2752516
  11.7 14.6 %copy-start.2 = (s32[1,16,2]{1,2,0:T(2,128)S(1)}, s32[1,16,2]{1,2,0:T(2,128)}, u32[]{:S(2)}) copy-start(s32[1,16,2]{1,2,0:T(2,128)} %constant.141) | copy-start | bytes 388
  11.7 14.6 %copy-start.3 = (s32[1,16,2]{1,2,0:T(2,128)S(1)}, s32[1,16,2]{1,2,0:T(2,128)}, u32[]{:S(2)}) copy-start(s32[1,16,2]{1,2,0:T(2,128)} %constant.142) | copy-start | bytes 388
  11.7 34.8 %all-to-all-start = ((bf16[16,24,1280]{2,1,0:T(8,128)(2,1)}), bf16[16,24,1280]{2,1,0:T(8,128)(2,1)S(1)}, u32[]{:S(2)}, u32[]{:S(2)}) async-start(bf16[16,24,1280]{2,1,0:T(8,128)(2,1)} %bitcast.11), calls=%async_computation | async-start | bytes 1966080 | tf_op jit(solution)/shard_map/all_to_all | solution.py:280
  20.9 79.7 %all-gather.3.cloned.1.call-start = ((), (), s32[]{:S(2)}) async-start(), calls=%async_computation.5 | async-start | bytes 4915200 | tf_op jit(solution)/shard_map/all_gather | solution.py:307
  21.2 8.3 %collective-permute-start = (bf16[128,1024]{1,0:T(8,128)(2,1)S(1)}, bf16[128,1024]{1,0:T(8,128)(2,1)S(1)}, u32[]{:S(2)}, u32[]{:S(2)}) collective-permute-start(bf16[128,1024]{1,0:T(8,128)(2,1)S(1)} %get-tuple-element.29), channel_id=1, source_target_pairs={{0,4},{4,8},{8,12},{12,0},{16,20},{20,24},{24,28},{28,16},{32,36},... | collective-permute-start | bytes 786440 | tf_op jit(solution)/shard_map/ppermute | solution.py:268
  22.6 13.6 %collective-permute-start.1 = (bf16[128,1024]{1,0:T(8,128)(2,1)S(1)}, bf16[128,1024]{1,0:T(8,128)(2,1)S(1)}, u32[]{:S(2)}, u32[]{:S(2)}) collective-permute-start(bf16[128,1024]{1,0:T(8,128)(2,1)S(1)} %get-tuple-element.30), channel_id=1, source_target_pairs={{0,8},{4,12},{8,0},{12,4},{16,24},{20,28},{24,16},{28,20},{32,40},... | collective-permute-start | bytes 786440 | tf_op jit(solution)/shard_map/ppermute | solution.py:268
  25.2 11.0 %collective-permute-start.2 = (bf16[128,1024]{1,0:T(8,128)(2,1)S(1)}, bf16[128,1024]{1,0:T(8,128)(2,1)S(1)}, u32[]{:S(2)}, u32[]{:S(2)}) collective-permute-start(bf16[128,1024]{1,0:T(8,128)(2,1)S(1)} %get-tuple-element.31), channel_id=1, source_target_pairs={{0,12},{4,0},{8,4},{12,8},{16,28},{20,16},{24,20},{28,24},{32,44},... | collective-permute-start | bytes 786440 | tf_op jit(solution)/shard_map/ppermute | solution.py:268
  46.4 7.6 %copy-start.8 = (bf16[24,7168]{1,0:T(8,128)(2,1)S(1)}, bf16[24,7168]{1,0:T(8,128)(2,1)}, u32[]{:S(2)}) copy-start(bf16[24,7168]{1,0:T(8,128)(2,1)} %get-tuple-element.34) | copy-start | bytes 1032196
  46.5 12.0 %copy-start.7 = (bf16[24,7168]{1,0:T(8,128)(2,1)S(1)}, bf16[24,7168]{1,0:T(8,128)(2,1)}, u32[]{:S(2)}) copy-start(bf16[24,7168]{1,0:T(8,128)(2,1)} %get-tuple-element.35) | copy-start | bytes 1032196
  46.5 14.4 %copy-start.6 = (bf16[24,7168]{1,0:T(8,128)(2,1)S(1)}, bf16[24,7168]{1,0:T(8,128)(2,1)}, u32[]{:S(2)}) copy-start(bf16[24,7168]{1,0:T(8,128)(2,1)} %get-tuple-element.36) | copy-start | bytes 1032196
  46.5 17.0 %copy-start.5 = (bf16[24,7168]{1,0:T(8,128)(2,1)S(1)}, bf16[24,7168]{1,0:T(8,128)(2,1)}, u32[]{:S(2)}) copy-start(bf16[24,7168]{1,0:T(8,128)(2,1)} %get-tuple-element.33) | copy-start | bytes 1032196
  48.2 104.8 %reduce-scatter.2.cloned.1.call-start = ((), (), s32[]{:S(2)}) async-start(), calls=%async_computation.4 | async-start | bytes 4915200 | tf_op jit(solution)/shard_map/reduce_scatter | solution.py:346
  48.2 10.3 %collective-permute-start.10 = (bf16[24,7168]{1,0:T(8,128)(2,1)}, bf16[24,7168]{1,0:T(8,128)(2,1)S(1)}, u32[]{:S(2)}, u32[]{:S(2)}) collective-permute-start(bf16[24,7168]{1,0:T(8,128)(2,1)} %get-tuple-element.39), channel_id=1, source_target_pairs={{0,64},{1,17},{2,66},{3,19},{4,68},{5,21},{6,70},{7,23},{8,72},{9,... | collective-permute-start | bytes 1032200 | tf_op jit(solution)/shard_map/ppermute | solution.py:308
  48.3 12.6 %collective-permute-start.11 = (bf16[24,7168]{1,0:T(8,128)(2,1)}, bf16[24,7168]{1,0:T(8,128)(2,1)S(1)}, u32[]{:S(2)}, u32[]{:S(2)}) collective-permute-start(bf16[24,7168]{1,0:T(8,128)(2,1)} %get-tuple-element.40), channel_id=1, source_target_pairs={{0,80},{1,193},{2,82},{3,195},{4,84},{5,197},{6,86},{7,199},{8,88}... | collective-permute-start | bytes 1032200 | tf_op jit(solution)/shard_map/ppermute | solution.py:308
  49.0 14.5 %collective-permute-start.8 = (bf16[24,7168]{1,0:T(8,128)(2,1)}, bf16[24,7168]{1,0:T(8,128)(2,1)S(1)}, u32[]{:S(2)}, u32[]{:S(2)}) collective-permute-start(bf16[24,7168]{1,0:T(8,128)(2,1)} %get-tuple-element.37), channel_id=1, source_target_pairs={{0,242},{1,33},{2,240},{3,35},{4,246},{5,37},{6,244},{7,39},{8,250... | collective-permute-start | bytes 1032200 | tf_op jit(solution)/shard_map/ppermute | solution.py:308
  51.3 18.9 %collective-permute-start.9 = (bf16[24,7168]{1,0:T(8,128)(2,1)S(1)}, bf16[24,7168]{1,0:T(8,128)(2,1)S(1)}, u32[]{:S(2)}, u32[]{:S(2)}) collective-permute-start(bf16[24,7168]{1,0:T(8,128)(2,1)S(1)} %copy-done.9), channel_id=1, source_target_pairs={{0,50},{1,209},{2,48},{3,211},{4,54},{5,213},{6,52},{7,215},{8,58}... | collective-permute-start | bytes 1032200 | tf_op jit(solution)/shard_map/ppermute | solution.py:308
  54.0 27.4 %collective-permute-start.4 = (bf16[24,7168]{1,0:T(8,128)(2,1)S(1)}, bf16[24,7168]{1,0:T(8,128)(2,1)S(1)}, u32[]{:S(2)}, u32[]{:S(2)}) collective-permute-start(bf16[24,7168]{1,0:T(8,128)(2,1)S(1)} %copy-done.8), channel_id=1, source_target_pairs={{0,160},{1,225},{2,162},{3,227},{4,164},{5,229},{6,166},{7,231},{8... | collective-permute-start | bytes 1032200 | tf_op jit(solution)/shard_map/ppermute | solution.py:308
  58.5 23.0 %collective-permute-start.5 = (bf16[24,7168]{1,0:T(8,128)(2,1)S(1)}, bf16[24,7168]{1,0:T(8,128)(2,1)S(1)}, u32[]{:S(2)}, u32[]{:S(2)}) collective-permute-start(bf16[24,7168]{1,0:T(8,128)(2,1)S(1)} %copy-done.7), channel_id=1, source_target_pairs={{0,96},{1,179},{2,98},{3,177},{4,100},{5,183},{6,102},{7,181},{8,1... | collective-permute-start | bytes 1032200 | tf_op jit(solution)/shard_map/ppermute | solution.py:308
  60.9 27.4 %collective-permute-start.6 = (bf16[24,7168]{1,0:T(8,128)(2,1)S(1)}, bf16[24,7168]{1,0:T(8,128)(2,1)S(1)}, u32[]{:S(2)}, u32[]{:S(2)}) collective-permute-start(bf16[24,7168]{1,0:T(8,128)(2,1)S(1)} %copy-done.6), channel_id=1, source_target_pairs={{0,144},{1,115},{2,146},{3,113},{4,148},{5,119},{6,150},{7,117},{8... | collective-permute-start | bytes 1032200 | tf_op jit(solution)/shard_map/ppermute | solution.py:308
  63.4 26.7 %collective-permute-start.3 = (bf16[24,7168]{1,0:T(8,128)(2,1)S(1)}, bf16[24,7168]{1,0:T(8,128)(2,1)S(1)}, u32[]{:S(2)}, u32[]{:S(2)}) collective-permute-start(bf16[24,7168]{1,0:T(8,128)(2,1)S(1)} %copy-done.5), channel_id=1, source_target_pairs={{0,0},{1,129},{2,2},{3,131},{4,4},{5,133},{6,6},{7,135},{8,8},{9,1... | collective-permute-start | bytes 1032200 | tf_op jit(solution)/shard_map/ppermute | solution.py:308
  70.3 25.0 %collective-permute-start.12 = (bf16[96,7168]{1,0:T(8,128)(2,1)S(1)}, bf16[96,7168]{1,0:T(8,128)(2,1)S(1)}, u32[]{:S(2)}, u32[]{:S(2)}) collective-permute-start(bf16[96,7168]{1,0:T(8,128)(2,1)S(1)} %join.3.refs_1_.refs_3_), channel_id=1, source_target_pairs={{0,1},{1,0},{2,3},{3,2},{4,5},{5,4},{6,7},{7,6},{8,9},{9,8},{10,11... | collective-permute-start | bytes 4128776 | tf_op jit(solution)/shard_map/ppermute | solution.py:319
  90.3 5.0 %collective-permute-start.7 = (bf16[96,7168]{1,0:T(8,128)(2,1)S(1)}, bf16[96,7168]{1,0:T(8,128)(2,1)S(1)}, u32[]{:S(2)}, u32[]{:S(2)}) collective-permute-start(bf16[96,7168]{1,0:T(8,128)(2,1)S(1)} %join.2.refs_0_.refs_2_), channel_id=1, source_target_pairs={{0,1},{1,0},{2,3},{3,2},{4,5},{5,4},{6,7},{7,6},{8,9},{9,8},{10,11... | collective-permute-start | bytes 4128776 | tf_op jit(solution)/shard_map/ppermute | solution.py:319
  111.3 35.3 %all-to-all-start.1 = ((f16[16,40,896]{2,1,0:T(8,128)(2,1)}), f16[16,40,896]{2,1,0:T(8,128)(2,1)S(1)}, u32[]{:S(2)}, u32[]{:S(2)}) async-start(f16[16,40,896]{2,1,0:T(8,128)(2,1)} %bitcast.26), calls=%async_computation.2 | async-start | bytes 2293760 | tf_op jit(solution)/shard_map/all_to_all | solution.py:397
  148.5 41.0 %all-to-all-start.2 = ((f16[16,40,896]{2,1,0:T(8,128)(2,1)}), f16[16,40,896]{2,1,0:T(8,128)(2,1)S(1)}, u32[]{:S(2)}, u32[]{:S(2)}) async-start(f16[16,40,896]{2,1,0:T(8,128)(2,1)} %gather_fusion), calls=%async_computation.3 | async-start | bytes 2293760 | tf_op jit(solution)/shard_map/all_to_all | solution.py:398
  154.6 14.6 %collective-permute-start.13 = (bf16[96,640]{1,0:T(8,128)(2,1)S(1)}, bf16[96,640]{1,0:T(8,128)(2,1)S(1)}, u32[]{:S(2)}, u32[]{:S(2)}) collective-permute-start(bf16[96,640]{1,0:T(8,128)(2,1)S(1)} %get-tuple-element.44), channel_id=1, source_target_pairs={{0,64},{4,68},{8,72},{12,76},{16,80},{20,84},{24,88},{28,92},{32,9... | collective-permute-start | bytes 368648 | tf_op jit(solution)/shard_map/ppermute | solution.py:353
  156.1 15.8 %collective-permute-start.14 = (bf16[96,640]{1,0:T(8,128)(2,1)S(1)}, bf16[96,640]{1,0:T(8,128)(2,1)S(1)}, u32[]{:S(2)}, u32[]{:S(2)}) collective-permute-start(bf16[96,640]{1,0:T(8,128)(2,1)S(1)} %get-tuple-element.45), channel_id=1, source_target_pairs={{0,128},{4,132},{8,136},{12,140},{16,144},{20,148},{24,152},{28,15... | collective-permute-start | bytes 368648 | tf_op jit(solution)/shard_map/ppermute | solution.py:353
  158.5 13.6 %collective-permute-start.15 = (bf16[96,640]{1,0:T(8,128)(2,1)S(1)}, bf16[96,640]{1,0:T(8,128)(2,1)S(1)}, u32[]{:S(2)}, u32[]{:S(2)}) collective-permute-start(bf16[96,640]{1,0:T(8,128)(2,1)S(1)} %get-tuple-element.46), channel_id=1, source_target_pairs={{0,192},{4,196},{8,200},{12,204},{16,208},{20,212},{24,216},{28,22... | collective-permute-start | bytes 368648 | tf_op jit(solution)/shard_map/ppermute | solution.py:353
  172.1 6.9 %collective-permute-start.16 = (bf16[96,640]{1,0:T(8,128)(2,1)S(1)}, bf16[96,640]{1,0:T(8,128)(2,1)S(1)}, u32[]{:S(2)}, u32[]{:S(2)}) collective-permute-start(bf16[96,640]{1,0:T(8,128)(2,1)S(1)} %get-tuple-element.48), channel_id=1, source_target_pairs={{0,16},{4,20},{8,24},{12,28},{16,32},{20,36},{24,40},{28,44},{32,4... | collective-permute-start | bytes 368648 | tf_op jit(solution)/shard_map/ppermute | solution.py:357
  172.2 15.6 %collective-permute-start.17 = (bf16[96,640]{1,0:T(8,128)(2,1)S(1)}, bf16[96,640]{1,0:T(8,128)(2,1)S(1)}, u32[]{:S(2)}, u32[]{:S(2)}) collective-permute-start(bf16[96,640]{1,0:T(8,128)(2,1)S(1)} %get-tuple-element.49), channel_id=1, source_target_pairs={{0,32},{4,36},{8,40},{12,44},{16,48},{20,52},{24,56},{28,60},{32,0... | collective-permute-start | bytes 368648 | tf_op jit(solution)/shard_map/ppermute | solution.py:357
  177.0 10.9 %collective-permute-start.18 = (bf16[96,640]{1,0:T(8,128)(2,1)S(1)}, bf16[96,640]{1,0:T(8,128)(2,1)S(1)}, u32[]{:S(2)}, u32[]{:S(2)}) collective-permute-start(bf16[96,640]{1,0:T(8,128)(2,1)S(1)} %get-tuple-element.50), channel_id=1, source_target_pairs={{0,48},{4,52},{8,56},{12,60},{16,0},{20,4},{24,8},{28,12},{32,16},... | collective-permute-start | bytes 368648 | tf_op jit(solution)/shard_map/ppermute | solution.py:357
  (2 other events, 6.0 us)
Sparse Core Ops, SparseCore 0:
  48.3 47.8 all-gather.2
  100.7 46.0 reduce-scatter.1

commit v8 on v7

--- a/solution.py
+++ b/solution.py
@@ -159,23 +159,24 @@
 def back_kernel(*refs):
     w_ref, out_ref, laid_ref = refs[4], refs[-2], refs[-1]
     quarter = refs[0].shape[0]
-    source = pl.program_id(0) if laid_ref.shape[1] == RUN else 0
     for kind in range(2):
         for at in range(2):
             rows = refs[2 * kind + at][...]
-            laid_ref[kind, source, at * quarter : (at + 1) * quarter] = rows
-    out_ref[0] = contract(laid_ref[0, source], w_ref[...], ((1,), (1,)))
+            laid_ref[kind, 0, at * quarter : (at + 1) * quarter] = rows
+    out_ref[0] = contract(laid_ref[0, 0], w_ref[...], ((1,), (1,)))
 
 
 def update_kernel(
-    h_own_ref, h_extra_ref, own_ref, first_ref, second_ref, w_ref, m_ref, v_ref, out_ref
+    h_own_ref, h_extra_ref, *refs
 ):
+    c_refs = refs[:4]
+    w_ref, m_ref, v_ref, out_ref = refs[4:]
     block, width = w_ref.shape
-    half = own_ref.shape[2]
+    half = c_refs[0].shape[2]
     depth = RUN * half
     total = jnp.zeros(w_ref.shape, jnp.float32)
     for kind, h_ref in enumerate((h_own_ref, h_extra_ref)):
-        for at, part in enumerate((own_ref[kind], (first_ref, second_ref)[kind][0])):
+        for at, part in enumerate((c_refs[kind][0], c_refs[2 + kind][0])):
             rows = h_ref[:, at * half : (at + 1) * half].reshape(depth, block)
             total += contract(rows, part.reshape(depth, width), ((0,), (0,)))
     m_new = beta_one * m_ref[...] + (1.0 - beta_one) * total
@@ -330,18 +331,16 @@
             + [pl.BlockSpec(memory_space=pl.ANY)] * at,
             out_specs=[
                 pl.BlockSpec((1, ROWS // 2, hidden), lambda s, at=at: (s, at, 0)),
-                pl.BlockSpec((2, 1, ROWS // 2, width), lambda s: (0, s, 0, 0))
-                if at
-                else pl.BlockSpec(memory_space=pltpu.VMEM),
+                pl.BlockSpec((2, 1, ROWS // 2, width), lambda s: (0, s, 0, 0)),
             ],
             out_shape=[
                 pltpu.HBM((RUN, ROWS, hidden), jnp.float32),
-                (pltpu.VMEM, pltpu.HBM)[at]((2, RUN, ROWS // 2, width), jnp.bfloat16),
+                pltpu.HBM((2, RUN, ROWS // 2, width), jnp.bfloat16),
             ],
             input_output_aliases={5: 0} if at else {},
             compiler_params=params(24),
             name="back",
-        )(*pair, *pair, in_hbm(weight), *([partial_back] if at else []))
+        )(*pair, *pair, weight, *([partial_back] if at else []))
         laid.append(rows)
     summed = lax.psum_scatter(
         partial_back, "ep", scatter_dimension=0, axis_index_groups=SAME_RUN, tiled=False
@@ -349,7 +348,7 @@
     part = jax.ShapeDtypeStruct((ROWS // GRID, hidden), jnp.bfloat16)
     back = pl.pallas_call(
         return_kernel, out_shape=[part] * GRID, compiler_params=params(8), name="return"
-    )(home_to, home_from, summed)
+    )(home_to, home_from, in_hbm(summed))
     back = [back[0]] + [lax.ppermute(back[k], "ep", along_grid(k, 0)) for k in range(1, GRID)]
     back = pl.pallas_call(
         turn_kernel, out_shape=[part] * GRID, compiler_params=params(8), name="turn"
@@ -372,10 +371,9 @@
             pl.BlockSpec((RUN, ROWS, block), lambda i: (0, 0, i)),
             pl.BlockSpec((RUN, ROWS, block), lambda i: (0, 0, grid + i)),
         ]
-        + [pl.BlockSpec(memory_space=pltpu.VMEM)]
         + [
             pl.BlockSpec((1, RUN, ROWS // 2, width), lambda i, k=k: (k, 0, 0, 0))
-            for k in range(2)
+            for k in (0, 1, 0, 1)
         ]
         + [pl.BlockSpec((block, width), lambda i: (i, 0))] * 3,
         out_specs=pl.BlockSpec((block, width), lambda i: (i, 0)),
@@ -385,10 +383,8 @@
     )(
         in_hbm(all_h),
         in_hbm(all_h),
-        laid[0],
-        in_hbm(laid[1]),
-        in_hbm(laid[1]),
-        in_hbm(weight),
+        *[in_hbm(rows) for rows in laid for _ in range(2)],
+        weight,
         in_hbm(first_moment[0]),
         in_hbm(second_moment[0]),
     )

time: 200 us -> 198 us (0.990)
  no operation moved by 1% of the time
where the time goes in v8:
time: 198 us; the launch traced here: 197 us
  waiting for transfers between devices  82.3 us (42%)
  starting transfers between devices  60.1 us (30%)
  Pallas kernels  29.6 us (15%)
  between operations  14.4 us (7%)
  local copies, waits for them, and re-layouts  5.31 us (3%)
  other arithmetic  4.93 us (2%)
    all_to_all x1, waiting for transfers between devices, local(): lax.all_to_all(spread, 'ep', 0, 0, axis_index_groups=SAME_Y, tiled=True)  29.7 us
    ppermute x8, waiting for transfers between devices, local(): lax.ppermute(send_c[i], ('ep', 'dp'), nearest(i))  15.7 us
    ppermute x8, starting transfers between devices, local(): lax.ppermute(send_c[i], ('ep', 'dp'), nearest(i))  14.9 us
    ppermute x3, waiting for transfers between devices, local(): lax.ppermute(back[k], 'ep', along_grid(k, 0))  12.4 us
    ppermute x2, starting transfers between devices, local(): mate_c.append(lax.ppermute(own_c[-1], 'dp', OTHER_CORE))  11.4 us
    ppermute x3, waiting for transfers between devices, local(): lax.ppermute(back[k], 'ep', along_grid(0, k))  10.5 us
    pallas_call x1, Pallas kernels, local(): pl.pallas_call(update_kernel, grid=(grid,), in_specs=[pl.BlockSpec((RUN,...  9.99 us
    ppermute x3, waiting for transfers between devices, local(): lax.ppermute(packed[s], 'ep', along_y(s))  9.33 us
  transfers between devices with their start and end apart: 24, of which 13 were waited for; matrix products, arithmetic and copies ran while one was open for 3% of the time, Pallas kernels for 13%

profile of v8, /device:TPU:1, one launch (start us, length us, event | category | flops | bytes accessed | tf_op | source)
XLA Modules:
  0.0 196.6 jit_solution(5724849903345136968)
XLA Ops:
  10.1 1.6 send_h.1
  11.7 9.2 %all-to-all-start = ((bf16[16,24,1280]{2,1,0:T(8,128)(2,1)}), bf16[16,24,1280]{2,1,0:T(8,128)(2,1)S(1)}, u32[]{:S(2)}, u32[]{:S(2)}) async-start(bf16[16,24,1280]{2,1,0:T(8,128)(2,1)} %bitcast.11), calls=%async_computation | async-start | bytes 1966080 | tf_op jit(solution)/shard_map/all_to_all | solution.py:281
  22.6 2.6 %collective-permute-start.1 = (bf16[128,1024]{1,0:T(8,128)(2,1)S(1)}, bf16[128,1024]{1,0:T(8,128)(2,1)S(1)}, u32[]{:S(2)}, u32[]{:S(2)}) collective-permute-start(bf16[128,1024]{1,0:T(8,128)(2,1)S(1)} %get-tuple-element.30), channel_id=1, source_target_pairs={{0,8},{4,12},{8,0},{12,4},{16,24},{20,28},{24,16},{28,20},{32,40},... | collective-permute-start | bytes 786440 | tf_op jit(solution)/shard_map/ppermute | solution.py:269
  26.9 2.6 %collective-permute-done = bf16[128,1024]{1,0:T(8,128)(2,1)S(1)} collective-permute-done((bf16[128,1024]{1,0:T(8,128)(2,1)S(1)}, bf16[128,1024]{1,0:T(8,128)(2,1)S(1)}, u32[]{:S(2)}, u32[]{:S(2)}) %collective-permute-start) | collective-permute-done | bytes 262176 | tf_op jit(solution)/shard_map/ppermute | solution.py:269
  29.5 6.7 %collective-permute-done.1 = bf16[128,1024]{1,0:T(8,128)(2,1)S(1)} collective-permute-done((bf16[128,1024]{1,0:T(8,128)(2,1)S(1)}, bf16[128,1024]{1,0:T(8,128)(2,1)S(1)}, u32[]{:S(2)}, u32[]{:S(2)}) %collective-permute-start.1) | collective-permute-done | bytes 262176 | tf_op jit(solution)/shard_map/ppermute | solution.py:269
  36.4 5.5 %send_c.1 = (bf16[24,7168]{1,0:T(8,128)(2,1)}, bf16[24,7168]{1,0:T(8,128)(2,1)}, bf16[24,7168]{1,0:T(8,128)(2,1)}, bf16[24,7168]{1,0:T(8,128)(2,1)}, bf16[24,716...) custom-call(s32[1]{0:T(128)} %bitcast.13.y_ref, ...), custom_call_target="tpu_custom_call" | custom-call | tf_op jit(solution)/shard_map/send_c/pallas_call | solution.py:283
  41.9 4.6 %all-to-all-done = bf16[16,24,1280]{2,1,0:T(8,128)(2,1)S(1)} async-done(((bf16[16,24,1280]{2,1,0:T(8,128)(2,1)}), bf16[16,24,1280]{2,1,0:T(8,128)(2,1)S(1)}, u32[]{:S(2)}, u32[]{:S(2)}) %all-to-all-start) | async-done | bytes 983072 | tf_op jit(solution)/shard_map/all_to_all | solution.py:281
  46.5 1.7 order_h.1
  49.0 2.3 %collective-permute-start.8 = (bf16[24,7168]{1,0:T(8,128)(2,1)}, bf16[24,7168]{1,0:T(8,128)(2,1)S(1)}, u32[]{:S(2)}, u32[]{:S(2)}) collective-permute-start(bf16[24,7168]{1,0:T(8,128)(2,1)} %get-tuple-element.37), channel_id=1, source_target_pairs={{0,242},{1,33},{2,240},{3,35},{4,246},{5,37},{6,244},{7,39},{8,250... | collective-permute-start | bytes 1032200 | tf_op jit(solution)/shard_map/ppermute | solution.py:309
  51.3 2.7 %collective-permute-start.9 = (bf16[24,7168]{1,0:T(8,128)(2,1)S(1)}, bf16[24,7168]{1,0:T(8,128)(2,1)S(1)}, u32[]{:S(2)}, u32[]{:S(2)}) collective-permute-start(bf16[24,7168]{1,0:T(8,128)(2,1)S(1)} %copy-done.9), channel_id=1, source_target_pairs={{0,50},{1,209},{2,48},{3,211},{4,54},{5,213},{6,52},{7,215},{8,58}... | collective-permute-start | bytes 1032200 | tf_op jit(solution)/shard_map/ppermute | solution.py:309
  54.0 4.4 %collective-permute-done.10.refs_2_ = bf16[24,7168]{1,0:T(8,128)(2,1)S(1)} collective-permute-done((bf16[24,7168]{1,0:T(8,128)(2,1)}, bf16[24,7168]{1,0:T(8,128)(2,1)S(1)}, u32[]{:S(2)}, u32[]{:S(2)}) %collective-permute-start.10) | collective-permute-done | bytes 344096 | tf_op jit(solution)/shard_map/ppermute | solution.py:309
  58.5 2.4 %collective-permute-start.5 = (bf16[24,7168]{1,0:T(8,128)(2,1)S(1)}, bf16[24,7168]{1,0:T(8,128)(2,1)S(1)}, u32[]{:S(2)}, u32[]{:S(2)}) collective-permute-start(bf16[24,7168]{1,0:T(8,128)(2,1)S(1)} %copy-done.7), channel_id=1, source_target_pairs={{0,96},{1,179},{2,98},{3,177},{4,100},{5,183},{6,102},{7,181},{8,1... | collective-permute-start | bytes 1032200 | tf_op jit(solution)/shard_map/ppermute | solution.py:309
  60.9 2.6 %collective-permute-done.8.refs_0_ = bf16[24,7168]{1,0:T(8,128)(2,1)S(1)} collective-permute-done((bf16[24,7168]{1,0:T(8,128)(2,1)}, bf16[24,7168]{1,0:T(8,128)(2,1)S(1)}, u32[]{:S(2)}, u32[]{:S(2)}) %collective-permute-start.8) | collective-permute-done | bytes 344096 | tf_op jit(solution)/shard_map/ppermute | solution.py:309
  63.4 6.7 %collective-permute-start.3 = (bf16[24,7168]{1,0:T(8,128)(2,1)S(1)}, bf16[24,7168]{1,0:T(8,128)(2,1)S(1)}, u32[]{:S(2)}, u32[]{:S(2)}) collective-permute-start(bf16[24,7168]{1,0:T(8,128)(2,1)S(1)} %copy-done.5), channel_id=1, source_target_pairs={{0,0},{1,129},{2,2},{3,131},{4,4},{5,133},{6,6},{7,135},{8,8},{9,1... | collective-permute-start | bytes 1032200 | tf_op jit(solution)/shard_map/ppermute | solution.py:309
  70.3 11.2 %collective-permute-start.12 = (bf16[96,7168]{1,0:T(8,128)(2,1)S(1)}, bf16[96,7168]{1,0:T(8,128)(2,1)S(1)}, u32[]{:S(2)}, u32[]{:S(2)}) collective-permute-start(bf16[96,7168]{1,0:T(8,128)(2,1)S(1)} %join.3.refs_1_.refs_3_), channel_id=1, source_target_pairs={{0,1},{1,0},{2,3},{3,2},{4,5},{5,4},{6,7},{7,6},{8,9},{9,8},{10,11... | collective-permute-start | bytes 4128776 | tf_op jit(solution)/shard_map/ppermute | solution.py:320
  81.5 6.8 %collective-permute-done.6.refs_3_ = bf16[24,7168]{1,0:T(8,128)(2,1)S(1)} collective-permute-done((bf16[24,7168]{1,0:T(8,128)(2,1)S(1)}, bf16[24,7168]{1,0:T(8,128)(2,1)S(1)}, u32[]{:S(2)}, u32[]{:S(2)}) %collective-permute-start.6) | collective-permute-done | bytes 344096 | tf_op jit(solution)/shard_map/ppermute | solution.py:309
  88.3 1.9 collective-permute-done.3.refs_0_
  90.6 4.1 %back.2 = (f32[4,384,640]{2,1,0:T(8,128)}, bf16[2,4,192,896]{3,2,1,0:T(8,128)(2,1)}) custom-call(bf16[96,7168]{1,0:T(8,128)(2,1)S(1)} %join.2.refs_0_.refs_2_, bf16[96,7168]{1,0:T(8,128)(2,1)S(1)} %join.3.refs_1_.refs_3_, bf16[96,7168]{1,0:T(8,128)(2,1)S(1)} %join.2.refs_0_.refs_2_, bf16[96,7168]{1,0:T(8,128)(2,1)S(1)} %join.3.refs_1_.refs_3_, ...), custom_call_target="tpu_custom_call" | custom-call | tf_op jit(solution)/shard_map/back/pallas_call | solution.py:325
  94.6 4.1 %back.3 = (f32[4,384,640]{2,1,0:T(8,128)}, bf16[2,4,192,896]{3,2,1,0:T(8,128)(2,1)}) custom-call(bf16[96,7168]{1,0:T(8,128)(2,1)S(1)} %collective-permute-done.7.refs_0_.refs_2_, bf16[96,7168]{1,0:T(8,128)(2,1)S(1)} %collective-permute-done.12.refs_1_.refs_3_, ...), custom_call_target="tpu_custom_call", output_to_operand_aliasing={{0}: (5, {})} | custom-call | tf_op jit(solution)/shard_map/back/pallas_call | solution.py:325
  98.8 10.0 %update.1 = f32[640,896]{1,0:T(8,128)S(1)} custom-call(bf16[4,384,1280]{2,1,0:T(8,128)(2,1)} %bitcast.51, bf16[4,384,1280]{2,1,0:T(8,128)(2,1)} %bitcast.52, bf16[2,4,192,896]{3,2,1,0:T(8,128)(2,1)} %get-tuple-element.52.refs_0_.refs_1_, bf16[2,4,192,896]{3,2,1,0:T(8,128)(2,1)} %get-tuple-element.52.refs_0_.refs_1_, ...), custom_call_target="tpu_custom_call" | custom-call | tf_op jit(solution)/shard_map/update/pallas_call | solution.py:367
  109.9 5.5 %all-to-all-start.1 = ((f16[16,40,896]{2,1,0:T(8,128)(2,1)}), f16[16,40,896]{2,1,0:T(8,128)(2,1)S(1)}, u32[]{:S(2)}, u32[]{:S(2)}) async-start(f16[16,40,896]{2,1,0:T(8,128)(2,1)} %bitcast.26), calls=%async_computation.2 | async-start | bytes 2293760 | tf_op jit(solution)/shard_map/all_to_all | solution.py:393
  115.5 29.7 %all-to-all-done.1 = f16[16,40,896]{2,1,0:T(8,128)(2,1)S(1)} async-done(((f16[16,40,896]{2,1,0:T(8,128)(2,1)}), f16[16,40,896]{2,1,0:T(8,128)(2,1)S(1)}, u32[]{:S(2)}, u32[]{:S(2)}) %all-to-all-start.1) | async-done | bytes 1146912 | tf_op jit(solution)/shard_map/all_to_all | solution.py:393
  145.2 2.0 %gather_fusion = f16[16,40,896]{2,1,0:T(8,128)(2,1)} fusion(f16[16,40,896]{2,1,0:T(8,128)(2,1)S(1)} %all-to-all-done.1, s32[1024]{0:T(1024)S(1)} %pad_clamp_fusion), kind=kCustom, calls=%fused_computation | custom fusion | bytes 2293824 | tf_op jit(solution)/shard_map/gather | solution.py:394
  147.2 4.1 %all-to-all-start.2 = ((f16[16,40,896]{2,1,0:T(8,128)(2,1)}), f16[16,40,896]{2,1,0:T(8,128)(2,1)S(1)}, u32[]{:S(2)}, u32[]{:S(2)}) async-start(f16[16,40,896]{2,1,0:T(8,128)(2,1)} %gather_fusion), calls=%async_computation.3 | async-start | bytes 2293760 | tf_op jit(solution)/shard_map/all_to_all | solution.py:394
  151.6 1.7 return.1
  154.7 2.4 %collective-permute-start.14 = (bf16[96,640]{1,0:T(8,128)(2,1)S(1)}, bf16[96,640]{1,0:T(8,128)(2,1)S(1)}, u32[]{:S(2)}, u32[]{:S(2)}) collective-permute-start(bf16[96,640]{1,0:T(8,128)(2,1)S(1)} %get-tuple-element.45), channel_id=1, source_target_pairs={{0,128},{4,132},{8,136},{12,140},{16,144},{20,148},{24,152},{28,15... | collective-permute-start | bytes 368648 | tf_op jit(solution)/shard_map/ppermute | solution.py:352
  158.3 9.6 %collective-permute-done.13.refs_1_ = bf16[96,640]{1,0:T(8,128)(2,1)S(1)} collective-permute-done((bf16[96,640]{1,0:T(8,128)(2,1)S(1)}, bf16[96,640]{1,0:T(8,128)(2,1)S(1)}, u32[]{:S(2)}, u32[]{:S(2)}) %collective-permute-start.13) | collective-permute-done | bytes 122912 | tf_op jit(solution)/shard_map/ppermute | solution.py:352
  167.9 2.7 %collective-permute-done.14.refs_2_ = bf16[96,640]{1,0:T(8,128)(2,1)S(1)} collective-permute-done((bf16[96,640]{1,0:T(8,128)(2,1)S(1)}, bf16[96,640]{1,0:T(8,128)(2,1)S(1)}, u32[]{:S(2)}, u32[]{:S(2)}) %collective-permute-start.14) | collective-permute-done | bytes 122912 | tf_op jit(solution)/shard_map/ppermute | solution.py:352
  170.9 4.7 %collective-permute-start.17 = (bf16[96,640]{1,0:T(8,128)(2,1)S(1)}, bf16[96,640]{1,0:T(8,128)(2,1)S(1)}, u32[]{:S(2)}, u32[]{:S(2)}) collective-permute-start(bf16[96,640]{1,0:T(8,128)(2,1)S(1)} %get-tuple-element.49), channel_id=1, source_target_pairs={{0,32},{4,36},{8,40},{12,44},{16,48},{20,52},{24,56},{28,60},{32,0... | collective-permute-start | bytes 368648 | tf_op jit(solution)/shard_map/ppermute | solution.py:356
  176.0 1.7 collective-permute-done.16.refs_1_
  177.7 8.8 %collective-permute-done.17.refs_2_ = bf16[96,640]{1,0:T(8,128)(2,1)S(1)} collective-permute-done((bf16[96,640]{1,0:T(8,128)(2,1)S(1)}, bf16[96,640]{1,0:T(8,128)(2,1)S(1)}, u32[]{:S(2)}, u32[]{:S(2)}) %collective-permute-start.17) | collective-permute-done | bytes 122912 | tf_op jit(solution)/shard_map/ppermute | solution.py:356
  188.2 1.6 convert_multiply_fusion
  (84 shorter events, 14.2 us)
Async XLA Ops:
  11.7 9.2 %copy-start.4 = (f32[128,2]{0,1:T(2,128)S(1)}, f32[128,2]{0,1:T(2,128)}, u32[]{:S(2)}) copy-start(f32[128,2]{0,1:T(2,128)} %param.13) | copy-start | bytes 3076
  11.7 9.4 %copy-start.1 = (bf16[128,3584]{1,0:T(8,128)(2,1)S(1)}, bf16[128,3584]{1,0:T(8,128)(2,1)}, u32[]{:S(2)}) copy-start(bf16[128,3584]{1,0:T(8,128)(2,1)} %grad_ref.1) | copy-start | bytes 2752516
  11.7 14.6 %copy-start.2 = (s32[1,16,2]{1,2,0:T(2,128)S(1)}, s32[1,16,2]{1,2,0:T(2,128)}, u32[]{:S(2)}) copy-start(s32[1,16,2]{1,2,0:T(2,128)} %constant.141) | copy-start | bytes 388
  11.7 14.6 %copy-start.3 = (s32[1,16,2]{1,2,0:T(2,128)S(1)}, s32[1,16,2]{1,2,0:T(2,128)}, u32[]{:S(2)}) copy-start(s32[1,16,2]{1,2,0:T(2,128)} %constant.142) | copy-start | bytes 388
  11.7 34.8 %all-to-all-start = ((bf16[16,24,1280]{2,1,0:T(8,128)(2,1)}), bf16[16,24,1280]{2,1,0:T(8,128)(2,1)S(1)}, u32[]{:S(2)}, u32[]{:S(2)}) async-start(bf16[16,24,1280]{2,1,0:T(8,128)(2,1)} %bitcast.11), calls=%async_computation | async-start | bytes 1966080 | tf_op jit(solution)/shard_map/all_to_all | solution.py:281
  20.9 77.9 %all-gather.3.cloned.1.call-start = ((), (), s32[]{:S(2)}) async-start(), calls=%async_computation.5 | async-start | bytes 4915200 | tf_op jit(solution)/shard_map/all_gather | solution.py:308
  21.2 8.3 %collective-permute-start = (bf16[128,1024]{1,0:T(8,128)(2,1)S(1)}, bf16[128,1024]{1,0:T(8,128)(2,1)S(1)}, u32[]{:S(2)}, u32[]{:S(2)}) collective-permute-start(bf16[128,1024]{1,0:T(8,128)(2,1)S(1)} %get-tuple-element.29), channel_id=1, source_target_pairs={{0,4},{4,8},{8,12},{12,0},{16,20},{20,24},{24,28},{28,16},{32,36},... | collective-permute-start | bytes 786440 | tf_op jit(solution)/shard_map/ppermute | solution.py:269
  22.6 13.6 %collective-permute-start.1 = (bf16[128,1024]{1,0:T(8,128)(2,1)S(1)}, bf16[128,1024]{1,0:T(8,128)(2,1)S(1)}, u32[]{:S(2)}, u32[]{:S(2)}) collective-permute-start(bf16[128,1024]{1,0:T(8,128)(2,1)S(1)} %get-tuple-element.30), channel_id=1, source_target_pairs={{0,8},{4,12},{8,0},{12,4},{16,24},{20,28},{24,16},{28,20},{32,40},... | collective-permute-start | bytes 786440 | tf_op jit(solution)/shard_map/ppermute | solution.py:269
  25.2 11.0 %collective-permute-start.2 = (bf16[128,1024]{1,0:T(8,128)(2,1)S(1)}, bf16[128,1024]{1,0:T(8,128)(2,1)S(1)}, u32[]{:S(2)}, u32[]{:S(2)}) collective-permute-start(bf16[128,1024]{1,0:T(8,128)(2,1)S(1)} %get-tuple-element.31), channel_id=1, source_target_pairs={{0,12},{4,0},{8,4},{12,8},{16,28},{20,16},{24,20},{28,24},{32,44},... | collective-permute-start | bytes 786440 | tf_op jit(solution)/shard_map/ppermute | solution.py:269
  46.5 12.0 %copy-start.7 = (bf16[24,7168]{1,0:T(8,128)(2,1)S(1)}, bf16[24,7168]{1,0:T(8,128)(2,1)}, u32[]{:S(2)}) copy-start(bf16[24,7168]{1,0:T(8,128)(2,1)} %get-tuple-element.35) | copy-start | bytes 1032196
  46.5 14.4 %copy-start.6 = (bf16[24,7168]{1,0:T(8,128)(2,1)S(1)}, bf16[24,7168]{1,0:T(8,128)(2,1)}, u32[]{:S(2)}) copy-start(bf16[24,7168]{1,0:T(8,128)(2,1)} %get-tuple-element.36) | copy-start | bytes 1032196
  46.5 17.0 %copy-start.5 = (bf16[24,7168]{1,0:T(8,128)(2,1)S(1)}, bf16[24,7168]{1,0:T(8,128)(2,1)}, u32[]{:S(2)}) copy-start(bf16[24,7168]{1,0:T(8,128)(2,1)} %get-tuple-element.33) | copy-start | bytes 1032196
  48.2 103.4 %reduce-scatter.2.cloned.1.call-start = ((), (), s32[]{:S(2)}) async-start(), calls=%async_computation.4 | async-start | bytes 4915200 | tf_op jit(solution)/shard_map/reduce_scatter | solution.py:345
  48.2 10.3 %collective-permute-start.10 = (bf16[24,7168]{1,0:T(8,128)(2,1)}, bf16[24,7168]{1,0:T(8,128)(2,1)S(1)}, u32[]{:S(2)}, u32[]{:S(2)}) collective-permute-start(bf16[24,7168]{1,0:T(8,128)(2,1)} %get-tuple-element.39), channel_id=1, source_target_pairs={{0,64},{1,17},{2,66},{3,19},{4,68},{5,21},{6,70},{7,23},{8,72},{9,... | collective-permute-start | bytes 1032200 | tf_op jit(solution)/shard_map/ppermute | solution.py:309
  48.3 12.6 %collective-permute-start.11 = (bf16[24,7168]{1,0:T(8,128)(2,1)}, bf16[24,7168]{1,0:T(8,128)(2,1)S(1)}, u32[]{:S(2)}, u32[]{:S(2)}) collective-permute-start(bf16[24,7168]{1,0:T(8,128)(2,1)} %get-tuple-element.40), channel_id=1, source_target_pairs={{0,80},{1,193},{2,82},{3,195},{4,84},{5,197},{6,86},{7,199},{8,88}... | collective-permute-start | bytes 1032200 | tf_op jit(solution)/shard_map/ppermute | solution.py:309
  49.0 14.5 %collective-permute-start.8 = (bf16[24,7168]{1,0:T(8,128)(2,1)}, bf16[24,7168]{1,0:T(8,128)(2,1)S(1)}, u32[]{:S(2)}, u32[]{:S(2)}) collective-permute-start(bf16[24,7168]{1,0:T(8,128)(2,1)} %get-tuple-element.37), channel_id=1, source_target_pairs={{0,242},{1,33},{2,240},{3,35},{4,246},{5,37},{6,244},{7,39},{8,250... | collective-permute-start | bytes 1032200 | tf_op jit(solution)/shard_map/ppermute | solution.py:309
  51.3 18.9 %collective-permute-start.9 = (bf16[24,7168]{1,0:T(8,128)(2,1)S(1)}, bf16[24,7168]{1,0:T(8,128)(2,1)S(1)}, u32[]{:S(2)}, u32[]{:S(2)}) collective-permute-start(bf16[24,7168]{1,0:T(8,128)(2,1)S(1)} %copy-done.9), channel_id=1, source_target_pairs={{0,50},{1,209},{2,48},{3,211},{4,54},{5,213},{6,52},{7,215},{8,58}... | collective-permute-start | bytes 1032200 | tf_op jit(solution)/shard_map/ppermute | solution.py:309
  54.0 27.5 %collective-permute-start.4 = (bf16[24,7168]{1,0:T(8,128)(2,1)S(1)}, bf16[24,7168]{1,0:T(8,128)(2,1)S(1)}, u32[]{:S(2)}, u32[]{:S(2)}) collective-permute-start(bf16[24,7168]{1,0:T(8,128)(2,1)S(1)} %copy-done.8), channel_id=1, source_target_pairs={{0,160},{1,225},{2,162},{3,227},{4,164},{5,229},{6,166},{7,231},{8... | collective-permute-start | bytes 1032200 | tf_op jit(solution)/shard_map/ppermute | solution.py:309
  58.5 23.0 %collective-permute-start.5 = (bf16[24,7168]{1,0:T(8,128)(2,1)S(1)}, bf16[24,7168]{1,0:T(8,128)(2,1)S(1)}, u32[]{:S(2)}, u32[]{:S(2)}) collective-permute-start(bf16[24,7168]{1,0:T(8,128)(2,1)S(1)} %copy-done.7), channel_id=1, source_target_pairs={{0,96},{1,179},{2,98},{3,177},{4,100},{5,183},{6,102},{7,181},{8,1... | collective-permute-start | bytes 1032200 | tf_op jit(solution)/shard_map/ppermute | solution.py:309
  60.9 27.4 %collective-permute-start.6 = (bf16[24,7168]{1,0:T(8,128)(2,1)S(1)}, bf16[24,7168]{1,0:T(8,128)(2,1)S(1)}, u32[]{:S(2)}, u32[]{:S(2)}) collective-permute-start(bf16[24,7168]{1,0:T(8,128)(2,1)S(1)} %copy-done.6), channel_id=1, source_target_pairs={{0,144},{1,115},{2,146},{3,113},{4,148},{5,119},{6,150},{7,117},{8... | collective-permute-start | bytes 1032200 | tf_op jit(solution)/shard_map/ppermute | solution.py:309
  63.4 26.7 %collective-permute-start.3 = (bf16[24,7168]{1,0:T(8,128)(2,1)S(1)}, bf16[24,7168]{1,0:T(8,128)(2,1)S(1)}, u32[]{:S(2)}, u32[]{:S(2)}) collective-permute-start(bf16[24,7168]{1,0:T(8,128)(2,1)S(1)} %copy-done.5), channel_id=1, source_target_pairs={{0,0},{1,129},{2,2},{3,131},{4,4},{5,133},{6,6},{7,135},{8,8},{9,1... | collective-permute-start | bytes 1032200 | tf_op jit(solution)/shard_map/ppermute | solution.py:309
  70.3 20.3 %copy-start = (bf16[1,640,896]{2,1,0:T(8,128)(2,1)S(1)}, bf16[1,640,896]{2,1,0:T(8,128)(2,1)}, u32[]{:S(2)}) copy-start(bf16[1,640,896]{2,1,0:T(8,128)(2,1)} %param.15) | copy-start | bytes 3440644
  70.3 24.3 %collective-permute-start.12 = (bf16[96,7168]{1,0:T(8,128)(2,1)S(1)}, bf16[96,7168]{1,0:T(8,128)(2,1)S(1)}, u32[]{:S(2)}, u32[]{:S(2)}) collective-permute-start(bf16[96,7168]{1,0:T(8,128)(2,1)S(1)} %join.3.refs_1_.refs_3_), channel_id=1, source_target_pairs={{0,1},{1,0},{2,3},{3,2},{4,5},{5,4},{6,7},{7,6},{8,9},{9,8},{10,11... | collective-permute-start | bytes 4128776 | tf_op jit(solution)/shard_map/ppermute | solution.py:320
  90.3 4.4 %collective-permute-start.7 = (bf16[96,7168]{1,0:T(8,128)(2,1)S(1)}, bf16[96,7168]{1,0:T(8,128)(2,1)S(1)}, u32[]{:S(2)}, u32[]{:S(2)}) collective-permute-start(bf16[96,7168]{1,0:T(8,128)(2,1)S(1)} %join.2.refs_0_.refs_2_), channel_id=1, source_target_pairs={{0,1},{1,0},{2,3},{3,2},{4,5},{5,4},{6,7},{7,6},{8,9},{9,8},{10,11... | collective-permute-start | bytes 4128776 | tf_op jit(solution)/shard_map/ppermute | solution.py:320
  109.9 35.2 %all-to-all-start.1 = ((f16[16,40,896]{2,1,0:T(8,128)(2,1)}), f16[16,40,896]{2,1,0:T(8,128)(2,1)S(1)}, u32[]{:S(2)}, u32[]{:S(2)}) async-start(f16[16,40,896]{2,1,0:T(8,128)(2,1)} %bitcast.26), calls=%async_computation.2 | async-start | bytes 2293760 | tf_op jit(solution)/shard_map/all_to_all | solution.py:393
  147.2 41.1 %all-to-all-start.2 = ((f16[16,40,896]{2,1,0:T(8,128)(2,1)}), f16[16,40,896]{2,1,0:T(8,128)(2,1)S(1)}, u32[]{:S(2)}, u32[]{:S(2)}) async-start(f16[16,40,896]{2,1,0:T(8,128)(2,1)} %gather_fusion), calls=%async_computation.3 | async-start | bytes 2293760 | tf_op jit(solution)/shard_map/all_to_all | solution.py:394
  153.3 14.6 %collective-permute-start.13 = (bf16[96,640]{1,0:T(8,128)(2,1)S(1)}, bf16[96,640]{1,0:T(8,128)(2,1)S(1)}, u32[]{:S(2)}, u32[]{:S(2)}) collective-permute-start(bf16[96,640]{1,0:T(8,128)(2,1)S(1)} %get-tuple-element.44), channel_id=1, source_target_pairs={{0,64},{4,68},{8,72},{12,76},{16,80},{20,84},{24,88},{28,92},{32,9... | collective-permute-start | bytes 368648 | tf_op jit(solution)/shard_map/ppermute | solution.py:352
  154.7 15.8 %collective-permute-start.14 = (bf16[96,640]{1,0:T(8,128)(2,1)S(1)}, bf16[96,640]{1,0:T(8,128)(2,1)S(1)}, u32[]{:S(2)}, u32[]{:S(2)}) collective-permute-start(bf16[96,640]{1,0:T(8,128)(2,1)S(1)} %get-tuple-element.45), channel_id=1, source_target_pairs={{0,128},{4,132},{8,136},{12,140},{16,144},{20,148},{24,152},{28,15... | collective-permute-start | bytes 368648 | tf_op jit(solution)/shard_map/ppermute | solution.py:352
  157.1 13.6 %collective-permute-start.15 = (bf16[96,640]{1,0:T(8,128)(2,1)S(1)}, bf16[96,640]{1,0:T(8,128)(2,1)S(1)}, u32[]{:S(2)}, u32[]{:S(2)}) collective-permute-start(bf16[96,640]{1,0:T(8,128)(2,1)S(1)} %get-tuple-element.46), channel_id=1, source_target_pairs={{0,192},{4,196},{8,200},{12,204},{16,208},{20,212},{24,216},{28,22... | collective-permute-start | bytes 368648 | tf_op jit(solution)/shard_map/ppermute | solution.py:352
  170.8 6.9 %collective-permute-start.16 = (bf16[96,640]{1,0:T(8,128)(2,1)S(1)}, bf16[96,640]{1,0:T(8,128)(2,1)S(1)}, u32[]{:S(2)}, u32[]{:S(2)}) collective-permute-start(bf16[96,640]{1,0:T(8,128)(2,1)S(1)} %get-tuple-element.48), channel_id=1, source_target_pairs={{0,16},{4,20},{8,24},{12,28},{16,32},{20,36},{24,40},{28,44},{32,4... | collective-permute-start | bytes 368648 | tf_op jit(solution)/shard_map/ppermute | solution.py:356
  170.9 15.6 %collective-permute-start.17 = (bf16[96,640]{1,0:T(8,128)(2,1)S(1)}, bf16[96,640]{1,0:T(8,128)(2,1)S(1)}, u32[]{:S(2)}, u32[]{:S(2)}) collective-permute-start(bf16[96,640]{1,0:T(8,128)(2,1)S(1)} %get-tuple-element.49), channel_id=1, source_target_pairs={{0,32},{4,36},{8,40},{12,44},{16,48},{20,52},{24,56},{28,60},{32,0... | collective-permute-start | bytes 368648 | tf_op jit(solution)/shard_map/ppermute | solution.py:356
  175.6 10.9 %collective-permute-start.18 = (bf16[96,640]{1,0:T(8,128)(2,1)S(1)}, bf16[96,640]{1,0:T(8,128)(2,1)S(1)}, u32[]{:S(2)}, u32[]{:S(2)}) collective-permute-start(bf16[96,640]{1,0:T(8,128)(2,1)S(1)} %get-tuple-element.50), channel_id=1, source_target_pairs={{0,48},{4,52},{8,56},{12,60},{16,0},{20,4},{24,8},{28,12},{32,16},... | collective-permute-start | bytes 368648 | tf_op jit(solution)/shard_map/ppermute | solution.py:356
  (2 other events, 12.4 us)
Sparse Core Ops, SparseCore 0:
  48.3 47.8 all-gather.2
  98.9 47.3 reduce-scatter.1

commit v9 on v8

--- a/solution.py
+++ b/solution.py
@@ -159,11 +159,14 @@
 def back_kernel(*refs):
     w_ref, out_ref, laid_ref = refs[4], refs[-2], refs[-1]
     quarter = refs[0].shape[0]
+    sources, half, width = laid_ref.shape[1:]
     for kind in range(2):
         for at in range(2):
-            rows = refs[2 * kind + at][...]
-            laid_ref[kind, 0, at * quarter : (at + 1) * quarter] = rows
-    out_ref[0] = contract(laid_ref[0, 0], w_ref[...], ((1,), (1,)))
+            for source in range(sources):
+                rows = refs[2 * kind + at][:, source * width : (source + 1) * width]
+                laid_ref[kind, source, at * quarter : (at + 1) * quarter] = rows
+    rows = contract(laid_ref[0].reshape(sources * half, width), w_ref[...], ((1,), (1,)))
+    out_ref[...] = rows.reshape(sources, half, rows.shape[1])
 
 
 def update_kernel(
@@ -324,14 +327,14 @@
     for at, pair in enumerate((own_c, mate_c)):
         partial_back, rows = pl.pallas_call(
             back_kernel,
-            grid=(RUN,),
-            in_specs=[pl.BlockSpec((ROWS // 4, width), lambda s: (0, s))] * 2
-            + [pl.BlockSpec((ROWS // 4, width), lambda s: (0, RUN + s))] * 2
+            grid=(2,),
+            in_specs=[pl.BlockSpec((ROWS // 4, 2 * width), lambda s: (0, s))] * 2
+            + [pl.BlockSpec((ROWS // 4, 2 * width), lambda s: (0, 2 + s))] * 2
             + [whole((hidden, width))]
             + [pl.BlockSpec(memory_space=pl.ANY)] * at,
             out_specs=[
-                pl.BlockSpec((1, ROWS // 2, hidden), lambda s, at=at: (s, at, 0)),
-                pl.BlockSpec((2, 1, ROWS // 2, width), lambda s: (0, s, 0, 0)),
+                pl.BlockSpec((2, ROWS // 2, hidden), lambda s, at=at: (s, at, 0)),
+                pl.BlockSpec((2, 2, ROWS // 2, width), lambda s: (0, s, 0, 0)),
             ],
             out_shape=[
                 pltpu.HBM((RUN, ROWS, hidden), jnp.float32),

time: 198 us -> 197 us (level)
  no operation moved by 1% of the time
where the time goes in v9:
time: 197 us; the launch traced here: 195 us
  waiting for transfers between devices  81.7 us (41%)
  starting transfers between devices  60.7 us (31%)
  Pallas kernels  28.4 us (14%)
  between operations  14.4 us (7%)
  local copies, waits for them, and re-layouts  5.31 us (3%)
  other arithmetic  4.93 us (3%)
    all_to_all x1, waiting for transfers between devices, local(): lax.all_to_all(spread, 'ep', 0, 0, axis_index_groups=SAME_Y, tiled=True)  29.1 us
    ppermute x8, waiting for transfers between devices, local(): lax.ppermute(send_c[i], ('ep', 'dp'), nearest(i))  15.7 us
    ppermute x8, starting transfers between devices, local(): lax.ppermute(send_c[i], ('ep', 'dp'), nearest(i))  14.9 us
    ppermute x3, waiting for transfers between devices, local(): lax.ppermute(back[k], 'ep', along_grid(k, 0))  12.4 us
    ppermute x2, starting transfers between devices, local(): mate_c.append(lax.ppermute(own_c[-1], 'dp', OTHER_CORE))  11.4 us
    ppermute x3, waiting for transfers between devices, local(): lax.ppermute(back[k], 'ep', along_grid(0, k))  10.5 us
    pallas_call x1, Pallas kernels, local(): pl.pallas_call(update_kernel, grid=(grid,), in_specs=[pl.BlockSpec((RUN,...  9.99 us
    ppermute x3, waiting for transfers between devices, local(): lax.ppermute(packed[s], 'ep', along_y(s))  9.33 us
  transfers between devices with their start and end apart: 24, of which 13 were waited for; matrix products, arithmetic and copies ran while one was open for 3% of the time, Pallas kernels for 13%

profile of v9, /device:TPU:1, one launch (start us, length us, event | category | flops | bytes accessed | tf_op | source)
XLA Modules:
  0.0 195.4 jit_solution(6941795454364504954)
XLA Ops:
  10.1 1.6 send_h.1
  11.7 9.2 %all-to-all-start = ((bf16[16,24,1280]{2,1,0:T(8,128)(2,1)}), bf16[16,24,1280]{2,1,0:T(8,128)(2,1)S(1)}, u32[]{:S(2)}, u32[]{:S(2)}) async-start(bf16[16,24,1280]{2,1,0:T(8,128)(2,1)} %bitcast.11), calls=%async_computation | async-start | bytes 1966080 | tf_op jit(solution)/shard_map/all_to_all | solution.py:284
  22.6 2.6 %collective-permute-start.1 = (bf16[128,1024]{1,0:T(8,128)(2,1)S(1)}, bf16[128,1024]{1,0:T(8,128)(2,1)S(1)}, u32[]{:S(2)}, u32[]{:S(2)}) collective-permute-start(bf16[128,1024]{1,0:T(8,128)(2,1)S(1)} %get-tuple-element.30), channel_id=1, source_target_pairs={{0,8},{4,12},{8,0},{12,4},{16,24},{20,28},{24,16},{28,20},{32,40},... | collective-permute-start | bytes 786440 | tf_op jit(solution)/shard_map/ppermute | solution.py:272
  26.9 2.6 %collective-permute-done = bf16[128,1024]{1,0:T(8,128)(2,1)S(1)} collective-permute-done((bf16[128,1024]{1,0:T(8,128)(2,1)S(1)}, bf16[128,1024]{1,0:T(8,128)(2,1)S(1)}, u32[]{:S(2)}, u32[]{:S(2)}) %collective-permute-start) | collective-permute-done | bytes 262176 | tf_op jit(solution)/shard_map/ppermute | solution.py:272
  29.5 6.7 %collective-permute-done.1 = bf16[128,1024]{1,0:T(8,128)(2,1)S(1)} collective-permute-done((bf16[128,1024]{1,0:T(8,128)(2,1)S(1)}, bf16[128,1024]{1,0:T(8,128)(2,1)S(1)}, u32[]{:S(2)}, u32[]{:S(2)}) %collective-permute-start.1) | collective-permute-done | bytes 262176 | tf_op jit(solution)/shard_map/ppermute | solution.py:272
  36.4 5.5 %send_c.1 = (bf16[24,7168]{1,0:T(8,128)(2,1)}, bf16[24,7168]{1,0:T(8,128)(2,1)}, bf16[24,7168]{1,0:T(8,128)(2,1)}, bf16[24,7168]{1,0:T(8,128)(2,1)}, bf16[24,716...) custom-call(s32[1]{0:T(128)} %bitcast.13.y_ref, ...), custom_call_target="tpu_custom_call" | custom-call | tf_op jit(solution)/shard_map/send_c/pallas_call | solution.py:286
  41.9 4.6 %all-to-all-done = bf16[16,24,1280]{2,1,0:T(8,128)(2,1)S(1)} async-done(((bf16[16,24,1280]{2,1,0:T(8,128)(2,1)}), bf16[16,24,1280]{2,1,0:T(8,128)(2,1)S(1)}, u32[]{:S(2)}, u32[]{:S(2)}) %all-to-all-start) | async-done | bytes 983072 | tf_op jit(solution)/shard_map/all_to_all | solution.py:284
  46.5 1.7 order_h.1
  49.0 2.3 %collective-permute-start.8 = (bf16[24,7168]{1,0:T(8,128)(2,1)}, bf16[24,7168]{1,0:T(8,128)(2,1)S(1)}, u32[]{:S(2)}, u32[]{:S(2)}) collective-permute-start(bf16[24,7168]{1,0:T(8,128)(2,1)} %get-tuple-element.37), channel_id=1, source_target_pairs={{0,242},{1,33},{2,240},{3,35},{4,246},{5,37},{6,244},{7,39},{8,250... | collective-permute-start | bytes 1032200 | tf_op jit(solution)/shard_map/ppermute | solution.py:312
  51.3 2.7 %collective-permute-start.9 = (bf16[24,7168]{1,0:T(8,128)(2,1)S(1)}, bf16[24,7168]{1,0:T(8,128)(2,1)S(1)}, u32[]{:S(2)}, u32[]{:S(2)}) collective-permute-start(bf16[24,7168]{1,0:T(8,128)(2,1)S(1)} %copy-done.9), channel_id=1, source_target_pairs={{0,50},{1,209},{2,48},{3,211},{4,54},{5,213},{6,52},{7,215},{8,58}... | collective-permute-start | bytes 1032200 | tf_op jit(solution)/shard_map/ppermute | solution.py:312
  54.0 4.4 %collective-permute-done.10.refs_2_ = bf16[24,7168]{1,0:T(8,128)(2,1)S(1)} collective-permute-done((bf16[24,7168]{1,0:T(8,128)(2,1)}, bf16[24,7168]{1,0:T(8,128)(2,1)S(1)}, u32[]{:S(2)}, u32[]{:S(2)}) %collective-permute-start.10) | collective-permute-done | bytes 344096 | tf_op jit(solution)/shard_map/ppermute | solution.py:312
  58.5 2.4 %collective-permute-start.5 = (bf16[24,7168]{1,0:T(8,128)(2,1)S(1)}, bf16[24,7168]{1,0:T(8,128)(2,1)S(1)}, u32[]{:S(2)}, u32[]{:S(2)}) collective-permute-start(bf16[24,7168]{1,0:T(8,128)(2,1)S(1)} %copy-done.7), channel_id=1, source_target_pairs={{0,96},{1,179},{2,98},{3,177},{4,100},{5,183},{6,102},{7,181},{8,1... | collective-permute-start | bytes 1032200 | tf_op jit(solution)/shard_map/ppermute | solution.py:312
  60.9 2.6 %collective-permute-done.8.refs_0_ = bf16[24,7168]{1,0:T(8,128)(2,1)S(1)} collective-permute-done((bf16[24,7168]{1,0:T(8,128)(2,1)}, bf16[24,7168]{1,0:T(8,128)(2,1)S(1)}, u32[]{:S(2)}, u32[]{:S(2)}) %collective-permute-start.8) | collective-permute-done | bytes 344096 | tf_op jit(solution)/shard_map/ppermute | solution.py:312
  63.4 6.7 %collective-permute-start.3 = (bf16[24,7168]{1,0:T(8,128)(2,1)S(1)}, bf16[24,7168]{1,0:T(8,128)(2,1)S(1)}, u32[]{:S(2)}, u32[]{:S(2)}) collective-permute-start(bf16[24,7168]{1,0:T(8,128)(2,1)S(1)} %copy-done.5), channel_id=1, source_target_pairs={{0,0},{1,129},{2,2},{3,131},{4,4},{5,133},{6,6},{7,135},{8,8},{9,1... | collective-permute-start | bytes 1032200 | tf_op jit(solution)/shard_map/ppermute | solution.py:312
  70.3 11.2 %collective-permute-start.12 = (bf16[96,7168]{1,0:T(8,128)(2,1)S(1)}, bf16[96,7168]{1,0:T(8,128)(2,1)S(1)}, u32[]{:S(2)}, u32[]{:S(2)}) collective-permute-start(bf16[96,7168]{1,0:T(8,128)(2,1)S(1)} %join.3.refs_1_.refs_3_), channel_id=1, source_target_pairs={{0,1},{1,0},{2,3},{3,2},{4,5},{5,4},{6,7},{7,6},{8,9},{9,8},{10,11... | collective-permute-start | bytes 4128776 | tf_op jit(solution)/shard_map/ppermute | solution.py:323
  81.5 6.8 %collective-permute-done.6.refs_3_ = bf16[24,7168]{1,0:T(8,128)(2,1)S(1)} collective-permute-done((bf16[24,7168]{1,0:T(8,128)(2,1)S(1)}, bf16[24,7168]{1,0:T(8,128)(2,1)S(1)}, u32[]{:S(2)}, u32[]{:S(2)}) %collective-permute-start.6) | collective-permute-done | bytes 344096 | tf_op jit(solution)/shard_map/ppermute | solution.py:312
  88.3 1.9 collective-permute-done.3.refs_0_
  90.6 3.5 %back.2 = (f32[4,384,640]{2,1,0:T(8,128)}, bf16[2,4,192,896]{3,2,1,0:T(8,128)(2,1)}) custom-call(bf16[96,7168]{1,0:T(8,128)(2,1)S(1)} %join.2.refs_0_.refs_2_, bf16[96,7168]{1,0:T(8,128)(2,1)S(1)} %join.3.refs_1_.refs_3_, bf16[96,7168]{1,0:T(8,128)(2,1)S(1)} %join.2.refs_0_.refs_2_, bf16[96,7168]{1,0:T(8,128)(2,1)S(1)} %join.3.refs_1_.refs_3_, ...), custom_call_target="tpu_custom_call" | custom-call | tf_op jit(solution)/shard_map/back/pallas_call | solution.py:328
  94.0 3.6 %back.3 = (f32[4,384,640]{2,1,0:T(8,128)}, bf16[2,4,192,896]{3,2,1,0:T(8,128)(2,1)}) custom-call(bf16[96,7168]{1,0:T(8,128)(2,1)S(1)} %collective-permute-done.7.refs_0_.refs_2_, bf16[96,7168]{1,0:T(8,128)(2,1)S(1)} %collective-permute-done.12.refs_1_.refs_3_, ...), custom_call_target="tpu_custom_call", output_to_operand_aliasing={{0}: (5, {})} | custom-call | tf_op jit(solution)/shard_map/back/pallas_call | solution.py:328
  97.6 10.0 %update.1 = f32[640,896]{1,0:T(8,128)S(1)} custom-call(bf16[4,384,1280]{2,1,0:T(8,128)(2,1)} %bitcast.51, bf16[4,384,1280]{2,1,0:T(8,128)(2,1)} %bitcast.52, bf16[2,4,192,896]{3,2,1,0:T(8,128)(2,1)} %get-tuple-element.52.refs_0_.refs_1_, bf16[2,4,192,896]{3,2,1,0:T(8,128)(2,1)} %get-tuple-element.52.refs_0_.refs_1_, ...), custom_call_target="tpu_custom_call" | custom-call | tf_op jit(solution)/shard_map/update/pallas_call | solution.py:370
  108.8 5.5 %all-to-all-start.1 = ((f16[16,40,896]{2,1,0:T(8,128)(2,1)}), f16[16,40,896]{2,1,0:T(8,128)(2,1)S(1)}, u32[]{:S(2)}, u32[]{:S(2)}) async-start(f16[16,40,896]{2,1,0:T(8,128)(2,1)} %bitcast.26), calls=%async_computation.2 | async-start | bytes 2293760 | tf_op jit(solution)/shard_map/all_to_all | solution.py:396
  114.3 29.1 %all-to-all-done.1 = f16[16,40,896]{2,1,0:T(8,128)(2,1)S(1)} async-done(((f16[16,40,896]{2,1,0:T(8,128)(2,1)}), f16[16,40,896]{2,1,0:T(8,128)(2,1)S(1)}, u32[]{:S(2)}, u32[]{:S(2)}) %all-to-all-start.1) | async-done | bytes 1146912 | tf_op jit(solution)/shard_map/all_to_all | solution.py:396
  143.4 2.0 %gather_fusion = f16[16,40,896]{2,1,0:T(8,128)(2,1)} fusion(f16[16,40,896]{2,1,0:T(8,128)(2,1)S(1)} %all-to-all-done.1, s32[1024]{0:T(1024)S(1)} %pad_clamp_fusion), kind=kCustom, calls=%fused_computation | custom fusion | bytes 2293824 | tf_op jit(solution)/shard_map/gather | solution.py:397
  145.4 4.6 %all-to-all-start.2 = ((f16[16,40,896]{2,1,0:T(8,128)(2,1)}), f16[16,40,896]{2,1,0:T(8,128)(2,1)S(1)}, u32[]{:S(2)}, u32[]{:S(2)}) async-start(f16[16,40,896]{2,1,0:T(8,128)(2,1)} %gather_fusion), calls=%async_computation.3 | async-start | bytes 2293760 | tf_op jit(solution)/shard_map/all_to_all | solution.py:397
  150.4 1.7 return.1
  153.5 2.4 %collective-permute-start.14 = (bf16[96,640]{1,0:T(8,128)(2,1)S(1)}, bf16[96,640]{1,0:T(8,128)(2,1)S(1)}, u32[]{:S(2)}, u32[]{:S(2)}) collective-permute-start(bf16[96,640]{1,0:T(8,128)(2,1)S(1)} %get-tuple-element.45), channel_id=1, source_target_pairs={{0,128},{4,132},{8,136},{12,140},{16,144},{20,148},{24,152},{28,15... | collective-permute-start | bytes 368648 | tf_op jit(solution)/shard_map/ppermute | solution.py:355
  157.1 9.5 %collective-permute-done.13.refs_1_ = bf16[96,640]{1,0:T(8,128)(2,1)S(1)} collective-permute-done((bf16[96,640]{1,0:T(8,128)(2,1)S(1)}, bf16[96,640]{1,0:T(8,128)(2,1)S(1)}, u32[]{:S(2)}, u32[]{:S(2)}) %collective-permute-start.13) | collective-permute-done | bytes 122912 | tf_op jit(solution)/shard_map/ppermute | solution.py:355
  166.7 2.7 %collective-permute-done.14.refs_2_ = bf16[96,640]{1,0:T(8,128)(2,1)S(1)} collective-permute-done((bf16[96,640]{1,0:T(8,128)(2,1)S(1)}, bf16[96,640]{1,0:T(8,128)(2,1)S(1)}, u32[]{:S(2)}, u32[]{:S(2)}) %collective-permute-start.14) | collective-permute-done | bytes 122912 | tf_op jit(solution)/shard_map/ppermute | solution.py:355
  169.7 4.7 %collective-permute-start.17 = (bf16[96,640]{1,0:T(8,128)(2,1)S(1)}, bf16[96,640]{1,0:T(8,128)(2,1)S(1)}, u32[]{:S(2)}, u32[]{:S(2)}) collective-permute-start(bf16[96,640]{1,0:T(8,128)(2,1)S(1)} %get-tuple-element.49), channel_id=1, source_target_pairs={{0,32},{4,36},{8,40},{12,44},{16,48},{20,52},{24,56},{28,60},{32,0... | collective-permute-start | bytes 368648 | tf_op jit(solution)/shard_map/ppermute | solution.py:359
  174.8 1.7 collective-permute-done.16.refs_1_
  176.5 8.8 %collective-permute-done.17.refs_2_ = bf16[96,640]{1,0:T(8,128)(2,1)S(1)} collective-permute-done((bf16[96,640]{1,0:T(8,128)(2,1)S(1)}, bf16[96,640]{1,0:T(8,128)(2,1)S(1)}, u32[]{:S(2)}, u32[]{:S(2)}) %collective-permute-start.17) | collective-permute-done | bytes 122912 | tf_op jit(solution)/shard_map/ppermute | solution.py:359
  187.0 1.6 convert_multiply_fusion
  (84 shorter events, 14.2 us)
Async XLA Ops:
  11.7 9.2 %copy-start.4 = (f32[128,2]{0,1:T(2,128)S(1)}, f32[128,2]{0,1:T(2,128)}, u32[]{:S(2)}) copy-start(f32[128,2]{0,1:T(2,128)} %param.13) | copy-start | bytes 3076
  11.7 9.4 %copy-start.1 = (bf16[128,3584]{1,0:T(8,128)(2,1)S(1)}, bf16[128,3584]{1,0:T(8,128)(2,1)}, u32[]{:S(2)}) copy-start(bf16[128,3584]{1,0:T(8,128)(2,1)} %grad_ref.1) | copy-start | bytes 2752516
  11.7 14.6 %copy-start.2 = (s32[1,16,2]{1,2,0:T(2,128)S(1)}, s32[1,16,2]{1,2,0:T(2,128)}, u32[]{:S(2)}) copy-start(s32[1,16,2]{1,2,0:T(2,128)} %constant.141) | copy-start | bytes 388
  11.7 14.6 %copy-start.3 = (s32[1,16,2]{1,2,0:T(2,128)S(1)}, s32[1,16,2]{1,2,0:T(2,128)}, u32[]{:S(2)}) copy-start(s32[1,16,2]{1,2,0:T(2,128)} %constant.142) | copy-start | bytes 388
  11.7 34.8 %all-to-all-start = ((bf16[16,24,1280]{2,1,0:T(8,128)(2,1)}), bf16[16,24,1280]{2,1,0:T(8,128)(2,1)S(1)}, u32[]{:S(2)}, u32[]{:S(2)}) async-start(bf16[16,24,1280]{2,1,0:T(8,128)(2,1)} %bitcast.11), calls=%async_computation | async-start | bytes 1966080 | tf_op jit(solution)/shard_map/all_to_all | solution.py:284
  20.9 76.8 %all-gather.3.cloned.1.call-start = ((), (), s32[]{:S(2)}) async-start(), calls=%async_computation.5 | async-start | bytes 4915200 | tf_op jit(solution)/shard_map/all_gather | solution.py:311
  21.2 8.3 %collective-permute-start = (bf16[128,1024]{1,0:T(8,128)(2,1)S(1)}, bf16[128,1024]{1,0:T(8,128)(2,1)S(1)}, u32[]{:S(2)}, u32[]{:S(2)}) collective-permute-start(bf16[128,1024]{1,0:T(8,128)(2,1)S(1)} %get-tuple-element.29), channel_id=1, source_target_pairs={{0,4},{4,8},{8,12},{12,0},{16,20},{20,24},{24,28},{28,16},{32,36},... | collective-permute-start | bytes 786440 | tf_op jit(solution)/shard_map/ppermute | solution.py:272
  22.6 13.6 %collective-permute-start.1 = (bf16[128,1024]{1,0:T(8,128)(2,1)S(1)}, bf16[128,1024]{1,0:T(8,128)(2,1)S(1)}, u32[]{:S(2)}, u32[]{:S(2)}) collective-permute-start(bf16[128,1024]{1,0:T(8,128)(2,1)S(1)} %get-tuple-element.30), channel_id=1, source_target_pairs={{0,8},{4,12},{8,0},{12,4},{16,24},{20,28},{24,16},{28,20},{32,40},... | collective-permute-start | bytes 786440 | tf_op jit(solution)/shard_map/ppermute | solution.py:272
  25.2 11.0 %collective-permute-start.2 = (bf16[128,1024]{1,0:T(8,128)(2,1)S(1)}, bf16[128,1024]{1,0:T(8,128)(2,1)S(1)}, u32[]{:S(2)}, u32[]{:S(2)}) collective-permute-start(bf16[128,1024]{1,0:T(8,128)(2,1)S(1)} %get-tuple-element.31), channel_id=1, source_target_pairs={{0,12},{4,0},{8,4},{12,8},{16,28},{20,16},{24,20},{28,24},{32,44},... | collective-permute-start | bytes 786440 | tf_op jit(solution)/shard_map/ppermute | solution.py:272
  46.5 12.0 %copy-start.7 = (bf16[24,7168]{1,0:T(8,128)(2,1)S(1)}, bf16[24,7168]{1,0:T(8,128)(2,1)}, u32[]{:S(2)}) copy-start(bf16[24,7168]{1,0:T(8,128)(2,1)} %get-tuple-element.35) | copy-start | bytes 1032196
  46.5 14.4 %copy-start.6 = (bf16[24,7168]{1,0:T(8,128)(2,1)S(1)}, bf16[24,7168]{1,0:T(8,128)(2,1)}, u32[]{:S(2)}) copy-start(bf16[24,7168]{1,0:T(8,128)(2,1)} %get-tuple-element.36) | copy-start | bytes 1032196
  46.5 17.0 %copy-start.5 = (bf16[24,7168]{1,0:T(8,128)(2,1)S(1)}, bf16[24,7168]{1,0:T(8,128)(2,1)}, u32[]{:S(2)}) copy-start(bf16[24,7168]{1,0:T(8,128)(2,1)} %get-tuple-element.33) | copy-start | bytes 1032196
  48.2 102.2 %reduce-scatter.2.cloned.1.call-start = ((), (), s32[]{:S(2)}) async-start(), calls=%async_computation.4 | async-start | bytes 4915200 | tf_op jit(solution)/shard_map/reduce_scatter | solution.py:348
  48.2 10.3 %collective-permute-start.10 = (bf16[24,7168]{1,0:T(8,128)(2,1)}, bf16[24,7168]{1,0:T(8,128)(2,1)S(1)}, u32[]{:S(2)}, u32[]{:S(2)}) collective-permute-start(bf16[24,7168]{1,0:T(8,128)(2,1)} %get-tuple-element.39), channel_id=1, source_target_pairs={{0,64},{1,17},{2,66},{3,19},{4,68},{5,21},{6,70},{7,23},{8,72},{9,... | collective-permute-start | bytes 1032200 | tf_op jit(solution)/shard_map/ppermute | solution.py:312
  48.3 12.6 %collective-permute-start.11 = (bf16[24,7168]{1,0:T(8,128)(2,1)}, bf16[24,7168]{1,0:T(8,128)(2,1)S(1)}, u32[]{:S(2)}, u32[]{:S(2)}) collective-permute-start(bf16[24,7168]{1,0:T(8,128)(2,1)} %get-tuple-element.40), channel_id=1, source_target_pairs={{0,80},{1,193},{2,82},{3,195},{4,84},{5,197},{6,86},{7,199},{8,88}... | collective-permute-start | bytes 1032200 | tf_op jit(solution)/shard_map/ppermute | solution.py:312
  49.0 14.5 %collective-permute-start.8 = (bf16[24,7168]{1,0:T(8,128)(2,1)}, bf16[24,7168]{1,0:T(8,128)(2,1)S(1)}, u32[]{:S(2)}, u32[]{:S(2)}) collective-permute-start(bf16[24,7168]{1,0:T(8,128)(2,1)} %get-tuple-element.37), channel_id=1, source_target_pairs={{0,242},{1,33},{2,240},{3,35},{4,246},{5,37},{6,244},{7,39},{8,250... | collective-permute-start | bytes 1032200 | tf_op jit(solution)/shard_map/ppermute | solution.py:312
  51.3 18.9 %collective-permute-start.9 = (bf16[24,7168]{1,0:T(8,128)(2,1)S(1)}, bf16[24,7168]{1,0:T(8,128)(2,1)S(1)}, u32[]{:S(2)}, u32[]{:S(2)}) collective-permute-start(bf16[24,7168]{1,0:T(8,128)(2,1)S(1)} %copy-done.9), channel_id=1, source_target_pairs={{0,50},{1,209},{2,48},{3,211},{4,54},{5,213},{6,52},{7,215},{8,58}... | collective-permute-start | bytes 1032200 | tf_op jit(solution)/shard_map/ppermute | solution.py:312
  54.0 27.5 %collective-permute-start.4 = (bf16[24,7168]{1,0:T(8,128)(2,1)S(1)}, bf16[24,7168]{1,0:T(8,128)(2,1)S(1)}, u32[]{:S(2)}, u32[]{:S(2)}) collective-permute-start(bf16[24,7168]{1,0:T(8,128)(2,1)S(1)} %copy-done.8), channel_id=1, source_target_pairs={{0,160},{1,225},{2,162},{3,227},{4,164},{5,229},{6,166},{7,231},{8... | collective-permute-start | bytes 1032200 | tf_op jit(solution)/shard_map/ppermute | solution.py:312
  58.5 23.0 %collective-permute-start.5 = (bf16[24,7168]{1,0:T(8,128)(2,1)S(1)}, bf16[24,7168]{1,0:T(8,128)(2,1)S(1)}, u32[]{:S(2)}, u32[]{:S(2)}) collective-permute-start(bf16[24,7168]{1,0:T(8,128)(2,1)S(1)} %copy-done.7), channel_id=1, source_target_pairs={{0,96},{1,179},{2,98},{3,177},{4,100},{5,183},{6,102},{7,181},{8,1... | collective-permute-start | bytes 1032200 | tf_op jit(solution)/shard_map/ppermute | solution.py:312
  60.9 27.4 %collective-permute-start.6 = (bf16[24,7168]{1,0:T(8,128)(2,1)S(1)}, bf16[24,7168]{1,0:T(8,128)(2,1)S(1)}, u32[]{:S(2)}, u32[]{:S(2)}) collective-permute-start(bf16[24,7168]{1,0:T(8,128)(2,1)S(1)} %copy-done.6), channel_id=1, source_target_pairs={{0,144},{1,115},{2,146},{3,113},{4,148},{5,119},{6,150},{7,117},{8... | collective-permute-start | bytes 1032200 | tf_op jit(solution)/shard_map/ppermute | solution.py:312
  63.4 26.7 %collective-permute-start.3 = (bf16[24,7168]{1,0:T(8,128)(2,1)S(1)}, bf16[24,7168]{1,0:T(8,128)(2,1)S(1)}, u32[]{:S(2)}, u32[]{:S(2)}) collective-permute-start(bf16[24,7168]{1,0:T(8,128)(2,1)S(1)} %copy-done.5), channel_id=1, source_target_pairs={{0,0},{1,129},{2,2},{3,131},{4,4},{5,133},{6,6},{7,135},{8,8},{9,1... | collective-permute-start | bytes 1032200 | tf_op jit(solution)/shard_map/ppermute | solution.py:312
  70.3 20.3 %copy-start = (bf16[1,640,896]{2,1,0:T(8,128)(2,1)S(1)}, bf16[1,640,896]{2,1,0:T(8,128)(2,1)}, u32[]{:S(2)}) copy-start(bf16[1,640,896]{2,1,0:T(8,128)(2,1)} %param.15) | copy-start | bytes 3440644
  70.3 23.7 %collective-permute-start.12 = (bf16[96,7168]{1,0:T(8,128)(2,1)S(1)}, bf16[96,7168]{1,0:T(8,128)(2,1)S(1)}, u32[]{:S(2)}, u32[]{:S(2)}) collective-permute-start(bf16[96,7168]{1,0:T(8,128)(2,1)S(1)} %join.3.refs_1_.refs_3_), channel_id=1, source_target_pairs={{0,1},{1,0},{2,3},{3,2},{4,5},{5,4},{6,7},{7,6},{8,9},{9,8},{10,11... | collective-permute-start | bytes 4128776 | tf_op jit(solution)/shard_map/ppermute | solution.py:323
  90.3 3.7 %collective-permute-start.7 = (bf16[96,7168]{1,0:T(8,128)(2,1)S(1)}, bf16[96,7168]{1,0:T(8,128)(2,1)S(1)}, u32[]{:S(2)}, u32[]{:S(2)}) collective-permute-start(bf16[96,7168]{1,0:T(8,128)(2,1)S(1)} %join.2.refs_0_.refs_2_), channel_id=1, source_target_pairs={{0,1},{1,0},{2,3},{3,2},{4,5},{5,4},{6,7},{7,6},{8,9},{9,8},{10,11... | collective-permute-start | bytes 4128776 | tf_op jit(solution)/shard_map/ppermute | solution.py:323
  108.8 34.6 %all-to-all-start.1 = ((f16[16,40,896]{2,1,0:T(8,128)(2,1)}), f16[16,40,896]{2,1,0:T(8,128)(2,1)S(1)}, u32[]{:S(2)}, u32[]{:S(2)}) async-start(f16[16,40,896]{2,1,0:T(8,128)(2,1)} %bitcast.26), calls=%async_computation.2 | async-start | bytes 2293760 | tf_op jit(solution)/shard_map/all_to_all | solution.py:396
  145.4 41.6 %all-to-all-start.2 = ((f16[16,40,896]{2,1,0:T(8,128)(2,1)}), f16[16,40,896]{2,1,0:T(8,128)(2,1)S(1)}, u32[]{:S(2)}, u32[]{:S(2)}) async-start(f16[16,40,896]{2,1,0:T(8,128)(2,1)} %gather_fusion), calls=%async_computation.3 | async-start | bytes 2293760 | tf_op jit(solution)/shard_map/all_to_all | solution.py:397
  152.1 14.6 %collective-permute-start.13 = (bf16[96,640]{1,0:T(8,128)(2,1)S(1)}, bf16[96,640]{1,0:T(8,128)(2,1)S(1)}, u32[]{:S(2)}, u32[]{:S(2)}) collective-permute-start(bf16[96,640]{1,0:T(8,128)(2,1)S(1)} %get-tuple-element.44), channel_id=1, source_target_pairs={{0,64},{4,68},{8,72},{12,76},{16,80},{20,84},{24,88},{28,92},{32,9... | collective-permute-start | bytes 368648 | tf_op jit(solution)/shard_map/ppermute | solution.py:355
  153.5 15.8 %collective-permute-start.14 = (bf16[96,640]{1,0:T(8,128)(2,1)S(1)}, bf16[96,640]{1,0:T(8,128)(2,1)S(1)}, u32[]{:S(2)}, u32[]{:S(2)}) collective-permute-start(bf16[96,640]{1,0:T(8,128)(2,1)S(1)} %get-tuple-element.45), channel_id=1, source_target_pairs={{0,128},{4,132},{8,136},{12,140},{16,144},{20,148},{24,152},{28,15... | collective-permute-start | bytes 368648 | tf_op jit(solution)/shard_map/ppermute | solution.py:355
  155.9 13.6 %collective-permute-start.15 = (bf16[96,640]{1,0:T(8,128)(2,1)S(1)}, bf16[96,640]{1,0:T(8,128)(2,1)S(1)}, u32[]{:S(2)}, u32[]{:S(2)}) collective-permute-start(bf16[96,640]{1,0:T(8,128)(2,1)S(1)} %get-tuple-element.46), channel_id=1, source_target_pairs={{0,192},{4,196},{8,200},{12,204},{16,208},{20,212},{24,216},{28,22... | collective-permute-start | bytes 368648 | tf_op jit(solution)/shard_map/ppermute | solution.py:355
  169.6 6.9 %collective-permute-start.16 = (bf16[96,640]{1,0:T(8,128)(2,1)S(1)}, bf16[96,640]{1,0:T(8,128)(2,1)S(1)}, u32[]{:S(2)}, u32[]{:S(2)}) collective-permute-start(bf16[96,640]{1,0:T(8,128)(2,1)S(1)} %get-tuple-element.48), channel_id=1, source_target_pairs={{0,16},{4,20},{8,24},{12,28},{16,32},{20,36},{24,40},{28,44},{32,4... | collective-permute-start | bytes 368648 | tf_op jit(solution)/shard_map/ppermute | solution.py:359
  169.7 15.6 %collective-permute-start.17 = (bf16[96,640]{1,0:T(8,128)(2,1)S(1)}, bf16[96,640]{1,0:T(8,128)(2,1)S(1)}, u32[]{:S(2)}, u32[]{:S(2)}) collective-permute-start(bf16[96,640]{1,0:T(8,128)(2,1)S(1)} %get-tuple-element.49), channel_id=1, source_target_pairs={{0,32},{4,36},{8,40},{12,44},{16,48},{20,52},{24,56},{28,60},{32,0... | collective-permute-start | bytes 368648 | tf_op jit(solution)/shard_map/ppermute | solution.py:359
  174.4 10.9 %collective-permute-start.18 = (bf16[96,640]{1,0:T(8,128)(2,1)S(1)}, bf16[96,640]{1,0:T(8,128)(2,1)S(1)}, u32[]{:S(2)}, u32[]{:S(2)}) collective-permute-start(bf16[96,640]{1,0:T(8,128)(2,1)S(1)} %get-tuple-element.50), channel_id=1, source_target_pairs={{0,48},{4,52},{8,56},{12,60},{16,0},{20,4},{24,8},{28,12},{32,16},... | collective-permute-start | bytes 368648 | tf_op jit(solution)/shard_map/ppermute | solution.py:359
  (2 other events, 12.4 us)
Sparse Core Ops, SparseCore 0:
  48.3 47.8 all-gather.2
  98.7 47.5 reduce-scatter.1
